TPU v7x, 32 devices: a whole 2x2x4 slice. The times are simulated.
32 devices in a mesh: dp: 8 (over y, x, core), mp: 4 (over z).
Axes of the slice: x: 2, y: 2, z: 4, core: 2. Of those that a mesh axis runs over, the one named last changes fastest.
Arguments:
- images_in: bfloat16 [192, 50, 1024], P('dp'), may hold values from -6 to 6
- out_cotangent: bfloat16 [192, 50, 1024], P('dp'), may hold values from -6 to 6
- norm1_gain: float32 [2, 1024], replicated, may hold values from 0.5 to 1.5
- norm1_bias: float32 [2, 1024], replicated, may hold values from -3 to 3
- qkv_weight: bfloat16 [2, 1024, 3, 1024], P(None, None, None, 'mp'), may hold values from -0.1875 to 0.1875
- qv_bias: float32 [2, 2, 1024], P(None, None, 'mp'), may hold values from -3 to 3
- proj_weight: bfloat16 [2, 1024, 1024], P(None, 'mp'), may hold values from -0.375 to 0.375
- proj_bias: float32 [2, 1024], replicated, may hold values from -3 to 3
- norm2_gain: float32 [2, 1024], replicated, may hold values from 0.5 to 1.5
- norm2_bias: float32 [2, 1024], replicated, may hold values from -3 to 3
- fc1_weight: bfloat16 [2, 1024, 4096], P(None, None, 'mp'), may hold values from -0.1875 to 0.1875
- fc1_bias: float32 [2, 4096], P(None, 'mp'), may hold values from -3 to 3
- fc2_weight: bfloat16 [2, 4096, 1024], P(None, 'mp'), may hold values from -0.09375 to 0.09375
- fc2_bias: float32 [2, 1024], replicated, may hold values from -3 to 3
Outputs:
- block_out: bfloat16 [192, 50, 1024], P('dp')
- input_grad: float32 [192, 50, 1024], P('dp')
- grad_norm1_gain: float32 [2, 1024], replicated
- grad_norm1_bias: float32 [2, 1024], replicated
- grad_qkv_weight: float32 [2, 1024, 3, 1024], P(None, 'dp', None, 'mp')
- grad_qv_bias: float32 [2, 2, 1024], P(None, None, 'mp')
- grad_proj_weight: float32 [2, 1024, 1024], P(None, 'mp', 'dp')
- grad_proj_bias: float32 [2, 1024], replicated
- grad_norm2_gain: float32 [2, 1024], replicated
- grad_norm2_bias: float32 [2, 1024], replicated
- grad_fc1_weight: float32 [2, 1024, 4096], P(None, 'dp', 'mp')
- grad_fc1_bias: float32 [2, 4096], P(None, 'mp')
- grad_fc2_weight: float32 [2, 4096, 1024], P(None, 'mp', 'dp')
- grad_fc2_bias: float32 [2, 1024], replicated
All inputs are finite; a program needn't handle non-finite values.
Results may differ from a plain program's by a relative error of at most 0.025.
Values may be sent and summed in bfloat16 or wider, within the bound.
No kernel may reach another device: no remote copies, remote signals or barrier semaphores. Data moves between devices by JAX's collectives and lax.ppermute only.
A program may use at most 192 MiB of HBM per device.

v0:
```python
import jax
import jax.numpy as jnp
from jax import lax
from jax.sharding import PartitionSpec as P

HEAD_DIM = 64


EPS = 1e-06


def gelu_exact(values):
    return jax.nn.gelu(values, approximate=False)


def norm_forward(rows, gain, bias):
    mean = jnp.mean(rows, axis=-1, keepdims=True)
    centered = rows - mean
    variance = jnp.mean(centered * centered, axis=-1, keepdims=True)
    inverse = lax.rsqrt(variance + EPS)
    scaled = centered * inverse
    return (scaled * gain + bias, scaled, inverse)


def norm_backward(grad, scaled, inverse, gain):
    grad_gain = jnp.sum(grad * scaled, axis=0)
    grad_bias = jnp.sum(grad, axis=0)
    inner = grad * gain
    mean_inner = jnp.mean(inner, axis=-1, keepdims=True)
    mean_proj = jnp.mean(inner * scaled, axis=-1, keepdims=True)
    return (inverse * (inner - mean_inner - scaled * mean_proj), grad_gain, grad_bias)


def attention_scores(query4, key4):
    scale = HEAD_DIM ** (-0.5)
    return jnp.einsum("bqhe,bkhe->bhqk", query4, key4, preferred_element_type=jnp.float32) * scale


def attention_forward(normed_b, wqkv, bqv, images, seq):
    qkv = jnp.einsum("nd,dtc->ntc", normed_b, wqkv, preferred_element_type=jnp.float32)
    query = (qkv[:, 0] + bqv[0]).astype(jnp.bfloat16)
    key = qkv[:, 1].astype(jnp.bfloat16)
    value = (qkv[:, 2] + bqv[1]).astype(jnp.bfloat16)
    count, cols = query.shape
    shape4 = (images, seq, cols // HEAD_DIM, HEAD_DIM)
    query4 = query.reshape(shape4)
    key4 = key.reshape(shape4)
    value4 = value.reshape(shape4)
    scores = attention_scores(query4, key4)
    top = jnp.max(scores, axis=-1, keepdims=True)
    expo = jnp.exp(scores - top)
    total = jnp.sum(expo, axis=-1, keepdims=True)
    probs = (expo / total).astype(jnp.bfloat16)
    logsum = top + jnp.log(total)
    mixed = jnp.einsum("bhqk,bkhe->bqhe", probs, value4, preferred_element_type=jnp.float32)
    return (query4, key4, value4, logsum, mixed.reshape(count, cols).astype(jnp.bfloat16))


def attention_backward(grad_mixed, normed_b, wqkv, query4, key4, value4, logsum):
    scale = HEAD_DIM ** (-0.5)
    count, cols = grad_mixed.shape
    grad4 = grad_mixed.astype(jnp.bfloat16).reshape(query4.shape)
    probs = jnp.exp(attention_scores(query4, key4) - logsum)
    probs_b = probs.astype(jnp.bfloat16)
    grad_probs = jnp.einsum("bqhe,bkhe->bhqk", grad4, value4, preferred_element_type=jnp.float32)
    grad_value = jnp.einsum(
        "bhqk,bqhe->bkhe", probs_b, grad4, preferred_element_type=jnp.float32
    ).astype(jnp.bfloat16)
    grad_scores = probs * (grad_probs - jnp.sum(grad_probs * probs, axis=-1, keepdims=True))
    grad_scores = grad_scores.astype(jnp.bfloat16)
    grad_query = (
        jnp.einsum("bhqk,bkhe->bqhe", grad_scores, key4, preferred_element_type=jnp.float32) * scale
    ).astype(jnp.bfloat16)
    grad_key = (
        jnp.einsum("bhqk,bqhe->bkhe", grad_scores, query4, preferred_element_type=jnp.float32)
        * scale
    ).astype(jnp.bfloat16)
    grad_qkv = jnp.stack(
        [
            grad_query.reshape(count, cols),
            grad_key.reshape(count, cols),
            grad_value.reshape(count, cols),
        ],
        axis=1,
    )
    grad_bqv = jnp.stack(
        [
            jnp.sum(grad_qkv[:, 0].astype(jnp.float32), axis=0),
            jnp.sum(grad_qkv[:, 2].astype(jnp.float32), axis=0),
        ]
    )
    grad_wqkv = jnp.einsum("nd,ntc->dtc", normed_b, grad_qkv, preferred_element_type=jnp.float32)
    grad_normed = jnp.einsum("ntc,dtc->nd", grad_qkv, wqkv, preferred_element_type=jnp.float32)
    return (grad_wqkv, grad_bqv, grad_normed)


def on_device(
    images_in,
    out_cotangent,
    norm1_gain,
    norm1_bias,
    qkv_weight,
    qv_bias,
    proj_weight,
    proj_bias,
    norm2_gain,
    norm2_bias,
    fc1_weight,
    fc1_bias,
    fc2_weight,
    fc2_bias,
):
    images, seq, width = images_in.shape
    count = images * seq
    layers = qkv_weight.shape[0]
    stream = images_in.reshape(count, width).astype(jnp.float32)
    saved = []
    for layer in range(layers):
        normed, scaled1, inverse1 = norm_forward(stream, norm1_gain[layer], norm1_bias[layer])
        normed_b = normed.astype(jnp.bfloat16)
        query4, key4, value4, logsum, mixed = attention_forward(
            normed_b, qkv_weight[layer], qv_bias[layer], images, seq
        )
        partial_out = jnp.dot(mixed, proj_weight[layer], preferred_element_type=jnp.float32)
        attended = lax.psum(partial_out.astype(jnp.bfloat16), "mp").astype(jnp.float32)
        middle = stream + attended + proj_bias[layer]
        normed2, scaled2, inverse2 = norm_forward(middle, norm2_gain[layer], norm2_bias[layer])
        normed2_b = normed2.astype(jnp.bfloat16)
        hidden = (
            jnp.dot(normed2_b, fc1_weight[layer], preferred_element_type=jnp.float32)
            + fc1_bias[layer]
        )
        active = gelu_exact(hidden).astype(jnp.bfloat16)
        partial_mlp = jnp.dot(active, fc2_weight[layer], preferred_element_type=jnp.float32)
        mlp_out = lax.psum(partial_mlp.astype(jnp.bfloat16), "mp").astype(jnp.float32)
        saved.append(
            (
                scaled1,
                inverse1,
                normed_b,
                query4,
                key4,
                value4,
                logsum,
                mixed,
                scaled2,
                inverse2,
                normed2_b,
                hidden,
                active,
            )
        )
        stream = middle + mlp_out + fc2_bias[layer]
    block_out = stream.reshape(images, seq, width).astype(jnp.bfloat16)
    grad = out_cotangent.reshape(count, width).astype(jnp.float32)
    big_grads = [None] * layers
    small_grads = [None] * layers
    for layer in reversed(range(layers)):
        (
            scaled1,
            inverse1,
            normed_b,
            query4,
            key4,
            value4,
            logsum,
            mixed,
            scaled2,
            inverse2,
            normed2_b,
            hidden,
            active,
        ) = saved[layer]
        grad_b = grad.astype(jnp.bfloat16)
        g_fc2_bias = jnp.sum(grad, axis=0)
        g_fc2 = jnp.einsum("nf,nd->fd", active, grad_b, preferred_element_type=jnp.float32)
        g_active = jnp.einsum(
            "nd,fd->nf", grad_b, fc2_weight[layer], preferred_element_type=jnp.float32
        )
        unused, gelu_pull = jax.vjp(gelu_exact, hidden)
        g_hidden = gelu_pull(g_active)[0].astype(jnp.bfloat16)
        g_fc1_bias = jnp.sum(g_hidden.astype(jnp.float32), axis=0)
        g_fc1 = jnp.einsum("nd,nf->df", normed2_b, g_hidden, preferred_element_type=jnp.float32)
        part_two = jnp.einsum(
            "nf,df->nd", g_hidden, fc1_weight[layer], preferred_element_type=jnp.float32
        )
        g_normed2 = lax.psum(part_two.astype(jnp.bfloat16), "mp").astype(jnp.float32)
        g_from_norm2, g_gain2, g_bias2 = norm_backward(
            g_normed2, scaled2, inverse2, norm2_gain[layer]
        )
        grad_mid = grad + g_from_norm2
        grad_mid_b = grad_mid.astype(jnp.bfloat16)
        g_proj_bias = jnp.sum(grad_mid, axis=0)
        g_proj = jnp.einsum("nc,nd->cd", mixed, grad_mid_b, preferred_element_type=jnp.float32)
        g_mixed = jnp.einsum(
            "nd,cd->nc", grad_mid_b, proj_weight[layer], preferred_element_type=jnp.float32
        )
        g_wqkv, g_bqv, part_one = attention_backward(
            g_mixed, normed_b, qkv_weight[layer], query4, key4, value4, logsum
        )
        g_normed1 = lax.psum(part_one.astype(jnp.bfloat16), "mp").astype(jnp.float32)
        g_from_norm1, g_gain1, g_bias1 = norm_backward(
            g_normed1, scaled1, inverse1, norm1_gain[layer]
        )
        grad = grad_mid + g_from_norm1
        layer_big = (g_wqkv, g_proj, g_fc1, g_fc2)
        layer_small = (
            g_gain1,
            g_bias1,
            g_bqv,
            g_proj_bias,
            g_gain2,
            g_bias2,
            g_fc1_bias,
            g_fc2_bias,
        )
        big_grads[layer] = layer_big
        small_grads[layer] = layer_small
    stacked_big = [
        jnp.stack([big_grads[index][item] for index in range(layers)]) for item in range(4)
    ]
    stacked_small = [
        jnp.stack([small_grads[index][item] for index in range(layers)]) for item in range(8)
    ]
    stacked_big = (
        lax.psum_scatter(stacked_big[0], "dp", scatter_dimension=1, tiled=True),
        lax.psum_scatter(stacked_big[1], "dp", scatter_dimension=2, tiled=True),
        lax.psum_scatter(stacked_big[2], "dp", scatter_dimension=1, tiled=True),
        lax.psum_scatter(stacked_big[3], "dp", scatter_dimension=2, tiled=True),
    )
    stacked_small = lax.psum(
        (
            stacked_small[0],
            stacked_small[1],
            stacked_small[2],
            stacked_small[3],
            stacked_small[4],
            stacked_small[5],
            stacked_small[6],
            stacked_small[7],
        ),
        "dp",
    )
    input_grad = grad.reshape(images, seq, width)
    return (
        block_out,
        input_grad,
        stacked_small[0],
        stacked_small[1],
        stacked_big[0],
        stacked_small[2],
        stacked_big[1],
        stacked_small[3],
        stacked_small[4],
        stacked_small[5],
        stacked_big[2],
        stacked_small[6],
        stacked_big[3],
        stacked_small[7],
    )


def solution(mesh):
    return jax.shard_map(
        on_device,
        mesh=mesh,
        in_specs=(
            P("dp", None, None),
            P("dp", None, None),
            P(),
            P(),
            P(None, None, None, "mp"),
            P(None, None, "mp"),
            P(None, "mp", None),
            P(),
            P(),
            P(),
            P(None, None, "mp"),
            P(None, "mp"),
            P(None, "mp", None),
            P(),
        ),
        out_specs=(
            P("dp", None, None),
            P("dp", None, None),
            P(),
            P(),
            P(None, "dp", None, "mp"),
            P(None, None, "mp"),
            P(None, "mp", "dp"),
            P(),
            P(),
            P(),
            P(None, "dp", "mp"),
            P(None, "mp"),
            P(None, "mp", "dp"),
            P(),
        ),
        check_vma=False,
    )
```

profile of v0, /device:TPU:0, one launch (start us, length us, event | category | flops | bytes accessed | tf_op | source)
XLA Modules:
  0.0 1274.9 jit_solution(11473632347433378090)
XLA Ops:
  12.9 2.9 copy.80
  15.8 4.7 reshape.249
  20.5 4.2 fusion.89
  28.2 3.3 squeeze.49
  31.5 3.2 squeeze.50
  34.7 3.1 multiply_reduce_fusion.7
  43.5 3.6 convolution_convert_fusion.5
  47.1 3.9 copy.79
  51.0 6.1 reshape.248
  57.2 91.5 %all-reduce.10.cloned.1.call-done = bf16[1200,1024]{1,0:T(8,128)(2,1)} async-done(((bf16[1200,1024]{1,0:T(8,128)(2,1)}), bf16[1200,1024]{1,0:T(8,128)(2,1)}) %all-reduce.10.cloned.1.call-update) | async-done | bytes 2457616 | tf_op jit(solution)/shard_map/psum | solution.py:125
  148.8 3.9 fusion.159
  153.4 3.3 copy-done.86
  156.6 15.7 %multiply_convert_fusion.1 = (bf16[1200,1024]{1,0:T(8,128)(2,1)S(1)}, f32[1200,1024]{1,0:T(8,128)}, f32[1200,1024]{1,0:T(8,128)}) fusion(f32[1024]{0:T(1024)S(1)} %bitcast.227, bf16[2,1024,1024]{2,1,0:T(8,128)(2,1)S(1)} %copy-done.86, f32[1200,1024]{1,0:T(8,128)S(1)} %get-tuple-element.101, f32[1024]{0:T(1024)S(1)} %bitcast.220, f32[1024]{0:T(1024)S(1)} %bitcast.196, ...), kind=kOutput, calls=%fused_computation.80 | convolution fusion | flops 2603827200 | bytes 19329024 | tf_op jit(solution)/shard_map/dot_general | solution.py:130
  172.4 4.0 convolution_convert_fusion.4
  177.4 97.0 %all-reduce.12.cloned.1.call-done = bf16[1200,1024]{1,0:T(8,128)(2,1)} async-done(((bf16[1200,1024]{1,0:T(8,128)(2,1)}), bf16[1200,1024]{1,0:T(8,128)(2,1)}) %all-reduce.12.cloned.1.call-update) | async-done | bytes 2457616 | tf_op jit(solution)/shard_map/psum | solution.py:135
  274.4 3.9 fusion.157
  279.0 3.0 copy-done.92
  291.2 3.1 multiply_reduce_fusion.6
  300.0 3.6 convolution_convert_fusion.3
  303.6 4.6 copy.91
  308.2 4.7 reshape.244
  312.9 88.6 %all-reduce.14.cloned.1.call-done = bf16[1200,1024]{1,0:T(8,128)(2,1)} async-done(((bf16[1200,1024]{1,0:T(8,128)(2,1)}), bf16[1200,1024]{1,0:T(8,128)(2,1)}) %all-reduce.14.cloned.1.call-update) | async-done | bytes 2457616 | tf_op jit(solution)/shard_map/psum | solution.py:125
  401.6 3.9 fusion.156
  406.2 3.3 copy-done.87
  409.5 14.7 %multiply_convert_fusion = (bf16[1200,1024]{1,0:T(8,128)(2,1)}, f32[1200,1024]{1,0:T(8,128)S(1)}, f32[1200,1024]{1,0:T(8,128)S(1)}) fusion(f32[1024]{0:T(1024)S(1)} %bitcast.226, bf16[2,1024,1024]{2,1,0:T(8,128)(2,1)S(1)} %copy-done.87, f32[1200,1024]{1,0:T(8,128)S(1)} %get-tuple-element.95, f32[1024]{0:T(1024)S(1)} %bitcast.222, f32[1024]{0:T(1024)S(1)} %bitcast.188, ...), kind=kOutput, calls=%fused_computation.61 | convolution fusion | flops 2603827200 | bytes 19329024 | tf_op jit(solution)/shard_map/dot_general | solution.py:130
  424.1 5.3 convert_reduce_fusion.5
  430.8 4.1 convolution_convert_fusion.1
  435.0 97.9 %all-reduce.16.cloned.1.call-done = bf16[1200,1024]{1,0:T(8,128)(2,1)} async-done(((bf16[1200,1024]{1,0:T(8,128)(2,1)}), bf16[1200,1024]{1,0:T(8,128)(2,1)}) %all-reduce.16.cloned.1.call-update) | async-done | bytes 2457616 | tf_op jit(solution)/shard_map/psum | solution.py:187
  532.9 4.8 fusion.30
  537.8 4.6 fusion.153
  547.1 3.4 multiply_reduce_fusion.5
  566.0 4.9 bitcast_convert_fusion.1
  571.0 98.0 %all-reduce.18.cloned.1.call-done = bf16[1200,1024]{1,0:T(8,128)(2,1)} async-done(((bf16[1200,1024]{1,0:T(8,128)(2,1)}), bf16[1200,1024]{1,0:T(8,128)(2,1)}) %all-reduce.18.cloned.1.call-update) | async-done | bytes 2457616 | tf_op jit(solution)/shard_map/psum | solution.py:201
  668.9 5.9 fusion.31
  674.9 5.6 fusion.149
  680.5 6.3 convert_reduce_fusion.6
  686.8 5.9 convolution_convert_fusion
  692.9 5.6 convolution_convert_fusion.2
  698.5 92.3 %all-reduce.20.cloned.1.call-done = bf16[1200,1024]{1,0:T(8,128)(2,1)} async-done(((bf16[1200,1024]{1,0:T(8,128)(2,1)}), bf16[1200,1024]{1,0:T(8,128)(2,1)}) %all-reduce.20.cloned.1.call-update) | async-done | bytes 2457616 | tf_op jit(solution)/shard_map/psum | solution.py:187
  790.8 5.4 fusion.32
  796.2 5.1 fusion.151
  806.2 3.4 multiply_reduce_fusion.4
  824.0 5.0 bitcast_convert_fusion
  830.0 3.3 convolution_bitcast_fusion.5
  833.3 3.8 convolution_bitcast_fusion.6
  839.4 5.3 convolution_bitcast_fusion.4
  847.4 3.4 pad_maximum_fusion.2
  852.7 4.8 convolution_bitcast_fusion
  857.5 5.0 convolution_bitcast_fusion.1
  862.5 4.1 pad_maximum_fusion.1
  867.3 6.6 convolution_bitcast_fusion.2
  873.9 5.1 convolution_bitcast_fusion.3
  879.1 4.1 pad_maximum_fusion
  885.7 121.1 %all-reduce.22.cloned.1.call-done = (bf16[1200,1024]{1,0:T(8,128)(2,1)}, bf16[1200,1024]{1,0:T(8,128)(2,1)}) async-done(((bf16[1200,1024]{1,0:T(8,128)(2,1)}, bf16[1200,1024]{1,0:T(8,128)(2,1)}), (bf16[1200,1024]{1,0:T(8,128)(2,1)}, bf16[1200,1024]{1,0:T(8,128)(2,1)})) %all-reduce.22.cloned.1.call-update) | async-done | bytes 4915216 | tf_op jit(solution)/shard_map/psum | solution.py:135
  1006.8 5.5 add_convert_fusion.3
  1012.4 2.8 convert_element_type.273
  1018.0 5.0 fusion.33
  1023.1 4.9 fusion.14
  1028.0 5.8 reshape.247
  1033.8 7.7 copy.109
  1041.5 25.5 %all-reduce = (f32[2,1024]{1,0:T(2,128)}, f32[2,1024]{1,0:T(2,128)}, f32[2,2,256]{2,1,0:T(2,128)}, f32[2,1024]{1,0:T(2,128)}, f32[2,1024]{1,0:T(2,128)}, /*index...) all-reduce(f32[2,1024]{1,0:T(2,128)S(1)} %pad_maximum_fusion.4, ...), channel_id=1, replica_groups=mesh['dp'=8,'mp'=4] {'dp'}, use_global_device_ids=true, to_apply=%region_32.0 | all-reduce | flops 15360 | bytes 122880 | tf_op jit(solution)/shard_map/psum | solution.py:231
  1067.0 50.3 %reduce-scatter.5.cloned.1.call-done = f32[2,128,3,256]{3,1,2,0:T(8,128)} async-done(((f32[2,1024,3,256]{3,1,2,0:T(8,128)}), f32[2,128,3,256]{3,1,2,0:T(8,128)}) %reduce-scatter.5.cloned.1.call-update) | async-done | bytes 786448 | tf_op jit(solution)/shard_map/reduce_scatter | solution.py:226
  1117.3 75.6 %reduce-scatter.11.cloned.1.call-done = f32[2,1024,128]{2,1,0:T(8,128)} async-done(((f32[2,1024,1024]{2,1,0:T(8,128)}), f32[2,1024,128]{2,1,0:T(8,128)}) %reduce-scatter.11.cloned.1.call-update) | async-done | bytes 1048592 | tf_op jit(solution)/shard_map/reduce_scatter | solution.py:229
  1192.9 75.4 %reduce-scatter.9.cloned.1.call-done = f32[2,128,1024]{2,1,0:T(8,128)} async-done(((f32[2,1024,1024]{2,1,0:T(8,128)}), f32[2,128,1024]{2,1,0:T(8,128)}) %reduce-scatter.9.cloned.1.call-update) | async-done | bytes 1048592 | tf_op jit(solution)/shard_map/reduce_scatter | solution.py:228
  (340 shorter events, 87.3 us)
Async XLA Ops:
  7.2 141.6 %all-reduce.10.cloned.1.call-start = ((), (), s32[]{:S(2)}) async-start(), calls=%async_computation.4 | async-start | bytes 4915200 | tf_op jit(solution)/shard_map/psum | solution.py:125
  8.9 270.1 %copy-start.77 = (f32[1,1024]{1,0:T(1,128)}, f32[1,1024]{1,0:T(1,128)S(1)}, u32[]{:S(2)}) copy-start(f32[1,1024]{1,0:T(1,128)S(1)} %get-tuple-element.116) | copy-start | bytes 12292
  26.6 8.1 copy-start.55
  26.6 12.0 copy-start.72
  47.1 227.3 %all-reduce.12.cloned.1.call-start = ((), (), s32[]{:S(2)}) async-start(), calls=%async_computation.5 | async-start | bytes 4915200 | tf_op jit(solution)/shard_map/psum | solution.py:135
  51.0 6.1 copy-start.67
  51.0 6.1 copy-start.68
  51.0 6.1 copy-start.69
  51.0 6.2 copy-start.70
  57.2 96.2 %copy-start.53 = (f32[1,1024]{1,0:T(1,128)}, f32[1,1024]{1,0:T(1,128)S(1)}, u32[]{:S(2)}) copy-start(f32[1,1024]{1,0:T(1,128)S(1)} %get-tuple-element.109) | copy-start | bytes 12292
  57.2 96.2 %copy-start.79 = (f32[1,1024]{1,0:T(1,128)}, f32[1,1024]{1,0:T(1,128)S(1)}, u32[]{:S(2)}) copy-start(f32[1,1024]{1,0:T(1,128)S(1)} %get-tuple-element.111) | copy-start | bytes 12292
  57.2 348.9 %copy-start.81 = (f32[1,1024]{1,0:T(1,128)}, f32[1,1024]{1,0:T(1,128)S(1)}, u32[]{:S(2)}) copy-start(f32[1,1024]{1,0:T(1,128)S(1)} %get-tuple-element.110) | copy-start | bytes 12292
  152.7 19.7 %copy-start = (f32[1200,1024]{1,0:T(8,128)}, f32[1200,1024]{1,0:T(8,128)S(1)}, u32[]{:S(2)}) copy-start(f32[1200,1024]{1,0:T(8,128)S(1)} %get-tuple-element.101) | copy-start | bytes 14745604
  152.7 19.6 %copy-start.47 = (f32[1200]{0:T(1024)}, f32[1200]{0:T(1024)S(1)}, u32[]{:S(2)}) copy-start(f32[1200]{0:T(1024)S(1)} %broadcast_multiply_fusion.11) | copy-start | bytes 14404
  153.4 19.0 %copy-start.49 = (f32[1200]{0:T(1024)}, f32[1200]{0:T(1024)S(1)}, u32[]{:S(2)}) copy-start(f32[1200]{0:T(1024)S(1)} %add_rsqrt_fusion.3) | copy-start | bytes 14404
  156.6 15.7 %copy-start.89 = (bf16[2,1024,1024]{2,1,0:T(8,128)(2,1)S(1)}, bf16[2,1024,1024]{2,1,0:T(8,128)(2,1)}, u32[]{:S(2)}) copy-start(bf16[2,1024,1024]{2,1,0:T(8,128)(2,1)} %param.26) | copy-start | bytes 12582916
  176.4 225.2 %all-reduce.14.cloned.1.call-start = ((), (), s32[]{:S(2)}) async-start(), calls=%async_computation.6 | async-start | bytes 4915200 | tf_op jit(solution)/shard_map/psum | solution.py:125
  176.7 118.4 %copy-start.74 = (f32[4,64]{1,0:T(4,128)}, f32[4,64]{1,0:T(4,128)S(1)}, u32[]{:S(2)}) copy-start(f32[4,64]{1,0:T(4,128)S(1)} %add.292) | copy-start | bytes 3076
  176.8 114.3 %copy-start.57 = (f32[4,64]{1,0:T(4,128)}, f32[4,64]{1,0:T(4,128)S(1)}, u32[]{:S(2)}) copy-start(f32[4,64]{1,0:T(4,128)S(1)} %add.295) | copy-start | bytes 3076
  278.3 6.1 copy-start.2
  303.6 229.3 %all-reduce.16.cloned.1.call-start = ((), (), s32[]{:S(2)}) async-start(), calls=%async_computation.7 | async-start | bytes 4915200 | tf_op jit(solution)/shard_map/psum | solution.py:187
  405.5 18.7 %copy-start.1 = (f32[1200,1024]{1,0:T(8,128)}, f32[1200,1024]{1,0:T(8,128)S(1)}, u32[]{:S(2)}) copy-start(f32[1200,1024]{1,0:T(8,128)S(1)} %get-tuple-element.95) | copy-start | bytes 14745604
  409.5 14.7 %copy-start.15 = (bf16[1200,1024]{1,0:T(8,128)(2,1)S(1)}, bf16[1200,1024]{1,0:T(8,128)(2,1)}, u32[]{:S(2)}) copy-start(bf16[1200,1024]{1,0:T(8,128)(2,1)} %reshape.244) | copy-start | bytes 7372804
  409.5 14.7 %copy-start.90 = (bf16[2,1024,1024]{2,1,0:T(8,128)(2,1)S(1)}, bf16[2,1024,1024]{2,1,0:T(8,128)(2,1)}, u32[]{:S(2)}) copy-start(bf16[2,1024,1024]{2,1,0:T(8,128)(2,1)} %param.26) | copy-start | bytes 12582916
  435.0 234.0 %all-reduce.18.cloned.1.call-start = ((), (), s32[]{:S(2)}) async-start(), calls=%async_computation.8 | async-start | bytes 4915200 | tf_op jit(solution)/shard_map/psum | solution.py:201
  532.9 4.9 copy-start.18
  537.8 6.9 copy-start.31
  570.9 219.8 %all-reduce.20.cloned.1.call-start = ((), (), s32[]{:S(2)}) async-start(), calls=%async_computation.9 | async-start | bytes 4915200 | tf_op jit(solution)/shard_map/psum | solution.py:187
  668.9 5.9 copy-start.22
  668.9 11.5 slice-start.4
  668.9 11.5 slice-start.6
  674.9 5.6 copy-start.91
  674.9 5.6 slice-start.5
  674.9 5.6 slice-start.7
  680.5 6.3 copy-start.10
  680.5 6.3 copy-start.88
  686.8 6.0 copy-start.38
  686.8 6.0 copy-start.46
  686.8 6.0 copy-start.95
  692.7 314.1 %all-reduce.22.cloned.1.call-start = ((), (), s32[]{:S(2)}) async-start(), calls=%async_computation.14 | async-start | bytes 9830400 | tf_op jit(solution)/shard_map/psum | solution.py:135
  692.9 97.9 %copy-start.48 = (f32[1200]{0:T(1024)S(1)}, f32[1200]{0:T(1024)}, u32[]{:S(2)}) copy-start(f32[1200]{0:T(1024)} %copy-done.47) | copy-start | bytes 14404
  692.9 97.9 %copy-start.50 = (f32[1200]{0:T(1024)S(1)}, f32[1200]{0:T(1024)}, u32[]{:S(2)}) copy-start(f32[1200]{0:T(1024)} %copy-done.49) | copy-start | bytes 14404
  692.9 97.9 %copy-start.54 = (f32[1,1024]{1,0:T(1,128)S(1)}, f32[1,1024]{1,0:T(1,128)}, u32[]{:S(2)}) copy-start(f32[1,1024]{1,0:T(1,128)} %copy-done.53) | copy-start | bytes 12292
  790.8 5.4 copy-start.21
  796.2 7.6 copy-start.32
  801.3 4.9 copy-start.6
  801.3 4.9 copy-start.73
  829.0 238.0 %reduce-scatter.7.cloned.1.call-start = ((), (), s32[]{:S(2)}) async-start(), calls=%async_computation.11 | async-start | bytes 2359296 | tf_op jit(solution)/shard_map/reduce_scatter | solution.py:227
  837.1 7.5 slice-start
  838.6 278.7 %reduce-scatter.5.cloned.1.call-start = ((), (), s32[]{:S(2)}) async-start(), calls=%async_computation.10 | async-start | bytes 7077888 | tf_op jit(solution)/shard_map/reduce_scatter | solution.py:226
  839.4 5.3 slice-start.1
  839.4 5.3 copy-start.44
  839.4 5.3 copy-start.52
  839.4 5.3 copy-start.61
  850.9 341.9 %reduce-scatter.11.cloned.1.call-start = ((), (), s32[]{:S(2)}) async-start(), calls=%async_computation.13 | async-start | bytes 9437184 | tf_op jit(solution)/shard_map/reduce_scatter | solution.py:229
  866.6 7.3 copy-start.80
  866.6 7.3 copy-start.96
  866.6 401.6 %reduce-scatter.9.cloned.1.call-start = ((), (), s32[]{:S(2)}) async-start(), calls=%async_computation.12 | async-start | bytes 9437184 | tf_op jit(solution)/shard_map/reduce_scatter | solution.py:228
  883.2 123.7 %copy-start.59 = (f32[1,1024]{1,0:T(1,128)S(1)}, f32[1,1024]{1,0:T(1,128)}, u32[]{:S(2)}) copy-start(f32[1,1024]{1,0:T(1,128)} %get-tuple-element.106) | copy-start | bytes 12292
  1012.4 10.6 slice-start.2
  1015.2 7.8 slice-start.3
  1018.0 5.0 copy-start.20
  1033.8 7.7 copy-start.63
  1033.8 7.7 copy-start.62
  (53 other events, 139.1 us)
Sparse Core Ops, SparseCore 0:
  47.2 101.4 all-reduce.9
  176.5 97.8 all-reduce.11
  303.7 97.8 all-reduce.13
  435.1 97.8 all-reduce.15
  571.1 97.8 all-reduce.17
  692.9 97.8 all-reduce.19
  829.1 177.6 all-reduce.21
  1011.0 40.3 reduce-scatter.6
  1055.4 61.8 reduce-scatter.4
  1121.5 71.2 reduce-scatter.10
  1196.9 71.2 reduce-scatter.8
where the time goes:
time: 1280 us; the launch traced here: 1270 us
  waiting for transfers between devices  888 us (69%)
  matrix products  149 us (12%)
  local copies, waits for them, and re-layouts  114 us (9%)
  other arithmetic  81.3 us (6%)
  blocking collectives  25.5 us (2%)
  between operations  15.6 us (1%)
    psum x2, waiting for transfers between devices, on_device(): lax.psum(partial_mlp.astype(jnp.bfloat16), 'mp').astype(jnp.float32)  218 us
    psum x2, waiting for transfers between devices, on_device(): lax.psum(part_two.astype(jnp.bfloat16), 'mp').astype(jnp.float32)  190 us
    psum x2, waiting for transfers between devices, on_device(): lax.psum(partial_out.astype(jnp.bfloat16), 'mp').astype(jnp.float32)  180 us
    psum x1, waiting for transfers between devices, on_device(): lax.psum(part_one.astype(jnp.bfloat16), 'mp').astype(jnp.float32)  98 us
    reduce_scatter x1, waiting for transfers between devices, on_device(): lax.psum_scatter(stacked_big[3], 'dp', scatter_dimension=2, tiled=True)  75.6 us
    reduce_scatter x1, waiting for transfers between devices, on_device(): lax.psum_scatter(stacked_big[2], 'dp', scatter_dimension=1, tiled=True)  75.4 us
    reduce_scatter x1, waiting for transfers between devices, on_device(): lax.psum_scatter(stacked_big[0], 'dp', scatter_dimension=1, tiled=True)  50.3 us
    unnamed x219, local copies, waits for them, and re-layouts  41.1 us
  transfers between devices with their start and end apart: 11, of which 10 were waited for; matrix products, arithmetic and copies ran while one was open for 9% of the time, Pallas kernels for 0%

commit v1 on v0

v1 whole, which is shorter than its diff:
```python
import functools

import jax
import jax.numpy as jnp
from jax import lax
from jax.experimental import pallas as pl
from jax.experimental.pallas import tpu as pltpu
from jax.sharding import PartitionSpec as P

HEAD_DIM = 64
EPS = 1e-06
F32 = jnp.float32
BF16 = jnp.bfloat16
ROWS = 304
WIN = 112
WIN_STEP = 96
BIG_NEG = -1e30
VMEM_LIMIT = 60 * 1024 * 1024


def dot_nn(a, b):
    return lax.dot_general(a, b, (((1,), (0,)), ((), ())), preferred_element_type=F32)


def dot_nt(a, b):
    return lax.dot_general(a, b, (((1,), (1,)), ((), ())), preferred_element_type=F32)


def dot_tn(a, b):
    return lax.dot_general(a, b, (((0,), (0,)), ((), ())), preferred_element_type=F32)


def params(micros):
    return dict(
        compiler_params=pltpu.CompilerParams(vmem_limit_bytes=VMEM_LIMIT),
        cost_estimate=pl.CostEstimate(
            flops=int(micros * 1e9), bytes_accessed=0, transcendentals=0
        ),
    )


VM = pl.BlockSpec(memory_space=pltpu.VMEM)
SM = pl.BlockSpec(memory_space=pltpu.SMEM)
HB = pl.BlockSpec(memory_space=pl.ANY)


def layer_norm(x, gain, bias):
    mean = jnp.mean(x, axis=-1, keepdims=True)
    centered = x - mean
    variance = jnp.mean(centered * centered, axis=-1, keepdims=True)
    return centered * lax.rsqrt(variance + EPS) * gain + bias


def own_selector(place, seq, mine):
    images = 4 * mine
    row = lax.broadcasted_iota(jnp.int32, (ROWS, images * seq), 0)
    col = lax.broadcasted_iota(jnp.int32, (ROWS, images * seq), 1)
    token = col // images
    image = col - token * images - place[DEPTH] * mine
    hit = (image >= 0) & (image < mine) & (row == image * seq + token)
    return jnp.where(hit, 1.0, 0.0).astype(BF16)


def enter_kernel(seq, mine, place, x_ref, gain_ref, beta_ref, x1_ref, a_ref):
    x = dot_nn(own_selector(place, seq, mine), x_ref[...])
    x1_ref[...] = x
    a_ref[...] = layer_norm(x, gain_ref[...], beta_ref[...]).astype(BF16)


def enter_back_kernel(seq, mine, place, x_ref, g_ref, gb_ref, sum_ref):
    g = dot_nn(own_selector(place, seq, mine), x_ref[...])
    g_ref[...] = g
    gb_ref[...] = g.astype(BF16)
    sum_ref[...] = jnp.broadcast_to(jnp.sum(g, axis=0, keepdims=True), sum_ref.shape)


def leave_kernel(seq, mine, parts_ref, out_ref):
    images = 4 * mine
    count = images * seq
    total = None
    for depth in range(4):
        row = lax.broadcasted_iota(jnp.int32, (count, ROWS), 0)
        col = lax.broadcasted_iota(jnp.int32, (count, ROWS), 1)
        token = row // images
        image = row - token * images - depth * mine
        hit = (image >= 0) & (image < mine) & (col == image * seq + token)
        part = dot_nn(jnp.where(hit, 1.0, 0.0).astype(BF16), parts_ref[depth])
        total = part if total is None else total + part
    out_ref[...] = total.astype(out_ref.dtype)


def residual_norm_kernel(
    x_ref, own_ref, far_ref, bias_ref, gain_ref, beta_ref, x1_ref, a_ref
):
    keep = lax.broadcasted_iota(jnp.int32, (ROWS, 1), 0) < 300
    bias = jnp.where(keep, bias_ref[...], 0.0)
    x1 = x_ref[...] + own_ref[...].astype(F32) + far_ref[...].astype(F32) + bias
    x1_ref[...] = x1
    a_ref[...] = layer_norm(x1, gain_ref[...], beta_ref[...]).astype(BF16)


def residual_kernel(x_ref, own_ref, far_ref, bias_ref, x1_ref):
    x1 = x_ref[...] + own_ref[...].astype(F32) + far_ref[...].astype(F32) + bias_ref[...]
    x1_ref[...] = x1.astype(BF16)


def norm_back_kernel(g_ref, own_ref, far_ref, x_ref, gain_ref, g1_ref, g1b_ref, sums_ref):
    x = x_ref[...]
    mean = jnp.mean(x, axis=-1, keepdims=True)
    centered = x - mean
    variance = jnp.mean(centered * centered, axis=-1, keepdims=True)
    inverse = lax.rsqrt(variance + EPS)
    xhat = centered * inverse
    da = own_ref[...].astype(F32) + far_ref[...].astype(F32)
    inner = da * gain_ref[...]
    mean_inner = jnp.mean(inner, axis=-1, keepdims=True)
    mean_proj = jnp.mean(inner * xhat, axis=-1, keepdims=True)
    g1 = g_ref[...] + inverse * (inner - mean_inner - xhat * mean_proj)
    g1_ref[...] = g1
    g1b_ref[...] = g1.astype(BF16)
    sums_ref[...] = jnp.zeros(sums_ref.shape, F32)
    sums_ref[0:1, :] = jnp.sum(da * xhat, axis=0, keepdims=True)
    sums_ref[1:2, :] = jnp.sum(da, axis=0, keepdims=True)
    sums_ref[2:3, :] = jnp.sum(g1, axis=0, keepdims=True)


def run_enter(place, images, mine, gain, beta):
    count, seq, width = images.shape
    flat = images.transpose(1, 0, 2).reshape(count * seq, width)
    return pl.pallas_call(
        functools.partial(enter_kernel, seq, mine),
        out_shape=(
            jax.ShapeDtypeStruct((ROWS, width), F32),
            jax.ShapeDtypeStruct((ROWS, width), BF16),
        ),
        in_specs=[SM, VM, VM, VM],
        out_specs=(VM, VM),
        **params(5),
    )(place, flat, gain[None], beta[None])


def run_enter_back(place, images, mine):
    count, seq, width = images.shape
    flat = images.transpose(1, 0, 2).reshape(count * seq, width)
    return pl.pallas_call(
        functools.partial(enter_back_kernel, seq, mine),
        out_shape=(
            jax.ShapeDtypeStruct((ROWS, width), F32),
            jax.ShapeDtypeStruct((ROWS, width), BF16),
            jax.ShapeDtypeStruct((8, width), F32),
        ),
        in_specs=[SM, VM],
        out_specs=(VM, VM, VM),
        **params(5),
    )(place, flat)


def run_leave(parts, seq, mine, dtype):
    images, width = 4 * mine, parts.shape[2]
    flat = pl.pallas_call(
        functools.partial(leave_kernel, seq, mine),
        out_shape=jax.ShapeDtypeStruct((images * seq, width), dtype),
        in_specs=[VM],
        out_specs=VM,
        **params(6),
    )(parts)
    return flat.reshape(seq, images, width).transpose(1, 0, 2)


def run_residual_norm(x, own, far, bias, gain, beta):
    return pl.pallas_call(
        residual_norm_kernel,
        out_shape=(
            jax.ShapeDtypeStruct(x.shape, F32),
            jax.ShapeDtypeStruct(x.shape, BF16),
        ),
        in_specs=[VM] * 6,
        out_specs=(VM, VM),
        **params(3),
    )(x, own, far, bias[None], gain[None], beta[None])


def run_residual(x, own, far, bias):
    return pl.pallas_call(
        residual_kernel,
        out_shape=jax.ShapeDtypeStruct(x.shape, BF16),
        in_specs=[VM] * 4,
        out_specs=VM,
        **params(2),
    )(x, own, far, bias[None])


def run_norm_back(g, own, far, x, gain):
    return pl.pallas_call(
        norm_back_kernel,
        out_shape=(
            jax.ShapeDtypeStruct(x.shape, F32),
            jax.ShapeDtypeStruct(x.shape, BF16),
            jax.ShapeDtypeStruct((8, x.shape[1]), F32),
        ),
        in_specs=[VM] * 5,
        out_specs=(VM, VM, VM),
        **params(4),
    )(g, own, far, x, gain[None])


SIDE, CORE, PAIR, DEPTH, PARTS = 0, 1, 2, 3, 4


def exact_rows(bias):
    high = bias.astype(BF16)
    rest = bias - high.astype(F32)
    mid = rest.astype(BF16)
    low = (rest - mid.astype(F32)).astype(BF16)
    return jnp.concatenate([high, mid, low, jnp.zeros((13, bias.shape[1]), BF16)], axis=0)


def pack_kernel(
    place, wqkv, wproj, w1, w2, bqv, b1, attn0, mlp0, attn1, mlp1, sems
):
    row = aligned(place[PARTS], 256)
    narrow, wide = aligned(place[PAIR], 128), aligned(place[PAIR], 512)
    copies = []
    for layer, (attn, mlp) in enumerate(((attn0, mlp0), (attn1, mlp1))):
        for item in range(3):
            copies.append(
                (
                    wqkv.at[layer, item, pl.ds(row, 256), pl.ds(narrow, 128)],
                    attn.at[0:256, pl.ds(item * 128, 128)],
                )
            )
        for half in range(2):
            copies.append(
                (
                    wproj.at[layer, pl.ds(narrow, 128), pl.ds(row + half * 128, 128)],
                    attn.at[pl.ds(half * 128, 128), 384:512],
                )
            )
            copies.append(
                (
                    w2.at[layer, pl.ds(wide + half * 256, 256), pl.ds(row, 256)],
                    mlp.at[256:512, pl.ds(half * 256, 256)],
                )
            )
        copies.append(
            (w1.at[layer, pl.ds(row, 256), pl.ds(wide, 512)], mlp.at[0:256, :])
        )
    copies = [
        pltpu.make_async_copy(src, dst, sems.at[index])
        for index, (src, dst) in enumerate(copies)
    ]
    for copy in copies:
        copy.start()
    for layer, (attn, mlp) in enumerate(((attn0, mlp0), (attn1, mlp1))):
        zero = jnp.zeros((1, 128), F32)
        bias = [bqv[layer, pl.ds(item, 1), pl.ds(narrow, 128)] for item in range(2)]
        attn[256:272, :] = exact_rows(jnp.concatenate([bias[0], zero, bias[1], zero], axis=1))
        mlp[512:528, :] = exact_rows(b1[pl.ds(layer, 1), pl.ds(wide, 512)])
    for copy in copies:
        copy.wait()


def run_pack(place, wqkv, wproj, w1, w2, bqv, b1):
    attn = jax.ShapeDtypeStruct((272, 512), BF16)
    mlp = jax.ShapeDtypeStruct((528, 512), BF16)
    return pl.pallas_call(
        pack_kernel,
        out_shape=(attn, mlp, attn, mlp),
        in_specs=[SM, HB, HB, HB, HB, VM, VM],
        out_specs=(VM, VM, VM, VM),
        scratch_shapes=[pltpu.SemaphoreType.DMA((16,))],
        **params(3),
    )(place, wqkv, wproj, w1, w2, bqv, b1)


def piece_sources(place, pieces, chunk):
    return [
        (src, place[PARTS + slot]) for slot, src in enumerate(pieces[4 * chunk - 4 : 4 * chunk])
    ]


def aligned(index, step):
    if isinstance(index, int):
        return index * step
    return pl.multiple_of(index * step, step)


def start_attention_copies(layer, place, wqkv, wproj, bqv, pieces, wq, wp, sems, bs=None):
    narrow = aligned(place[PAIR], 128)
    for item in range(3):
        pltpu.make_async_copy(
            wqkv.at[layer, item, :, pl.ds(narrow, 128)],
            wq.at[0, :, pl.ds(item * 128, 128)],
            sems.at[0, 0],
        ).start()
    pltpu.make_async_copy(
        wproj.at[layer, pl.ds(narrow, 128), :], wp.at[0], sems.at[1, 0]
    ).start()
    for chunk in range(1, 4):
        for slot, (src, index) in enumerate(piece_sources(place, pieces, chunk)):
            row = aligned(index, 256)
            pltpu.make_async_copy(
                src.at[0:256, 0:384], wq.at[chunk, pl.ds(row, 256), :], sems.at[0, chunk]
            ).start()
            for side in range(2):
                pltpu.make_async_copy(
                    src.at[pl.ds(side * 128, 128), 384:512],
                    wp.at[chunk, :, pl.ds(row + side * 128, 128)],
                    sems.at[1, chunk],
                ).start()
            if bs is not None and slot == 0:
                pltpu.make_async_copy(
                    src.at[256:272, 0:384], bs.at[chunk], sems.at[2, chunk]
                ).start()
    if bs is not None:
        bias = [bqv[layer, pl.ds(item, 1), pl.ds(narrow, 128)] for item in range(2)]
        zero = jnp.zeros((1, 128), F32)
        bs[0] = exact_rows(jnp.concatenate([bias[0], zero, bias[1]], axis=1))


def start_mlp_copies(layer, place, first, second, bias, pieces, w1, w2, sems, bs=None):
    wide = aligned(place[PAIR], 512)
    pltpu.make_async_copy(first.at[layer, :, pl.ds(wide, 512)], w1.at[0], sems.at[0, 0]).start()
    pltpu.make_async_copy(second.at[layer, pl.ds(wide, 512), :], w2.at[0], sems.at[1, 0]).start()
    for chunk in range(1, 4):
        for slot, (src, index) in enumerate(piece_sources(place, pieces, chunk)):
            row = aligned(index, 256)
            pltpu.make_async_copy(
                src.at[0:256, :], w1.at[chunk, pl.ds(row, 256), :], sems.at[0, chunk]
            ).start()
            for side in range(2):
                pltpu.make_async_copy(
                    src.at[256:512, pl.ds(side * 256, 256)],
                    w2.at[chunk, pl.ds(side * 256, 256), pl.ds(row, 256)],
                    sems.at[1, chunk],
                ).start()
            if bs is not None and slot == 0:
                pltpu.make_async_copy(
                    src.at[512:528, :], bs.at[chunk], sems.at[2, chunk]
                ).start()
    if bs is not None:
        bs[0] = exact_rows(bias[layer : layer + 1, pl.ds(wide, 512)])


def start_rows(own, far, rows, sems):
    copies = [
        pltpu.make_async_copy(own, rows.at[0:ROWS, :], sems.at[3, 0]),
        pltpu.make_async_copy(far, rows.at[pl.ds(ROWS, ROWS), :], sems.at[3, 1]),
    ]
    for copy in copies:
        copy.start()
    return copies


def wait_all(copies):
    for copy in copies:
        copy.wait()


def wait_chunk(chunk, bufs, sems):
    for slot, buf in enumerate(bufs):
        pltpu.make_async_copy(buf.at[chunk], buf.at[chunk], sems.at[slot, chunk]).wait()


def wait_bias(chunk, bs, sems):
    @pl.when(chunk > 0)
    def _():
        pltpu.make_async_copy(bs.at[chunk], bs.at[chunk], sems.at[2, chunk]).wait()


def window_masks(window):
    shape = (2 * WIN, WIN)
    row = lax.broadcasted_iota(jnp.int32, shape, 0)
    row = jnp.where(row >= WIN, row - WIN, row) - 4 * window
    col = lax.broadcasted_iota(jnp.int32, shape, 1) - 4 * window
    row_ok = (row >= 0) & (row < 100)
    col_ok = (col >= 0) & (col < 100)
    same = row_ok & col_ok & ((row >= 50) == (col >= 50))
    return jnp.where(same, 0.0, BIG_NEG).astype(F32)


def window_rows_ok(window):
    row = lax.broadcasted_iota(jnp.int32, (2 * WIN, 1), 0)
    row = jnp.where(row >= WIN, row - WIN, row) - 4 * window
    return (row >= 0) & (row < 100)


def stack_heads(values, first):
    zero = jnp.zeros_like(values)
    return jnp.concatenate(
        [jnp.where(first, values, zero), jnp.where(first, zero, values)], axis=0
    )


def first_head_lanes():
    return lax.broadcasted_iota(jnp.int32, (WIN, 2 * HEAD_DIM), 1) < HEAD_DIM


def window_probs(query, key, mask, rows_ok):
    scores = dot_nt(query, key) * (HEAD_DIM**-0.5) + mask
    top = jnp.max(scores, axis=-1, keepdims=True)
    expo = jnp.exp(scores - top)
    total = jnp.sum(expo, axis=-1, keepdims=True)
    return expo * jnp.where(rows_ok, 1.0 / total, 0.0)


def join_windows(parts):
    first, second, third = parts
    over = WIN - WIN_STEP
    return jnp.concatenate(
        [
            first[:WIN_STEP],
            first[WIN_STEP:] + second[:over],
            second[over:WIN_STEP],
            second[WIN_STEP:] + third[:over],
            third[over:],
        ],
        axis=0,
    )


def attention_forward_kernel(
    layer, place, a_own, a_far, wqkv, wproj, bqv, *refs
):
    pieces = refs[:12]
    qkv_ref, o_ref, r_own, r_far, wq, wp, bs, rows, total, masks, sems = refs[12:]
    copies = start_rows(a_own, a_far, rows, sems)
    start_attention_copies(layer, place, wqkv, wproj, bqv, pieces, wq, wp, sems, bs)
    for window in range(3):
        masks[window] = window_masks(window)
    wait_all(copies)

    def chunk_step(chunk, carry):
        wait_chunk(chunk, (wq, wp), sems)
        wait_bias(chunk, bs, sems)
        bias = jnp.sum(bs[chunk].astype(F32), axis=0, keepdims=True)
        qkv_ref[chunk] = (dot_nn(rows[...], wq[chunk]) + bias).astype(BF16)
        first = first_head_lanes()
        for block in range(2):
            outs = []
            for window in range(3):
                span = pl.ds(block * ROWS + window * WIN_STEP, WIN)
                query = stack_heads(qkv_ref[chunk, span, 0:128], first)
                probs = window_probs(
                    query, qkv_ref[chunk, span, 128:256], masks[window], window_rows_ok(window)
                )
                mixed = dot_nn(probs.astype(BF16), qkv_ref[chunk, span, 256:384])
                outs.append(jnp.where(first, mixed[:WIN], mixed[WIN:]))
            o_ref[chunk, pl.ds(block * ROWS, ROWS), :] = join_windows(outs).astype(BF16)
        part = dot_nn(o_ref[chunk], wp[chunk])

        @pl.when(chunk == 0)
        def _():
            total[...] = part

        @pl.when(chunk > 0)
        def _():
            total[...] += part

        return carry

    lax.fori_loop(0, 4, chunk_step, 0)
    r_own[...] = total[0:ROWS, :].astype(BF16)
    r_far[...] = total[ROWS:, :].astype(BF16)


def run_attention_forward(layer, place, a_own, a_far, weights, pieces):
    rows, width = 2 * ROWS, a_own.shape[1]
    return pl.pallas_call(
        functools.partial(attention_forward_kernel, layer),
        out_shape=(
            jax.ShapeDtypeStruct((4, rows, 384), BF16),
            jax.ShapeDtypeStruct((4, rows, 128), BF16),
            jax.ShapeDtypeStruct((ROWS, width), BF16),
            jax.ShapeDtypeStruct((ROWS, width), BF16),
        ),
        in_specs=[SM, HB, HB, HB, HB, VM] + [HB] * 12,
        out_specs=(VM, VM, VM, VM),
        scratch_shapes=[
            pltpu.VMEM((4, width, 384), BF16),
            pltpu.VMEM((4, 128, width), BF16),
            pltpu.VMEM((4, 16, 384), BF16),
            pltpu.VMEM((rows, width), BF16),
            pltpu.VMEM((rows, width), F32),
            pltpu.VMEM((3, 2 * WIN, WIN), F32),
            pltpu.SemaphoreType.DMA((4, 4)),
        ],
        **params(13),
    )(place, a_own, a_far, *weights, *pieces)


def attention_backward_kernel(
    layer, place, g_own, g_far, qkv_ref, wqkv, wproj, *refs
):
    pieces = refs[:12]
    dqkv_ref, sums_ref, d_own, d_far, wq, wp, rows, total, masks, gmix, sems = refs[12:]
    copies = start_rows(g_own, g_far, rows, sems)
    start_attention_copies(layer, place, wqkv, wproj, None, pieces, wq, wp, sems)
    for window in range(3):
        masks[window] = window_masks(window)
    wait_all(copies)

    def chunk_step(chunk, carry):
        wait_chunk(chunk, (wq, wp), sems)
        gmix[...] = dot_nt(rows[...], wp[chunk]).astype(BF16)
        first = first_head_lanes()
        scale = HEAD_DIM**-0.5
        sums = jnp.zeros((1, 384), F32)
        for block in range(2):
            outs = []
            for window in range(3):
                span = pl.ds(block * ROWS + window * WIN_STEP, WIN)
                query = stack_heads(qkv_ref[chunk, span, 0:128], first)
                key = qkv_ref[chunk, span, 128:256]
                grad = stack_heads(gmix[span, :], first)
                probs = window_probs(query, key, masks[window], window_rows_ok(window))
                gprobs = dot_nt(grad, qkv_ref[chunk, span, 256:384])
                gvalue = dot_tn(probs.astype(BF16), grad)
                inner = jnp.sum(gprobs * probs, axis=-1, keepdims=True)
                gscores = (probs * (gprobs - inner)).astype(BF16)
                gquery = dot_nn(gscores, key) * scale
                gkey = dot_tn(gscores, query) * scale
                outs.append((jnp.where(first, gquery[:WIN], gquery[WIN:]), gkey, gvalue))
            joined = jnp.concatenate(
                [join_windows([out[item] for out in outs]) for item in range(3)], axis=1
            ).astype(BF16)
            dqkv_ref[chunk, pl.ds(block * ROWS, ROWS), :] = joined
            sums += jnp.sum(joined.astype(F32), axis=0, keepdims=True)
        sums_ref[chunk] = jnp.broadcast_to(sums, (8, 384))
        part = dot_nt(dqkv_ref[chunk], wq[chunk])

        @pl.when(chunk == 0)
        def _():
            total[...] = part

        @pl.when(chunk > 0)
        def _():
            total[...] += part

        return carry

    lax.fori_loop(0, 4, chunk_step, 0)
    d_own[...] = total[0:ROWS, :].astype(BF16)
    d_far[...] = total[ROWS:, :].astype(BF16)


def run_attention_backward(layer, place, g_own, g_far, qkv, weights, pieces):
    rows, width = 2 * ROWS, g_own.shape[1]
    return pl.pallas_call(
        functools.partial(attention_backward_kernel, layer),
        out_shape=(
            jax.ShapeDtypeStruct((4, rows, 384), BF16),
            jax.ShapeDtypeStruct((4, 8, 384), F32),
            jax.ShapeDtypeStruct((ROWS, width), BF16),
            jax.ShapeDtypeStruct((ROWS, width), BF16),
        ),
        in_specs=[SM, HB, HB, VM, HB, HB] + [HB] * 12,
        out_specs=(VM, VM, VM, VM),
        scratch_shapes=[
            pltpu.VMEM((4, width, 384), BF16),
            pltpu.VMEM((4, 128, width), BF16),
            pltpu.VMEM((rows, width), BF16),
            pltpu.VMEM((rows, width), F32),
            pltpu.VMEM((3, 2 * WIN, WIN), F32),
            pltpu.VMEM((rows, 128), BF16),
            pltpu.SemaphoreType.DMA((4, 4)),
        ],
        **params(23),
    )(place, g_own, g_far, qkv, *weights[:2], *pieces)


def gelu_pair(u):
    size = jnp.abs(u) * (0.5**0.5)
    t = 1.0 / (1.0 + 0.3275911 * size)
    poly = t * (
        0.254829592
        + t * (-0.284496736 + t * (1.421413741 + t * (-1.453152027 + t * 1.061405429)))
    )
    bell = jnp.exp(-0.5 * u * u)
    tail = 0.5 * poly * bell
    phi = jnp.where(u >= 0.0, 1.0 - tail, tail)
    return u * phi, phi + u * bell * 0.3989422804014327


def mlp_forward_kernel(
    layer, place, a_own, a_far, first, second, bias_ref, *refs
):
    pieces = refs[:12]
    h_ref, slope_ref, m_own, m_far, w1, w2, bs, rows, total, sems = refs[12:]
    copies = start_rows(a_own, a_far, rows, sems)
    start_mlp_copies(layer, place, first, second, bias_ref, pieces, w1, w2, sems, bs)
    wait_all(copies)

    def chunk_step(chunk, carry):
        wait_chunk(chunk, (w1, w2), sems)
        wait_bias(chunk, bs, sems)
        bias = jnp.sum(bs[chunk].astype(F32), axis=0, keepdims=True)
        value, slope = gelu_pair(dot_nn(rows[...], w1[chunk]) + bias)
        h_ref[chunk] = value.astype(BF16)
        slope_ref[chunk] = slope.astype(BF16)
        part = dot_nn(h_ref[chunk], w2[chunk])

        @pl.when(chunk == 0)
        def _():
            total[...] = part

        @pl.when(chunk > 0)
        def _():
            total[...] += part

        return carry

    lax.fori_loop(0, 4, chunk_step, 0)
    m_own[...] = total[0:ROWS, :].astype(BF16)
    m_far[...] = total[ROWS:, :].astype(BF16)


def run_mlp_forward(layer, place, a_own, a_far, weights, pieces):
    rows, width = 2 * ROWS, a_own.shape[1]
    return pl.pallas_call(
        functools.partial(mlp_forward_kernel, layer),
        out_shape=(
            jax.ShapeDtypeStruct((4, rows, 512), BF16),
            jax.ShapeDtypeStruct((4, rows, 512), BF16),
            jax.ShapeDtypeStruct((ROWS, width), BF16),
            jax.ShapeDtypeStruct((ROWS, width), BF16),
        ),
        in_specs=[SM, HB, HB, HB, HB, VM] + [HB] * 12,
        out_specs=(VM, VM, VM, VM),
        scratch_shapes=[
            pltpu.VMEM((4, width, 512), BF16),
            pltpu.VMEM((4, 512, width), BF16),
            pltpu.VMEM((4, 16, 512), BF16),
            pltpu.VMEM((rows, width), BF16),
            pltpu.VMEM((rows, width), F32),
            pltpu.SemaphoreType.DMA((4, 4)),
        ],
        **params(17),
    )(place, a_own, a_far, *weights, *pieces)


def mlp_backward_kernel(
    layer, place, g_own, g_far, slope_ref, first, second, *refs
):
    pieces = refs[:12]
    du_ref, sums_ref, d_own, d_far, w1, w2, rows, total, sems = refs[12:]
    copies = start_rows(g_own, g_far, rows, sems)
    start_mlp_copies(layer, place, first, second, None, pieces, w1, w2, sems)
    wait_all(copies)

    def chunk_step(chunk, carry):
        wait_chunk(chunk, (w1, w2), sems)
        grad = dot_nt(rows[...], w2[chunk]) * slope_ref[chunk].astype(F32)
        grad = grad.astype(BF16)
        du_ref[chunk] = grad
        sums_ref[chunk] = jnp.broadcast_to(
            jnp.sum(grad.astype(F32), axis=0, keepdims=True), (8, 512)
        )
        part = dot_nt(du_ref[chunk], w1[chunk])

        @pl.when(chunk == 0)
        def _():
            total[...] = part

        @pl.when(chunk > 0)
        def _():
            total[...] += part

        return carry

    lax.fori_loop(0, 4, chunk_step, 0)
    d_own[...] = total[0:ROWS, :].astype(BF16)
    d_far[...] = total[ROWS:, :].astype(BF16)


def run_mlp_backward(layer, place, g_own, g_far, slope, weights, pieces):
    rows, width = 2 * ROWS, g_own.shape[1]
    return pl.pallas_call(
        functools.partial(mlp_backward_kernel, layer),
        out_shape=(
            jax.ShapeDtypeStruct((4, rows, 512), BF16),
            jax.ShapeDtypeStruct((4, 8, 512), F32),
            jax.ShapeDtypeStruct((ROWS, width), BF16),
            jax.ShapeDtypeStruct((ROWS, width), BF16),
        ),
        in_specs=[SM, HB, HB, VM, HB, HB] + [HB] * 12,
        out_specs=(VM, VM, VM, VM),
        scratch_shapes=[
            pltpu.VMEM((4, width, 512), BF16),
            pltpu.VMEM((4, 512, width), BF16),
            pltpu.VMEM((rows, width), BF16),
            pltpu.VMEM((rows, width), F32),
            pltpu.SemaphoreType.DMA((4, 4)),
        ],
        **params(13),
    )(place, g_own, g_far, slope, *weights[:2], *pieces)


def weight_grad_kernel(
    place, x1_own, x1_far, y1_ref, x2_own, x2_far, y2_ref,
    near_ref, away_ref, send_ref, rows, turned,
):
    span1 = y1_ref.shape[2]
    for index, (own, far) in enumerate(((x1_own, x1_far), (x2_own, x2_far))):
        rows[0:ROWS, :] = own[...]
        rows[ROWS:, :] = far[...]
        for c_side in range(2):
            for y_side in range(2):
                start = (place[SIDE] ^ y_side) * 512 + (place[CORE] ^ c_side) * 128
                start = pl.multiple_of(start, 128)
                cols = jnp.concatenate(
                    [rows[:, pl.ds(start, 128)], rows[:, pl.ds(start + 256, 128)]], axis=1
                )
                turned[index, 2 * c_side + y_side] = cols.T

    def chunk_step(chunk, carry):
        for slot, out in enumerate((near_ref, away_ref, send_ref.at[0], send_ref.at[1])):
            out[chunk, :, 0:span1] = dot_nn(turned[0, slot], y1_ref[chunk]).astype(BF16)
            out[chunk, :, span1:] = dot_nn(turned[1, slot], y2_ref[chunk]).astype(BF16)
        return carry

    lax.fori_loop(0, 4, chunk_step, 0)


def run_weight_grad(place, x1, y1, x2, y2):
    rows, width = 2 * ROWS, x1[0].shape[1]
    span = y1.shape[2] + y2.shape[2]
    half = jax.ShapeDtypeStruct((4, width // 4, span), BF16)
    both = jax.ShapeDtypeStruct((2, 4, width // 4, span), BF16)
    return pl.pallas_call(
        weight_grad_kernel,
        out_shape=(half, half, both),
        in_specs=[SM, VM, VM, VM, VM, VM, VM],
        out_specs=(VM, VM, VM),
        scratch_shapes=[
            pltpu.VMEM((rows, width), BF16),
            pltpu.VMEM((2, 4, width // 4, rows), BF16),
        ],
        **params(14),
    )(place, *x1, y1, *x2, y2)


def add_core_kernel(near, away, got, near_out, away_out):
    near_out[...] = (near[...].astype(F32) + got[0].astype(F32)).astype(BF16)
    away_out[...] = (away[...].astype(F32) + got[1].astype(F32)).astype(BF16)


def run_add_core(near, away, got):
    chunks, rows, span = near.shape
    one = pl.BlockSpec((1, rows, span), lambda step: (step, 0, 0))
    two = pl.BlockSpec((2, 1, rows, span), lambda step: (0, step, 0, 0))
    shape = jax.ShapeDtypeStruct(near.shape, BF16)
    return pl.pallas_call(
        add_core_kernel,
        grid=(chunks,),
        out_shape=(shape, shape),
        in_specs=[one, one, two],
        out_specs=(one, one),
        **params(4),
    )(near, away, got)


def add_side_kernel(near, got, *outs):
    for step, out in enumerate(outs):
        out[...] = (near[step].astype(F32) + got[step].astype(F32)).astype(out.dtype)


def run_add_side(near, got):
    chunks, rows, span = near.shape
    return pl.pallas_call(
        add_side_kernel,
        out_shape=tuple(
            jax.ShapeDtypeStruct((rows, span), BF16 if step else F32) for step in range(chunks)
        ),
        in_specs=[VM, VM],
        out_specs=(VM,) * chunks,
        **params(3),
    )(near, got)


def add_depth_kernel(place, first, second, third, fourth, stay, move):
    total = first[...]
    for part in (second, third, fourth):
        total += part[...].astype(F32)
    half = total.shape[0] // 2
    low, high = total[:half], total[half:]
    even = place[PAIR] == 0
    stay[...] = jnp.where(even, low, high).astype(BF16)
    move[...] = jnp.where(even, high, low).astype(BF16)


def run_add_depth(place, parts):
    rows, span = parts[0].shape
    shape = jax.ShapeDtypeStruct((rows // 2, span), BF16)
    return pl.pallas_call(
        add_depth_kernel,
        out_shape=(shape, shape),
        in_specs=[SM] + [VM] * 4,
        out_specs=(VM, VM),
        **params(2),
    )(place, *parts)


def finish_kernel(place, *refs):
    layers = (len(refs) - 4) // 4
    ins, (qkv, proj, fc1, fc2) = refs[: 4 * layers], refs[4 * layers :]
    for layer in range(layers):
        for side in range(2):
            attn, mlp = ins[4 * layer + side], ins[4 * layer + 2 + side]
            pair = place[PAIR] if side == 0 else 1 - place[PAIR]
            narrow, wide = aligned(pair, 128), aligned(pair, 512)
            for item in range(3):
                qkv[layer, item, :, pl.ds(narrow, 128)] = attn[
                    :, item * 128 : item * 128 + 128
                ].astype(F32)
            proj[layer, pl.ds(narrow, 128), :] = attn[:, 384:512].astype(F32).T
            fc1[layer, :, pl.ds(wide, 512)] = mlp[:, 0:512].astype(F32)
            fc2[layer, pl.ds(wide, 512), :] = mlp[:, 512:1024].astype(F32).T


def run_finish(place, parts):
    rows = parts[0].shape[0]
    return pl.pallas_call(
        finish_kernel,
        out_shape=(
            jax.ShapeDtypeStruct((2, 3, rows, 256), F32),
            jax.ShapeDtypeStruct((2, 256, rows), F32),
            jax.ShapeDtypeStruct((2, rows, 1024), F32),
            jax.ShapeDtypeStruct((2, 1024, rows), F32),
        ),
        in_specs=[SM] + [VM] * len(parts),
        out_specs=(VM,) * 4,
        **params(4),
    )(place, *parts)


def on_device(n_dp, n_mp, *args):
    (
        images_in, out_cotangent, norm1_gain, norm1_bias, qkv_weight, qv_bias, proj_weight,
        proj_bias, norm2_gain, norm2_bias, fc1_weight, fc1_bias, fc2_weight, fc2_bias,
    ) = args
    images, seq, width = images_in.shape
    layers = qkv_weight.shape[0]
    mine = images // n_mp
    count = mine * seq

    place = lax.axis_index("dp")
    depth = lax.axis_index("mp")
    core, pair, side = place & 1, (place >> 1) & 1, (place >> 2) & 1
    here = jnp.stack(
        [
            side, core, pair, depth,
            side * 2 + core, (1 - side) * 2 + core, side * 2 + 1 - core, (1 - side) * 2 + 1 - core,
        ]
    ).astype(jnp.int32)

    def swap(value, bit):
        return lax.ppermute(value, "dp", [(index, index ^ bit) for index in range(n_dp)])

    def shift(value, step):
        return lax.ppermute(
            value, "mp", [(index, (index + step) % n_mp) for index in range(n_mp)]
        )

    def after(value, *others):
        return lax.optimization_barrier((value, *others))[0]

    def shifts(piece):
        return {step: shift(piece, step) for step in (1, 3, 2)}

    def spread(gathered):
        out = []
        for step in range(1, n_mp):
            same = gathered[step]
            other = swap(same, 4)
            out += [same, other, swap(same, 1), swap(other, 1)]
        return out

    def sum_everywhere(value):
        for bit in range(n_dp.bit_length() - 1):
            value = value + swap(value, 1 << bit)
        for bit in range(n_mp.bit_length() - 1):
            pairs = [(index, index ^ (1 << bit)) for index in range(n_mp)]
            value = value + lax.ppermute(value, "mp", pairs)
        return value

    wqkv = qkv_weight.transpose(0, 2, 1, 3)
    attn_weights = (wqkv, proj_weight, qv_bias)
    mlp_weights = (fc1_weight, fc2_weight, fc1_bias)
    packed = run_pack(here, wqkv, proj_weight, fc1_weight, fc2_weight, qv_bias, fc1_bias)
    moved = shifts(packed[0])
    attn_pieces, mlp_pieces = [spread(moved)], []

    stream, normed = run_enter(here, images_in, mine, norm1_gain[0], norm1_bias[0])
    grad, grad_b, fc2_sum = run_enter_back(here, out_cotangent, mine)
    grad_b_far = swap(grad_b, 2)

    saved = []
    for layer in range(layers):
        moved = shifts(after(packed[2 * layer + 1], moved[2]))
        normed_far = swap(normed, 2)
        if layer == 0:
            normed = after(normed, moved[1], grad_b_far)
            mlp_pieces.append(spread(moved))
        qkv, mixed, own, away = run_attention_forward(
            layer, here, normed, normed_far, attn_weights, attn_pieces[layer]
        )
        if layer > 0:
            mlp_pieces.append(spread({step: after(moved[step], own) for step in moved}))
        middle, normed2 = run_residual_norm(
            stream, own, swap(away, 2), proj_bias[layer], norm2_gain[layer], norm2_bias[layer]
        )
        normed2_far = swap(normed2, 2)
        active, slope, own, away = run_mlp_forward(
            layer, here, normed2, normed2_far, mlp_weights, mlp_pieces[layer]
        )
        if layer + 1 < layers:
            moved = shifts(after(packed[2 * layer + 2], moved[2]))
            attn_pieces.append(spread({step: after(moved[step], own) for step in moved}))
        saved.append(
            (stream, (normed, normed_far), qkv, mixed, middle, (normed2, normed2_far), active, slope)
        )
        if layer + 1 < layers:
            stream, normed = run_residual_norm(
                middle, own, swap(away, 2), fc2_bias[layer], norm1_gain[layer + 1],
                norm1_bias[layer + 1],
            )
        else:
            last = run_residual(middle, own, swap(away, 2), fc2_bias[layer])
    block_out = run_leave(lax.all_gather(last, "mp"), seq, mine, BF16)

    class Sum:
        def start(self, x1, y1, x2, y2):
            self.near, self.away, send = run_weight_grad(here, x1, y1, x2, y2)
            self.got = swap(send, 1)
            return self.near

        def add_core(self):
            self.near, away = run_add_core(self.near, self.away, self.got)
            self.got = swap(away, 4)
            return self.near

        def add_side(self):
            parts = run_add_side(self.near, self.got)
            self.parts = [parts[0]] + [shift(parts[step], -step) for step in range(1, n_mp)]
            return parts[0]

        def add_depth(self):
            self.stay, move = run_add_depth(here, self.parts)
            if n_dp == 8:
                move = swap(move, 2)
            self.move = move
            return self.stay

    sums = {(layer, kind): Sum() for layer in range(layers) for kind in ("attn", "mlp")}
    small = [None] * layers
    fc2_sum = fc2_sum[0]
    for layer in reversed(range(layers)):
        stream, normed, qkv, mixed, middle, normed2, active, slope = saved[layer]
        mlp, attn = sums[layer, "mlp"], sums[layer, "attn"]
        upper_mlp, upper_attn = sums.get((layer + 1, "mlp")), sums.get((layer + 1, "attn"))
        if upper_attn:
            grad_b = after(grad_b, upper_attn.add_core())
        du, fc1_sum, own, away = run_mlp_backward(
            layer, here, grad_b, grad_b_far, slope, mlp_weights, mlp_pieces[layer]
        )
        waits = [mlp.start(normed2, du, (grad_b, grad_b_far), active)]
        if upper_attn:
            waits.append(upper_attn.add_side())
        grad, grad_b, sums2 = run_norm_back(
            after(grad, *waits), own, swap(away, 2), middle, norm2_gain[layer]
        )
        grad_b_far = swap(grad_b, 2)
        waits = [mlp.add_core()]
        if upper_mlp:
            waits.append(upper_mlp.add_depth())
        grad_b = after(grad_b, *waits)
        dqkv, qv_sum, own, away = run_attention_backward(
            layer, here, grad_b, grad_b_far, qkv, attn_weights, attn_pieces[layer]
        )
        waits = [attn.start(normed, dqkv, (grad_b, grad_b_far), mixed), mlp.add_side()]
        if upper_attn:
            waits.append(upper_attn.add_depth())
        grad, grad_b, sums1 = run_norm_back(
            after(grad, *waits), own, swap(away, 2), stream, norm1_gain[layer]
        )
        if layer:
            grad_b_far = swap(grad_b, 2)

        def by_quarter(value):
            quarter = lax.broadcasted_iota(jnp.int32, (n_mp, 1, 1), 0)
            half = lax.broadcasted_iota(jnp.int32, (1, 2, 1), 1)
            full = sum(
                jnp.where(quarter == (depth - step) % n_mp, value[step][None, None, :], 0.0)
                for step in range(n_mp)
            )
            return jnp.where(half == pair, full, 0.0)

        qv = qv_sum[:, 0]
        small[layer] = (
            jnp.stack([sums1[0], sums1[1], sums2[2], sums2[0], sums2[1], fc2_sum]),
            jnp.stack([by_quarter(qv[:, 0:128]), by_quarter(qv[:, 256:384])], axis=1),
            by_quarter(fc1_sum[:, 0]),
        )
        fc2_sum = sums1[2]

    input_grad = run_leave(lax.all_gather(grad_b, "mp"), seq, mine, F32)
    first = sums[0, "attn"]
    first.add_core()
    first.add_side()
    sums[0, "mlp"].add_depth()
    first.add_depth()

    stacked = [jnp.stack([small[layer][item] for layer in range(layers)]) for item in range(3)]
    flat = sum_everywhere(jnp.concatenate([part.reshape(-1, 128) for part in stacked]))
    ends = [part.size // 128 for part in stacked]
    rows = flat[: ends[0]].reshape(stacked[0].shape)
    qv = flat[ends[0] : ends[0] + ends[1]].reshape(stacked[1].shape)
    fc1 = flat[ends[0] + ends[1] :].reshape(stacked[2].shape)
    qv = lax.dynamic_index_in_dim(qv, depth, 1, keepdims=False).reshape(layers, 2, -1)
    fc1 = lax.dynamic_index_in_dim(fc1, depth, 1, keepdims=False).reshape(layers, -1)

    order = [sums[layer, kind] for layer in range(layers) for kind in ("attn", "mlp")]
    if n_dp == 8:
        parts = [part for item in order for part in (item.stay, item.move)]
    else:
        parts = [part for item in order for part in spread_rows(item, n_dp, place, pair)]
    g_qkv, g_proj, g_fc1, g_fc2 = run_finish(here, parts)
    return (
        block_out, input_grad, rows[:, 0], rows[:, 1], g_qkv.transpose(0, 2, 1, 3), qv, g_proj,
        rows[:, 2], rows[:, 3], rows[:, 4], g_fc1, fc1, g_fc2, rows[:, 5],
    )


def spread_rows(item, n_dp, place, pair):
    far = n_dp // 8
    value = jnp.stack(
        [jnp.where(pair == 0, item.stay, item.move), jnp.where(pair == 0, item.move, item.stay)]
    ).astype(F32)
    groups = [[8 * group + index for group in range(far)] for index in range(8)]
    value = lax.psum(value, "dp", axis_index_groups=groups)
    groups = [[8 * group + index for index in range(8)] for group in range(far)]
    value = lax.all_gather(value, "dp", axis_index_groups=groups)
    rows, span = value.shape[2:]
    value = value.reshape(2, 2, 2, 2, rows, span).transpose(0, 3, 2, 4, 1, 5)
    value = value.reshape(8 * rows, 2, span)
    value = lax.dynamic_slice_in_dim(value, place * (8 * rows // n_dp), 8 * rows // n_dp, 0)
    mine = lax.dynamic_index_in_dim(value, pair, 1, keepdims=False)
    other = lax.dynamic_index_in_dim(value, 1 - pair, 1, keepdims=False)
    return mine, other


def solution(mesh):
    n_dp, n_mp = mesh.shape["dp"], mesh.shape["mp"]
    return jax.shard_map(
        functools.partial(on_device, n_dp, n_mp),
        mesh=mesh,
        in_specs=(
            P("dp", None, None),
            P("dp", None, None),
            P(),
            P(),
            P(None, None, None, "mp"),
            P(None, None, "mp"),
            P(None, "mp", None),
            P(),
            P(),
            P(),
            P(None, None, "mp"),
            P(None, "mp"),
            P(None, "mp", None),
            P(),
        ),
        out_specs=(
            P("dp", None, None),
            P("dp", None, None),
            P(),
            P(),
            P(None, "dp", None, "mp"),
            P(None, None, "mp"),
            P(None, "mp", "dp"),
            P(),
            P(),
            P(),
            P(None, "dp", "mp"),
            P(None, "mp"),
            P(None, "mp", "dp"),
            P(),
        ),
        check_vma=False,
    )
```

time: 1280 us -> 850 us (0.66)
  waiting for transfers between devices: 888 us -> 369 us
  Pallas kernels: 0 us -> 289 us
  matrix products: 149 us -> 0 us
  starting transfers between devices: 1.25 us -> 126 us
  other arithmetic: 81.3 us -> 0.58 us
  local copies, waits for them, and re-layouts: 114 us -> 40.3 us
  blocking collectives: 25.5 us -> 0 us
    psum x7 -> x0, waiting for transfers between devices: 686 us -> none  [the longest x2 218 us: on_device(): lax.psum(partial_mlp.astype(jnp.bfloat16), 'mp').astype(jnp.float32)]
    ppermute x0 -> x93, waiting for transfers between devices: none -> 369 us  [the longest x24 164 us: shift(): lax.ppermute(value, 'mp', [(index, (index + step) % n_mp) for index in ra...]
    pallas_call x0 -> x38, Pallas kernels: none -> 289 us  [the longest x2 54.2 us: run_attention_backward(): pl.pallas_call(functools.partial(attention_backward_kernel, layer), out_s...]
    reduce_scatter x4 -> x0, waiting for transfers between devices: 201 us -> none  [the longest x1 75.6 us: on_device(): lax.psum_scatter(stacked_big[3], 'dp', scatter_dimension=2, tiled=True)]
    dot_general x36 -> x0, matrix products: 149 us -> none  [the longest x2 30.3 us: on_device(): jnp.dot(normed2_b, fc1_weight[layer], preferred_element_type=jnp.float32)]
    ppermute x0 -> x93, starting transfers between devices: none -> 126 us  [the longest x24 69.1 us: shift(): lax.ppermute(value, 'mp', [(index, (index + step) % n_mp) for index in ra...]
    reduce_sum x18 -> x0, other arithmetic: 55 us -> none  [the longest x4 21.1 us: norm_backward(): grad_gain = jnp.sum(grad * scaled, axis=0)]
    convert_element_type x17 -> x0, local copies, waits for them, and re-layouts: 36.7 us -> none  [the longest x2 9.96 us: on_device(): stream = images_in.reshape(count, width).astype(jnp.float32)]
  transfers between devices with their start and end apart: 11 -> 95, of which waited for: 10 -> 39; matrix products, arithmetic and copies ran while one was open for 9% -> 2% of each run, Pallas kernels for 0% -> 21%
where the time goes in v1:
time: 850 us; the launch traced here: 841 us
  waiting for transfers between devices  369 us (43%)
  Pallas kernels  289 us (34%)
  starting transfers between devices  126 us (15%)
  local copies, waits for them, and re-layouts  40.3 us (5%)
  between operations  15.5 us (2%)
    ppermute x24, waiting for transfers between devices, shift(): lax.ppermute(value, 'mp', [(index, (index + step) % n_mp) for index in ra...  164 us
    ppermute x67, waiting for transfers between devices, swap(): lax.ppermute(value, 'dp', [(index, index ^ bit) for index in range(n_dp)])  160 us
    ppermute x24, starting transfers between devices, shift(): lax.ppermute(value, 'mp', [(index, (index + step) % n_mp) for index in ra...  69.1 us
    pallas_call x2, Pallas kernels, run_attention_backward(): pl.pallas_call(functools.partial(attention_backward_kernel, layer), out_s...  54.2 us
    ppermute x67, starting transfers between devices, swap(): lax.ppermute(value, 'dp', [(index, index ^ bit) for index in range(n_dp)])  47.8 us
    pallas_call x4, Pallas kernels, run_weight_grad(): pl.pallas_call(weight_grad_kernel, out_shape=(half, half, both), in_specs...  46.5 us
    ppermute x2, waiting for transfers between devices, sum_everywhere(): value = value + lax.ppermute(value, 'mp', pairs)  45 us
    pallas_call x2, Pallas kernels, run_mlp_forward(): pl.pallas_call(functools.partial(mlp_forward_kernel, layer), out_shape=(j...  32.4 us
  transfers between devices with their start and end apart: 95, of which 39 were waited for; matrix products, arithmetic and copies ran while one was open for 2% of the time, Pallas kernels for 21%

profile of v1, /device:TPU:0, one launch (start us, length us, event | category | flops | bytes accessed | tf_op | source)
XLA Modules:
  0.0 840.6 jit_solution(3598953080731540273)
XLA Ops:
  7.9 3.5 shard_map.246
  11.4 4.1 collective-permute-start
  17.5 4.0 shard_map.247
  24.3 5.8 collective-permute-done.refs_4_
  30.1 5.2 collective-permute-start.1
  39.2 3.9 shard_map.245
  46.8 4.2 collective-permute-done.12.refs_9_
  50.9 4.6 collective-permute-done.5.refs_1_
  60.0 12.3 %shard_map.248 = (bf16[4,608,384]{2,1,0:T(8,128)(2,1)}, bf16[4,608,128]{2,1,0:T(8,128)(2,1)}, bf16[304,1024]{1,0:T(8,128)(2,1)}, bf16[304,1024]{1,0:T(8,128)(2,1)}) custom-call(s32[8]{0:T(128)} %stack.76.place, bf16[304,1024]{1,0:T(8,128)(2,1)} %get-tuple-element.143.a_own.x1_own, bf16[304,1024]{1,0:T(8,128)(2,1)} %copy-done.11, ...), custom_call_target="tpu_custom_call" | custom-call | flops 12999999488 | tf_op jit(solution)/shard_map/pallas_call | solution.py:469
  73.9 13.1 %collective-permute-start.20 = (bf16[528,512]{1,0:T(8,128)(2,1)S(1)}, bf16[528,512]{1,0:T(8,128)(2,1)S(1)}, u32[]{:S(2)}, u32[]{:S(2)}) collective-permute-start(bf16[528,512]{1,0:T(8,128)(2,1)S(1)} %copy-done.41), channel_id=1, source_target_pairs={{0,2},{1,3},{2,0},{3,1},{4,6},{5,7},{6,4},{7,5},{8,10},{9,11},{10,... | collective-permute-start | bytes 1622024 | tf_op jit(solution)/shard_map/ppermute | solution.py:861
  87.0 3.4 collective-permute-start.24
  92.5 19.0 %collective-permute-done.20.refs_4_ = bf16[528,512]{1,0:T(8,128)(2,1)S(1)} collective-permute-done((bf16[528,512]{1,0:T(8,128)(2,1)S(1)}, bf16[528,512]{1,0:T(8,128)(2,1)S(1)}, u32[]{:S(2)}, u32[]{:S(2)}) %collective-permute-start.20) | collective-permute-done | bytes 540704 | tf_op jit(solution)/shard_map/ppermute | solution.py:861
  118.5 7.1 collective-permute-done.21.refs_5_
  125.6 6.9 collective-permute-done.25.refs_9_
  137.9 16.2 %shard_map.250 = (bf16[4,608,512]{2,1,0:T(8,128)(2,1)}, bf16[4,608,512]{2,1,0:T(8,128)(2,1)}, bf16[304,1024]{1,0:T(8,128)(2,1)}, bf16[304,1024]{1,0:T(8,128)(2,1)}) custom-call(s32[8]{0:T(128)} %stack.76.place, bf16[304,1024]{1,0:T(8,128)(2,1)} %get-tuple-element.147.a_own.x1_own, bf16[304,1024]{1,0:T(8,128)(2,1)} %copy-done.13, ...), custom_call_target="tpu_custom_call" | custom-call | flops 16999999488 | tf_op jit(solution)/shard_map/pallas_call | solution.py:620
  155.1 16.6 %collective-permute-start.38 = (bf16[272,512]{1,0:T(8,128)(2,1)}, bf16[272,512]{1,0:T(8,128)(2,1)S(1)}, u32[]{:S(2)}, u32[]{:S(2)}) collective-permute-start(bf16[272,512]{1,0:T(8,128)(2,1)} %get-tuple-element.153), channel_id=1, source_target_pairs={{0,3},{1,0},{2,1},{3,2},{4,7},{5,4},{6,5},{7,6},{8,11},{9,8},{10,9... | collective-permute-start | bytes 835592 | tf_op jit(solution)/shard_map/ppermute | solution.py:861
  173.2 6.0 collective-permute-done.38.refs_8_
  185.7 9.2 %collective-permute-done.34.refs_4_ = bf16[272,512]{1,0:T(8,128)(2,1)S(1)} collective-permute-done((bf16[272,512]{1,0:T(8,128)(2,1)}, bf16[272,512]{1,0:T(8,128)(2,1)S(1)}, u32[]{:S(2)}, u32[]{:S(2)}) %collective-permute-start.34) | collective-permute-done | bytes 278560 | tf_op jit(solution)/shard_map/ppermute | solution.py:861
  197.2 7.3 collective-permute-done.35.refs_5_
  205.0 3.4 collective-permute-done.31.refs_1_
  211.6 12.2 %shard_map.252 = (bf16[4,608,384]{2,1,0:T(8,128)(2,1)}, bf16[4,608,128]{2,1,0:T(8,128)(2,1)}, bf16[304,1024]{1,0:T(8,128)(2,1)}, bf16[304,1024]{1,0:T(8,128)(2,1)}) custom-call(s32[8]{0:T(128)} %stack.76.place, bf16[304,1024]{1,0:T(8,128)(2,1)} %get-tuple-element.151.a_own.x1_own, bf16[304,1024]{1,0:T(8,128)(2,1)} %copy-done.15, ...), custom_call_target="tpu_custom_call" | custom-call | flops 12999999488 | tf_op jit(solution)/shard_map/pallas_call | solution.py:469
  227.8 35.2 %collective-permute-done.48.refs_4_ = bf16[528,512]{1,0:T(8,128)(2,1)S(1)} collective-permute-done((bf16[528,512]{1,0:T(8,128)(2,1)S(1)}, bf16[528,512]{1,0:T(8,128)(2,1)S(1)}, u32[]{:S(2)}, u32[]{:S(2)}) %collective-permute-start.48) | collective-permute-done | bytes 540704 | tf_op jit(solution)/shard_map/ppermute | solution.py:861
  269.4 8.9 %collective-permute-done.49.refs_5_ = bf16[528,512]{1,0:T(8,128)(2,1)} collective-permute-done((bf16[528,512]{1,0:T(8,128)(2,1)S(1)}, bf16[528,512]{1,0:T(8,128)(2,1)}, u32[]{:S(2)}, u32[]{:S(2)}) %collective-permute-start.49) | collective-permute-done | bytes 540704 | tf_op jit(solution)/shard_map/ppermute | solution.py:858
  278.8 9.2 %collective-permute-done.45.refs_1_ = bf16[528,512]{1,0:T(8,128)(2,1)} collective-permute-done((bf16[528,512]{1,0:T(8,128)(2,1)S(1)}, bf16[528,512]{1,0:T(8,128)(2,1)}, u32[]{:S(2)}, u32[]{:S(2)}) %collective-permute-start.45) | collective-permute-done | bytes 540704 | tf_op jit(solution)/shard_map/ppermute | solution.py:858
  291.9 16.2 %shard_map.254 = (bf16[4,608,512]{2,1,0:T(8,128)(2,1)}, bf16[4,608,512]{2,1,0:T(8,128)(2,1)}, bf16[304,1024]{1,0:T(8,128)(2,1)}, bf16[304,1024]{1,0:T(8,128)(2,1)}) custom-call(s32[8]{0:T(128)} %stack.76.place, bf16[304,1024]{1,0:T(8,128)(2,1)} %get-tuple-element.160.a_own.x1_own, bf16[304,1024]{1,0:T(8,128)(2,1)} %copy-done.20, ...), custom_call_target="tpu_custom_call" | custom-call | flops 16999999488 | tf_op jit(solution)/shard_map/pallas_call | solution.py:620
  308.1 12.5 %shard_map.257 = (bf16[4,608,512]{2,1,0:T(8,128)(2,1)}, f32[4,8,512]{2,1,0:T(8,128)}, bf16[304,1024]{1,0:T(8,128)(2,1)}, bf16[304,1024]{1,0:T(8,128)(2,1)}) custom-call(s32[8]{0:T(128)} %stack.76.place, bf16[304,1024]{1,0:T(8,128)(2,1)} %get-tuple-element.142.g_own.x2_own, bf16[304,1024]{1,0:T(8,128)(2,1)} %copy-done.12, ...), custom_call_target="tpu_custom_call" | custom-call | flops 12999999488 | tf_op jit(solution)/shard_map/pallas_call | solution.py:678
  320.6 13.6 %shard_map.258 = (bf16[4,256,1024]{2,1,0:T(8,128)(2,1)}, bf16[4,256,1024]{2,1,0:T(8,128)(2,1)}, bf16[2,4,256,1024]{3,2,1,0:T(8,128)(2,1)}) custom-call(s32[8]{0:T(128)} %stack.76.place, bf16[304,1024]{1,0:T(8,128)(2,1)} %get-tuple-element.160.a_own.x1_own, bf16[304,1024]{1,0:T(8,128)(2,1)} %copy-done.20, bf16[4,608,512]{2,1,0:T(8,128)(2,1)} %get-tuple-element.170.y1_ref, ...), custom_call_target="tpu_custom_call" | custom-call | flops 14000000000 | tf_op jit(solution)/shard_map/pallas_call | solution.py:730
  335.4 15.2 %collective-permute-done.57.far_ref = bf16[304,1024]{1,0:T(8,128)(2,1)S(1)} collective-permute-done((bf16[304,1024]{1,0:T(8,128)(2,1)S(1)}, bf16[304,1024]{1,0:T(8,128)(2,1)S(1)}, u32[]{:S(2)}, u32[]{:S(2)}) %collective-permute-start.57) | collective-permute-done | bytes 622624 | tf_op jit(solution)/shard_map/ppermute | solution.py:858
  351.5 4.3 shard_map.259
  356.8 5.9 shard_map.260
  363.6 7.8 collective-permute-done.59.g_far.x2_far
  372.3 31.4 %shard_map.261 = (bf16[4,608,384]{2,1,0:T(8,128)(2,1)}, f32[4,8,384]{2,1,0:T(8,128)}, bf16[304,1024]{1,0:T(8,128)(2,1)}, bf16[304,1024]{1,0:T(8,128)(2,1)}) custom-call(s32[8]{0:T(128)} %stack.76.place, bf16[304,1024]{1,0:T(8,128)(2,1)} %get-tuple-element.181.g_own.x2_own, bf16[304,1024]{1,0:T(8,128)(2,1)} %copy-done.24, ...), custom_call_target="tpu_custom_call" | custom-call | flops 23000000512 | tf_op jit(solution)/shard_map/pallas_call | solution.py:549
  403.8 9.7 %shard_map.262 = (bf16[4,256,512]{2,1,0:T(8,128)(2,1)}, bf16[4,256,512]{2,1,0:T(8,128)(2,1)}, bf16[2,4,256,512]{3,2,1,0:T(8,128)(2,1)}) custom-call(s32[8]{0:T(128)} %stack.76.place, bf16[304,1024]{1,0:T(8,128)(2,1)} %get-tuple-element.151.a_own.x1_own, bf16[304,1024]{1,0:T(8,128)(2,1)} %copy-done.15, bf16[4,608,384]{2,1,0:T(8,128)(2,1)} %get-tuple-element.183.y1_ref, ...), custom_call_target="tpu_custom_call" | custom-call | flops 14000000000 | tf_op jit(solution)/shard_map/pallas_call | solution.py:730
  415.9 3.8 shard_map.263
  419.7 10.2 %collective-permute-done.61.far_ref = bf16[304,1024]{1,0:T(8,128)(2,1)S(1)} collective-permute-done((bf16[304,1024]{1,0:T(8,128)(2,1)S(1)}, bf16[304,1024]{1,0:T(8,128)(2,1)S(1)}, u32[]{:S(2)}, u32[]{:S(2)}) %collective-permute-start.61) | collective-permute-done | bytes 622624 | tf_op jit(solution)/shard_map/ppermute | solution.py:858
  430.7 4.4 shard_map.264
  436.1 4.2 shard_map.265
  440.3 10.6 %collective-permute-done.63.g_far.x2_far = bf16[304,1024]{1,0:T(8,128)(2,1)S(1)} collective-permute-done((bf16[304,1024]{1,0:T(8,128)(2,1)}, bf16[304,1024]{1,0:T(8,128)(2,1)S(1)}, u32[]{:S(2)}, u32[]{:S(2)}) %collective-permute-start.63) | collective-permute-done | bytes 622624 | tf_op jit(solution)/shard_map/ppermute | solution.py:858
  451.7 12.5 %shard_map.266 = (bf16[4,608,512]{2,1,0:T(8,128)(2,1)}, f32[4,8,512]{2,1,0:T(8,128)}, bf16[304,1024]{1,0:T(8,128)(2,1)}, bf16[304,1024]{1,0:T(8,128)(2,1)}) custom-call(s32[8]{0:T(128)} %stack.76.place, bf16[304,1024]{1,0:T(8,128)(2,1)} %get-tuple-element.196.g_own.x2_own, bf16[304,1024]{1,0:T(8,128)(2,1)} %copy-done.27, ...), custom_call_target="tpu_custom_call" | custom-call | flops 12999999488 | tf_op jit(solution)/shard_map/pallas_call | solution.py:678
  464.3 13.6 %shard_map.267 = (bf16[4,256,1024]{2,1,0:T(8,128)(2,1)}, bf16[4,256,1024]{2,1,0:T(8,128)(2,1)}, bf16[2,4,256,1024]{3,2,1,0:T(8,128)(2,1)}) custom-call(s32[8]{0:T(128)} %stack.76.place, bf16[304,1024]{1,0:T(8,128)(2,1)} %get-tuple-element.147.a_own.x1_own, bf16[304,1024]{1,0:T(8,128)(2,1)} %copy-done.13, bf16[4,608,512]{2,1,0:T(8,128)(2,1)} %get-tuple-element.198.y1_ref, ...), custom_call_target="tpu_custom_call" | custom-call | flops 14000000000 | tf_op jit(solution)/shard_map/pallas_call | solution.py:730
  482.0 12.2 %collective-permute-done.56.far_ref = bf16[304,1024]{1,0:T(8,128)(2,1)S(1)} collective-permute-done((bf16[304,1024]{1,0:T(8,128)(2,1)S(1)}, bf16[304,1024]{1,0:T(8,128)(2,1)S(1)}, u32[]{:S(2)}, u32[]{:S(2)}) %collective-permute-start.56) | collective-permute-done | bytes 622624 | tf_op jit(solution)/shard_map/ppermute | solution.py:858
  504.0 21.3 %collective-permute-done.67.second = bf16[256,1024]{1,0:T(8,128)(2,1)S(1)} collective-permute-done((bf16[256,1024]{1,0:T(8,128)(2,1)}, bf16[256,1024]{1,0:T(8,128)(2,1)S(1)}, u32[]{:S(2)}, u32[]{:S(2)}) %collective-permute-start.67) | collective-permute-done | bytes 524320 | tf_op jit(solution)/shard_map/ppermute | solution.py:861
  525.3 54.1 %collective-permute-done.68.third = bf16[256,1024]{1,0:T(8,128)(2,1)} collective-permute-done((bf16[256,1024]{1,0:T(8,128)(2,1)}, bf16[256,1024]{1,0:T(8,128)(2,1)}, u32[]{:S(2)}, u32[]{:S(2)}) %collective-permute-start.68) | collective-permute-done | bytes 524320 | tf_op jit(solution)/shard_map/ppermute | solution.py:861
  587.3 7.8 collective-permute-done.65.far_ref
  595.9 4.4 shard_map.269
  601.2 11.7 %collective-permute-start.73 = (bf16[256,512]{1,0:T(8,128)(2,1)}, bf16[256,512]{1,0:T(8,128)(2,1)S(1)}, u32[]{:S(2)}, u32[]{:S(2)}) collective-permute-start(bf16[256,512]{1,0:T(8,128)(2,1)} %get-tuple-element.223), channel_id=1, source_target_pairs={{0,2},{1,3},{2,0},{3,1},{4,6},{5,7},{6,4},{7,5},{8,10},{9,11},{10,... | collective-permute-start | bytes 786440 | tf_op jit(solution)/shard_map/ppermute | solution.py:861
  616.3 6.1 shard_map.270
  624.3 22.8 %shard_map.272 = (bf16[4,608,384]{2,1,0:T(8,128)(2,1)}, f32[4,8,384]{2,1,0:T(8,128)}, bf16[304,1024]{1,0:T(8,128)(2,1)}, bf16[304,1024]{1,0:T(8,128)(2,1)}) custom-call(s32[8]{0:T(128)} %stack.76.place, bf16[304,1024]{1,0:T(8,128)(2,1)} %get-tuple-element.215.g_own.x2_own, bf16[304,1024]{1,0:T(8,128)(2,1)} %copy-done.19, ...), custom_call_target="tpu_custom_call" | custom-call | flops 23000000512 | tf_op jit(solution)/shard_map/pallas_call | solution.py:549
  647.1 9.7 %shard_map.273 = (bf16[4,256,512]{2,1,0:T(8,128)(2,1)}, bf16[4,256,512]{2,1,0:T(8,128)(2,1)}, bf16[2,4,256,512]{3,2,1,0:T(8,128)(2,1)}) custom-call(s32[8]{0:T(128)} %stack.76.place, bf16[304,1024]{1,0:T(8,128)(2,1)} %get-tuple-element.143.a_own.x1_own, bf16[304,1024]{1,0:T(8,128)(2,1)} %copy-done.11, bf16[4,608,384]{2,1,0:T(8,128)(2,1)} %get-tuple-element.217.y1_ref, ...), custom_call_target="tpu_custom_call" | custom-call | flops 14000000000 | tf_op jit(solution)/shard_map/pallas_call | solution.py:730
  662.8 5.6 collective-permute-done.71.got
  668.3 3.9 shard_map.274
  672.2 4.6 collective-permute-done.75.far_ref
  677.6 4.3 shard_map.276
  684.3 4.3 shard_map.278
  690.7 3.9 collective-permute-done.77
  695.7 20.8 %collective-permute-done.78 = f32[192,128]{1,0:T(8,128)S(1)} collective-permute-done((f32[192,128]{1,0:T(8,128)S(1)}, f32[192,128]{1,0:T(8,128)S(1)}, u32[]{:S(2)}, u32[]{:S(2)}) %collective-permute-start.78) | collective-permute-done | bytes 98336 | tf_op jit(solution)/shard_map/ppermute | solution.py:858
  718.0 3.5 collective-permute-start.87
  722.4 5.3 collective-permute-done.79
  727.6 7.3 collective-permute-start.80
  734.9 8.9 %shard_map.256 = bf16[1200,1024]{1,0:T(8,128)(2,1)} custom-call(bf16[4,304,1024]{2,1,0:T(8,128)(2,1)} %bitcast.127), custom_call_target="tpu_custom_call" | custom-call | flops 6000000000 | tf_op jit(solution)/shard_map/pallas_call | solution.py:160
  743.9 39.7 %collective-permute-done.80 = f32[192,128]{1,0:T(8,128)S(1)} collective-permute-done((f32[192,128]{1,0:T(8,128)S(1)}, f32[192,128]{1,0:T(8,128)S(1)}, u32[]{:S(2)}, u32[]{:S(2)}) %collective-permute-start.80) | collective-permute-done | bytes 98336 | tf_op jit(solution)/shard_map/ppermute | solution.py:884
  798.7 11.6 %collective-permute-done.84.third = bf16[256,512]{1,0:T(8,128)(2,1)S(1)} collective-permute-done((bf16[256,512]{1,0:T(8,128)(2,1)}, bf16[256,512]{1,0:T(8,128)(2,1)S(1)}, u32[]{:S(2)}, u32[]{:S(2)}) %collective-permute-start.84) | collective-permute-done | bytes 262176 | tf_op jit(solution)/shard_map/ppermute | solution.py:861
  820.2 3.3 shard_map.282
  823.5 9.8 %shard_map.277 = f32[1200,1024]{1,0:T(8,128)} custom-call(bf16[4,304,1024]{2,1,0:T(8,128)(2,1)} %bitcast.128), custom_call_target="tpu_custom_call" | custom-call | flops 6000000000 | tf_op jit(solution)/shard_map/pallas_call | solution.py:160
  (403 shorter events, 141.2 us)
Async XLA Ops:
  7.2 727.7 %all-gather.5.cloned.1.call-start = ((), (), s32[]{:S(2)}) async-start(), calls=%async_computation | async-start | bytes 3112960 | tf_op jit(solution)/shard_map/all_gather | solution.py:930
  11.4 18.7 %collective-permute-start = (bf16[272,512]{1,0:T(8,128)(2,1)}, bf16[272,512]{1,0:T(8,128)(2,1)S(1)}, u32[]{:S(2)}, u32[]{:S(2)}) collective-permute-start(bf16[272,512]{1,0:T(8,128)(2,1)} %get-tuple-element.140), channel_id=1, source_target_pairs={{0,2},{1,3},{2,0},{3,1},{4,6},{5,7},{6,4},{7,5},{8,10},{9,11},{10,... | collective-permute-start | bytes 835592 | tf_op jit(solution)/shard_map/ppermute | solution.py:861
  15.5 21.6 %collective-permute-start.11 = (bf16[272,512]{1,0:T(8,128)(2,1)}, bf16[272,512]{1,0:T(8,128)(2,1)S(1)}, u32[]{:S(2)}, u32[]{:S(2)}) collective-permute-start(bf16[272,512]{1,0:T(8,128)(2,1)} %get-tuple-element.140), channel_id=1, source_target_pairs={{0,3},{1,0},{2,1},{3,2},{4,7},{5,4},{6,5},{7,6},{8,11},{9,8},{10,9... | collective-permute-start | bytes 835592 | tf_op jit(solution)/shard_map/ppermute | solution.py:861
  16.9 20.5 %collective-permute-start.4 = (bf16[272,512]{1,0:T(8,128)(2,1)}, bf16[272,512]{1,0:T(8,128)(2,1)S(1)}, u32[]{:S(2)}, u32[]{:S(2)}) collective-permute-start(bf16[272,512]{1,0:T(8,128)(2,1)} %get-tuple-element.140), channel_id=1, source_target_pairs={{0,1},{1,2},{2,3},{3,0},{4,5},{5,6},{6,7},{7,4},{8,9},{9,10},{10,1... | collective-permute-start | bytes 835592 | tf_op jit(solution)/shard_map/ppermute | solution.py:861
  21.6 35.7 %collective-permute-start.2 = (bf16[304,1024]{1,0:T(8,128)(2,1)}, bf16[304,1024]{1,0:T(8,128)(2,1)S(1)}, u32[]{:S(2)}, u32[]{:S(2)}) collective-permute-start(bf16[304,1024]{1,0:T(8,128)(2,1)} %get-tuple-element.142.g_own.x2_own), channel_id=1, source_target_pairs={{0,8},{4,12},{8,0},{12,4},{16,24},{20,28},{24,16},{28,20},{1,9},{5... | collective-permute-start | bytes 1867784 | tf_op jit(solution)/shard_map/ppermute | solution.py:858
  30.1 27.5 %collective-permute-start.1 = (bf16[528,512]{1,0:T(8,128)(2,1)S(1)}, bf16[528,512]{1,0:T(8,128)(2,1)S(1)}, u32[]{:S(2)}, u32[]{:S(2)}) collective-permute-start(bf16[528,512]{1,0:T(8,128)(2,1)S(1)} %copy-done.41), channel_id=1, source_target_pairs={{0,1},{1,2},{2,3},{3,0},{4,5},{5,6},{6,7},{7,4},{8,9},{9,10},{10,1... | collective-permute-start | bytes 1622024 | tf_op jit(solution)/shard_map/ppermute | solution.py:861
  37.3 18.2 %collective-permute-start.5 = (bf16[272,512]{1,0:T(8,128)(2,1)S(1)}, bf16[272,512]{1,0:T(8,128)(2,1)}, u32[]{:S(2)}, u32[]{:S(2)}) collective-permute-start(bf16[272,512]{1,0:T(8,128)(2,1)S(1)} %collective-permute-done.4.refs_0_), channel_id=1, source_target_pairs={{0,16},{4,20},{8,24},{12,28},{16,0},{20,4},{24,8},{28,12},{1,17},{... | collective-permute-start | bytes 835592 | tf_op jit(solution)/shard_map/ppermute | solution.py:858
  72.3 40.7 %collective-permute-start.15 = (bf16[304,1024]{1,0:T(8,128)(2,1)}, bf16[304,1024]{1,0:T(8,128)(2,1)S(1)}, u32[]{:S(2)}, u32[]{:S(2)}) collective-permute-start(bf16[304,1024]{1,0:T(8,128)(2,1)} %get-tuple-element.145), channel_id=1, source_target_pairs={{0,8},{4,12},{8,0},{12,4},{16,24},{20,28},{24,16},{28,20},{1,9},{5... | collective-permute-start | bytes 1867784 | tf_op jit(solution)/shard_map/ppermute | solution.py:858
  73.9 37.6 %collective-permute-start.20 = (bf16[528,512]{1,0:T(8,128)(2,1)S(1)}, bf16[528,512]{1,0:T(8,128)(2,1)S(1)}, u32[]{:S(2)}, u32[]{:S(2)}) collective-permute-start(bf16[528,512]{1,0:T(8,128)(2,1)S(1)} %copy-done.41), channel_id=1, source_target_pairs={{0,2},{1,3},{2,0},{3,1},{4,6},{5,7},{6,4},{7,5},{8,10},{9,11},{10,... | collective-permute-start | bytes 1622024 | tf_op jit(solution)/shard_map/ppermute | solution.py:861
  87.0 26.1 %collective-permute-start.24 = (bf16[528,512]{1,0:T(8,128)(2,1)S(1)}, bf16[528,512]{1,0:T(8,128)(2,1)S(1)}, u32[]{:S(2)}, u32[]{:S(2)}) collective-permute-start(bf16[528,512]{1,0:T(8,128)(2,1)S(1)} %copy-done.41), channel_id=1, source_target_pairs={{0,3},{1,0},{2,1},{3,2},{4,7},{5,4},{6,5},{7,6},{8,11},{9,8},{10,9... | collective-permute-start | bytes 1622024 | tf_op jit(solution)/shard_map/ppermute | solution.py:861
  90.4 27.1 %collective-permute-start.17 = (bf16[528,512]{1,0:T(8,128)(2,1)S(1)}, bf16[528,512]{1,0:T(8,128)(2,1)S(1)}, u32[]{:S(2)}, u32[]{:S(2)}) collective-permute-start(bf16[528,512]{1,0:T(8,128)(2,1)S(1)} %collective-permute-done.1.refs_0_), channel_id=1, source_target_pairs={{0,16},{4,20},{8,24},{12,28},{16,0},{20,4},{24,8},{28,12},{1,17},{... | collective-permute-start | bytes 1622024 | tf_op jit(solution)/shard_map/ppermute | solution.py:858
  92.5 40.0 %collective-permute-start.18 = (bf16[528,512]{1,0:T(8,128)(2,1)S(1)}, bf16[528,512]{1,0:T(8,128)(2,1)}, u32[]{:S(2)}, u32[]{:S(2)}) collective-permute-start(bf16[528,512]{1,0:T(8,128)(2,1)S(1)} %collective-permute-done.1.refs_0_), channel_id=1, source_target_pairs={{0,4},{4,0},{8,12},{12,8},{16,20},{20,16},{24,28},{28,24},{1,5},{5... | collective-permute-start | bytes 1622024 | tf_op jit(solution)/shard_map/ppermute | solution.py:858
  111.5 14.1 %collective-permute-start.21 = (bf16[528,512]{1,0:T(8,128)(2,1)S(1)}, bf16[528,512]{1,0:T(8,128)(2,1)}, u32[]{:S(2)}, u32[]{:S(2)}) collective-permute-start(bf16[528,512]{1,0:T(8,128)(2,1)S(1)} %collective-permute-done.20.refs_4_), channel_id=1, source_target_pairs={{0,16},{4,20},{8,24},{12,28},{16,0},{20,4},{24,8},{28,12},{1,17},{... | collective-permute-start | bytes 1622024 | tf_op jit(solution)/shard_map/ppermute | solution.py:858
  113.0 20.0 %collective-permute-start.22 = (bf16[528,512]{1,0:T(8,128)(2,1)S(1)}, bf16[528,512]{1,0:T(8,128)(2,1)}, u32[]{:S(2)}, u32[]{:S(2)}) collective-permute-start(bf16[528,512]{1,0:T(8,128)(2,1)S(1)} %collective-permute-done.20.refs_4_), channel_id=1, source_target_pairs={{0,4},{4,0},{8,12},{12,8},{16,20},{20,16},{24,28},{28,24},{1,5},{5... | collective-permute-start | bytes 1622024 | tf_op jit(solution)/shard_map/ppermute | solution.py:858
  113.1 19.5 %collective-permute-start.25 = (bf16[528,512]{1,0:T(8,128)(2,1)S(1)}, bf16[528,512]{1,0:T(8,128)(2,1)}, u32[]{:S(2)}, u32[]{:S(2)}) collective-permute-start(bf16[528,512]{1,0:T(8,128)(2,1)S(1)} %collective-permute-done.24.refs_8_), channel_id=1, source_target_pairs={{0,16},{4,20},{8,24},{12,28},{16,0},{20,4},{24,8},{28,12},{1,17},{... | collective-permute-start | bytes 1622024 | tf_op jit(solution)/shard_map/ppermute | solution.py:858
  117.4 19.6 %collective-permute-start.16 = (bf16[304,1024]{1,0:T(8,128)(2,1)}, bf16[304,1024]{1,0:T(8,128)(2,1)S(1)}, u32[]{:S(2)}, u32[]{:S(2)}) collective-permute-start(bf16[304,1024]{1,0:T(8,128)(2,1)} %get-tuple-element.147.a_own.x1_own), channel_id=1, source_target_pairs={{0,8},{4,12},{8,0},{12,4},{16,24},{20,28},{24,16},{28,20},{1,9},{5... | collective-permute-start | bytes 1867784 | tf_op jit(solution)/shard_map/ppermute | solution.py:858
  154.1 26.1 %collective-permute-start.28 = (bf16[304,1024]{1,0:T(8,128)(2,1)}, bf16[304,1024]{1,0:T(8,128)(2,1)S(1)}, u32[]{:S(2)}, u32[]{:S(2)}) collective-permute-start(bf16[304,1024]{1,0:T(8,128)(2,1)} %get-tuple-element.149), channel_id=1, source_target_pairs={{0,8},{4,12},{8,0},{12,4},{16,24},{20,28},{24,16},{28,20},{1,9},{5... | collective-permute-start | bytes 1867784 | tf_op jit(solution)/shard_map/ppermute | solution.py:858
  155.1 24.0 %collective-permute-start.38 = (bf16[272,512]{1,0:T(8,128)(2,1)}, bf16[272,512]{1,0:T(8,128)(2,1)S(1)}, u32[]{:S(2)}, u32[]{:S(2)}) collective-permute-start(bf16[272,512]{1,0:T(8,128)(2,1)} %get-tuple-element.153), channel_id=1, source_target_pairs={{0,3},{1,0},{2,1},{3,2},{4,7},{5,4},{6,5},{7,6},{8,11},{9,8},{10,9... | collective-permute-start | bytes 835592 | tf_op jit(solution)/shard_map/ppermute | solution.py:861
  172.4 22.5 %collective-permute-start.34 = (bf16[272,512]{1,0:T(8,128)(2,1)}, bf16[272,512]{1,0:T(8,128)(2,1)S(1)}, u32[]{:S(2)}, u32[]{:S(2)}) collective-permute-start(bf16[272,512]{1,0:T(8,128)(2,1)} %get-tuple-element.153), channel_id=1, source_target_pairs={{0,2},{1,3},{2,0},{3,1},{4,6},{5,7},{6,4},{7,5},{8,10},{9,11},{10,... | collective-permute-start | bytes 835592 | tf_op jit(solution)/shard_map/ppermute | solution.py:861
  172.4 23.5 %collective-permute-start.30 = (bf16[272,512]{1,0:T(8,128)(2,1)}, bf16[272,512]{1,0:T(8,128)(2,1)S(1)}, u32[]{:S(2)}, u32[]{:S(2)}) collective-permute-start(bf16[272,512]{1,0:T(8,128)(2,1)} %get-tuple-element.153), channel_id=1, source_target_pairs={{0,1},{1,2},{2,3},{3,0},{4,5},{5,6},{6,7},{7,4},{8,9},{9,10},{10,1... | collective-permute-start | bytes 835592 | tf_op jit(solution)/shard_map/ppermute | solution.py:861
  179.2 16.7 %collective-permute-start.39 = (bf16[272,512]{1,0:T(8,128)(2,1)S(1)}, bf16[272,512]{1,0:T(8,128)(2,1)S(1)}, u32[]{:S(2)}, u32[]{:S(2)}) collective-permute-start(bf16[272,512]{1,0:T(8,128)(2,1)S(1)} %collective-permute-done.38.refs_8_), channel_id=1, source_target_pairs={{0,16},{4,20},{8,24},{12,28},{16,0},{20,4},{24,8},{28,12},{1,17},{... | collective-permute-start | bytes 835592 | tf_op jit(solution)/shard_map/ppermute | solution.py:858
  184.2 26.5 %collective-permute-start.29 = (bf16[304,1024]{1,0:T(8,128)(2,1)}, bf16[304,1024]{1,0:T(8,128)(2,1)S(1)}, u32[]{:S(2)}, u32[]{:S(2)}) collective-permute-start(bf16[304,1024]{1,0:T(8,128)(2,1)} %get-tuple-element.151.a_own.x1_own), channel_id=1, source_target_pairs={{0,8},{4,12},{8,0},{12,4},{16,24},{20,28},{24,16},{28,20},{1,9},{5... | collective-permute-start | bytes 1867784 | tf_op jit(solution)/shard_map/ppermute | solution.py:858
  208.5 17.8 %collective-permute-start.52 = (bf16[528,512]{1,0:T(8,128)(2,1)S(1)}, bf16[528,512]{1,0:T(8,128)(2,1)S(1)}, u32[]{:S(2)}, u32[]{:S(2)}) collective-permute-start(bf16[528,512]{1,0:T(8,128)(2,1)S(1)} %copy-done.40), channel_id=1, source_target_pairs={{0,3},{1,0},{2,1},{3,2},{4,7},{5,4},{6,5},{7,6},{8,11},{9,8},{10,9... | collective-permute-start | bytes 1622024 | tf_op jit(solution)/shard_map/ppermute | solution.py:861
  223.9 40.6 %collective-permute-start.42 = (bf16[304,1024]{1,0:T(8,128)(2,1)}, bf16[304,1024]{1,0:T(8,128)(2,1)S(1)}, u32[]{:S(2)}, u32[]{:S(2)}) collective-permute-start(bf16[304,1024]{1,0:T(8,128)(2,1)} %get-tuple-element.158), channel_id=1, source_target_pairs={{0,8},{4,12},{8,0},{12,4},{16,24},{20,28},{24,16},{28,20},{1,9},{5... | collective-permute-start | bytes 1867784 | tf_op jit(solution)/shard_map/ppermute | solution.py:858
  224.9 38.1 %collective-permute-start.48 = (bf16[528,512]{1,0:T(8,128)(2,1)S(1)}, bf16[528,512]{1,0:T(8,128)(2,1)S(1)}, u32[]{:S(2)}, u32[]{:S(2)}) collective-permute-start(bf16[528,512]{1,0:T(8,128)(2,1)S(1)} %copy-done.40), channel_id=1, source_target_pairs={{0,2},{1,3},{2,0},{3,1},{4,6},{5,7},{6,4},{7,5},{8,10},{9,11},{10,... | collective-permute-start | bytes 1622024 | tf_op jit(solution)/shard_map/ppermute | solution.py:861
  224.9 39.6 %collective-permute-start.44 = (bf16[528,512]{1,0:T(8,128)(2,1)S(1)}, bf16[528,512]{1,0:T(8,128)(2,1)S(1)}, u32[]{:S(2)}, u32[]{:S(2)}) collective-permute-start(bf16[528,512]{1,0:T(8,128)(2,1)S(1)} %copy-done.40), channel_id=1, source_target_pairs={{0,1},{1,2},{2,3},{3,0},{4,5},{5,6},{6,7},{7,4},{8,9},{9,10},{10,1... | collective-permute-start | bytes 1622024 | tf_op jit(solution)/shard_map/ppermute | solution.py:861
  226.2 42.3 %collective-permute-start.53 = (bf16[528,512]{1,0:T(8,128)(2,1)S(1)}, bf16[528,512]{1,0:T(8,128)(2,1)S(1)}, u32[]{:S(2)}, u32[]{:S(2)}) collective-permute-start(bf16[528,512]{1,0:T(8,128)(2,1)S(1)} %collective-permute-done.52.refs_8_), channel_id=1, source_target_pairs={{0,16},{4,20},{8,24},{12,28},{16,0},{20,4},{24,8},{28,12},{1,17},{... | collective-permute-start | bytes 1622024 | tf_op jit(solution)/shard_map/ppermute | solution.py:858
  227.8 41.6 %collective-permute-start.54 = (bf16[528,512]{1,0:T(8,128)(2,1)S(1)}, bf16[528,512]{1,0:T(8,128)(2,1)S(1)}, u32[]{:S(2)}, u32[]{:S(2)}) collective-permute-start(bf16[528,512]{1,0:T(8,128)(2,1)S(1)} %collective-permute-done.52.refs_8_), channel_id=1, source_target_pairs={{0,4},{4,0},{8,12},{12,8},{16,20},{20,16},{24,28},{28,24},{1,5},{5... | collective-permute-start | bytes 1622024 | tf_op jit(solution)/shard_map/ppermute | solution.py:858
  263.0 15.3 %collective-permute-start.49 = (bf16[528,512]{1,0:T(8,128)(2,1)S(1)}, bf16[528,512]{1,0:T(8,128)(2,1)}, u32[]{:S(2)}, u32[]{:S(2)}) collective-permute-start(bf16[528,512]{1,0:T(8,128)(2,1)S(1)} %collective-permute-done.48.refs_4_), channel_id=1, source_target_pairs={{0,16},{4,20},{8,24},{12,28},{16,0},{20,4},{24,8},{28,12},{1,17},{... | collective-permute-start | bytes 1622024 | tf_op jit(solution)/shard_map/ppermute | solution.py:858
  264.5 23.5 %collective-permute-start.45 = (bf16[528,512]{1,0:T(8,128)(2,1)S(1)}, bf16[528,512]{1,0:T(8,128)(2,1)}, u32[]{:S(2)}, u32[]{:S(2)}) collective-permute-start(bf16[528,512]{1,0:T(8,128)(2,1)S(1)} %collective-permute-done.44.refs_0_), channel_id=1, source_target_pairs={{0,16},{4,20},{8,24},{12,28},{16,0},{20,4},{24,8},{28,12},{1,17},{... | collective-permute-start | bytes 1622024 | tf_op jit(solution)/shard_map/ppermute | solution.py:858
  268.5 22.5 %collective-permute-start.43 = (bf16[304,1024]{1,0:T(8,128)(2,1)}, bf16[304,1024]{1,0:T(8,128)(2,1)S(1)}, u32[]{:S(2)}, u32[]{:S(2)}) collective-permute-start(bf16[304,1024]{1,0:T(8,128)(2,1)} %get-tuple-element.160.a_own.x1_own), channel_id=1, source_target_pairs={{0,8},{4,12},{8,0},{12,4},{16,24},{20,28},{24,16},{28,20},{1,9},{5... | collective-permute-start | bytes 1867784 | tf_op jit(solution)/shard_map/ppermute | solution.py:858
  269.4 18.6 %collective-permute-start.46 = (bf16[528,512]{1,0:T(8,128)(2,1)S(1)}, bf16[528,512]{1,0:T(8,128)(2,1)S(1)}, u32[]{:S(2)}, u32[]{:S(2)}) collective-permute-start(bf16[528,512]{1,0:T(8,128)(2,1)S(1)} %collective-permute-done.44.refs_0_), channel_id=1, source_target_pairs={{0,4},{4,0},{8,12},{12,8},{16,20},{20,16},{24,28},{28,24},{1,5},{5... | collective-permute-start | bytes 1622024 | tf_op jit(solution)/shard_map/ppermute | solution.py:858
  334.2 22.6 %collective-permute-start.58 = (bf16[2,4,256,1024]{3,2,1,0:T(8,128)(2,1)}, bf16[2,4,256,1024]{3,2,1,0:T(8,128)(2,1)}, u32[]{:S(2)}, u32[]{:S(2)}) collective-permute-start(bf16[2,4,256,1024]{3,2,1,0:T(8,128)(2,1)} %get-tuple-element.179), channel_id=1, source_target_pairs={{0,4},{4,0},{8,12},{12,8},{16,20},{20,16},{24,28},{28,24},{1,5},{5... | collective-permute-start | bytes 12582920 | tf_op jit(solution)/shard_map/ppermute | solution.py:858
  334.3 16.3 %collective-permute-start.57 = (bf16[304,1024]{1,0:T(8,128)(2,1)S(1)}, bf16[304,1024]{1,0:T(8,128)(2,1)S(1)}, u32[]{:S(2)}, u32[]{:S(2)}) collective-permute-start(bf16[304,1024]{1,0:T(8,128)(2,1)S(1)} %copy-done.29), channel_id=1, source_target_pairs={{0,8},{4,12},{8,0},{12,4},{16,24},{20,28},{24,16},{28,20},{1,9},{5... | collective-permute-start | bytes 1867784 | tf_op jit(solution)/shard_map/ppermute | solution.py:858
  355.7 15.7 %collective-permute-start.59 = (bf16[304,1024]{1,0:T(8,128)(2,1)}, bf16[304,1024]{1,0:T(8,128)(2,1)S(1)}, u32[]{:S(2)}, u32[]{:S(2)}) collective-permute-start(bf16[304,1024]{1,0:T(8,128)(2,1)} %get-tuple-element.181.g_own.x2_own), channel_id=1, source_target_pairs={{0,8},{4,12},{8,0},{12,4},{16,24},{20,28},{24,16},{28,20},{1,9},{5... | collective-permute-start | bytes 1867784 | tf_op jit(solution)/shard_map/ppermute | solution.py:858
  362.7 51.9 %collective-permute-start.60 = (bf16[4,256,1024]{2,1,0:T(8,128)(2,1)}, bf16[4,256,1024]{2,1,0:T(8,128)(2,1)S(1)}, u32[]{:S(2)}, u32[]{:S(2)}) collective-permute-start(bf16[4,256,1024]{2,1,0:T(8,128)(2,1)} %get-tuple-element.186), channel_id=1, source_target_pairs={{0,16},{4,20},{8,24},{12,28},{16,0},{20,4},{24,8},{28,12},{1,17},{... | collective-permute-start | bytes 6291464 | tf_op jit(solution)/shard_map/ppermute | solution.py:858
  413.5 22.7 %collective-permute-start.62 = (bf16[2,4,256,512]{3,2,1,0:T(8,128)(2,1)}, bf16[2,4,256,512]{3,2,1,0:T(8,128)(2,1)}, u32[]{:S(2)}, u32[]{:S(2)}) collective-permute-start(bf16[2,4,256,512]{3,2,1,0:T(8,128)(2,1)} %get-tuple-element.194), channel_id=1, source_target_pairs={{0,4},{4,0},{8,12},{12,8},{16,20},{20,16},{24,28},{28,24},{1,5},{5... | collective-permute-start | bytes 6291464 | tf_op jit(solution)/shard_map/ppermute | solution.py:858
  413.5 16.4 %collective-permute-start.61 = (bf16[304,1024]{1,0:T(8,128)(2,1)S(1)}, bf16[304,1024]{1,0:T(8,128)(2,1)S(1)}, u32[]{:S(2)}, u32[]{:S(2)}) collective-permute-start(bf16[304,1024]{1,0:T(8,128)(2,1)S(1)} %copy-done.25), channel_id=1, source_target_pairs={{0,8},{4,12},{8,0},{12,4},{16,24},{20,28},{24,16},{28,20},{1,9},{5... | collective-permute-start | bytes 1867784 | tf_op jit(solution)/shard_map/ppermute | solution.py:858
  435.1 15.8 %collective-permute-start.63 = (bf16[304,1024]{1,0:T(8,128)(2,1)}, bf16[304,1024]{1,0:T(8,128)(2,1)S(1)}, u32[]{:S(2)}, u32[]{:S(2)}) collective-permute-start(bf16[304,1024]{1,0:T(8,128)(2,1)} %get-tuple-element.196.g_own.x2_own), channel_id=1, source_target_pairs={{0,8},{4,12},{8,0},{12,4},{16,24},{20,28},{24,16},{28,20},{1,9},{5... | collective-permute-start | bytes 1867784 | tf_op jit(solution)/shard_map/ppermute | solution.py:858
  477.8 138.5 %collective-permute-start.66 = (bf16[2,4,256,1024]{3,2,1,0:T(8,128)(2,1)}, bf16[2,4,256,1024]{3,2,1,0:T(8,128)(2,1)}, u32[]{:S(2)}, u32[]{:S(2)}) collective-permute-start(bf16[2,4,256,1024]{3,2,1,0:T(8,128)(2,1)} %get-tuple-element.209), channel_id=1, source_target_pairs={{0,4},{4,0},{8,12},{12,8},{16,20},{20,16},{24,28},{28,24},{1,5},{5... | collective-permute-start | bytes 12582920 | tf_op jit(solution)/shard_map/ppermute | solution.py:858
  477.8 16.4 %collective-permute-start.56 = (bf16[304,1024]{1,0:T(8,128)(2,1)S(1)}, bf16[304,1024]{1,0:T(8,128)(2,1)S(1)}, u32[]{:S(2)}, u32[]{:S(2)}) collective-permute-start(bf16[304,1024]{1,0:T(8,128)(2,1)S(1)} %copy-done.14), channel_id=1, source_target_pairs={{0,8},{4,12},{8,0},{12,4},{16,24},{20,28},{24,16},{28,20},{1,9},{5... | collective-permute-start | bytes 1867784 | tf_op jit(solution)/shard_map/ppermute | solution.py:858
  498.0 325.5 %all-gather.7.cloned.1.call-start = ((), (), s32[]{:S(2)}) async-start(), calls=%async_computation.1 | async-start | bytes 3112960 | tf_op jit(solution)/shard_map/all_gather | solution.py:1007
  498.8 26.4 %collective-permute-start.67 = (bf16[256,1024]{1,0:T(8,128)(2,1)}, bf16[256,1024]{1,0:T(8,128)(2,1)S(1)}, u32[]{:S(2)}, u32[]{:S(2)}) collective-permute-start(bf16[256,1024]{1,0:T(8,128)(2,1)} %get-tuple-element.211), channel_id=1, source_target_pairs={{0,3},{1,0},{2,1},{3,2},{4,7},{5,4},{6,5},{7,6},{8,11},{9,8},{10,9... | collective-permute-start | bytes 1572872 | tf_op jit(solution)/shard_map/ppermute | solution.py:861
  498.9 80.6 %collective-permute-start.68 = (bf16[256,1024]{1,0:T(8,128)(2,1)}, bf16[256,1024]{1,0:T(8,128)(2,1)}, u32[]{:S(2)}, u32[]{:S(2)}) collective-permute-start(bf16[256,1024]{1,0:T(8,128)(2,1)} %get-tuple-element.212), channel_id=1, source_target_pairs={{0,2},{1,3},{2,0},{3,1},{4,6},{5,7},{6,4},{7,5},{8,10},{9,11},{10,... | collective-permute-start | bytes 1572872 | tf_op jit(solution)/shard_map/ppermute | solution.py:861
  498.9 80.5 %collective-permute-start.69 = (bf16[256,1024]{1,0:T(8,128)(2,1)S(1)}, bf16[256,1024]{1,0:T(8,128)(2,1)}, u32[]{:S(2)}, u32[]{:S(2)}) collective-permute-start(bf16[256,1024]{1,0:T(8,128)(2,1)S(1)} %copy-done.52), channel_id=1, source_target_pairs={{0,1},{1,2},{2,3},{3,0},{4,5},{5,6},{6,7},{7,4},{8,9},{9,10},{10,1... | collective-permute-start | bytes 1572872 | tf_op jit(solution)/shard_map/ppermute | solution.py:861
  500.9 82.8 %collective-permute-start.64 = (bf16[4,256,512]{2,1,0:T(8,128)(2,1)S(1)}, bf16[4,256,512]{2,1,0:T(8,128)(2,1)S(1)}, u32[]{:S(2)}, u32[]{:S(2)}) collective-permute-start(bf16[4,256,512]{2,1,0:T(8,128)(2,1)S(1)} %copy-done.8), channel_id=1, source_target_pairs={{0,16},{4,20},{8,24},{12,28},{16,0},{20,4},{24,8},{28,12},{1,17},{... | collective-permute-start | bytes 3145736 | tf_op jit(solution)/shard_map/ppermute | solution.py:858
  600.3 23.1 %collective-permute-start.70 = (bf16[304,1024]{1,0:T(8,128)(2,1)}, bf16[304,1024]{1,0:T(8,128)(2,1)S(1)}, u32[]{:S(2)}, u32[]{:S(2)}) collective-permute-start(bf16[304,1024]{1,0:T(8,128)(2,1)} %get-tuple-element.215.g_own.x2_own), channel_id=1, source_target_pairs={{0,8},{4,12},{8,0},{12,4},{16,24},{20,28},{24,16},{28,20},{1,9},{5... | collective-permute-start | bytes 1867784 | tf_op jit(solution)/shard_map/ppermute | solution.py:858
  601.1 55.6 %collective-permute-start.72 = (bf16[256,512]{1,0:T(8,128)(2,1)}, bf16[256,512]{1,0:T(8,128)(2,1)S(1)}, u32[]{:S(2)}, u32[]{:S(2)}) collective-permute-start(bf16[256,512]{1,0:T(8,128)(2,1)} %get-tuple-element.222), channel_id=1, source_target_pairs={{0,3},{1,0},{2,1},{3,2},{4,7},{5,4},{6,5},{7,6},{8,11},{9,8},{10,9... | collective-permute-start | bytes 786440 | tf_op jit(solution)/shard_map/ppermute | solution.py:861
  601.2 55.5 %collective-permute-start.73 = (bf16[256,512]{1,0:T(8,128)(2,1)}, bf16[256,512]{1,0:T(8,128)(2,1)S(1)}, u32[]{:S(2)}, u32[]{:S(2)}) collective-permute-start(bf16[256,512]{1,0:T(8,128)(2,1)} %get-tuple-element.223), channel_id=1, source_target_pairs={{0,2},{1,3},{2,0},{3,1},{4,6},{5,7},{6,4},{7,5},{8,10},{9,11},{10,... | collective-permute-start | bytes 786440 | tf_op jit(solution)/shard_map/ppermute | solution.py:861
  612.9 43.9 %collective-permute-start.74 = (bf16[256,512]{1,0:T(8,128)(2,1)}, bf16[256,512]{1,0:T(8,128)(2,1)S(1)}, u32[]{:S(2)}, u32[]{:S(2)}) collective-permute-start(bf16[256,512]{1,0:T(8,128)(2,1)} %get-tuple-element.224), channel_id=1, source_target_pairs={{0,1},{1,2},{2,3},{3,0},{4,5},{5,6},{6,7},{7,4},{8,9},{9,10},{10,1... | collective-permute-start | bytes 786440 | tf_op jit(solution)/shard_map/ppermute | solution.py:861
  622.4 45.9 %collective-permute-start.71 = (bf16[4,256,1024]{2,1,0:T(8,128)(2,1)}, bf16[4,256,1024]{2,1,0:T(8,128)(2,1)}, u32[]{:S(2)}, u32[]{:S(2)}) collective-permute-start(bf16[4,256,1024]{2,1,0:T(8,128)(2,1)} %get-tuple-element.220), channel_id=1, source_target_pairs={{0,16},{4,20},{8,24},{12,28},{16,0},{20,4},{24,8},{28,12},{1,17},{... | collective-permute-start | bytes 6291464 | tf_op jit(solution)/shard_map/ppermute | solution.py:858
  656.7 26.3 %collective-permute-start.81 = (bf16[2,4,256,512]{3,2,1,0:T(8,128)(2,1)}, bf16[2,4,256,512]{3,2,1,0:T(8,128)(2,1)S(1)}, u32[]{:S(2)}, u32[]{:S(2)}) collective-permute-start(bf16[2,4,256,512]{3,2,1,0:T(8,128)(2,1)} %get-tuple-element.240), channel_id=1, source_target_pairs={{0,4},{4,0},{8,12},{12,8},{16,20},{20,16},{24,28},{28,24},{1,5},{5... | collective-permute-start | bytes 6291464 | tf_op jit(solution)/shard_map/ppermute | solution.py:858
  660.4 16.4 %collective-permute-start.75 = (bf16[304,1024]{1,0:T(8,128)(2,1)S(1)}, bf16[304,1024]{1,0:T(8,128)(2,1)S(1)}, u32[]{:S(2)}, u32[]{:S(2)}) collective-permute-start(bf16[304,1024]{1,0:T(8,128)(2,1)S(1)} %copy-done.18), channel_id=1, source_target_pairs={{0,8},{4,12},{8,0},{12,4},{16,24},{20,28},{24,16},{28,20},{1,9},{5... | collective-permute-start | bytes 1867784 | tf_op jit(solution)/shard_map/ppermute | solution.py:858
  688.6 95.0 %collective-permute-start.82 = (bf16[4,256,512]{2,1,0:T(8,128)(2,1)}, bf16[4,256,512]{2,1,0:T(8,128)(2,1)S(1)}, u32[]{:S(2)}, u32[]{:S(2)}) collective-permute-start(bf16[4,256,512]{2,1,0:T(8,128)(2,1)} %get-tuple-element.242), channel_id=1, source_target_pairs={{0,16},{4,20},{8,24},{12,28},{16,0},{20,4},{24,8},{28,12},{1,17},{... | collective-permute-start | bytes 3145736 | tf_op jit(solution)/shard_map/ppermute | solution.py:858
  694.7 21.8 %collective-permute-start.78 = (f32[192,128]{1,0:T(8,128)S(1)}, f32[192,128]{1,0:T(8,128)S(1)}, u32[]{:S(2)}, u32[]{:S(2)}) collective-permute-start(f32[192,128]{1,0:T(8,128)S(1)} %add.240), channel_id=1, source_target_pairs={{0,16},{4,20},{8,24},{12,28},{16,0},{20,4},{24,8},{28,12},{1,17},{... | collective-permute-start | bytes 294920 | tf_op jit(solution)/shard_map/ppermute | solution.py:858
  718.0 70.2 %collective-permute-start.87 = (bf16[256,1024]{1,0:T(8,128)(2,1)}, bf16[256,1024]{1,0:T(8,128)(2,1)S(1)}, u32[]{:S(2)}, u32[]{:S(2)}) collective-permute-start(bf16[256,1024]{1,0:T(8,128)(2,1)} %get-tuple-element.249), channel_id=1, source_target_pairs={{0,3},{1,0},{2,1},{3,2},{4,7},{5,4},{6,5},{7,6},{8,11},{9,8},{10,9... | collective-permute-start | bytes 1572872 | tf_op jit(solution)/shard_map/ppermute | solution.py:861
  721.5 68.3 %collective-permute-start.88 = (bf16[256,1024]{1,0:T(8,128)(2,1)S(1)}, bf16[256,1024]{1,0:T(8,128)(2,1)}, u32[]{:S(2)}, u32[]{:S(2)}) collective-permute-start(bf16[256,1024]{1,0:T(8,128)(2,1)S(1)} %copy-done.54), channel_id=1, source_target_pairs={{0,2},{1,3},{2,0},{3,1},{4,6},{5,7},{6,4},{7,5},{8,10},{9,11},{10,... | collective-permute-start | bytes 1572872 | tf_op jit(solution)/shard_map/ppermute | solution.py:861
  721.5 69.8 %collective-permute-start.89 = (bf16[256,1024]{1,0:T(8,128)(2,1)S(1)}, bf16[256,1024]{1,0:T(8,128)(2,1)}, u32[]{:S(2)}, u32[]{:S(2)}) collective-permute-start(bf16[256,1024]{1,0:T(8,128)(2,1)S(1)} %copy-done.53), channel_id=1, source_target_pairs={{0,1},{1,2},{2,3},{3,0},{4,5},{5,6},{6,7},{7,4},{8,9},{9,10},{10,1... | collective-permute-start | bytes 1572872 | tf_op jit(solution)/shard_map/ppermute | solution.py:861
  727.6 55.9 %collective-permute-start.80 = (f32[192,128]{1,0:T(8,128)S(1)}, f32[192,128]{1,0:T(8,128)S(1)}, u32[]{:S(2)}, u32[]{:S(2)}) collective-permute-start(f32[192,128]{1,0:T(8,128)S(1)} %add.242), channel_id=1, source_target_pairs={{0,2},{1,3},{2,0},{3,1},{4,6},{5,7},{6,4},{7,5},{8,10},{9,11},{10,... | collective-permute-start | bytes 294920 | tf_op jit(solution)/shard_map/ppermute | solution.py:884
  788.2 22.1 %collective-permute-start.84 = (bf16[256,512]{1,0:T(8,128)(2,1)}, bf16[256,512]{1,0:T(8,128)(2,1)S(1)}, u32[]{:S(2)}, u32[]{:S(2)}) collective-permute-start(bf16[256,512]{1,0:T(8,128)(2,1)} %get-tuple-element.245), channel_id=1, source_target_pairs={{0,2},{1,3},{2,0},{3,1},{4,6},{5,7},{6,4},{7,5},{8,10},{9,11},{10,... | collective-permute-start | bytes 786440 | tf_op jit(solution)/shard_map/ppermute | solution.py:861
  788.2 22.1 %collective-permute-start.85 = (bf16[256,512]{1,0:T(8,128)(2,1)}, bf16[256,512]{1,0:T(8,128)(2,1)S(1)}, u32[]{:S(2)}, u32[]{:S(2)}) collective-permute-start(bf16[256,512]{1,0:T(8,128)(2,1)} %get-tuple-element.246), channel_id=1, source_target_pairs={{0,1},{1,2},{2,3},{3,0},{4,5},{5,6},{6,7},{7,4},{8,9},{9,10},{10,1... | collective-permute-start | bytes 786440 | tf_op jit(solution)/shard_map/ppermute | solution.py:861
  789.8 29.5 %collective-permute-start.92 = (bf16[128,1024]{1,0:T(8,128)(2,1)S(1)}, bf16[128,1024]{1,0:T(8,128)(2,1)S(1)}, u32[]{:S(2)}, u32[]{:S(2)}) collective-permute-start(bf16[128,1024]{1,0:T(8,128)(2,1)S(1)} %copy-done.77), channel_id=1, source_target_pairs={{0,8},{4,12},{8,0},{12,4},{16,24},{20,28},{24,16},{28,20},{1,9},{5... | collective-permute-start | bytes 786440 | tf_op jit(solution)/shard_map/ppermute | solution.py:858
  791.3 28.0 %collective-permute-start.91 = (bf16[128,512]{1,0:T(8,128)(2,1)}, bf16[128,512]{1,0:T(8,128)(2,1)S(1)}, u32[]{:S(2)}, u32[]{:S(2)}) collective-permute-start(bf16[128,512]{1,0:T(8,128)(2,1)} %get-tuple-element.254), channel_id=1, source_target_pairs={{0,8},{4,12},{8,0},{12,4},{16,24},{20,28},{24,16},{28,20},{1,9},{5... | collective-permute-start | bytes 393224 | tf_op jit(solution)/shard_map/ppermute | solution.py:858
  796.9 22.4 %collective-permute-start.90 = (bf16[128,1024]{1,0:T(8,128)(2,1)}, bf16[128,1024]{1,0:T(8,128)(2,1)S(1)}, u32[]{:S(2)}, u32[]{:S(2)}) collective-permute-start(bf16[128,1024]{1,0:T(8,128)(2,1)} %get-tuple-element.253), channel_id=1, source_target_pairs={{0,8},{4,12},{8,0},{12,4},{16,24},{20,28},{24,16},{28,20},{1,9},{5... | collective-permute-start | bytes 786440 | tf_op jit(solution)/shard_map/ppermute | solution.py:858
  (119 other events, 1288.9 us)
Sparse Core Ops, SparseCore 0:
  498.1 86.2 all-gather.4
  682.1 61.6 all-gather.6

commit v2 on v1

v2 whole, which is shorter than its diff:
```python
import functools

import jax
import jax.numpy as jnp
from jax import lax
from jax.experimental import pallas as pl
from jax.experimental.pallas import tpu as pltpu
from jax.sharding import Mesh
from jax.sharding import PartitionSpec as P

HEAD_DIM = 64
EPS = 1e-06
F32 = jnp.float32
BF16 = jnp.bfloat16
ROWS = 304
WIN = 112
WIN_STEP = 96
BIG_NEG = -1e30
VMEM_LIMIT = 60 * 1024 * 1024


def dot_nn(a, b):
    return lax.dot_general(a, b, (((1,), (0,)), ((), ())), preferred_element_type=F32)


def dot_nt(a, b):
    return lax.dot_general(a, b, (((1,), (1,)), ((), ())), preferred_element_type=F32)


def dot_tn(a, b):
    return lax.dot_general(a, b, (((0,), (0,)), ((), ())), preferred_element_type=F32)


def params(micros):
    return dict(
        compiler_params=pltpu.CompilerParams(vmem_limit_bytes=VMEM_LIMIT),
        cost_estimate=pl.CostEstimate(
            flops=int(micros * 4e9), bytes_accessed=0, transcendentals=0
        ),
    )


VM = pl.BlockSpec(memory_space=pltpu.VMEM)
SM = pl.BlockSpec(memory_space=pltpu.SMEM)
HB = pl.BlockSpec(memory_space=pl.ANY)


def layer_norm(x, gain, bias):
    mean = jnp.mean(x, axis=-1, keepdims=True)
    centered = x - mean
    variance = jnp.mean(centered * centered, axis=-1, keepdims=True)
    return centered * lax.rsqrt(variance + EPS) * gain + bias


def own_selector(place, seq, mine):
    images = 4 * mine
    row = lax.broadcasted_iota(jnp.int32, (ROWS, images * seq), 0)
    col = lax.broadcasted_iota(jnp.int32, (ROWS, images * seq), 1)
    token = col // images
    image = col - token * images - place[DEPTH] * mine
    hit = (image >= 0) & (image < mine) & (row == image * seq + token)
    return jnp.where(hit, 1.0, 0.0).astype(BF16)


def enter_kernel(seq, mine, place, x_ref, gain_ref, beta_ref, x1_ref, a_ref):
    x = dot_nn(own_selector(place, seq, mine), x_ref[...])
    x1_ref[...] = x
    a_ref[...] = layer_norm(x, gain_ref[...], beta_ref[...]).astype(BF16)


def enter_back_kernel(seq, mine, place, x_ref, g_ref, gb_ref, sum_ref):
    g = dot_nn(own_selector(place, seq, mine), x_ref[...])
    g_ref[...] = g
    gb_ref[...] = g.astype(BF16)
    sum_ref[...] = jnp.broadcast_to(jnp.sum(g, axis=0, keepdims=True), sum_ref.shape)


def leave_kernel(seq, mine, place, *refs):
    parts, out_ref = refs[:-1], refs[-1]
    images = 4 * mine
    count = images * seq
    row = lax.broadcasted_iota(jnp.int32, (count, ROWS), 0)
    col = lax.broadcasted_iota(jnp.int32, (count, ROWS), 1)
    token = row // images
    want = row - token * images
    total = None
    for step, part_ref in zip((0, 1, 3, 2), parts):
        image = want - ((place[DEPTH] - step) & 3) * mine
        hit = (image >= 0) & (image < mine) & (col == image * seq + token)
        part = dot_nn(jnp.where(hit, 1.0, 0.0).astype(BF16), part_ref[...])
        total = part if total is None else total + part
    out_ref[...] = total.astype(out_ref.dtype)


def residual_norm_kernel(
    x_ref, own_ref, far_ref, bias_ref, gain_ref, beta_ref, x1_ref, a_ref, far, sem
):
    copy = pltpu.make_async_copy(far_ref, far, sem)
    copy.start()
    keep = lax.broadcasted_iota(jnp.int32, (ROWS, 1), 0) < 300
    bias = jnp.where(keep, bias_ref[...], 0.0)
    copy.wait()
    x1 = x_ref[...] + own_ref[...].astype(F32) + far[...].astype(F32) + bias
    x1_ref[...] = x1
    a_ref[...] = layer_norm(x1, gain_ref[...], beta_ref[...]).astype(BF16)


def residual_kernel(x_ref, own_ref, far_ref, bias_ref, x1_ref, far, sem):
    copy = pltpu.make_async_copy(far_ref, far, sem)
    copy.start()
    copy.wait()
    x1 = x_ref[...] + own_ref[...].astype(F32) + far[...].astype(F32) + bias_ref[...]
    x1_ref[...] = x1.astype(BF16)


def norm_back_kernel(
    g_ref, own_ref, far_ref, x_ref, gain_ref, g1_ref, g1b_ref, sums_ref, far, sem
):
    copy = pltpu.make_async_copy(far_ref, far, sem)
    copy.start()
    x = x_ref[...]
    mean = jnp.mean(x, axis=-1, keepdims=True)
    centered = x - mean
    variance = jnp.mean(centered * centered, axis=-1, keepdims=True)
    inverse = lax.rsqrt(variance + EPS)
    xhat = centered * inverse
    copy.wait()
    da = own_ref[...].astype(F32) + far[...].astype(F32)
    inner = da * gain_ref[...]
    mean_inner = jnp.mean(inner, axis=-1, keepdims=True)
    mean_proj = jnp.mean(inner * xhat, axis=-1, keepdims=True)
    g1 = g_ref[...] + inverse * (inner - mean_inner - xhat * mean_proj)
    g1_ref[...] = g1
    g1b_ref[...] = g1.astype(BF16)
    sums_ref[...] = jnp.zeros(sums_ref.shape, F32)
    sums_ref[0:1, :] = jnp.sum(da * xhat, axis=0, keepdims=True)
    sums_ref[1:2, :] = jnp.sum(da, axis=0, keepdims=True)
    sums_ref[2:3, :] = jnp.sum(g1, axis=0, keepdims=True)


def run_enter(place, images, mine, gain, beta):
    count, seq, width = images.shape
    flat = images.transpose(1, 0, 2).reshape(count * seq, width)
    return pl.pallas_call(
        functools.partial(enter_kernel, seq, mine),
        out_shape=(
            jax.ShapeDtypeStruct((ROWS, width), F32),
            jax.ShapeDtypeStruct((ROWS, width), BF16),
        ),
        in_specs=[SM, VM, VM, VM],
        out_specs=(VM, VM),
        **params(5),
    )(place, flat, gain[None], beta[None])


def run_enter_back(place, images, mine):
    count, seq, width = images.shape
    flat = images.transpose(1, 0, 2).reshape(count * seq, width)
    return pl.pallas_call(
        functools.partial(enter_back_kernel, seq, mine),
        out_shape=(
            jax.ShapeDtypeStruct((ROWS, width), F32),
            jax.ShapeDtypeStruct((ROWS, width), BF16),
            jax.ShapeDtypeStruct((8, width), F32),
        ),
        in_specs=[SM, VM],
        out_specs=(VM, VM, VM),
        **params(5),
    )(place, flat)


def run_leave(place, parts, seq, mine, dtype):
    images, width = 4 * mine, parts[0].shape[1]
    flat = pl.pallas_call(
        functools.partial(leave_kernel, seq, mine),
        out_shape=jax.ShapeDtypeStruct((images * seq, width), dtype),
        in_specs=[SM, VM, VM, VM, VM],
        out_specs=VM,
        **params(9),
    )(place, *parts)
    return flat.reshape(seq, images, width).transpose(1, 0, 2)


def run_residual_norm(x, own, far, bias, gain, beta):
    return pl.pallas_call(
        residual_norm_kernel,
        out_shape=(
            jax.ShapeDtypeStruct(x.shape, F32),
            jax.ShapeDtypeStruct(x.shape, BF16),
        ),
        in_specs=[VM, VM, HB, VM, VM, VM],
        out_specs=(VM, VM),
        scratch_shapes=[pltpu.VMEM((ROWS, x.shape[1]), BF16), pltpu.SemaphoreType.DMA],
        **params(3),
    )(x, own, far, bias[None], gain[None], beta[None])


def run_residual(x, own, far, bias):
    return pl.pallas_call(
        residual_kernel,
        out_shape=jax.ShapeDtypeStruct(x.shape, BF16),
        in_specs=[VM, VM, HB, VM],
        out_specs=VM,
        scratch_shapes=[pltpu.VMEM((ROWS, x.shape[1]), BF16), pltpu.SemaphoreType.DMA],
        **params(2),
    )(x, own, far, bias[None])


def run_norm_back(g, own, far, x, gain):
    return pl.pallas_call(
        norm_back_kernel,
        out_shape=(
            jax.ShapeDtypeStruct(x.shape, F32),
            jax.ShapeDtypeStruct(x.shape, BF16),
            jax.ShapeDtypeStruct((8, x.shape[1]), F32),
        ),
        in_specs=[VM, VM, HB, VM, VM],
        out_specs=(VM, VM, VM),
        scratch_shapes=[pltpu.VMEM((ROWS, x.shape[1]), BF16), pltpu.SemaphoreType.DMA],
        **params(4),
    )(g, own, far, x, gain[None])


SIDE, CORE, PAIR, DEPTH, PARTS = 0, 1, 2, 3, 4

ATTN_ROWS, MLP_ROWS = 272, 528
ATTN_SPAN, MLP_SPAN = pl.ds(MLP_ROWS, ATTN_ROWS), pl.ds(0, MLP_ROWS)


def exact_rows(bias):
    high = bias.astype(BF16)
    rest = bias - high.astype(F32)
    mid = rest.astype(BF16)
    low = (rest - mid.astype(F32)).astype(BF16)
    return jnp.concatenate([high, mid, low, jnp.zeros((13, bias.shape[1]), BF16)], axis=0)


def pack_kernel(
    place, wqkv, wproj, w1, w2, bqv, b1, attn0, middle, mlp1, sems
):
    row = aligned(place[PARTS], 256)
    narrow, wide = aligned(place[PAIR], 128), aligned(place[PAIR], 512)
    copies = []
    mlp0, attn1 = middle.at[0:MLP_ROWS], middle.at[MLP_ROWS:]
    for layer, (attn, mlp) in enumerate(((attn0, mlp0), (attn1, mlp1))):
        for item in range(3):
            copies.append(
                (
                    wqkv.at[layer, item, pl.ds(row, 256), pl.ds(narrow, 128)],
                    attn.at[0:256, pl.ds(item * 128, 128)],
                )
            )
        for half in range(2):
            copies.append(
                (
                    wproj.at[layer, pl.ds(narrow, 128), pl.ds(row + half * 128, 128)],
                    attn.at[pl.ds(half * 128, 128), 384:512],
                )
            )
            copies.append(
                (
                    w2.at[layer, pl.ds(wide + half * 256, 256), pl.ds(row, 256)],
                    mlp.at[256:512, pl.ds(half * 256, 256)],
                )
            )
        copies.append(
            (w1.at[layer, pl.ds(row, 256), pl.ds(wide, 512)], mlp.at[0:256, :])
        )
    copies = [
        pltpu.make_async_copy(src, dst, sems.at[index])
        for index, (src, dst) in enumerate(copies)
    ]
    for copy in copies:
        copy.start()
    for layer, (attn, mlp) in enumerate(((attn0, mlp0), (attn1, mlp1))):
        zero = jnp.zeros((1, 128), F32)
        bias = [bqv[layer, pl.ds(item, 1), pl.ds(narrow, 128)] for item in range(2)]
        attn[256:272, :] = exact_rows(jnp.concatenate([bias[0], zero, bias[1], zero], axis=1))
        mlp[512:528, :] = exact_rows(b1[pl.ds(layer, 1), pl.ds(wide, 512)])
    for copy in copies:
        copy.wait()


def run_pack(place, wqkv, wproj, w1, w2, bqv, b1):
    return pl.pallas_call(
        pack_kernel,
        out_shape=tuple(
            jax.ShapeDtypeStruct((rows, 512), BF16)
            for rows in (ATTN_ROWS, MLP_ROWS + ATTN_ROWS, MLP_ROWS)
        ),
        in_specs=[SM, HB, HB, HB, HB, VM, VM],
        out_specs=(VM, VM, VM),
        scratch_shapes=[pltpu.SemaphoreType.DMA((16,))],
        **params(3),
    )(place, wqkv, wproj, w1, w2, bqv, b1)


def piece_sources(place, pieces, own):
    if not own:
        array, rows = pieces
        return [
            (depth, 2 * side + core, array.at[side, core, depth, rows])
            for depth in range(4)
            for side in range(2)
            for core in range(2)
        ]
    return [
        ((place[DEPTH] - step) & 3, place[PARTS + slot], pieces[4 * step - 4 + slot])
        for step in range(1, 4)
        for slot in range(4)
    ]


def aligned(index, step):
    if isinstance(index, int):
        return index * step
    return pl.multiple_of(index * step, step)


def start_attention_copies(layer, place, wqkv, wproj, bqv, pieces, wq, wp, sems, bs=None):
    own = len(pieces) > 2
    for index, (depth, part, src) in enumerate(piece_sources(place, pieces, own)):
        row = aligned(part, 256)
        pltpu.make_async_copy(
            src.at[0:256, 0:384], wq.at[depth, pl.ds(row, 256), :], sems.at[0, depth]
        ).start()
        for side in range(2):
            pltpu.make_async_copy(
                src.at[pl.ds(side * 128, 128), 384:512],
                wp.at[depth, :, pl.ds(row + side * 128, 128)],
                sems.at[1, depth],
            ).start()
        if bs is not None and index % 4 == 0:
            pltpu.make_async_copy(src.at[256:272, 0:384], bs.at[depth], sems.at[2, depth]).start()
    if own:
        depth, narrow = place[DEPTH], aligned(place[PAIR], 128)
        for item in range(3):
            pltpu.make_async_copy(
                wqkv.at[layer, item, :, pl.ds(narrow, 128)],
                wq.at[depth, :, pl.ds(item * 128, 128)],
                sems.at[0, depth],
            ).start()
        pltpu.make_async_copy(
            wproj.at[layer, pl.ds(narrow, 128), :], wp.at[depth], sems.at[1, depth]
        ).start()
        if bs is not None:
            bias = [bqv[layer, pl.ds(item, 1), pl.ds(narrow, 128)] for item in range(2)]
            zero = jnp.zeros((1, 128), F32)
            bs[depth] = exact_rows(jnp.concatenate([bias[0], zero, bias[1]], axis=1))


def start_mlp_copies(pieces, w1, w2, sems, bs=None):
    for index, (depth, part, src) in enumerate(piece_sources(None, pieces, False)):
        row = part * 256
        pltpu.make_async_copy(
            src.at[0:256, :], w1.at[depth, pl.ds(row, 256), :], sems.at[0, depth]
        ).start()
        for side in range(2):
            pltpu.make_async_copy(
                src.at[256:512, pl.ds(side * 256, 256)],
                w2.at[depth, pl.ds(side * 256, 256), pl.ds(row, 256)],
                sems.at[1, depth],
            ).start()
        if bs is not None and index % 4 == 0:
            pltpu.make_async_copy(src.at[512:528, :], bs.at[depth], sems.at[2, depth]).start()


def start_rows(source, rows, sems):
    copy = pltpu.make_async_copy(source, rows, sems.at[3, 0])
    copy.start()
    return copy


def wait_chunk(chunk, bufs, sems):
    for slot, buf in enumerate(bufs):
        pltpu.make_async_copy(buf.at[chunk], buf.at[chunk], sems.at[slot, chunk]).wait()


def wait_bias(chunk, bs, sems, own=None):
    def wait():
        pltpu.make_async_copy(bs.at[chunk], bs.at[chunk], sems.at[2, chunk]).wait()

    if own is None:
        wait()
    else:
        pl.when(chunk != own)(wait)


def window_masks(window):
    shape = (2 * WIN, WIN)
    row = lax.broadcasted_iota(jnp.int32, shape, 0)
    row = jnp.where(row >= WIN, row - WIN, row) - 4 * window
    col = lax.broadcasted_iota(jnp.int32, shape, 1) - 4 * window
    row_ok = (row >= 0) & (row < 100)
    col_ok = (col >= 0) & (col < 100)
    same = row_ok & col_ok & ((row >= 50) == (col >= 50))
    return jnp.where(same, 0.0, BIG_NEG).astype(F32)


def window_rows_ok(window):
    row = lax.broadcasted_iota(jnp.int32, (2 * WIN, 1), 0)
    row = jnp.where(row >= WIN, row - WIN, row) - 4 * window
    return (row >= 0) & (row < 100)


def stack_heads(values, first):
    zero = jnp.zeros_like(values)
    return jnp.concatenate(
        [jnp.where(first, values, zero), jnp.where(first, zero, values)], axis=0
    )


def first_head_lanes():
    return lax.broadcasted_iota(jnp.int32, (WIN, 2 * HEAD_DIM), 1) < HEAD_DIM


def window_probs(query, key, mask, rows_ok):
    scores = dot_nt(query, key) * (HEAD_DIM**-0.5) + mask
    top = jnp.max(scores, axis=-1, keepdims=True)
    expo = jnp.exp(scores - top)
    total = jnp.sum(expo, axis=-1, keepdims=True)
    return expo * jnp.where(rows_ok, 1.0 / total, 0.0)


def join_windows(parts):
    first, second, third = parts
    over = WIN - WIN_STEP
    return jnp.concatenate(
        [
            first[:WIN_STEP],
            first[WIN_STEP:] + second[:over],
            second[over:WIN_STEP],
            second[WIN_STEP:] + third[:over],
            third[over:],
        ],
        axis=0,
    )


def attention_forward_kernel(layer, count, place, a_ref, wqkv, wproj, bqv, *refs):
    pieces = refs[:count] if count > 1 else (refs[0], ATTN_SPAN)
    qkv_ref, o_ref, r_ref, wq, wp, bs, rows, total, masks, sems = refs[count:]
    own_quarter = place[DEPTH] if count > 1 else None
    copy = start_rows(a_ref, rows, sems)
    start_attention_copies(layer, place, wqkv, wproj, bqv, pieces, wq, wp, sems, bs)
    for window in range(3):
        masks[window] = window_masks(window)
    copy.wait()

    def chunk_step(chunk, carry):
        wait_chunk(chunk, (wq, wp), sems)
        wait_bias(chunk, bs, sems, own_quarter)
        bias = jnp.sum(bs[chunk].astype(F32), axis=0, keepdims=True)
        qkv_ref[chunk] = (dot_nn(rows[...], wq[chunk]) + bias).astype(BF16)
        first = first_head_lanes()
        outs = []
        for window in range(3):
            span = pl.ds(window * WIN_STEP, WIN)
            query = stack_heads(qkv_ref[chunk, span, 0:128], first)
            probs = window_probs(
                query, qkv_ref[chunk, span, 128:256], masks[window], window_rows_ok(window)
            )
            mixed = dot_nn(probs.astype(BF16), qkv_ref[chunk, span, 256:384])
            outs.append(jnp.where(first, mixed[:WIN], mixed[WIN:]))
        o_ref[chunk] = join_windows(outs).astype(BF16)
        add_part(chunk, total, dot_nn(o_ref[chunk], wp[chunk]))
        return carry

    lax.fori_loop(0, 4, chunk_step, 0)
    r_ref[...] = total[...].astype(BF16)


def add_part(chunk, total, part):
    @pl.when(chunk == 0)
    def _():
        total[...] = part

    @pl.when(chunk > 0)
    def _():
        total[...] += part


def run_attention_forward(layer, place, rows, weights, pieces):
    width = rows.shape[1]
    return pl.pallas_call(
        functools.partial(attention_forward_kernel, layer, len(pieces)),
        out_shape=(
            jax.ShapeDtypeStruct((4, ROWS, 384), BF16),
            jax.ShapeDtypeStruct((4, ROWS, 128), BF16),
            jax.ShapeDtypeStruct((ROWS, width), BF16),
        ),
        in_specs=[SM, HB, HB, HB, VM] + [HB] * len(pieces),
        out_specs=(VM,) * 3,
        scratch_shapes=[
            pltpu.VMEM((4, width, 384), BF16),
            pltpu.VMEM((4, 128, width), BF16),
            pltpu.VMEM((4, 16, 384), BF16),
            pltpu.VMEM((ROWS, width), BF16),
            pltpu.VMEM((ROWS, width), F32),
            pltpu.VMEM((3, 2 * WIN, WIN), F32),
            pltpu.SemaphoreType.DMA((4, 4)),
        ],
        **params(7),
    )(place, rows, *weights, *pieces)


def attention_backward_kernel(layer, count, place, g_ref, qkv_ref, wqkv, wproj, *refs):
    pieces = refs[:count] if count > 1 else (refs[0], ATTN_SPAN)
    dqkv_ref, sums_ref, d_ref, wq, wp, rows, total, masks, gmix, sems = refs[count:]
    copy = start_rows(g_ref, rows, sems)
    start_attention_copies(layer, place, wqkv, wproj, None, pieces, wq, wp, sems)
    for window in range(3):
        masks[window] = window_masks(window)
    copy.wait()

    def chunk_step(chunk, carry):
        wait_chunk(chunk, (wq, wp), sems)
        gmix[...] = dot_nt(rows[...], wp[chunk]).astype(BF16)
        first = first_head_lanes()
        scale = HEAD_DIM**-0.5
        outs = []
        for window in range(3):
            span = pl.ds(window * WIN_STEP, WIN)
            query = stack_heads(qkv_ref[chunk, span, 0:128], first)
            key = qkv_ref[chunk, span, 128:256]
            grad = stack_heads(gmix[span, :], first)
            probs = window_probs(query, key, masks[window], window_rows_ok(window))
            gprobs = dot_nt(grad, qkv_ref[chunk, span, 256:384])
            gvalue = dot_tn(probs.astype(BF16), grad)
            inner = jnp.sum(gprobs * probs, axis=-1, keepdims=True)
            gscores = (probs * (gprobs - inner)).astype(BF16)
            gquery = dot_nn(gscores, key) * scale
            gkey = dot_tn(gscores, query) * scale
            outs.append((jnp.where(first, gquery[:WIN], gquery[WIN:]), gkey, gvalue))
        joined = jnp.concatenate(
            [join_windows([out[item] for out in outs]) for item in range(3)], axis=1
        ).astype(BF16)
        dqkv_ref[chunk] = joined
        sums_ref[chunk] = jnp.broadcast_to(
            jnp.sum(joined.astype(F32), axis=0, keepdims=True), (8, 384)
        )
        add_part(chunk, total, dot_nt(dqkv_ref[chunk], wq[chunk]))
        return carry

    lax.fori_loop(0, 4, chunk_step, 0)
    d_ref[...] = total[...].astype(BF16)


def run_attention_backward(layer, place, grad, qkv, weights, pieces):
    width = grad.shape[1]
    return pl.pallas_call(
        functools.partial(attention_backward_kernel, layer, len(pieces)),
        out_shape=(
            jax.ShapeDtypeStruct((4, ROWS, 384), BF16),
            jax.ShapeDtypeStruct((4, 8, 384), F32),
            jax.ShapeDtypeStruct((ROWS, width), BF16),
        ),
        in_specs=[SM, HB, VM, HB, HB] + [HB] * len(pieces),
        out_specs=(VM,) * 3,
        scratch_shapes=[
            pltpu.VMEM((4, width, 384), BF16),
            pltpu.VMEM((4, 128, width), BF16),
            pltpu.VMEM((ROWS, width), BF16),
            pltpu.VMEM((ROWS, width), F32),
            pltpu.VMEM((3, 2 * WIN, WIN), F32),
            pltpu.VMEM((ROWS, 128), BF16),
            pltpu.SemaphoreType.DMA((4, 4)),
        ],
        **params(12),
    )(place, grad, qkv, *weights[:2], *pieces)


def gelu_pair(u):
    size = jnp.abs(u) * (0.5**0.5)
    t = 1.0 / (1.0 + 0.3275911 * size)
    poly = t * (
        0.254829592
        + t * (-0.284496736 + t * (1.421413741 + t * (-1.453152027 + t * 1.061405429)))
    )
    bell = jnp.exp(-0.5 * u * u)
    tail = 0.5 * poly * bell
    phi = jnp.where(u >= 0.0, 1.0 - tail, tail)
    return u * phi, phi + u * bell * 0.3989422804014327


def mlp_forward_kernel(
    a_ref, pieces, h_ref, slope_ref, m_ref, w1, w2, bs, rows, total, sems
):
    copy = start_rows(a_ref, rows, sems)
    start_mlp_copies((pieces, MLP_SPAN), w1, w2, sems, bs)
    copy.wait()

    def chunk_step(chunk, carry):
        wait_chunk(chunk, (w1, w2), sems)
        wait_bias(chunk, bs, sems)
        bias = jnp.sum(bs[chunk].astype(F32), axis=0, keepdims=True)
        value, slope = gelu_pair(dot_nn(rows[...], w1[chunk]) + bias)
        h_ref[chunk] = value.astype(BF16)
        slope_ref[chunk] = slope.astype(BF16)
        add_part(chunk, total, dot_nn(h_ref[chunk], w2[chunk]))
        return carry

    lax.fori_loop(0, 4, chunk_step, 0)
    m_ref[...] = total[...].astype(BF16)


def run_mlp_forward(rows, pieces):
    width = rows.shape[1]
    return pl.pallas_call(
        mlp_forward_kernel,
        out_shape=(
            jax.ShapeDtypeStruct((4, ROWS, 512), BF16),
            jax.ShapeDtypeStruct((4, ROWS, 512), BF16),
            jax.ShapeDtypeStruct((ROWS, width), BF16),
        ),
        in_specs=[HB, HB],
        out_specs=(VM,) * 3,
        scratch_shapes=[
            pltpu.VMEM((4, width, 512), BF16),
            pltpu.VMEM((4, 512, width), BF16),
            pltpu.VMEM((4, 16, 512), BF16),
            pltpu.VMEM((ROWS, width), BF16),
            pltpu.VMEM((ROWS, width), F32),
            pltpu.SemaphoreType.DMA((4, 4)),
        ],
        **params(8),
    )(rows, pieces)


def mlp_backward_kernel(
    g_ref, slope_ref, pieces, du_ref, sums_ref, d_ref, w1, w2, rows, total, sems
):
    copy = start_rows(g_ref, rows, sems)
    start_mlp_copies((pieces, MLP_SPAN), w1, w2, sems)
    copy.wait()

    def chunk_step(chunk, carry):
        wait_chunk(chunk, (w1, w2), sems)
        grad = dot_nt(rows[...], w2[chunk]) * slope_ref[chunk].astype(F32)
        grad = grad.astype(BF16)
        du_ref[chunk] = grad
        sums_ref[chunk] = jnp.broadcast_to(
            jnp.sum(grad.astype(F32), axis=0, keepdims=True), (8, 512)
        )
        add_part(chunk, total, dot_nt(du_ref[chunk], w1[chunk]))
        return carry

    lax.fori_loop(0, 4, chunk_step, 0)
    d_ref[...] = total[...].astype(BF16)


def run_mlp_backward(grad, slope, pieces):
    width = grad.shape[1]
    return pl.pallas_call(
        mlp_backward_kernel,
        out_shape=(
            jax.ShapeDtypeStruct((4, ROWS, 512), BF16),
            jax.ShapeDtypeStruct((4, 8, 512), F32),
            jax.ShapeDtypeStruct((ROWS, width), BF16),
        ),
        in_specs=[HB, VM, HB],
        out_specs=(VM,) * 3,
        scratch_shapes=[
            pltpu.VMEM((4, width, 512), BF16),
            pltpu.VMEM((4, 512, width), BF16),
            pltpu.VMEM((ROWS, width), BF16),
            pltpu.VMEM((ROWS, width), F32),
            pltpu.SemaphoreType.DMA((4, 4)),
        ],
        **params(7),
    )(grad, slope, pieces)


def weight_grad_kernel(
    kind, place, x1_own, x1_far, y1_own, y1_far, x2_own, x2_far, y2_own, y2_far, *refs
):
    (xs, y1, y2, turned, sems), refs = refs[-5:], refs[:-5]
    if kind == "relative":
        near_ref, away_ref, send_ref = refs
        outs = (near_ref, send_ref.at[0], away_ref, send_ref.at[1])
    else:
        outs = [refs[-1].at[side, core] for side in range(2) for core in range(2)]
    top, low = pl.ds(0, ROWS), pl.ds(ROWS, ROWS)
    pairs = [
        (x1_own, xs.at[0, top]),
        (x1_far, xs.at[0, low]),
        (x2_own, xs.at[1, top]),
        (x2_far, xs.at[1, low]),
        (y1_own, y1.at[:, top]),
        (y1_far, y1.at[:, low]),
        (y2_own, y2.at[:, top]),
        (y2_far, y2.at[:, low]),
    ]
    if kind == "extra":
        pairs += [
            (refs[0].at[slot // 2, slot % 2], out.at[:, 256:384, :])
            for slot, out in enumerate(outs)
        ]
    copies = [
        pltpu.make_async_copy(src, dst, sems.at[index]) for index, (src, dst) in enumerate(pairs)
    ]
    for copy in copies:
        copy.start()
    span1, span2 = y1.shape[2], y2.shape[2]
    span = span1 + span2
    for index in range(2):
        copies[2 * index].wait()
        copies[2 * index + 1].wait()
        for slot in range(4):
            side, core = slot // 2, slot % 2
            if kind == "relative":
                start = (place[SIDE] ^ side) * 512 + (place[CORE] ^ core) * 128
                start = pl.multiple_of(start, 128)
            else:
                start = side * 512 + core * 128
            cols = jnp.concatenate(
                [xs[index, :, pl.ds(start, 128)], xs[index, :, pl.ds(start + 256, 128)]], axis=1
            )
            turned[index, slot] = cols.T
    for copy in copies[4:8]:
        copy.wait()

    def chunk_step(chunk, carry):
        for slot, out in enumerate(outs):
            first = dot_nn(turned[0, slot], y1[chunk]).astype(BF16)
            second = dot_nn(turned[1, slot], y2[chunk]).astype(BF16)
            if kind == "compact":
                for side in range(2):
                    rows = slice(128 * side, 128 * side + 128)
                    out[chunk, :, span * side : span * side + span1] = first[rows]
                    out[chunk, :, span * side + span1 : span * side + span] = second[rows]
            else:
                out[chunk, 0:256, 0:span1] = first
                out[chunk, 0:256, span1:span] = second
        return carry

    lax.fori_loop(0, 4, chunk_step, 0)
    for copy in copies[8:]:
        copy.wait()


def run_weight_grad(kind, place, x1, y1, x2, y2, *extra):
    rows, width = 2 * ROWS, x1[0].shape[1]
    span1, span2 = y1[0].shape[2], y2[0].shape[2]
    span = span1 + span2
    if kind == "relative":
        half = jax.ShapeDtypeStruct((4, width // 4, span), BF16)
        shapes = (half, half, jax.ShapeDtypeStruct((2, *half.shape), BF16))
    else:
        shape = {"plain": (256, span), "compact": (128, 2 * span), "extra": (384, span)}[kind]
        shapes = (jax.ShapeDtypeStruct((2, 2, 4, *shape), BF16),)
    return pl.pallas_call(
        functools.partial(weight_grad_kernel, kind),
        out_shape=shapes,
        in_specs=[SM] + [HB] * (8 + len(extra)),
        out_specs=(VM,) * len(shapes),
        scratch_shapes=[
            pltpu.VMEM((2, rows, width), BF16),
            pltpu.VMEM((4, rows, span1), BF16),
            pltpu.VMEM((4, rows, span2), BF16),
            pltpu.VMEM((2, 4, width // 4, rows), BF16),
            pltpu.SemaphoreType.DMA((12,)),
        ],
        **params(14 if span1 > 384 else 10),
    )(place, *x1, *y1, *x2, *y2, *extra)


def add_core_kernel(near, away, got, near_out, away_out):
    near_out[...] = (near[...].astype(F32) + got[0].astype(F32)).astype(BF16)
    away_out[...] = (away[...].astype(F32) + got[1].astype(F32)).astype(BF16)


def run_add_core(near, away, got):
    chunks, rows, span = near.shape
    one = pl.BlockSpec((1, rows, span), lambda step: (step, 0, 0))
    two = pl.BlockSpec((2, 1, rows, span), lambda step: (0, step, 0, 0))
    shape = jax.ShapeDtypeStruct(near.shape, BF16)
    return pl.pallas_call(
        add_core_kernel,
        grid=(chunks,),
        out_shape=(shape, shape),
        in_specs=[one, one, two],
        out_specs=(one, one),
        **params(4),
    )(near, away, got)


def add_side_kernel(place, near, got, *outs):
    for step, out in enumerate(outs):
        depth = (place[DEPTH] + step) & 3
        out[...] = (near[depth].astype(F32) + got[depth].astype(F32)).astype(out.dtype)


def run_add_side(place, near, got):
    chunks, rows, span = near.shape
    return pl.pallas_call(
        add_side_kernel,
        out_shape=tuple(
            jax.ShapeDtypeStruct((rows, span), BF16 if step else F32) for step in range(chunks)
        ),
        in_specs=[SM, VM, VM],
        out_specs=(VM,) * chunks,
        **params(3),
    )(place, near, got)


def add_depth_kernel(place, *refs):
    parts, (stay, move) = refs[:-2], refs[-2:]
    total = parts[0][...].astype(F32)
    for part in parts[1:]:
        total += part[...].astype(F32)
    half = total.shape[0] // 2
    low, high = total[:half], total[half:]
    even = place[PAIR] == 0
    stay[...] = jnp.where(even, low, high).astype(BF16)
    move[...] = jnp.where(even, high, low).astype(BF16)


def run_add_depth(place, parts):
    rows, span = parts[0].shape
    shape = jax.ShapeDtypeStruct((rows // 2, span), BF16)
    return pl.pallas_call(
        add_depth_kernel,
        out_shape=(shape, shape),
        in_specs=[SM] + [VM] * len(parts),
        out_specs=(VM, VM),
        **params(2),
    )(place, *parts)


def collect_kernel(place, fc2_last, *refs):
    out = refs[-1]
    layers = (len(refs) - 1) // 6
    narrow, wide = aligned(place[PAIR], 128), aligned(place[PAIR], 512)
    out[...] = jnp.zeros(out.shape, F32)
    for layer in range(layers):
        sums1, sums2, qv_own, qv_far, fc1_own, fc1_far = refs[6 * layer : 6 * layer + 6]
        row = 12 * layer
        out[row : row + 2, :] = sums1[0:2, :]
        out[row + 2 : row + 3, :] = sums2[2:3, :]
        out[row + 3 : row + 5, :] = sums2[0:2, :]
        above = refs[6 * layer + 6][2:3, :] if layer + 1 < layers else fc2_last[0:1, :]
        out[row + 5 : row + 6, :] = above
        for depth in range(4):
            qv = qv_own[depth, 0:1, :] + qv_far[depth, 0:1, :]
            for item in range(2):
                out[row + 6 + item, pl.ds(depth * 256 + narrow, 128)] = qv[
                    0, 256 * item : 256 * item + 128
                ]
            fc1 = fc1_own[depth, 0:1, :] + fc1_far[depth, 0:1, :]
            out[pl.ds(row + 8 + depth, 1), pl.ds(wide, 512)] = fc1


def run_collect(place, fc2_last, parts):
    layers = len(parts) // 6
    return pl.pallas_call(
        collect_kernel,
        out_shape=jax.ShapeDtypeStruct((12 * layers, 1024), F32),
        in_specs=[SM] + [VM] * (1 + len(parts)),
        out_specs=VM,
        **params(2),
    )(place, fc2_last, *parts)


def release_kernel(place, total, *outs):
    rows, (qv, fc1) = outs[:6], outs[6:]
    quarter = aligned(place[DEPTH], 256)
    for layer in range(fc1.shape[0]):
        for index, out in enumerate(rows):
            out[layer : layer + 1, :] = total[pl.ds(12 * layer + index, 1), :]
        for item in range(2):
            qv[layer, item : item + 1, :] = total[
                pl.ds(12 * layer + 6 + item, 1), pl.ds(quarter, 256)
            ]
        fc1[layer : layer + 1, :] = total[pl.ds(12 * layer + 8 + place[DEPTH], 1), :]


def run_release(place, total):
    layers = total.shape[0] // 12
    row = jax.ShapeDtypeStruct((layers, 1024), F32)
    return pl.pallas_call(
        release_kernel,
        out_shape=(row,) * 6 + (jax.ShapeDtypeStruct((layers, 2, 256), F32), row),
        in_specs=[SM, VM],
        out_specs=(VM,) * 8,
        **params(2),
    )(place, total)


def split_kernel(place, total, *outs):
    even = place[PAIR] == 0
    stay, move = outs[:2]
    low, high = total[0:128, :], total[128:256, :]
    stay[...] = jnp.where(even, low, high)
    move[...] = jnp.where(even, high, low)
    if len(outs) > 2:
        stay, move = outs[2:]
        low, high = total[256:384, 0:512], total[256:384, 512:1024]
        stay[...] = jnp.where(even, low, high)
        move[...] = jnp.where(even, high, low)


def run_split(place, total):
    spans = (1024, 1024, 512, 512) if total.shape[0] > 256 else (1024, 1024)
    return pl.pallas_call(
        split_kernel,
        out_shape=tuple(jax.ShapeDtypeStruct((128, span), BF16) for span in spans),
        in_specs=[SM, VM],
        out_specs=(VM,) * len(spans),
        **params(2),
    )(place, total)


def finish_kernel(place, *refs):
    layers = (len(refs) - 4) // 4
    ins, (qkv, proj, fc1, fc2) = refs[: 4 * layers], refs[4 * layers :]
    for layer in range(layers):
        for side in range(2):
            attn, mlp = ins[4 * layer + side], ins[4 * layer + 2 + side]
            pair = place[PAIR] if side == 0 else 1 - place[PAIR]
            narrow, wide = aligned(pair, 128), aligned(pair, 512)
            for item in range(3):
                qkv[layer, item, :, pl.ds(narrow, 128)] = attn[
                    :, item * 128 : item * 128 + 128
                ].astype(F32)
            proj[layer, pl.ds(narrow, 128), :] = attn[:, 384:512].astype(F32).T
            fc1[layer, :, pl.ds(wide, 512)] = mlp[:, 0:512].astype(F32)
            fc2[layer, pl.ds(wide, 512), :] = mlp[:, 512:1024].astype(F32).T


def run_finish(place, parts):
    rows = parts[0].shape[0]
    return pl.pallas_call(
        finish_kernel,
        out_shape=(
            jax.ShapeDtypeStruct((2, 3, rows, 256), F32),
            jax.ShapeDtypeStruct((2, 256, rows), F32),
            jax.ShapeDtypeStruct((2, rows, 1024), F32),
            jax.ShapeDtypeStruct((2, 1024, rows), F32),
        ),
        in_specs=[SM] + [VM] * len(parts),
        out_specs=(VM,) * 4,
        **params(4),
    )(place, *parts)


def on_device(*args):
    (
        images_in, out_cotangent, norm1_gain, norm1_bias, qkv_weight, qv_bias, proj_weight,
        proj_bias, norm2_gain, norm2_bias, fc1_weight, fc1_bias, fc2_weight, fc2_bias,
    ) = args
    images, seq, _ = images_in.shape
    layers = qkv_weight.shape[0]
    n_far, n_mp = lax.axis_size("far"), lax.axis_size("mp")
    mine = images // n_mp

    side, pair, core = lax.axis_index("y"), lax.axis_index("x"), lax.axis_index("core")
    depth = lax.axis_index("mp")
    here = jnp.stack(
        [
            side, core, pair, depth,
            side * 2 + core, (1 - side) * 2 + core, side * 2 + 1 - core, (1 - side) * 2 + 1 - core,
        ]
    ).astype(jnp.int32)

    def swap(value, axis):
        return lax.ppermute(value, axis, [(0, 1), (1, 0)])

    def shift(value, step):
        return lax.ppermute(
            value, "mp", [(index, (index + step) % n_mp) for index in range(n_mp)]
        )

    def after(value, *others):
        return lax.optimization_barrier((value, *others))[0]

    wqkv = qkv_weight.transpose(0, 2, 1, 3)
    attn_weights = (wqkv, proj_weight, qv_bias)
    packed = run_pack(here, wqkv, proj_weight, fc1_weight, fc2_weight, qv_bias, fc1_bias)
    attn_pieces, mlp_pieces = [[]], []
    moved = []
    for step in (1, 3, 2):
        same = shift(packed[0], step)
        moved.append(same)
        other = swap(same, "y")
        attn_pieces[0].append((step, [same, other, swap(same, "core"), swap(other, "core")]))
    attn_pieces[0] = [array for _, arrays in sorted(attn_pieces[0]) for array in arrays]
    stream, normed = run_enter(here, images_in, mine, norm1_gain[0], norm1_bias[0])
    grad, grad_b, fc2_sum = run_enter_back(here, out_cotangent, mine)
    grad_b_far = swap(grad_b, "x")
    gathered = [*moved, normed, grad_b]
    for index in (1, 2):
        gathered = lax.all_gather(after(packed[index], *gathered), ("y", "core", "mp"))
        value = gathered.reshape(2, 2, n_mp, *gathered.shape[1:])
        mlp_pieces.append(value)
        attn_pieces.append([value])
        gathered = [gathered]

    def both(run, own, far, *waits):
        results = run(own)
        return list(zip(results, run(after(far, *waits) if waits else far)))

    saved = []
    for layer in range(layers):
        normed_far = swap(normed, "x")
        qkv, mixed, part = both(
            lambda rows: run_attention_forward(layer, here, rows, attn_weights, attn_pieces[layer]),
            normed, normed_far,
        )
        middle, normed2 = run_residual_norm(
            stream, part[0], swap(part[1], "x"), proj_bias[layer], norm2_gain[layer],
            norm2_bias[layer],
        )
        normed2_far = swap(normed2, "x")
        active, slope, part = both(
            lambda rows: run_mlp_forward(rows, mlp_pieces[layer]), normed2, normed2_far
        )
        saved.append(
            (stream, (normed, normed_far), qkv, mixed, middle, (normed2, normed2_far), active, slope)
        )
        if layer + 1 < layers:
            stream, normed = run_residual_norm(
                middle, part[0], swap(part[1], "x"), fc2_bias[layer], norm1_gain[layer + 1],
                norm1_bias[layer + 1],
            )
        else:
            last = run_residual(middle, part[0], swap(part[1], "x"), fc2_bias[layer])

    gathered = lax.all_gather(last, "mp")
    block_out = run_leave(
        here,
        [lax.dynamic_index_in_dim(gathered, (depth - step) % n_mp, 0, False) for step in (0, 1, 3, 2)],
        seq, mine, BF16,
    )

    def gather_sum(grads):
        flat = grads.reshape(-1, grads.shape[-1])
        return run_split(here, lax.psum_scatter(flat, ("y", "core", "mp"), tiled=True))

    above, ready = (), [None] * (2 * layers)
    small = [None] * layers
    for layer in reversed(range(layers)):
        stream, normed, qkv, mixed, middle, normed2, active, slope = saved[layer]
        slopes, qkvs = list(slope), list(qkv)
        du, fc1_sum, part = both(
            lambda rows: run_mlp_backward(rows, slopes.pop(0), mlp_pieces[layer]),
            grad_b, grad_b_far,
        )
        (grads,) = run_weight_grad(
            "extra" if above else "plain", here, normed2, du, (grad_b, grad_b_far), active, *above
        )
        sums = gather_sum(grads)
        ready[2 * layer + 1] = sums[:2]
        if above:
            ready[2 * layer + 2] = sums[2:]
        grad, grad_b, sums2 = run_norm_back(
            grad, part[0], swap(part[1], "x"), middle, norm2_gain[layer]
        )
        grad_b_far = swap(grad_b, "x")
        dqkv, qv_sum, part = both(
            lambda rows: run_attention_backward(
                layer, here, rows, qkvs.pop(0), attn_weights, attn_pieces[layer]
            ),
            grad_b, grad_b_far,
        )
        above = run_weight_grad(
            "compact" if layer else "relative", here, normed, dqkv, (grad_b, grad_b_far), mixed
        )
        grad, grad_b, sums1 = run_norm_back(
            grad, part[0], swap(part[1], "x"), stream, norm1_gain[layer]
        )
        if layer:
            grad_b_far = swap(grad_b, "x")
        small[layer] = [sums1, sums2, *qv_sum, *fc1_sum]

    parts = {step: shift(grad_b, step) for step in (1, 3, 2)}
    input_grad = run_leave(here, [grad_b] + [parts[step] for step in (1, 3, 2)], seq, mine, F32)

    near, away, send = above
    near, away = run_add_core(near, away, swap(send, "core"))
    pieces = run_add_side(here, near, swap(away, "y"))
    pieces = [pieces[0]] + [shift(pieces[step], step) for step in range(1, n_mp)]
    ready[0] = run_add_depth(here, pieces)

    total = run_collect(here, fc2_sum, [part for parts in small for part in parts])
    for axis in ("core", "x", "y"):
        total = total + swap(total, axis)
    for bit in range(n_far.bit_length() - 1):
        pairs = [(index, index ^ (1 << bit)) for index in range(n_far)]
        total = total + lax.ppermute(total, "far", pairs)
    total = after(total, *parts.values())
    for bit in range(n_mp.bit_length() - 1):
        pairs = [(index, index ^ (1 << bit)) for index in range(n_mp)]
        total = total + lax.ppermute(total, "mp", pairs)
    n1g, n1b, pb, n2g, n2b, f2b, qv, fc1 = run_release(here, total)

    if n_far == 1:
        parts = [part for stay, move in ready for part in (stay, swap(move, "x"))]
    else:
        parts = [part for stay, move in ready for part in spread_rows(stay, move)]
    g_qkv, g_proj, g_fc1, g_fc2 = run_finish(here, parts)
    return (
        block_out, input_grad, n1g, n1b, g_qkv.transpose(0, 2, 1, 3), qv, g_proj, pb, n2g, n2b,
        g_fc1, fc1, g_fc2, f2b,
    )


def spread_rows(stay, move):
    pair = lax.axis_index("x")
    value = jnp.stack(
        [jnp.where(pair == 0, stay, move), jnp.where(pair == 0, move, stay)]
    ).astype(F32)
    value = lax.psum(value, "far")
    value = lax.all_gather(value, ("y", "x", "core"))
    rows, span = value.shape[2:]
    value = value.reshape(2, 2, 2, 2, rows, span).transpose(0, 3, 2, 4, 1, 5)
    value = value.reshape(8 * rows, 2, span)
    count = rows // lax.axis_size("far")
    place = lax.axis_index(("far", "y", "x", "core"))
    value = lax.dynamic_slice_in_dim(value, place * count, count, 0)
    mine = lax.dynamic_index_in_dim(value, pair, 1, keepdims=False)
    other = lax.dynamic_index_in_dim(value, 1 - pair, 1, keepdims=False)
    return mine, other


def solution(mesh):
    n_dp, n_mp = mesh.shape["dp"], mesh.shape["mp"]
    fine = Mesh(mesh.devices.reshape(n_dp // 8, 2, 2, 2, n_mp), ("far", "y", "x", "core", "mp"))
    dp = ("far", "y", "x", "core")
    return jax.shard_map(
        on_device,
        mesh=fine,
        in_specs=(
            P(dp, None, None),
            P(dp, None, None),
            P(),
            P(),
            P(None, None, None, "mp"),
            P(None, None, "mp"),
            P(None, "mp", None),
            P(),
            P(),
            P(),
            P(None, None, "mp"),
            P(None, "mp"),
            P(None, "mp", None),
            P(),
        ),
        out_specs=(
            P(dp, None, None),
            P(dp, None, None),
            P(),
            P(),
            P(None, dp, None, "mp"),
            P(None, None, "mp"),
            P(None, "mp", dp),
            P(),
            P(),
            P(),
            P(None, dp, "mp"),
            P(None, "mp"),
            P(None, "mp", dp),
            P(),
        ),
        check_vma=False,
    )
```

time: 850 us -> 650 us (0.76)
  waiting for transfers between devices: 369 us -> 254 us
  starting transfers between devices: 126 us -> 46 us
  local copies, waits for them, and re-layouts: 40.3 us -> 23.2 us
  Pallas kernels: 289 us -> 303 us
    ppermute x69 -> x36, waiting for transfers between devices: 205 us -> 117 us  [the longest x34 117 us: swap(): return lax.ppermute(value, axis, [(0, 1), (1, 0)])]
    ppermute x24 -> x9, waiting for transfers between devices: 164 us -> 101 us  [shift(): lax.ppermute(value, 'mp', [(index, (index + step) % n_mp) for index in ra...]
    ppermute x24 -> x9, starting transfers between devices: 69.1 us -> 14.3 us  [shift(): lax.ppermute(value, 'mp', [(index, (index + step) % n_mp) for index in ra...]
    pallas_call x13 -> x25, Pallas kernels: 186 us -> 228 us  [the longest x4 55.5 us: run_attention_backward(): pl.pallas_call(functools.partial(attention_backward_kernel, layer, len(pi...]
    all_gather x2 -> x3, waiting for transfers between devices: 0.01 us -> 27.1 us  [the longest x2 27.1 us: on_device(): lax.all_gather(after(packed[index], *gathered), ('y', 'core', 'mp'))]
    ppermute x69 -> x36, starting transfers between devices: 56.6 us -> 31.5 us  [the longest x34 31.1 us: swap(): return lax.ppermute(value, axis, [(0, 1), (1, 0)])]
    pallas_call x4 -> x1, Pallas kernels: 20.4 us -> 4.4 us  [run_add_core(): pl.pallas_call(add_core_kernel, grid=(chunks,), out_shape=(shape, shape),...]
    unnamed x186 -> x86, local copies, waits for them, and re-layouts: 26.6 us -> 16 us
  transfers between devices with their start and end apart: 95 -> 50, of which waited for: 39 -> 27; matrix products, arithmetic and copies ran while one was open for 2% -> 1% of each run, Pallas kernels for 21% -> 46%
where the time goes in v2:
time: 650 us; the launch traced here: 642 us
  Pallas kernels  303 us (47%)
  waiting for transfers between devices  254 us (39%)
  starting transfers between devices  46 us (7%)
  local copies, waits for them, and re-layouts  23.2 us (4%)
  between operations  14.6 us (2%)
    ppermute x34, waiting for transfers between devices, swap(): return lax.ppermute(value, axis, [(0, 1), (1, 0)])  117 us
    ppermute x9, waiting for transfers between devices, shift(): lax.ppermute(value, 'mp', [(index, (index + step) % n_mp) for index in ra...  101 us
    pallas_call x4, Pallas kernels, run_attention_backward(): pl.pallas_call(functools.partial(attention_backward_kernel, layer, len(pi...  55.5 us
    pallas_call x4, Pallas kernels, run_weight_grad(): pl.pallas_call(functools.partial(weight_grad_kernel, kind), out_shape=sha...  50 us
    pallas_call x4, Pallas kernels, run_attention_forward(): pl.pallas_call(functools.partial(attention_forward_kernel, layer, len(pie...  38.6 us
    pallas_call x4, Pallas kernels, run_mlp_forward(): pl.pallas_call(mlp_forward_kernel, out_shape=(jax.ShapeDtypeStruct((4, RO...  38.1 us
    pallas_call x4, Pallas kernels, run_mlp_backward(): pl.pallas_call(mlp_backward_kernel, out_shape=(jax.ShapeDtypeStruct((4, R...  34.5 us
    ppermute x34, starting transfers between devices, swap(): return lax.ppermute(value, axis, [(0, 1), (1, 0)])  31.1 us
  transfers between devices with their start and end apart: 50, of which 27 were waited for; matrix products, arithmetic and copies ran while one was open for 1% of the time, Pallas kernels for 46%

profile of v2, /device:TPU:0, one launch (start us, length us, event | category | flops | bytes accessed | tf_op | source)
XLA Modules:
  0.0 642.3 jit_solution(8713884212944855707)
XLA Ops:
  7.9 3.6 shard_map.246
  11.5 5.1 collective-permute-start.8
  18.8 3.9 shard_map.250
  22.7 3.9 shard_map.245
  26.7 4.1 collective-permute-done.refs_0_
  30.8 9.7 %collective-permute-done.4.refs_4_ = bf16[272,512]{1,0:T(8,128)(2,1)S(1)} collective-permute-done((bf16[272,512]{1,0:T(8,128)(2,1)}, bf16[272,512]{1,0:T(8,128)(2,1)S(1)}, u32[]{:S(2)}, u32[]{:S(2)}) %collective-permute-start.4) | collective-permute-done | bytes 278560 | tf_op jit(solution)/shard_map/ppermute | solution.py:970
  44.7 5.5 collective-permute-done.9.refs_9_
  51.8 8.8 %collective-permute-done.1.refs_1_ = bf16[272,512]{1,0:T(8,128)(2,1)S(1)} collective-permute-done((bf16[272,512]{1,0:T(8,128)(2,1)S(1)}, bf16[272,512]{1,0:T(8,128)(2,1)S(1)}, u32[]{:S(2)}, u32[]{:S(2)}) %collective-permute-start.1) | collective-permute-done | bytes 278560 | tf_op jit(solution)/shard_map/ppermute | solution.py:967
  60.6 8.2 %collective-permute-done.5.refs_5_ = bf16[272,512]{1,0:T(8,128)(2,1)S(1)} collective-permute-done((bf16[272,512]{1,0:T(8,128)(2,1)S(1)}, bf16[272,512]{1,0:T(8,128)(2,1)S(1)}, u32[]{:S(2)}, u32[]{:S(2)}) %collective-permute-start.5) | collective-permute-done | bytes 278560 | tf_op jit(solution)/shard_map/ppermute | solution.py:967
  72.6 10.0 %shard_map.248 = (bf16[4,304,384]{2,1,0:T(8,128)(2,1)}, bf16[4,304,128]{2,1,0:T(8,128)(2,1)}, bf16[304,1024]{1,0:T(8,128)(2,1)}) custom-call(s32[8]{0:T(128)} %stack.35.place, bf16[304,1024]{1,0:T(8,128)(2,1)} %copy-done.8, bf16[2,3,1024,256]{3,2,1,0:T(8,128)(2,1)} %bitcast.51, bf16[2,256,1024]{2,1,0:T(8,128)(2,1)} %wproj.17, f32[2,2,256]{2,1,0:T(2,128)} %bqv.9, ...), custom_call_target="tpu_custom_call" | custom-call | flops 28000000000 | tf_op jit(solution)/shard_map/pallas_call | solution.py:485
  84.2 10.7 %shard_map.247 = (bf16[4,304,384]{2,1,0:T(8,128)(2,1)}, bf16[4,304,128]{2,1,0:T(8,128)(2,1)}, bf16[304,1024]{1,0:T(8,128)(2,1)}) custom-call(s32[8]{0:T(128)} %stack.35.place, bf16[304,1024]{1,0:T(8,128)(2,1)} %get-tuple-element.120.a_ref.x1_own, bf16[2,3,1024,256]{3,2,1,0:T(8,128)(2,1)} %bitcast.52, bf16[2,256,1024]{2,1,0:T(8,128)(2,1)} %wproj.17, ...), custom_call_target="tpu_custom_call" | custom-call | flops 28000000000 | tf_op jit(solution)/shard_map/pallas_call | solution.py:485
  94.9 4.3 collective-permute-done.13.far_ref
  100.1 4.1 shard_map.249
  106.4 13.7 %collective-permute-done.14.a_ref.x1_far = bf16[304,1024]{1,0:T(8,128)(2,1)S(1)} collective-permute-done((bf16[304,1024]{1,0:T(8,128)(2,1)}, bf16[304,1024]{1,0:T(8,128)(2,1)S(1)}, u32[]{:S(2)}, u32[]{:S(2)}) %collective-permute-start.14) | collective-permute-done | bytes 622624 | tf_op jit(solution)/shard_map/ppermute | solution.py:967
  120.1 27.1 %all-gather.7.cloned.1.call-done = bf16[12800,512]{1,0:T(8,128)(2,1)} async-done(((bf16[800,512]{1,0:T(8,128)(2,1)}), bf16[12800,512]{1,0:T(8,128)(2,1)}) %all-gather.7.cloned.1.call-update) | async-done | bytes 13107216 | tf_op jit(solution)/shard_map/all_gather | solution.py:993
  147.2 9.5 %shard_map.252 = (bf16[4,304,512]{2,1,0:T(8,128)(2,1)}, bf16[4,304,512]{2,1,0:T(8,128)(2,1)}, bf16[304,1024]{1,0:T(8,128)(2,1)}) custom-call(bf16[304,1024]{1,0:T(8,128)(2,1)} %copy-done.10, bf16[2,2,4,800,512]{4,3,2,1,0:T(8,128)(2,1)} %bitcast.38), custom_call_target="tpu_custom_call" | custom-call | flops 32000000000 | tf_op jit(solution)/shard_map/pallas_call | solution.py:609
  158.3 9.5 %shard_map.251 = (bf16[4,304,512]{2,1,0:T(8,128)(2,1)}, bf16[4,304,512]{2,1,0:T(8,128)(2,1)}, bf16[304,1024]{1,0:T(8,128)(2,1)}) custom-call(bf16[304,1024]{1,0:T(8,128)(2,1)} %get-tuple-element.125.a_ref.x1_own, bf16[2,2,4,800,512]{4,3,2,1,0:T(8,128)(2,1)} %bitcast.39), custom_call_target="tpu_custom_call" | custom-call | flops 32000000000 | tf_op jit(solution)/shard_map/pallas_call | solution.py:609
  167.8 5.4 collective-permute-done.15.far_ref
  174.1 4.1 shard_map.253
  180.2 15.1 %collective-permute-done.16.a_ref.x1_far = bf16[304,1024]{1,0:T(8,128)(2,1)S(1)} collective-permute-done((bf16[304,1024]{1,0:T(8,128)(2,1)}, bf16[304,1024]{1,0:T(8,128)(2,1)S(1)}, u32[]{:S(2)}, u32[]{:S(2)}) %collective-permute-start.16) | collective-permute-done | bytes 622624 | tf_op jit(solution)/shard_map/ppermute | solution.py:967
  196.2 8.9 %shard_map.255 = (bf16[4,304,384]{2,1,0:T(8,128)(2,1)}, bf16[4,304,128]{2,1,0:T(8,128)(2,1)}, bf16[304,1024]{1,0:T(8,128)(2,1)}) custom-call(s32[8]{0:T(128)} %stack.35.place, bf16[304,1024]{1,0:T(8,128)(2,1)} %copy-done.11, bf16[2,3,1024,256]{3,2,1,0:T(8,128)(2,1)} %bitcast.53, bf16[2,256,1024]{2,1,0:T(8,128)(2,1)} %wproj.17, f32[2,2,256]{2,1,0:T(2,128)} %bqv.9, ...), custom_call_target="tpu_custom_call" | custom-call | flops 28000000000 | tf_op jit(solution)/shard_map/pallas_call | solution.py:485
  206.6 9.0 %shard_map.254 = (bf16[4,304,384]{2,1,0:T(8,128)(2,1)}, bf16[4,304,128]{2,1,0:T(8,128)(2,1)}, bf16[304,1024]{1,0:T(8,128)(2,1)}) custom-call(s32[8]{0:T(128)} %stack.35.place, bf16[304,1024]{1,0:T(8,128)(2,1)} %get-tuple-element.132.a_ref.x1_own, bf16[2,3,1024,256]{3,2,1,0:T(8,128)(2,1)} %bitcast.54, bf16[2,256,1024]{2,1,0:T(8,128)(2,1)} %wproj.17, ...), custom_call_target="tpu_custom_call" | custom-call | flops 28000000000 | tf_op jit(solution)/shard_map/pallas_call | solution.py:485
  215.6 5.0 collective-permute-done.17.far_ref
  221.5 4.1 shard_map.256
  227.1 9.5 %shard_map.257 = (bf16[4,304,512]{2,1,0:T(8,128)(2,1)}, bf16[4,304,512]{2,1,0:T(8,128)(2,1)}, bf16[304,1024]{1,0:T(8,128)(2,1)}) custom-call(bf16[304,1024]{1,0:T(8,128)(2,1)} %get-tuple-element.136.a_ref.x1_own, bf16[2,2,4,528,512]{4,3,2,1,0:T(8,128)(2,1)} %bitcast.46), custom_call_target="tpu_custom_call" | custom-call | flops 32000000000 | tf_op jit(solution)/shard_map/pallas_call | solution.py:609
  236.6 8.5 %shard_map.261 = (bf16[4,304,512]{2,1,0:T(8,128)(2,1)}, f32[4,8,512]{2,1,0:T(8,128)}, bf16[304,1024]{1,0:T(8,128)(2,1)}) custom-call(bf16[304,1024]{1,0:T(8,128)(2,1)} %get-tuple-element.127.g_ref.x2_own, bf16[4,304,512]{2,1,0:T(8,128)(2,1)} %get-tuple-element.142.slope_ref, bf16[2,2,4,528,512]{4,3,2,1,0:T(8,128)(2,1)} %bitcast.47), custom_call_target="tpu_custom_call" | custom-call | flops 28000000000 | tf_op jit(solution)/shard_map/pallas_call | solution.py:654
  246.0 9.5 %shard_map.258 = (bf16[4,304,512]{2,1,0:T(8,128)(2,1)}, bf16[4,304,512]{2,1,0:T(8,128)(2,1)}, bf16[304,1024]{1,0:T(8,128)(2,1)}) custom-call(bf16[304,1024]{1,0:T(8,128)(2,1)} %copy-done.12, bf16[2,2,4,528,512]{4,3,2,1,0:T(8,128)(2,1)} %bitcast.48), custom_call_target="tpu_custom_call" | custom-call | flops 32000000000 | tf_op jit(solution)/shard_map/pallas_call | solution.py:609
  256.2 8.5 %shard_map.262 = (bf16[4,304,512]{2,1,0:T(8,128)(2,1)}, f32[4,8,512]{2,1,0:T(8,128)}, bf16[304,1024]{1,0:T(8,128)(2,1)}) custom-call(bf16[304,1024]{1,0:T(8,128)(2,1)} %collective-permute-done.20.g_ref.x2_far, bf16[4,304,512]{2,1,0:T(8,128)(2,1)} %get-tuple-element.144.slope_ref, bf16[2,2,4,528,512]{4,3,2,1,0:T(8,128)(2,1)} %bitcast.49), custom_call_target="tpu_custom_call" | custom-call | flops 28000000000 | tf_op jit(solution)/shard_map/pallas_call | solution.py:654
  266.3 6.6 %collective-permute-done.19.far_ref = bf16[304,1024]{1,0:T(8,128)(2,1)S(1)} collective-permute-done((bf16[304,1024]{1,0:T(8,128)(2,1)}, bf16[304,1024]{1,0:T(8,128)(2,1)S(1)}, u32[]{:S(2)}, u32[]{:S(2)}) %collective-permute-start.19) | collective-permute-done | bytes 622624 | tf_op jit(solution)/shard_map/ppermute | solution.py:967
  273.7 3.6 shard_map.259
  277.4 14.4 %shard_map.283 = bf16[2,2,4,256,1024]{4,3,2,1,0:T(8,128)(2,1)} custom-call(s32[8]{0:T(128)} %stack.35.place, bf16[304,1024]{1,0:T(8,128)(2,1)} %get-tuple-element.136.a_ref.x1_own, bf16[304,1024]{1,0:T(8,128)(2,1)} %copy-done.12, bf16[4,304,512]{2,1,0:T(8,128)(2,1)} %get-tuple-element.208.y1_own, bf16[4,304,512]{2,1,0:T(8,128)(2,1)} %get-tuple-element.209.y1_far, ...), custom_call_target="tpu_custom_call" | custom-call | flops 56000000000 | tf_op jit(solution)/shard_map/pallas_call | solution.py:752
  292.7 5.0 shard_map.263
  298.3 13.4 %shard_map.264 = (bf16[4,304,384]{2,1,0:T(8,128)(2,1)}, f32[4,8,384]{2,1,0:T(8,128)}, bf16[304,1024]{1,0:T(8,128)(2,1)}) custom-call(s32[8]{0:T(128)} %stack.35.place, bf16[304,1024]{1,0:T(8,128)(2,1)} %get-tuple-element.147.g_ref.x2_own, bf16[4,304,384]{2,1,0:T(8,128)(2,1)} %get-tuple-element.148.qkv_ref, bf16[2,3,1024,256]{3,2,1,0:T(8,128)(2,1)} %bitcast.55, ...), custom_call_target="tpu_custom_call" | custom-call | flops 48000000000 | tf_op jit(solution)/shard_map/pallas_call | solution.py:551
  312.5 13.4 %shard_map.265 = (bf16[4,304,384]{2,1,0:T(8,128)(2,1)}, f32[4,8,384]{2,1,0:T(8,128)}, bf16[304,1024]{1,0:T(8,128)(2,1)}) custom-call(s32[8]{0:T(128)} %stack.35.place, bf16[304,1024]{1,0:T(8,128)(2,1)} %copy-done.18, bf16[4,304,384]{2,1,0:T(8,128)(2,1)} %get-tuple-element.150.qkv_ref, bf16[2,3,1024,256]{3,2,1,0:T(8,128)(2,1)} %bitcast.56, ...), custom_call_target="tpu_custom_call" | custom-call | flops 48000000000 | tf_op jit(solution)/shard_map/pallas_call | solution.py:551
  327.4 10.2 %shard_map.280.refs_0_ = bf16[2,2,4,128,1024]{4,3,2,1,0:T(8,128)(2,1)} custom-call(s32[8]{0:T(128)} %stack.35.place, bf16[304,1024]{1,0:T(8,128)(2,1)} %get-tuple-element.132.a_ref.x1_own, bf16[304,1024]{1,0:T(8,128)(2,1)} %copy-done.11, bf16[4,304,384]{2,1,0:T(8,128)(2,1)} %get-tuple-element.200.y1_own, bf16[4,304,384]{2,1,0:T(8,128)(2,1)} %get-tuple-element.201.y1_far, ...), custom_call_target="tpu_custom_call" | custom-call | flops 40000000000 | tf_op jit(solution)/shard_map/pallas_call | solution.py:752
  338.5 5.3 shard_map.266
  344.4 8.9 %shard_map.267 = (bf16[4,304,512]{2,1,0:T(8,128)(2,1)}, f32[4,8,512]{2,1,0:T(8,128)}, bf16[304,1024]{1,0:T(8,128)(2,1)}) custom-call(bf16[304,1024]{1,0:T(8,128)(2,1)} %get-tuple-element.153.g_ref.x2_own, bf16[4,304,512]{2,1,0:T(8,128)(2,1)} %get-tuple-element.154.slope_ref, bf16[2,2,4,800,512]{4,3,2,1,0:T(8,128)(2,1)} %bitcast.44), custom_call_target="tpu_custom_call" | custom-call | flops 28000000000 | tf_op jit(solution)/shard_map/pallas_call | solution.py:654
  355.2 8.5 %shard_map.268 = (bf16[4,304,512]{2,1,0:T(8,128)(2,1)}, f32[4,8,512]{2,1,0:T(8,128)}, bf16[304,1024]{1,0:T(8,128)(2,1)}) custom-call(bf16[304,1024]{1,0:T(8,128)(2,1)} %copy-done.17, bf16[4,304,512]{2,1,0:T(8,128)(2,1)} %get-tuple-element.156.slope_ref, bf16[2,2,4,800,512]{4,3,2,1,0:T(8,128)(2,1)} %bitcast.45), custom_call_target="tpu_custom_call" | custom-call | flops 28000000000 | tf_op jit(solution)/shard_map/pallas_call | solution.py:654
  364.3 15.9 %shard_map.281 = bf16[2,2,4,384,1024]{4,3,2,1,0:T(8,128)(2,1)} custom-call(s32[8]{0:T(128)} %stack.35.place, bf16[304,1024]{1,0:T(8,128)(2,1)} %get-tuple-element.125.a_ref.x1_own, bf16[304,1024]{1,0:T(8,128)(2,1)} %copy-done.10, bf16[4,304,512]{2,1,0:T(8,128)(2,1)} %get-tuple-element.196.y1_own, bf16[4,304,512]{2,1,0:T(8,128)(2,1)} %get-tuple-element.197.y1_far, ...), custom_call_target="tpu_custom_call" | custom-call | flops 56000000000 | tf_op jit(solution)/shard_map/pallas_call | solution.py:752
  381.1 4.9 shard_map.269
  387.6 14.3 %shard_map.270 = (bf16[4,304,384]{2,1,0:T(8,128)(2,1)}, f32[4,8,384]{2,1,0:T(8,128)}, bf16[304,1024]{1,0:T(8,128)(2,1)}) custom-call(s32[8]{0:T(128)} %stack.35.place, bf16[304,1024]{1,0:T(8,128)(2,1)} %get-tuple-element.159.g_ref.x2_own, bf16[4,304,384]{2,1,0:T(8,128)(2,1)} %get-tuple-element.160.qkv_ref, bf16[2,3,1024,256]{3,2,1,0:T(8,128)(2,1)} %bitcast.57, ...), custom_call_target="tpu_custom_call" | custom-call | flops 48000000000 | tf_op jit(solution)/shard_map/pallas_call | solution.py:551
  402.8 14.4 %shard_map.271 = (bf16[4,304,384]{2,1,0:T(8,128)(2,1)}, f32[4,8,384]{2,1,0:T(8,128)}, bf16[304,1024]{1,0:T(8,128)(2,1)}) custom-call(s32[8]{0:T(128)} %stack.35.place, bf16[304,1024]{1,0:T(8,128)(2,1)} %copy-done.14, bf16[4,304,384]{2,1,0:T(8,128)(2,1)} %get-tuple-element.162.qkv_ref, bf16[2,3,1024,256]{3,2,1,0:T(8,128)(2,1)} %bitcast.58, ...), custom_call_target="tpu_custom_call" | custom-call | flops 48000000000 | tf_op jit(solution)/shard_map/pallas_call | solution.py:551
  417.8 9.6 %shard_map.276 = (bf16[4,256,512]{2,1,0:T(8,128)(2,1)}, bf16[4,256,512]{2,1,0:T(8,128)(2,1)}, bf16[2,4,256,512]{3,2,1,0:T(8,128)(2,1)}) custom-call(s32[8]{0:T(128)} %stack.35.place, bf16[304,1024]{1,0:T(8,128)(2,1)} %get-tuple-element.120.a_ref.x1_own, bf16[304,1024]{1,0:T(8,128)(2,1)} %copy-done.8, bf16[4,304,384]{2,1,0:T(8,128)(2,1)} %get-tuple-element.181.y1_own, ...), custom_call_target="tpu_custom_call" | custom-call | flops 40000000000 | tf_op jit(solution)/shard_map/pallas_call | solution.py:752
  428.5 4.9 shard_map.272
  433.5 3.8 collective-permute-start.29
  442.9 3.6 collective-permute-done.32
  447.2 3.5 dynamic-slice_bitcast_fusion
  452.4 11.9 %collective-permute-done.29.refs_2_ = bf16[304,1024]{1,0:T(8,128)(2,1)} collective-permute-done((bf16[304,1024]{1,0:T(8,128)(2,1)}, bf16[304,1024]{1,0:T(8,128)(2,1)}, u32[]{:S(2)}, u32[]{:S(2)}) %collective-permute-start.29) | collective-permute-done | bytes 622624 | tf_op jit(solution)/shard_map/ppermute | solution.py:970
  464.3 57.1 %collective-permute-done.30.refs_3_ = bf16[304,1024]{1,0:T(8,128)(2,1)} collective-permute-done((bf16[304,1024]{1,0:T(8,128)(2,1)}, bf16[304,1024]{1,0:T(8,128)(2,1)}, u32[]{:S(2)}, u32[]{:S(2)}) %collective-permute-start.30) | collective-permute-done | bytes 622624 | tf_op jit(solution)/shard_map/ppermute | solution.py:970
  522.8 4.4 shard_map.277
  527.6 8.7 %shard_map.260 = bf16[1200,1024]{1,0:T(8,128)(2,1)} custom-call(s32[8]{0:T(128)} %stack.35.place, bf16[304,1024]{1,0:T(8,128)(2,1)} %get-tuple-element.227.refs_0_, bf16[304,1024]{1,0:T(8,128)(2,1)} %get-tuple-element.226.refs_1_, bf16[304,1024]{1,0:T(8,128)(2,1)} %get-tuple-element.225.refs_2_, bf16[304,1024]{1,0:T(8,128)(2,1)} %get-tuple-element.224.refs_3_), custom_call_target="tpu_custom_call" | custom-call | flops 35999997952 | tf_op jit(solution)/shard_map/pallas_call | solution.py:174
  536.7 29.3 %collective-permute-done.37.got = bf16[4,256,512]{2,1,0:T(8,128)(2,1)S(1)} collective-permute-done((bf16[4,256,512]{2,1,0:T(8,128)(2,1)}, bf16[4,256,512]{2,1,0:T(8,128)(2,1)S(1)}, u32[]{:S(2)}, u32[]{:S(2)}) %collective-permute-start.37) | collective-permute-done | bytes 1048608 | tf_op jit(solution)/shard_map/ppermute | solution.py:967
  567.0 2.8 shard_map.278
  571.8 2.4 collective-permute-start.40
  574.1 10.0 %shard_map.273 = f32[1200,1024]{1,0:T(8,128)} custom-call(s32[8]{0:T(128)} %stack.35.place, bf16[304,1024]{1,0:T(8,128)(2,1)} %get-tuple-element.164.refs_0_, bf16[304,1024]{1,0:T(8,128)(2,1)} %copy-done.9, bf16[304,1024]{1,0:T(8,128)(2,1)} %collective-permute-done.29.refs_2_, bf16[304,1024]{1,0:T(8,128)(2,1)} %collective-permute-done.30.refs_3_), custom_call_target="tpu_custom_call" | custom-call | flops 35999997952 | tf_op jit(solution)/shard_map/pallas_call | solution.py:174
  584.8 13.9 %collective-permute-done.39.refs_2_ = bf16[256,512]{1,0:T(8,128)(2,1)S(1)} collective-permute-done((bf16[256,512]{1,0:T(8,128)(2,1)}, bf16[256,512]{1,0:T(8,128)(2,1)S(1)}, u32[]{:S(2)}, u32[]{:S(2)}) %collective-permute-start.39) | collective-permute-done | bytes 262176 | tf_op jit(solution)/shard_map/ppermute | solution.py:970
  598.7 2.9 collective-permute-done.40.refs_3_
  602.3 2.1 shard_map.279
  604.4 2.4 collective-permute-start.41
  608.7 8.7 %reduce-scatter.3.cloned.1.call-done.total = bf16[384,1024]{1,0:T(8,128)(2,1)} async-done(((bf16[6144,1024]{1,0:T(8,128)(2,1)}), bf16[384,1024]{1,0:T(8,128)(2,1)}) %reduce-scatter.3.cloned.1.call-update) | async-done | bytes 786448 | tf_op jit(solution)/shard_map/reduce_scatter | solution.py:1038
  617.4 2.1 shard_map.282
  619.4 2.5 collective-permute-start.42
  623.5 7.9 %collective-permute-done.43.refs_5_ = bf16[128,512]{1,0:T(8,128)(2,1)S(1)} collective-permute-done((bf16[128,512]{1,0:T(8,128)(2,1)}, bf16[128,512]{1,0:T(8,128)(2,1)S(1)}, u32[]{:S(2)}, u32[]{:S(2)}) %collective-permute-start.43) | collective-permute-done | bytes 131104 | tf_op jit(solution)/shard_map/ppermute | solution.py:967
  632.2 3.3 shard_map.285
  (180 shorter events, 61.4 us)
Async XLA Ops:
  7.2 140.1 %all-gather.7.cloned.1.call-start = ((), (), s32[]{:S(2)}) async-start(), calls=%async_computation.4 | async-start | bytes 13926400 | tf_op jit(solution)/shard_map/all_gather | solution.py:993
  7.9 9.7 %copy-start = (f32[2,1024]{1,0:T(2,128)S(1)}, f32[2,1024]{1,0:T(2,128)}, u32[]{:S(2)}) copy-start(f32[2,1024]{1,0:T(2,128)} %param.16) | copy-start | bytes 24580
  7.9 10.3 %copy-start.1 = (f32[2,1024]{1,0:T(2,128)S(1)}, f32[2,1024]{1,0:T(2,128)}, u32[]{:S(2)}) copy-start(f32[2,1024]{1,0:T(2,128)} %param.17) | copy-start | bytes 24580
  11.5 15.2 %collective-permute-start.8 = (bf16[272,512]{1,0:T(8,128)(2,1)}, bf16[272,512]{1,0:T(8,128)(2,1)S(1)}, u32[]{:S(2)}, u32[]{:S(2)}) collective-permute-start(bf16[272,512]{1,0:T(8,128)(2,1)} %get-tuple-element.121), channel_id=1, source_target_pairs={{0,3},{1,0},{2,1},{3,2},{4,7},{5,4},{6,5},{7,6},{8,11},{9,8},{10,9... | collective-permute-start | bytes 835592 | tf_op jit(solution)/shard_map/ppermute | solution.py:970
  16.6 14.2 %collective-permute-start = (bf16[272,512]{1,0:T(8,128)(2,1)}, bf16[272,512]{1,0:T(8,128)(2,1)S(1)}, u32[]{:S(2)}, u32[]{:S(2)}) collective-permute-start(bf16[272,512]{1,0:T(8,128)(2,1)} %get-tuple-element.121), channel_id=1, source_target_pairs={{0,1},{1,2},{2,3},{3,0},{4,5},{5,6},{6,7},{7,4},{8,9},{9,10},{10,1... | collective-permute-start | bytes 835592 | tf_op jit(solution)/shard_map/ppermute | solution.py:970
  16.6 23.9 %collective-permute-start.4 = (bf16[272,512]{1,0:T(8,128)(2,1)}, bf16[272,512]{1,0:T(8,128)(2,1)S(1)}, u32[]{:S(2)}, u32[]{:S(2)}) collective-permute-start(bf16[272,512]{1,0:T(8,128)(2,1)} %get-tuple-element.121), channel_id=1, source_target_pairs={{0,2},{1,3},{2,0},{3,1},{4,6},{5,7},{6,4},{7,5},{8,10},{9,11},{10,... | collective-permute-start | bytes 835592 | tf_op jit(solution)/shard_map/ppermute | solution.py:970
  26.6 42.8 %copy-start.2 = (f32[2,1024]{1,0:T(2,128)S(1)}, f32[2,1024]{1,0:T(2,128)}, u32[]{:S(2)}) copy-start(f32[2,1024]{1,0:T(2,128)} %param.22) | copy-start | bytes 24580
  26.6 43.5 %copy-start.4 = (f32[2,1024]{1,0:T(2,128)S(1)}, f32[2,1024]{1,0:T(2,128)}, u32[]{:S(2)}) copy-start(f32[2,1024]{1,0:T(2,128)} %param.23) | copy-start | bytes 24580
  26.7 43.5 %copy-start.5 = (f32[2,1024]{1,0:T(2,128)S(1)}, f32[2,1024]{1,0:T(2,128)}, u32[]{:S(2)}) copy-start(f32[2,1024]{1,0:T(2,128)} %param.21) | copy-start | bytes 24580
  26.7 44.6 %copy-start.24 = (bf16[272,512]{1,0:T(8,128)(2,1)}, bf16[272,512]{1,0:T(8,128)(2,1)S(1)}, u32[]{:S(2)}) copy-start(bf16[272,512]{1,0:T(8,128)(2,1)S(1)} %collective-permute-done.8.refs_8_) | copy-start | bytes 835588
  30.8 40.4 %copy-start.25 = (bf16[272,512]{1,0:T(8,128)(2,1)}, bf16[272,512]{1,0:T(8,128)(2,1)S(1)}, u32[]{:S(2)}) copy-start(bf16[272,512]{1,0:T(8,128)(2,1)S(1)} %collective-permute-done.refs_0_) | copy-start | bytes 835588
  40.5 30.7 %copy-start.26 = (bf16[272,512]{1,0:T(8,128)(2,1)}, bf16[272,512]{1,0:T(8,128)(2,1)S(1)}, u32[]{:S(2)}) copy-start(bf16[272,512]{1,0:T(8,128)(2,1)S(1)} %collective-permute-done.4.refs_4_) | copy-start | bytes 835588
  40.5 186.6 %all-gather.9.cloned.1.call-start = ((), (), s32[]{:S(2)}) async-start(), calls=%async_computation.5 | async-start | bytes 9191424 | tf_op jit(solution)/shard_map/all_gather | solution.py:993
  40.6 9.7 %collective-permute-start.9 = (bf16[272,512]{1,0:T(8,128)(2,1)S(1)}, bf16[272,512]{1,0:T(8,128)(2,1)S(1)}, u32[]{:S(2)}, u32[]{:S(2)}) collective-permute-start(bf16[272,512]{1,0:T(8,128)(2,1)S(1)} %collective-permute-done.8.refs_8_), channel_id=1, source_target_pairs={{0,16},{16,0},{1,17},{17,1},{2,18},{18,2},{3,19},{19,3},{4,20},{20... | collective-permute-start | bytes 835592 | tf_op jit(solution)/shard_map/ppermute | solution.py:967
  42.1 18.5 %collective-permute-start.1 = (bf16[272,512]{1,0:T(8,128)(2,1)S(1)}, bf16[272,512]{1,0:T(8,128)(2,1)S(1)}, u32[]{:S(2)}, u32[]{:S(2)}) collective-permute-start(bf16[272,512]{1,0:T(8,128)(2,1)S(1)} %collective-permute-done.refs_0_), channel_id=1, source_target_pairs={{0,16},{16,0},{1,17},{17,1},{2,18},{18,2},{3,19},{19,3},{4,20},{20... | collective-permute-start | bytes 835592 | tf_op jit(solution)/shard_map/ppermute | solution.py:967
  42.7 26.2 %collective-permute-start.5 = (bf16[272,512]{1,0:T(8,128)(2,1)S(1)}, bf16[272,512]{1,0:T(8,128)(2,1)S(1)}, u32[]{:S(2)}, u32[]{:S(2)}) collective-permute-start(bf16[272,512]{1,0:T(8,128)(2,1)S(1)} %collective-permute-done.4.refs_4_), channel_id=1, source_target_pairs={{0,16},{16,0},{1,17},{17,1},{2,18},{18,2},{3,19},{19,3},{4,20},{20... | collective-permute-start | bytes 835592 | tf_op jit(solution)/shard_map/ppermute | solution.py:967
  44.2 24.7 %collective-permute-start.10 = (bf16[272,512]{1,0:T(8,128)(2,1)S(1)}, bf16[272,512]{1,0:T(8,128)(2,1)S(1)}, u32[]{:S(2)}, u32[]{:S(2)}) collective-permute-start(bf16[272,512]{1,0:T(8,128)(2,1)S(1)} %collective-permute-done.8.refs_8_), channel_id=1, source_target_pairs={{0,4},{4,0},{1,5},{5,1},{2,6},{6,2},{3,7},{7,3},{8,12},{12,8},{9,1... | collective-permute-start | bytes 835592 | tf_op jit(solution)/shard_map/ppermute | solution.py:967
  44.2 25.2 %collective-permute-start.2 = (bf16[272,512]{1,0:T(8,128)(2,1)S(1)}, bf16[272,512]{1,0:T(8,128)(2,1)S(1)}, u32[]{:S(2)}, u32[]{:S(2)}) collective-permute-start(bf16[272,512]{1,0:T(8,128)(2,1)S(1)} %collective-permute-done.refs_0_), channel_id=1, source_target_pairs={{0,4},{4,0},{1,5},{5,1},{2,6},{6,2},{3,7},{7,3},{8,12},{12,8},{9,1... | collective-permute-start | bytes 835592 | tf_op jit(solution)/shard_map/ppermute | solution.py:967
  50.2 21.0 %copy-start.27 = (bf16[272,512]{1,0:T(8,128)(2,1)}, bf16[272,512]{1,0:T(8,128)(2,1)S(1)}, u32[]{:S(2)}) copy-start(bf16[272,512]{1,0:T(8,128)(2,1)S(1)} %collective-permute-done.9.refs_9_) | copy-start | bytes 835588
  50.2 20.5 %collective-permute-start.12 = (bf16[304,1024]{1,0:T(8,128)(2,1)}, bf16[304,1024]{1,0:T(8,128)(2,1)S(1)}, u32[]{:S(2)}, u32[]{:S(2)}) collective-permute-start(bf16[304,1024]{1,0:T(8,128)(2,1)} %get-tuple-element.120.a_ref.x1_own), channel_id=1, source_target_pairs={{0,8},{8,0},{1,9},{9,1},{2,10},{10,2},{3,11},{11,3},{4,12},{12,4},... | collective-permute-start | bytes 1867784 | tf_op jit(solution)/shard_map/ppermute | solution.py:967
  51.7 395.5 %all-gather.11.cloned.1.call-start = ((), (), s32[]{:S(2)}) async-start(), calls=%async_computation.6 | async-start | bytes 3112960 | tf_op jit(solution)/shard_map/all_gather | solution.py:1029
  60.6 10.6 %copy-start.28 = (bf16[272,512]{1,0:T(8,128)(2,1)}, bf16[272,512]{1,0:T(8,128)(2,1)S(1)}, u32[]{:S(2)}) copy-start(bf16[272,512]{1,0:T(8,128)(2,1)S(1)} %collective-permute-done.1.refs_1_) | copy-start | bytes 835588
  60.6 10.1 %collective-permute-start.6 = (bf16[272,512]{1,0:T(8,128)(2,1)S(1)}, bf16[272,512]{1,0:T(8,128)(2,1)S(1)}, u32[]{:S(2)}, u32[]{:S(2)}) collective-permute-start(bf16[272,512]{1,0:T(8,128)(2,1)S(1)} %collective-permute-done.4.refs_4_), channel_id=1, source_target_pairs={{0,4},{4,0},{1,5},{5,1},{2,6},{6,2},{3,7},{7,3},{8,12},{12,8},{9,1... | collective-permute-start | bytes 835592 | tf_op jit(solution)/shard_map/ppermute | solution.py:967
  68.9 1.9 collective-permute-start.11
  68.9 1.9 collective-permute-start.3
  69.4 1.8 collective-permute-start.7
  82.6 16.6 %collective-permute-start.13 = (bf16[304,1024]{1,0:T(8,128)(2,1)}, bf16[304,1024]{1,0:T(8,128)(2,1)S(1)}, u32[]{:S(2)}, u32[]{:S(2)}) collective-permute-start(bf16[304,1024]{1,0:T(8,128)(2,1)} %get-tuple-element.123), channel_id=1, source_target_pairs={{0,8},{8,0},{1,9},{9,1},{2,10},{10,2},{3,11},{11,3},{4,12},{12,4},... | collective-permute-start | bytes 1867784 | tf_op jit(solution)/shard_map/ppermute | solution.py:967
  104.2 15.9 %collective-permute-start.14 = (bf16[304,1024]{1,0:T(8,128)(2,1)}, bf16[304,1024]{1,0:T(8,128)(2,1)S(1)}, u32[]{:S(2)}, u32[]{:S(2)}) collective-permute-start(bf16[304,1024]{1,0:T(8,128)(2,1)} %get-tuple-element.125.a_ref.x1_own), channel_id=1, source_target_pairs={{0,8},{8,0},{1,9},{9,1},{2,10},{10,2},{3,11},{11,3},{4,12},{12,4},... | collective-permute-start | bytes 1867784 | tf_op jit(solution)/shard_map/ppermute | solution.py:967
  120.1 27.1 %copy-start.10 = (bf16[304,1024]{1,0:T(8,128)(2,1)}, bf16[304,1024]{1,0:T(8,128)(2,1)S(1)}, u32[]{:S(2)}) copy-start(bf16[304,1024]{1,0:T(8,128)(2,1)S(1)} %collective-permute-done.14.a_ref.x1_far) | copy-start | bytes 1867780
  156.8 16.5 %collective-permute-start.15 = (bf16[304,1024]{1,0:T(8,128)(2,1)}, bf16[304,1024]{1,0:T(8,128)(2,1)S(1)}, u32[]{:S(2)}, u32[]{:S(2)}) collective-permute-start(bf16[304,1024]{1,0:T(8,128)(2,1)} %get-tuple-element.130), channel_id=1, source_target_pairs={{0,8},{8,0},{1,9},{9,1},{2,10},{10,2},{3,11},{11,3},{4,12},{12,4},... | collective-permute-start | bytes 1867784 | tf_op jit(solution)/shard_map/ppermute | solution.py:967
  178.2 17.2 %collective-permute-start.16 = (bf16[304,1024]{1,0:T(8,128)(2,1)}, bf16[304,1024]{1,0:T(8,128)(2,1)S(1)}, u32[]{:S(2)}, u32[]{:S(2)}) collective-permute-start(bf16[304,1024]{1,0:T(8,128)(2,1)} %get-tuple-element.132.a_ref.x1_own), channel_id=1, source_target_pairs={{0,8},{8,0},{1,9},{9,1},{2,10},{10,2},{3,11},{11,3},{4,12},{12,4},... | collective-permute-start | bytes 1867784 | tf_op jit(solution)/shard_map/ppermute | solution.py:967
  179.7 76.5 %collective-permute-start.20 = (bf16[304,1024]{1,0:T(8,128)(2,1)}, bf16[304,1024]{1,0:T(8,128)(2,1)}, u32[]{:S(2)}, u32[]{:S(2)}) collective-permute-start(bf16[304,1024]{1,0:T(8,128)(2,1)} %get-tuple-element.127.g_ref.x2_own), channel_id=1, source_target_pairs={{0,8},{8,0},{1,9},{9,1},{2,10},{10,2},{3,11},{11,3},{4,12},{12,4},... | collective-permute-start | bytes 1867784 | tf_op jit(solution)/shard_map/ppermute | solution.py:967
  205.1 15.5 %collective-permute-start.17 = (bf16[304,1024]{1,0:T(8,128)(2,1)}, bf16[304,1024]{1,0:T(8,128)(2,1)S(1)}, u32[]{:S(2)}, u32[]{:S(2)}) collective-permute-start(bf16[304,1024]{1,0:T(8,128)(2,1)} %get-tuple-element.134), channel_id=1, source_target_pairs={{0,8},{8,0},{1,9},{9,1},{2,10},{10,2},{3,11},{11,3},{4,12},{12,4},... | collective-permute-start | bytes 1867784 | tf_op jit(solution)/shard_map/ppermute | solution.py:967
  225.6 19.6 %collective-permute-start.18 = (bf16[304,1024]{1,0:T(8,128)(2,1)}, bf16[304,1024]{1,0:T(8,128)(2,1)S(1)}, u32[]{:S(2)}, u32[]{:S(2)}) collective-permute-start(bf16[304,1024]{1,0:T(8,128)(2,1)} %get-tuple-element.136.a_ref.x1_own), channel_id=1, source_target_pairs={{0,8},{8,0},{1,9},{9,1},{2,10},{10,2},{3,11},{11,3},{4,12},{12,4},... | collective-permute-start | bytes 1867784 | tf_op jit(solution)/shard_map/ppermute | solution.py:967
  255.6 17.2 %collective-permute-start.19 = (bf16[304,1024]{1,0:T(8,128)(2,1)}, bf16[304,1024]{1,0:T(8,128)(2,1)S(1)}, u32[]{:S(2)}, u32[]{:S(2)}) collective-permute-start(bf16[304,1024]{1,0:T(8,128)(2,1)} %get-tuple-element.140), channel_id=1, source_target_pairs={{0,8},{8,0},{1,9},{9,1},{2,10},{10,2},{3,11},{11,3},{4,12},{12,4},... | collective-permute-start | bytes 1867784 | tf_op jit(solution)/shard_map/ppermute | solution.py:967
  264.7 27.1 %collective-permute-start.21 = (bf16[304,1024]{1,0:T(8,128)(2,1)}, bf16[304,1024]{1,0:T(8,128)(2,1)S(1)}, u32[]{:S(2)}, u32[]{:S(2)}) collective-permute-start(bf16[304,1024]{1,0:T(8,128)(2,1)} %get-tuple-element.145), channel_id=1, source_target_pairs={{0,8},{8,0},{1,9},{9,1},{2,10},{10,2},{3,11},{11,3},{4,12},{12,4},... | collective-permute-start | bytes 1867784 | tf_op jit(solution)/shard_map/ppermute | solution.py:967
  277.3 329.5 %reduce-scatter.5.cloned.1.call-start = ((), (), s32[]{:S(2)}) async-start(), calls=%async_computation.3 | async-start | bytes 8912896 | tf_op jit(solution)/shard_map/reduce_scatter | solution.py:1038
  291.8 325.6 %reduce-scatter.3.cloned.1.call-start = ((), (), s32[]{:S(2)}) async-start(), calls=%async_computation.2 | async-start | bytes 13369344 | tf_op jit(solution)/shard_map/reduce_scatter | solution.py:1038
  297.7 14.0 %collective-permute-start.22 = (bf16[304,1024]{1,0:T(8,128)(2,1)}, bf16[304,1024]{1,0:T(8,128)(2,1)S(1)}, u32[]{:S(2)}, u32[]{:S(2)}) collective-permute-start(bf16[304,1024]{1,0:T(8,128)(2,1)} %get-tuple-element.147.g_ref.x2_own), channel_id=1, source_target_pairs={{0,8},{8,0},{1,9},{9,1},{2,10},{10,2},{3,11},{11,3},{4,12},{12,4},... | collective-permute-start | bytes 1867784 | tf_op jit(solution)/shard_map/ppermute | solution.py:967
  325.9 11.7 %collective-permute-start.23 = (bf16[304,1024]{1,0:T(8,128)(2,1)}, bf16[304,1024]{1,0:T(8,128)(2,1)S(1)}, u32[]{:S(2)}, u32[]{:S(2)}) collective-permute-start(bf16[304,1024]{1,0:T(8,128)(2,1)} %get-tuple-element.151), channel_id=1, source_target_pairs={{0,8},{8,0},{1,9},{9,1},{2,10},{10,2},{3,11},{11,3},{4,12},{12,4},... | collective-permute-start | bytes 1867784 | tf_op jit(solution)/shard_map/ppermute | solution.py:967
  343.8 10.5 %collective-permute-start.24 = (bf16[304,1024]{1,0:T(8,128)(2,1)}, bf16[304,1024]{1,0:T(8,128)(2,1)S(1)}, u32[]{:S(2)}, u32[]{:S(2)}) collective-permute-start(bf16[304,1024]{1,0:T(8,128)(2,1)} %get-tuple-element.153.g_ref.x2_own), channel_id=1, source_target_pairs={{0,8},{8,0},{1,9},{9,1},{2,10},{10,2},{3,11},{11,3},{4,12},{12,4},... | collective-permute-start | bytes 1867784 | tf_op jit(solution)/shard_map/ppermute | solution.py:967
  363.7 16.5 %collective-permute-start.25 = (bf16[304,1024]{1,0:T(8,128)(2,1)}, bf16[304,1024]{1,0:T(8,128)(2,1)S(1)}, u32[]{:S(2)}, u32[]{:S(2)}) collective-permute-start(bf16[304,1024]{1,0:T(8,128)(2,1)} %get-tuple-element.157), channel_id=1, source_target_pairs={{0,8},{8,0},{1,9},{9,1},{2,10},{10,2},{3,11},{11,3},{4,12},{12,4},... | collective-permute-start | bytes 1867784 | tf_op jit(solution)/shard_map/ppermute | solution.py:967
  386.0 15.9 %collective-permute-start.26 = (bf16[304,1024]{1,0:T(8,128)(2,1)}, bf16[304,1024]{1,0:T(8,128)(2,1)S(1)}, u32[]{:S(2)}, u32[]{:S(2)}) collective-permute-start(bf16[304,1024]{1,0:T(8,128)(2,1)} %get-tuple-element.159.g_ref.x2_own), channel_id=1, source_target_pairs={{0,8},{8,0},{1,9},{9,1},{2,10},{10,2},{3,11},{11,3},{4,12},{12,4},... | collective-permute-start | bytes 1867784 | tf_op jit(solution)/shard_map/ppermute | solution.py:967
  417.2 10.5 %collective-permute-start.27 = (bf16[304,1024]{1,0:T(8,128)(2,1)}, bf16[304,1024]{1,0:T(8,128)(2,1)S(1)}, u32[]{:S(2)}, u32[]{:S(2)}) collective-permute-start(bf16[304,1024]{1,0:T(8,128)(2,1)} %get-tuple-element.163), channel_id=1, source_target_pairs={{0,8},{8,0},{1,9},{9,1},{2,10},{10,2},{3,11},{11,3},{4,12},{12,4},... | collective-permute-start | bytes 1867784 | tf_op jit(solution)/shard_map/ppermute | solution.py:967
  427.4 94.1 %collective-permute-start.36 = (bf16[2,4,256,512]{3,2,1,0:T(8,128)(2,1)}, bf16[2,4,256,512]{3,2,1,0:T(8,128)(2,1)S(1)}, u32[]{:S(2)}, u32[]{:S(2)}) collective-permute-start(bf16[2,4,256,512]{3,2,1,0:T(8,128)(2,1)} %get-tuple-element.187), channel_id=1, source_target_pairs={{0,4},{4,0},{1,5},{5,1},{2,6},{6,2},{3,7},{7,3},{8,12},{12,8},{9,1... | collective-permute-start | bytes 6291464 | tf_op jit(solution)/shard_map/ppermute | solution.py:967
  433.5 19.0 %collective-permute-start.28 = (bf16[304,1024]{1,0:T(8,128)(2,1)}, bf16[304,1024]{1,0:T(8,128)(2,1)S(1)}, u32[]{:S(2)}, u32[]{:S(2)}) collective-permute-start(bf16[304,1024]{1,0:T(8,128)(2,1)} %get-tuple-element.164.refs_0_), channel_id=1, source_target_pairs={{0,1},{1,2},{2,3},{3,0},{4,5},{5,6},{6,7},{7,4},{8,9},{9,10},{10,1... | collective-permute-start | bytes 1867784 | tf_op jit(solution)/shard_map/ppermute | solution.py:970
  433.5 30.8 %collective-permute-start.29 = (bf16[304,1024]{1,0:T(8,128)(2,1)}, bf16[304,1024]{1,0:T(8,128)(2,1)}, u32[]{:S(2)}, u32[]{:S(2)}) collective-permute-start(bf16[304,1024]{1,0:T(8,128)(2,1)} %get-tuple-element.164.refs_0_), channel_id=1, source_target_pairs={{0,3},{1,0},{2,1},{3,2},{4,7},{5,4},{6,5},{7,6},{8,11},{9,8},{10,9... | collective-permute-start | bytes 1867784 | tf_op jit(solution)/shard_map/ppermute | solution.py:970
  437.3 84.1 %collective-permute-start.30 = (bf16[304,1024]{1,0:T(8,128)(2,1)}, bf16[304,1024]{1,0:T(8,128)(2,1)}, u32[]{:S(2)}, u32[]{:S(2)}) collective-permute-start(bf16[304,1024]{1,0:T(8,128)(2,1)} %get-tuple-element.164.refs_0_), channel_id=1, source_target_pairs={{0,2},{1,3},{2,0},{3,1},{4,6},{5,7},{6,4},{7,5},{8,10},{9,11},{10,... | collective-permute-start | bytes 1867784 | tf_op jit(solution)/shard_map/ppermute | solution.py:970
  439.1 1.5 collective-permute-start.31
  441.6 4.9 collective-permute-start.32
  446.5 4.7 collective-permute-start.33
  452.4 74.8 %copy-start.9 = (bf16[304,1024]{1,0:T(8,128)(2,1)}, bf16[304,1024]{1,0:T(8,128)(2,1)S(1)}, u32[]{:S(2)}) copy-start(bf16[304,1024]{1,0:T(8,128)(2,1)S(1)} %collective-permute-done.28.refs_1_) | copy-start | bytes 1867780
  521.5 14.9 %collective-permute-start.34 = (f32[24,1024]{1,0:T(8,128)S(1)}, f32[24,1024]{1,0:T(8,128)S(1)}, u32[]{:S(2)}, u32[]{:S(2)}) collective-permute-start(f32[24,1024]{1,0:T(8,128)S(1)} %add.74), channel_id=1, source_target_pairs={{0,1},{1,0},{2,3},{3,2},{4,5},{5,4},{6,7},{7,6},{8,9},{9,8},{10,11... | collective-permute-start | bytes 294920 | tf_op jit(solution)/shard_map/ppermute | solution.py:1094
  527.2 38.8 %collective-permute-start.37 = (bf16[4,256,512]{2,1,0:T(8,128)(2,1)}, bf16[4,256,512]{2,1,0:T(8,128)(2,1)S(1)}, u32[]{:S(2)}, u32[]{:S(2)}) collective-permute-start(bf16[4,256,512]{2,1,0:T(8,128)(2,1)} %get-tuple-element.189), channel_id=1, source_target_pairs={{0,16},{16,0},{1,17},{17,1},{2,18},{18,2},{3,19},{19,3},{4,20},{20... | collective-permute-start | bytes 3145736 | tf_op jit(solution)/shard_map/ppermute | solution.py:967
  536.3 47.8 %collective-permute-start.35 = (f32[24,1024]{1,0:T(8,128)S(1)}, f32[24,1024]{1,0:T(8,128)S(1)}, u32[]{:S(2)}, u32[]{:S(2)}) collective-permute-start(f32[24,1024]{1,0:T(8,128)S(1)} %add.75), channel_id=1, source_target_pairs={{0,2},{1,3},{2,0},{3,1},{4,6},{5,7},{6,4},{7,5},{8,10},{9,11},{10,... | collective-permute-start | bytes 294920 | tf_op jit(solution)/shard_map/ppermute | solution.py:1094
  569.8 14.9 %collective-permute-start.38 = (bf16[256,512]{1,0:T(8,128)(2,1)}, bf16[256,512]{1,0:T(8,128)(2,1)S(1)}, u32[]{:S(2)}, u32[]{:S(2)}) collective-permute-start(bf16[256,512]{1,0:T(8,128)(2,1)} %get-tuple-element.191), channel_id=1, source_target_pairs={{0,1},{1,2},{2,3},{3,0},{4,5},{5,6},{6,7},{7,4},{8,9},{9,10},{10,1... | collective-permute-start | bytes 786440 | tf_op jit(solution)/shard_map/ppermute | solution.py:970
  571.8 26.9 %collective-permute-start.39 = (bf16[256,512]{1,0:T(8,128)(2,1)}, bf16[256,512]{1,0:T(8,128)(2,1)S(1)}, u32[]{:S(2)}, u32[]{:S(2)}) collective-permute-start(bf16[256,512]{1,0:T(8,128)(2,1)} %get-tuple-element.192), channel_id=1, source_target_pairs={{0,2},{1,3},{2,0},{3,1},{4,6},{5,7},{6,4},{7,5},{8,10},{9,11},{10,... | collective-permute-start | bytes 786440 | tf_op jit(solution)/shard_map/ppermute | solution.py:970
  571.8 29.8 %collective-permute-start.40 = (bf16[256,512]{1,0:T(8,128)(2,1)}, bf16[256,512]{1,0:T(8,128)(2,1)S(1)}, u32[]{:S(2)}, u32[]{:S(2)}) collective-permute-start(bf16[256,512]{1,0:T(8,128)(2,1)} %get-tuple-element.193), channel_id=1, source_target_pairs={{0,3},{1,0},{2,1},{3,2},{4,7},{5,4},{6,5},{7,6},{8,11},{9,8},{10,9... | collective-permute-start | bytes 786440 | tf_op jit(solution)/shard_map/ppermute | solution.py:970
  584.8 16.8 %copy-start.38 = (bf16[256,512]{1,0:T(8,128)(2,1)}, bf16[256,512]{1,0:T(8,128)(2,1)S(1)}, u32[]{:S(2)}) copy-start(bf16[256,512]{1,0:T(8,128)(2,1)S(1)} %collective-permute-done.38.refs_1_) | copy-start | bytes 786436
  604.4 19.1 %collective-permute-start.41 = (bf16[128,512]{1,0:T(8,128)(2,1)}, bf16[128,512]{1,0:T(8,128)(2,1)S(1)}, u32[]{:S(2)}, u32[]{:S(2)}) collective-permute-start(bf16[128,512]{1,0:T(8,128)(2,1)} %get-tuple-element.195), channel_id=1, source_target_pairs={{0,8},{8,0},{1,9},{9,1},{2,10},{10,2},{3,11},{11,3},{4,12},{12,4},... | collective-permute-start | bytes 393224 | tf_op jit(solution)/shard_map/ppermute | solution.py:967
  608.7 14.8 %collective-permute-start.44 = (bf16[128,1024]{1,0:T(8,128)(2,1)}, bf16[128,1024]{1,0:T(8,128)(2,1)S(1)}, u32[]{:S(2)}, u32[]{:S(2)}) collective-permute-start(bf16[128,1024]{1,0:T(8,128)(2,1)} %get-tuple-element.213), channel_id=1, source_target_pairs={{0,8},{8,0},{1,9},{9,1},{2,10},{10,2},{3,11},{11,3},{4,12},{12,4},... | collective-permute-start | bytes 786440 | tf_op jit(solution)/shard_map/ppermute | solution.py:967
  619.4 12.0 %collective-permute-start.42 = (bf16[128,1024]{1,0:T(8,128)(2,1)}, bf16[128,1024]{1,0:T(8,128)(2,1)S(1)}, u32[]{:S(2)}, u32[]{:S(2)}) collective-permute-start(bf16[128,1024]{1,0:T(8,128)(2,1)} %get-tuple-element.205), channel_id=1, source_target_pairs={{0,8},{8,0},{1,9},{9,1},{2,10},{10,2},{3,11},{11,3},{4,12},{12,4},... | collective-permute-start | bytes 786440 | tf_op jit(solution)/shard_map/ppermute | solution.py:967
  621.9 9.6 %collective-permute-start.43 = (bf16[128,512]{1,0:T(8,128)(2,1)}, bf16[128,512]{1,0:T(8,128)(2,1)S(1)}, u32[]{:S(2)}, u32[]{:S(2)}) collective-permute-start(bf16[128,512]{1,0:T(8,128)(2,1)} %get-tuple-element.207), channel_id=1, source_target_pairs={{0,8},{8,0},{1,9},{9,1},{2,10},{10,2},{3,11},{11,3},{4,12},{12,4},... | collective-permute-start | bytes 393224 | tf_op jit(solution)/shard_map/ppermute | solution.py:967
  623.5 8.0 %copy-start.41 = (bf16[128,512]{1,0:T(8,128)(2,1)}, bf16[128,512]{1,0:T(8,128)(2,1)S(1)}, u32[]{:S(2)}) copy-start(bf16[128,512]{1,0:T(8,128)(2,1)S(1)} %collective-permute-done.41.refs_1_) | copy-start | bytes 393220
  (29 other events, 43.1 us)
Sparse Core Ops, SparseCore 0:
  40.6 106.5 all-gather.6
  149.5 74.7 all-gather.8
  277.4 49.9 all-gather.10
  331.3 103.6 reduce-scatter.4
  438.9 178.4 reduce-scatter.2

commit v3 on v2

--- a/solution.py
+++ b/solution.py
@@ -31,11 +31,14 @@
     return lax.dot_general(a, b, (((0,), (0,)), ((), ())), preferred_element_type=F32)
 
 
+COST = 4e9
+
+
 def params(micros):
     return dict(
         compiler_params=pltpu.CompilerParams(vmem_limit_bytes=VMEM_LIMIT),
         cost_estimate=pl.CostEstimate(
-            flops=int(micros * 4e9), bytes_accessed=0, transcendentals=0
+            flops=int(micros * COST), bytes_accessed=0, transcendentals=0
         ),
     )
 
@@ -84,10 +87,13 @@
     token = row // images
     want = row - token * images
     total = None
-    for step, part_ref in zip((0, 1, 3, 2), parts):
-        image = want - ((place[DEPTH] - step) & 3) * mine
+    for index, step in enumerate((0, 1, 3, 2)):
+        depth, rows = index, parts[0].at[index] if len(parts) == 1 else parts[index]
+        if len(parts) > 1:
+            depth = (place[DEPTH] - step) & 3
+        image = want - depth * mine
         hit = (image >= 0) & (image < mine) & (col == image * seq + token)
-        part = dot_nn(jnp.where(hit, 1.0, 0.0).astype(BF16), part_ref[...])
+        part = dot_nn(jnp.where(hit, 1.0, 0.0).astype(BF16), rows[...])
         total = part if total is None else total + part
     out_ref[...] = total.astype(out_ref.dtype)
 
@@ -170,15 +176,15 @@
 
 
 def run_leave(place, parts, seq, mine, dtype):
-    images, width = 4 * mine, parts[0].shape[1]
+    images, width = 4 * mine, parts[0].shape[-1]
     flat = pl.pallas_call(
         functools.partial(leave_kernel, seq, mine),
         out_shape=jax.ShapeDtypeStruct((images * seq, width), dtype),
-        in_specs=[SM, VM, VM, VM, VM],
+        in_specs=[SM] + [VM] * len(parts),
         out_specs=VM,
         **params(9),
     )(place, *parts)
-    return flat.reshape(seq, images, width).transpose(1, 0, 2)
+    return flat
 
 
 def run_residual_norm(x, own, far, bias, gain, beta):
@@ -671,137 +677,96 @@
     )(grad, slope, pieces)
 
 
+SEND, AWAY, NEAR, ALL = 0, 1, 2, 3
+STAGE_SLOTS = (((0, 1), (1, 1)), ((1, 0),), ((0, 0),), ((0, 0), (0, 1), (1, 0), (1, 1)))
+
+
 def weight_grad_kernel(
-    kind, place, x1_own, x1_far, y1_own, y1_far, x2_own, x2_far, y2_own, y2_far, *refs
+    stage, place, x1_own, x1_far, y1_own, y1_far, x2_own, x2_far, y2_own, y2_far, *refs
 ):
-    (xs, y1, y2, turned, sems), refs = refs[-5:], refs[:-5]
-    if kind == "relative":
-        near_ref, away_ref, send_ref = refs
-        outs = (near_ref, send_ref.at[0], away_ref, send_ref.at[1])
-    else:
-        outs = [refs[-1].at[side, core] for side in range(2) for core in range(2)]
-    top, low = pl.ds(0, ROWS), pl.ds(ROWS, ROWS)
-    pairs = [
-        (x1_own, xs.at[0, top]),
-        (x1_far, xs.at[0, low]),
-        (x2_own, xs.at[1, top]),
-        (x2_far, xs.at[1, low]),
-        (y1_own, y1.at[:, top]),
-        (y1_far, y1.at[:, low]),
-        (y2_own, y2.at[:, top]),
-        (y2_far, y2.at[:, low]),
-    ]
-    if kind == "extra":
-        pairs += [
-            (refs[0].at[slot // 2, slot % 2], out.at[:, 256:384, :])
-            for slot, out in enumerate(outs)
-        ]
-    copies = [
-        pltpu.make_async_copy(src, dst, sems.at[index]) for index, (src, dst) in enumerate(pairs)
-    ]
+    slots = STAGE_SLOTS[stage]
+    (xs, y1, y2, turned, added, sems), refs = refs[-6:], refs[:-6]
+    out_ref = refs[-1]
+    got = [refs[0].at[0 if stage == NEAR else 1], *refs[1:-1]] if stage in (AWAY, NEAR) else []
+    outs = [out_ref.at[slot] for slot in range(len(slots))] if len(slots) > 1 else [out_ref]
+    copies = []
+    for slot, (side, core) in enumerate(slots):
+        if stage != ALL:
+            side, core = place[SIDE] ^ side, place[CORE] ^ core
+        start = aligned(4 * side + core, 128)
+        for index, sources in enumerate(((x1_own, x1_far), (x2_own, x2_far))):
+            for half, source in enumerate(sources):
+                for run in range(2):
+                    copies.append(
+                        pltpu.make_async_copy(
+                            source.at[:, pl.ds(start + 256 * run, 128)],
+                            xs.at[index, slot, pl.ds(ROWS * half, ROWS), pl.ds(128 * run, 128)],
+                            sems.at[4, 8 * slot + 4 * index + 2 * half + run],
+                        )
+                    )
     for copy in copies:
         copy.start()
-    span1, span2 = y1.shape[2], y2.shape[2]
-    span = span1 + span2
-    for index in range(2):
-        copies[2 * index].wait()
-        copies[2 * index + 1].wait()
-        for slot in range(4):
-            side, core = slot // 2, slot % 2
-            if kind == "relative":
-                start = (place[SIDE] ^ side) * 512 + (place[CORE] ^ core) * 128
-                start = pl.multiple_of(start, 128)
-            else:
-                start = side * 512 + core * 128
-            cols = jnp.concatenate(
-                [xs[index, :, pl.ds(start, 128)], xs[index, :, pl.ds(start + 256, 128)]], axis=1
-            )
-            turned[index, slot] = cols.T
-    for copy in copies[4:8]:
+    for chunk in range(4):
+        for index, (source, target) in enumerate(
+            ((y1_own, y1), (y1_far, y1), (y2_own, y2), (y2_far, y2))
+        ):
+            pltpu.make_async_copy(
+                source.at[chunk],
+                target.at[chunk, pl.ds(ROWS * (index % 2), ROWS)],
+                sems.at[chunk, index],
+            ).start()
+        for index, source in enumerate(got):
+            pltpu.make_async_copy(
+                source.at[chunk], added.at[index, chunk], sems.at[chunk, 4 + index]
+            ).start()
+    for copy in copies:
         copy.wait()
+    for slot in range(len(slots)):
+        for index in range(2):
+            turned[index, slot] = xs[index, slot].T
+    span1 = y1.shape[2]
 
     def chunk_step(chunk, carry):
+        for index, target in enumerate((y1, y1, y2, y2)):
+            half = target.at[chunk, pl.ds(ROWS * (index % 2), ROWS)]
+            pltpu.make_async_copy(half, half, sems.at[chunk, index]).wait()
+        for index in range(len(got)):
+            array = added.at[index, chunk]
+            pltpu.make_async_copy(array, array, sems.at[chunk, 4 + index]).wait()
         for slot, out in enumerate(outs):
-            first = dot_nn(turned[0, slot], y1[chunk]).astype(BF16)
-            second = dot_nn(turned[1, slot], y2[chunk]).astype(BF16)
-            if kind == "compact":
-                for side in range(2):
-                    rows = slice(128 * side, 128 * side + 128)
-                    out[chunk, :, span * side : span * side + span1] = first[rows]
-                    out[chunk, :, span * side + span1 : span * side + span] = second[rows]
-            else:
-                out[chunk, 0:256, 0:span1] = first
-                out[chunk, 0:256, span1:span] = second
+            first = dot_nn(turned[0, slot], y1[chunk])
+            second = dot_nn(turned[1, slot], y2[chunk])
+            for index in range(len(got)):
+                first += added[index, chunk, :, 0:span1].astype(F32)
+                second += added[index, chunk, :, span1:].astype(F32)
+            out[chunk, :, 0:span1] = first.astype(BF16)
+            out[chunk, :, span1:] = second.astype(BF16)
         return carry
 
     lax.fori_loop(0, 4, chunk_step, 0)
-    for copy in copies[8:]:
-        copy.wait()
-
-
-def run_weight_grad(kind, place, x1, y1, x2, y2, *extra):
+
+
+def run_weight_grad(stage, place, x1, y1, x2, y2, *got):
     rows, width = 2 * ROWS, x1[0].shape[1]
     span1, span2 = y1[0].shape[2], y2[0].shape[2]
-    span = span1 + span2
-    if kind == "relative":
-        half = jax.ShapeDtypeStruct((4, width // 4, span), BF16)
-        shapes = (half, half, jax.ShapeDtypeStruct((2, *half.shape), BF16))
-    else:
-        shape = {"plain": (256, span), "compact": (128, 2 * span), "extra": (384, span)}[kind]
-        shapes = (jax.ShapeDtypeStruct((2, 2, 4, *shape), BF16),)
-    return pl.pallas_call(
-        functools.partial(weight_grad_kernel, kind),
-        out_shape=shapes,
-        in_specs=[SM] + [HB] * (8 + len(extra)),
-        out_specs=(VM,) * len(shapes),
+    part = width // 4
+    shape = (4, part, span1 + span2)
+    slots = len(STAGE_SLOTS[stage])
+    return pl.pallas_call(
+        functools.partial(weight_grad_kernel, stage),
+        out_shape=jax.ShapeDtypeStruct((slots, *shape) if slots > 1 else shape, BF16),
+        in_specs=[SM] + [HB] * (8 + len(got)),
+        out_specs=VM,
         scratch_shapes=[
-            pltpu.VMEM((2, rows, width), BF16),
+            pltpu.VMEM((2, slots, rows, part), BF16),
             pltpu.VMEM((4, rows, span1), BF16),
             pltpu.VMEM((4, rows, span2), BF16),
-            pltpu.VMEM((2, 4, width // 4, rows), BF16),
-            pltpu.SemaphoreType.DMA((12,)),
+            pltpu.VMEM((2, slots, part, rows), BF16),
+            pltpu.VMEM((max(len(got), 1), *shape), BF16),
+            pltpu.SemaphoreType.DMA((5, 32)),
         ],
-        **params(14 if span1 > 384 else 10),
-    )(place, *x1, *y1, *x2, *y2, *extra)
-
-
-def add_core_kernel(near, away, got, near_out, away_out):
-    near_out[...] = (near[...].astype(F32) + got[0].astype(F32)).astype(BF16)
-    away_out[...] = (away[...].astype(F32) + got[1].astype(F32)).astype(BF16)
-
-
-def run_add_core(near, away, got):
-    chunks, rows, span = near.shape
-    one = pl.BlockSpec((1, rows, span), lambda step: (step, 0, 0))
-    two = pl.BlockSpec((2, 1, rows, span), lambda step: (0, step, 0, 0))
-    shape = jax.ShapeDtypeStruct(near.shape, BF16)
-    return pl.pallas_call(
-        add_core_kernel,
-        grid=(chunks,),
-        out_shape=(shape, shape),
-        in_specs=[one, one, two],
-        out_specs=(one, one),
-        **params(4),
-    )(near, away, got)
-
-
-def add_side_kernel(place, near, got, *outs):
-    for step, out in enumerate(outs):
-        depth = (place[DEPTH] + step) & 3
-        out[...] = (near[depth].astype(F32) + got[depth].astype(F32)).astype(out.dtype)
-
-
-def run_add_side(place, near, got):
-    chunks, rows, span = near.shape
-    return pl.pallas_call(
-        add_side_kernel,
-        out_shape=tuple(
-            jax.ShapeDtypeStruct((rows, span), BF16 if step else F32) for step in range(chunks)
-        ),
-        in_specs=[SM, VM, VM],
-        out_specs=(VM,) * chunks,
-        **params(3),
-    )(place, near, got)
+        **params((4 if span1 > 384 else 3) * slots + 2),
+    )(place, *x1, *y1, *x2, *y2, *got)
 
 
 def add_depth_kernel(place, *refs):
@@ -887,30 +852,6 @@
     )(place, total)
 
 
-def split_kernel(place, total, *outs):
-    even = place[PAIR] == 0
-    stay, move = outs[:2]
-    low, high = total[0:128, :], total[128:256, :]
-    stay[...] = jnp.where(even, low, high)
-    move[...] = jnp.where(even, high, low)
-    if len(outs) > 2:
-        stay, move = outs[2:]
-        low, high = total[256:384, 0:512], total[256:384, 512:1024]
-        stay[...] = jnp.where(even, low, high)
-        move[...] = jnp.where(even, high, low)
-
-
-def run_split(place, total):
-    spans = (1024, 1024, 512, 512) if total.shape[0] > 256 else (1024, 1024)
-    return pl.pallas_call(
-        split_kernel,
-        out_shape=tuple(jax.ShapeDtypeStruct((128, span), BF16) for span in spans),
-        in_specs=[SM, VM],
-        out_specs=(VM,) * len(spans),
-        **params(2),
-    )(place, total)
-
-
 def finish_kernel(place, *refs):
     layers = (len(refs) - 4) // 4
     ins, (qkv, proj, fc1, fc2) = refs[: 4 * layers], refs[4 * layers :]
@@ -988,9 +929,9 @@
     stream, normed = run_enter(here, images_in, mine, norm1_gain[0], norm1_bias[0])
     grad, grad_b, fc2_sum = run_enter_back(here, out_cotangent, mine)
     grad_b_far = swap(grad_b, "x")
-    gathered = [*moved, normed, grad_b]
+    gathered = []
     for index in (1, 2):
-        gathered = lax.all_gather(after(packed[index], *gathered), ("y", "core", "mp"))
+        gathered = lax.all_gather((after(packed[index], *gathered) if gathered else packed[index]), ("y", "core", "mp"))
         value = gathered.reshape(2, 2, n_mp, *gathered.shape[1:])
         mlp_pieces.append(value)
         attn_pieces.append([value])
@@ -1013,7 +954,8 @@
         )
         normed2_far = swap(normed2, "x")
         active, slope, part = both(
-            lambda rows: run_mlp_forward(rows, mlp_pieces[layer]), normed2, normed2_far
+            lambda rows: run_mlp_forward(rows, mlp_pieces[layer]),
+            after(normed2, grad_b_far), normed2_far,
         )
         saved.append(
             (stream, (normed, normed_far), qkv, mixed, middle, (normed2, normed2_far), active, slope)
@@ -1026,33 +968,44 @@
         else:
             last = run_residual(middle, part[0], swap(part[1], "x"), fc2_bias[layer])
 
-    gathered = lax.all_gather(last, "mp")
-    block_out = run_leave(
-        here,
-        [lax.dynamic_index_in_dim(gathered, (depth - step) % n_mp, 0, False) for step in (0, 1, 3, 2)],
-        seq, mine, BF16,
-    )
-
-    def gather_sum(grads):
-        flat = grads.reshape(-1, grads.shape[-1])
-        return run_split(here, lax.psum_scatter(flat, ("y", "core", "mp"), tiled=True))
-
-    above, ready = (), [None] * (2 * layers)
+    class Sum:
+        def __init__(self, *arrays):
+            self.arrays = arrays
+            self.core = swap(run_weight_grad(SEND, here, *arrays), "core")
+
+        def away(self):
+            kept = run_weight_grad(AWAY, here, *self.arrays, self.core)
+            self.side = swap(kept, "y")
+            return kept
+
+        def near(self, *waits):
+            side = after(self.side, *waits) if waits else self.side
+            kept = run_weight_grad(NEAR, here, *self.arrays, self.core, side)
+            flat = kept.reshape(-1, kept.shape[-1])
+            self.total = lax.psum_scatter(flat, "mp", tiled=True)
+            return kept
+
+        def result(self):
+            return run_add_depth(here, [self.total])
+
+    class SumAtOnce(Sum):
+        def __init__(self, *arrays):
+            grads = run_weight_grad(ALL, here, *arrays)
+            flat = grads.reshape(-1, grads.shape[-1])
+            self.total = lax.psum_scatter(flat, ("y", "core", "mp"), tiled=True)
+
+    attn, mlp, groups = None, None, []
     small = [None] * layers
     for layer in reversed(range(layers)):
         stream, normed, qkv, mixed, middle, normed2, active, slope = saved[layer]
         slopes, qkvs = list(slope), list(qkv)
         du, fc1_sum, part = both(
             lambda rows: run_mlp_backward(rows, slopes.pop(0), mlp_pieces[layer]),
-            grad_b, grad_b_far,
+            grad_b, grad_b_far, *([attn.away()] if attn else []),
         )
-        (grads,) = run_weight_grad(
-            "extra" if above else "plain", here, normed2, du, (grad_b, grad_b_far), active, *above
-        )
-        sums = gather_sum(grads)
-        ready[2 * layer + 1] = sums[:2]
-        if above:
-            ready[2 * layer + 2] = sums[2:]
+        mlp = (SumAtOnce if layer else Sum)(normed2, du, (grad_b, grad_b_far), active)
+        if layer:
+            last = after(last, mlp.total)
         grad, grad_b, sums2 = run_norm_back(
             grad, part[0], swap(part[1], "x"), middle, norm2_gain[layer]
         )
@@ -1061,44 +1014,49 @@
             lambda rows: run_attention_backward(
                 layer, here, rows, qkvs.pop(0), attn_weights, attn_pieces[layer]
             ),
-            grad_b, grad_b_far,
+            grad_b, grad_b_far, *([] if layer else [mlp.away()]),
         )
-        above = run_weight_grad(
-            "compact" if layer else "relative", here, normed, dqkv, (grad_b, grad_b_far), mixed
-        )
+        above, attn = attn, Sum(normed, dqkv, (grad_b, grad_b_far), mixed)
+        if above:
+            grad = after(grad, above.near())
         grad, grad_b, sums1 = run_norm_back(
             grad, part[0], swap(part[1], "x"), stream, norm1_gain[layer]
         )
         if layer:
             grad_b_far = swap(grad_b, "x")
         small[layer] = [sums1, sums2, *qv_sum, *fc1_sum]
-
-    parts = {step: shift(grad_b, step) for step in (1, 3, 2)}
-    input_grad = run_leave(here, [grad_b] + [parts[step] for step in (1, 3, 2)], seq, mine, F32)
-
-    near, away, send = above
-    near, away = run_add_core(near, away, swap(send, "core"))
-    pieces = run_add_side(here, near, swap(away, "y"))
-    pieces = [pieces[0]] + [shift(pieces[step], step) for step in range(1, n_mp)]
-    ready[0] = run_add_depth(here, pieces)
-
-    total = run_collect(here, fc2_sum, [part for parts in small for part in parts])
+        groups = [attn, mlp, *groups]
+
+    block_out = run_leave(here, [lax.all_gather(last, "mp")], seq, mine, BF16)
+    parts = [shift(grad_b, step) for step in (1, 3, 2)]
+    attn.core = after(attn.core, grad_b)
+    attn.away()
+    kept = mlp.near(parts[0])
+    kept = attn.near(kept, block_out, *parts)
+    parts = [after(part, kept) for part in parts]
+    input_grad = run_leave(here, [grad_b, *parts], seq, mine, F32)
+    total = run_collect(here, fc2_sum, [part for group in small for part in group])
+    total = after(total, kept)
     for axis in ("core", "x", "y"):
         total = total + swap(total, axis)
     for bit in range(n_far.bit_length() - 1):
         pairs = [(index, index ^ (1 << bit)) for index in range(n_far)]
         total = total + lax.ppermute(total, "far", pairs)
-    total = after(total, *parts.values())
+    total = after(total, *parts)
     for bit in range(n_mp.bit_length() - 1):
         pairs = [(index, index ^ (1 << bit)) for index in range(n_mp)]
         total = total + lax.ppermute(total, "mp", pairs)
     n1g, n1b, pb, n2g, n2b, f2b, qv, fc1 = run_release(here, total)
 
+    ready = [group.result() for group in groups]
     if n_far == 1:
         parts = [part for stay, move in ready for part in (stay, swap(move, "x"))]
     else:
         parts = [part for stay, move in ready for part in spread_rows(stay, move)]
     g_qkv, g_proj, g_fc1, g_fc2 = run_finish(here, parts)
+    block_out, input_grad = (
+        value.reshape(seq, images, -1).transpose(1, 0, 2) for value in (block_out, input_grad)
+    )
     return (
         block_out, input_grad, n1g, n1b, g_qkv.transpose(0, 2, 1, 3), qv, g_proj, pb, n2g, n2b,
         g_fc1, fc1, g_fc2, f2b,

time: 650 us -> 601 us (0.925)
  waiting for transfers between devices: 254 us -> 179 us
  Pallas kernels: 303 us -> 328 us
  starting transfers between devices: 46 us -> 52.7 us
    ppermute x9 -> x6, waiting for transfers between devices: 101 us -> 55.7 us  [shift(): lax.ppermute(value, 'mp', [(index, (index + step) % n_mp) for index in ra...]
    ppermute x34 -> x38, waiting for transfers between devices: 117 us -> 73.4 us  [swap(): return lax.ppermute(value, axis, [(0, 1), (1, 0)])]
    reduce_scatter x2 -> x4, waiting for transfers between devices: 8.68 us -> 30.7 us  [the longest x3 30.7 us: near(): self.total = lax.psum_scatter(flat, 'mp', tiled=True)]
    pallas_call x8 -> x10, Pallas kernels: 61.2 us -> 82.3 us  [run_weight_grad(): pl.pallas_call(functools.partial(weight_grad_kernel, stage), out_shape=ja...]
    all_gather x3, waiting for transfers between devices: 27.1 us -> 19.3 us  [the longest x2 19.3 us: on_device(): lax.all_gather(after(packed[index], *gathered) if gathered else packed[in...]
    ppermute x34 -> x38, starting transfers between devices: 31.1 us -> 36.3 us  [swap(): return lax.ppermute(value, axis, [(0, 1), (1, 0)])]
    ppermute x9 -> x6, starting transfers between devices: 14.3 us -> 10.9 us  [shift(): lax.ppermute(value, 'mp', [(index, (index + step) % n_mp) for index in ra...]
    unnamed x86 -> x88, local copies, waits for them, and re-layouts: 16 us -> 16.2 us
  transfers between devices with their start and end apart: 50 -> 53, of which waited for: 27 -> 21; matrix products, arithmetic and copies ran while one was open for 1% -> 1% of each run, Pallas kernels for 46% -> 52%
where the time goes in v3:
time: 601 us; the launch traced here: 596 us
  Pallas kernels  328 us (55%)
  waiting for transfers between devices  179 us (30%)
  starting transfers between devices  52.7 us (9%)
  local copies, waits for them, and re-layouts  19.9 us (3%)
  between operations  15.2 us (3%)
    pallas_call x10, Pallas kernels, run_weight_grad(): pl.pallas_call(functools.partial(weight_grad_kernel, stage), out_shape=ja...  82.3 us
    ppermute x38, waiting for transfers between devices, swap(): return lax.ppermute(value, axis, [(0, 1), (1, 0)])  73.4 us
    pallas_call x4, Pallas kernels, run_attention_backward(): pl.pallas_call(functools.partial(attention_backward_kernel, layer, len(pi...  55.7 us
    ppermute x6, waiting for transfers between devices, shift(): lax.ppermute(value, 'mp', [(index, (index + step) % n_mp) for index in ra...  55.7 us
    pallas_call x4, Pallas kernels, run_mlp_forward(): pl.pallas_call(mlp_forward_kernel, out_shape=(jax.ShapeDtypeStruct((4, RO...  38 us
    pallas_call x4, Pallas kernels, run_attention_forward(): pl.pallas_call(functools.partial(attention_forward_kernel, layer, len(pie...  37.7 us
    ppermute x38, starting transfers between devices, swap(): return lax.ppermute(value, axis, [(0, 1), (1, 0)])  36.3 us
    pallas_call x4, Pallas kernels, run_mlp_backward(): pl.pallas_call(mlp_backward_kernel, out_shape=(jax.ShapeDtypeStruct((4, R...  34 us
  transfers between devices with their start and end apart: 53, of which 21 were waited for; matrix products, arithmetic and copies ran while one was open for 1% of the time, Pallas kernels for 52%

profile of v3, /device:TPU:0, one launch (start us, length us, event | category | flops | bytes accessed | tf_op | source)
XLA Modules:
  0.0 595.8 jit_solution(15121635839397321644)
XLA Ops:
  7.9 3.6 shard_map.246
  11.5 3.1 collective-permute-start
  14.6 2.6 collective-permute-start.4
  19.8 4.7 collective-permute-done.refs_0_
  26.2 3.9 shard_map.245
  31.8 16.4 %collective-permute-done.4.refs_4_ = bf16[272,512]{1,0:T(8,128)(2,1)S(1)} collective-permute-done((bf16[272,512]{1,0:T(8,128)(2,1)}, bf16[272,512]{1,0:T(8,128)(2,1)S(1)}, u32[]{:S(2)}, u32[]{:S(2)}) %collective-permute-start.4) | collective-permute-done | bytes 278560 | tf_op jit(solution)/shard_map/ppermute | solution.py:911
  50.3 4.0 shard_map.250
  54.6 3.1 collective-permute-done.5.refs_5_
  58.2 4.3 collective-permute-done.9.refs_9_
  66.4 10.0 %shard_map.248 = (bf16[4,304,384]{2,1,0:T(8,128)(2,1)}, bf16[4,304,128]{2,1,0:T(8,128)(2,1)}, bf16[304,1024]{1,0:T(8,128)(2,1)}) custom-call(s32[8]{0:T(128)} %stack.35.place, bf16[304,1024]{1,0:T(8,128)(2,1)} %copy-done.11, bf16[2,3,1024,256]{3,2,1,0:T(8,128)(2,1)} %bitcast.46, bf16[2,256,1024]{2,1,0:T(8,128)(2,1)} %wproj.17, f32[2,2,256]{2,1,0:T(2,128)} %bqv.9, ...), custom_call_target="tpu_custom_call" | custom-call | flops 28000000000 | tf_op jit(solution)/shard_map/pallas_call | solution.py:491
  77.0 10.0 %shard_map.247 = (bf16[4,304,384]{2,1,0:T(8,128)(2,1)}, bf16[4,304,128]{2,1,0:T(8,128)(2,1)}, bf16[304,1024]{1,0:T(8,128)(2,1)}) custom-call(s32[8]{0:T(128)} %stack.35.place, bf16[304,1024]{1,0:T(8,128)(2,1)} %get-tuple-element.123.a_ref.x1_own, bf16[2,3,1024,256]{3,2,1,0:T(8,128)(2,1)} %bitcast.47, bf16[2,256,1024]{2,1,0:T(8,128)(2,1)} %wproj.17, ...), custom_call_target="tpu_custom_call" | custom-call | flops 28000000000 | tf_op jit(solution)/shard_map/pallas_call | solution.py:491
  87.0 6.8 %collective-permute-done.13.far_ref = bf16[304,1024]{1,0:T(8,128)(2,1)S(1)} collective-permute-done((bf16[304,1024]{1,0:T(8,128)(2,1)}, bf16[304,1024]{1,0:T(8,128)(2,1)S(1)}, u32[]{:S(2)}, u32[]{:S(2)}) %collective-permute-start.13) | collective-permute-done | bytes 622624 | tf_op jit(solution)/shard_map/ppermute | solution.py:908
  94.7 4.1 shard_map.249
  101.0 13.8 %collective-permute-done.15.a_ref.x1_far = bf16[304,1024]{1,0:T(8,128)(2,1)S(1)} collective-permute-done((bf16[304,1024]{1,0:T(8,128)(2,1)}, bf16[304,1024]{1,0:T(8,128)(2,1)S(1)}, u32[]{:S(2)}, u32[]{:S(2)}) %collective-permute-start.15) | collective-permute-done | bytes 622624 | tf_op jit(solution)/shard_map/ppermute | solution.py:908
  114.8 19.3 %all-gather.7.cloned.1.call-done = bf16[12800,512]{1,0:T(8,128)(2,1)} async-done(((bf16[800,512]{1,0:T(8,128)(2,1)}), bf16[12800,512]{1,0:T(8,128)(2,1)}) %all-gather.7.cloned.1.call-update) | async-done | bytes 13107216 | tf_op jit(solution)/shard_map/all_gather | solution.py:934
  134.1 9.5 %shard_map.252 = (bf16[4,304,512]{2,1,0:T(8,128)(2,1)}, bf16[4,304,512]{2,1,0:T(8,128)(2,1)}, bf16[304,1024]{1,0:T(8,128)(2,1)}) custom-call(bf16[304,1024]{1,0:T(8,128)(2,1)} %copy-done.12, bf16[2,2,4,800,512]{4,3,2,1,0:T(8,128)(2,1)} %bitcast.33), custom_call_target="tpu_custom_call" | custom-call | flops 32000000000 | tf_op jit(solution)/shard_map/pallas_call | solution.py:615
  145.1 9.5 %shard_map.251 = (bf16[4,304,512]{2,1,0:T(8,128)(2,1)}, bf16[4,304,512]{2,1,0:T(8,128)(2,1)}, bf16[304,1024]{1,0:T(8,128)(2,1)}) custom-call(bf16[304,1024]{1,0:T(8,128)(2,1)} %get-tuple-element.130.a_ref.x1_own, bf16[2,2,4,800,512]{4,3,2,1,0:T(8,128)(2,1)} %bitcast.34), custom_call_target="tpu_custom_call" | custom-call | flops 32000000000 | tf_op jit(solution)/shard_map/pallas_call | solution.py:615
  154.7 5.4 collective-permute-done.16.far_ref
  160.9 4.1 shard_map.253
  166.5 14.2 %collective-permute-done.17.a_ref.x1_far = bf16[304,1024]{1,0:T(8,128)(2,1)S(1)} collective-permute-done((bf16[304,1024]{1,0:T(8,128)(2,1)}, bf16[304,1024]{1,0:T(8,128)(2,1)S(1)}, u32[]{:S(2)}, u32[]{:S(2)}) %collective-permute-start.17) | collective-permute-done | bytes 622624 | tf_op jit(solution)/shard_map/ppermute | solution.py:908
  181.6 8.9 %shard_map.255 = (bf16[4,304,384]{2,1,0:T(8,128)(2,1)}, bf16[4,304,128]{2,1,0:T(8,128)(2,1)}, bf16[304,1024]{1,0:T(8,128)(2,1)}) custom-call(s32[8]{0:T(128)} %stack.35.place, bf16[304,1024]{1,0:T(8,128)(2,1)} %copy-done.13, bf16[2,3,1024,256]{3,2,1,0:T(8,128)(2,1)} %bitcast.48, bf16[2,256,1024]{2,1,0:T(8,128)(2,1)} %wproj.17, f32[2,2,256]{2,1,0:T(2,128)} %bqv.9, ...), custom_call_target="tpu_custom_call" | custom-call | flops 28000000000 | tf_op jit(solution)/shard_map/pallas_call | solution.py:491
  192.0 8.9 %shard_map.254 = (bf16[4,304,384]{2,1,0:T(8,128)(2,1)}, bf16[4,304,128]{2,1,0:T(8,128)(2,1)}, bf16[304,1024]{1,0:T(8,128)(2,1)}) custom-call(s32[8]{0:T(128)} %stack.35.place, bf16[304,1024]{1,0:T(8,128)(2,1)} %get-tuple-element.135.a_ref.x1_own, bf16[2,3,1024,256]{3,2,1,0:T(8,128)(2,1)} %bitcast.49, bf16[2,256,1024]{2,1,0:T(8,128)(2,1)} %wproj.17, ...), custom_call_target="tpu_custom_call" | custom-call | flops 28000000000 | tf_op jit(solution)/shard_map/pallas_call | solution.py:491
  200.9 4.5 collective-permute-done.18.far_ref
  206.3 4.2 shard_map.256
  212.0 9.5 %shard_map.257 = (bf16[4,304,512]{2,1,0:T(8,128)(2,1)}, bf16[4,304,512]{2,1,0:T(8,128)(2,1)}, bf16[304,1024]{1,0:T(8,128)(2,1)}) custom-call(bf16[304,1024]{1,0:T(8,128)(2,1)} %get-tuple-element.140.a_ref.x1_own, bf16[2,2,4,528,512]{4,3,2,1,0:T(8,128)(2,1)} %bitcast.41), custom_call_target="tpu_custom_call" | custom-call | flops 32000000000 | tf_op jit(solution)/shard_map/pallas_call | solution.py:615
  221.5 8.5 %shard_map.260 = (bf16[4,304,512]{2,1,0:T(8,128)(2,1)}, f32[4,8,512]{2,1,0:T(8,128)}, bf16[304,1024]{1,0:T(8,128)(2,1)}) custom-call(bf16[304,1024]{1,0:T(8,128)(2,1)} %get-tuple-element.129.g_ref.x2_own, bf16[4,304,512]{2,1,0:T(8,128)(2,1)} %get-tuple-element.145.slope_ref, bf16[2,2,4,528,512]{4,3,2,1,0:T(8,128)(2,1)} %bitcast.42), custom_call_target="tpu_custom_call" | custom-call | flops 28000000000 | tf_op jit(solution)/shard_map/pallas_call | solution.py:660
  230.9 9.5 %shard_map.258 = (bf16[4,304,512]{2,1,0:T(8,128)(2,1)}, bf16[4,304,512]{2,1,0:T(8,128)(2,1)}, bf16[304,1024]{1,0:T(8,128)(2,1)}) custom-call(bf16[304,1024]{1,0:T(8,128)(2,1)} %copy-done.21, bf16[2,2,4,528,512]{4,3,2,1,0:T(8,128)(2,1)} %bitcast.43), custom_call_target="tpu_custom_call" | custom-call | flops 32000000000 | tf_op jit(solution)/shard_map/pallas_call | solution.py:615
  241.1 8.5 %shard_map.261 = (bf16[4,304,512]{2,1,0:T(8,128)(2,1)}, f32[4,8,512]{2,1,0:T(8,128)}, bf16[304,1024]{1,0:T(8,128)(2,1)}) custom-call(bf16[304,1024]{1,0:T(8,128)(2,1)} %copy-done.19, bf16[4,304,512]{2,1,0:T(8,128)(2,1)} %get-tuple-element.147.slope_ref, bf16[2,2,4,528,512]{4,3,2,1,0:T(8,128)(2,1)} %bitcast.44), custom_call_target="tpu_custom_call" | custom-call | flops 28000000000 | tf_op jit(solution)/shard_map/pallas_call | solution.py:660
  251.0 15.1 %shard_map.262 = bf16[4,4,256,1024]{3,2,1,0:T(8,128)(2,1)} custom-call(s32[8]{0:T(128)} %stack.35.place, bf16[304,1024]{1,0:T(8,128)(2,1)} %get-tuple-element.140.a_ref.x1_own, bf16[304,1024]{1,0:T(8,128)(2,1)} %copy-done.21, bf16[4,304,512]{2,1,0:T(8,128)(2,1)} %get-tuple-element.146.y1_own, bf16[4,304,512]{2,1,0:T(8,128)(2,1)} %get-tuple-element.148.y1_far, ...), custom_call_target="tpu_custom_call" | custom-call | flops 71999995904 | tf_op jit(solution)/shard_map/pallas_call | solution.py:755
  266.2 3.1 collective-permute-done.21.far_ref
  270.2 5.4 shard_map.264
  277.0 13.6 %shard_map.265 = (bf16[4,304,384]{2,1,0:T(8,128)(2,1)}, f32[4,8,384]{2,1,0:T(8,128)}, bf16[304,1024]{1,0:T(8,128)(2,1)}) custom-call(s32[8]{0:T(128)} %stack.35.place, bf16[304,1024]{1,0:T(8,128)(2,1)} %get-tuple-element.156.g_ref.x2_own, bf16[4,304,384]{2,1,0:T(8,128)(2,1)} %get-tuple-element.157.qkv_ref, bf16[2,3,1024,256]{3,2,1,0:T(8,128)(2,1)} %bitcast.50, ...), custom_call_target="tpu_custom_call" | custom-call | flops 48000000000 | tf_op jit(solution)/shard_map/pallas_call | solution.py:557
  290.6 3.7 shard_map.259
  295.1 13.4 %shard_map.266 = (bf16[4,304,384]{2,1,0:T(8,128)(2,1)}, f32[4,8,384]{2,1,0:T(8,128)}, bf16[304,1024]{1,0:T(8,128)(2,1)}) custom-call(s32[8]{0:T(128)} %stack.35.place, bf16[304,1024]{1,0:T(8,128)(2,1)} %copy-done.20, bf16[4,304,384]{2,1,0:T(8,128)(2,1)} %get-tuple-element.159.qkv_ref, bf16[2,3,1024,256]{3,2,1,0:T(8,128)(2,1)} %bitcast.51, ...), custom_call_target="tpu_custom_call" | custom-call | flops 48000000000 | tf_op jit(solution)/shard_map/pallas_call | solution.py:557
  309.3 8.0 %shard_map.269 = bf16[2,4,256,512]{3,2,1,0:T(8,128)(2,1)} custom-call(s32[8]{0:T(128)} %stack.35.place, bf16[304,1024]{1,0:T(8,128)(2,1)} %get-tuple-element.135.a_ref.x1_own, bf16[304,1024]{1,0:T(8,128)(2,1)} %copy-done.13, bf16[4,304,384]{2,1,0:T(8,128)(2,1)} %get-tuple-element.165.y1_own, bf16[4,304,384]{2,1,0:T(8,128)(2,1)} %get-tuple-element.166.y1_far, ...), custom_call_target="tpu_custom_call" | custom-call | flops 32000000000 | tf_op jit(solution)/shard_map/pallas_call | solution.py:755
  317.4 6.4 %collective-permute-done.23.far_ref = bf16[304,1024]{1,0:T(8,128)(2,1)S(1)} collective-permute-done((bf16[304,1024]{1,0:T(8,128)(2,1)}, bf16[304,1024]{1,0:T(8,128)(2,1)S(1)}, u32[]{:S(2)}, u32[]{:S(2)}) %collective-permute-start.23) | collective-permute-done | bytes 622624 | tf_op jit(solution)/shard_map/ppermute | solution.py:908
  324.7 5.0 shard_map.267
  330.0 8.5 %shard_map.268 = (bf16[4,304,512]{2,1,0:T(8,128)(2,1)}, f32[4,8,512]{2,1,0:T(8,128)}, bf16[304,1024]{1,0:T(8,128)(2,1)}) custom-call(bf16[304,1024]{1,0:T(8,128)(2,1)} %get-tuple-element.162.g_ref.x2_own, bf16[4,304,512]{2,1,0:T(8,128)(2,1)} %get-tuple-element.163.slope_ref, bf16[2,2,4,800,512]{4,3,2,1,0:T(8,128)(2,1)} %bitcast.39), custom_call_target="tpu_custom_call" | custom-call | flops 28000000000 | tf_op jit(solution)/shard_map/pallas_call | solution.py:660
  339.9 6.3 %shard_map.270 = bf16[4,256,512]{2,1,0:T(8,128)(2,1)} custom-call(s32[8]{0:T(128)} %stack.35.place, bf16[304,1024]{1,0:T(8,128)(2,1)} %get-tuple-element.135.a_ref.x1_own, bf16[304,1024]{1,0:T(8,128)(2,1)} %copy-done.13, bf16[4,304,384]{2,1,0:T(8,128)(2,1)} %get-tuple-element.165.y1_own, bf16[4,304,384]{2,1,0:T(8,128)(2,1)} %get-tuple-element.166.y1_far, ...), custom_call_target="tpu_custom_call" | custom-call | flops 20000000000 | tf_op jit(solution)/shard_map/pallas_call | solution.py:755
  347.9 8.5 %shard_map.271 = (bf16[4,304,512]{2,1,0:T(8,128)(2,1)}, f32[4,8,512]{2,1,0:T(8,128)}, bf16[304,1024]{1,0:T(8,128)(2,1)}) custom-call(bf16[304,1024]{1,0:T(8,128)(2,1)} %copy-done.14, bf16[4,304,512]{2,1,0:T(8,128)(2,1)} %get-tuple-element.170.slope_ref, bf16[2,2,4,800,512]{4,3,2,1,0:T(8,128)(2,1)} %bitcast.40), custom_call_target="tpu_custom_call" | custom-call | flops 28000000000 | tf_op jit(solution)/shard_map/pallas_call | solution.py:660
  358.3 10.0 %shard_map.275 = bf16[2,4,256,1024]{3,2,1,0:T(8,128)(2,1)} custom-call(s32[8]{0:T(128)} %stack.35.place, bf16[304,1024]{1,0:T(8,128)(2,1)} %get-tuple-element.130.a_ref.x1_own, bf16[304,1024]{1,0:T(8,128)(2,1)} %copy-done.12, bf16[4,304,512]{2,1,0:T(8,128)(2,1)} %get-tuple-element.177.y1_own, bf16[4,304,512]{2,1,0:T(8,128)(2,1)} %get-tuple-element.178.y1_far, ...), custom_call_target="tpu_custom_call" | custom-call | flops 40000000000 | tf_op jit(solution)/shard_map/pallas_call | solution.py:755
  368.4 2.6 collective-permute-done.26.far_ref
  371.9 5.0 shard_map.272
  378.6 14.4 %shard_map.274 = (bf16[4,304,384]{2,1,0:T(8,128)(2,1)}, f32[4,8,384]{2,1,0:T(8,128)}, bf16[304,1024]{1,0:T(8,128)(2,1)}) custom-call(s32[8]{0:T(128)} %stack.35.place, bf16[304,1024]{1,0:T(8,128)(2,1)} %get-tuple-element.174.g_ref.x2_own, bf16[4,304,384]{2,1,0:T(8,128)(2,1)} %get-tuple-element.175.qkv_ref, bf16[2,3,1024,256]{3,2,1,0:T(8,128)(2,1)} %bitcast.52, ...), custom_call_target="tpu_custom_call" | custom-call | flops 48000000000 | tf_op jit(solution)/shard_map/pallas_call | solution.py:557
  394.0 6.4 %shard_map.273 = bf16[4,256,512]{2,1,0:T(8,128)(2,1)} custom-call(s32[8]{0:T(128)} %stack.35.place, bf16[304,1024]{1,0:T(8,128)(2,1)} %get-tuple-element.135.a_ref.x1_own, bf16[304,1024]{1,0:T(8,128)(2,1)} %copy-done.13, bf16[4,304,384]{2,1,0:T(8,128)(2,1)} %get-tuple-element.165.y1_own, bf16[4,304,384]{2,1,0:T(8,128)(2,1)} %get-tuple-element.166.y1_far, ...), custom_call_target="tpu_custom_call" | custom-call | flops 20000000000 | tf_op jit(solution)/shard_map/pallas_call | solution.py:755
  400.5 7.5 %shard_map.276 = bf16[4,256,1024]{2,1,0:T(8,128)(2,1)} custom-call(s32[8]{0:T(128)} %stack.35.place, bf16[304,1024]{1,0:T(8,128)(2,1)} %get-tuple-element.130.a_ref.x1_own, bf16[304,1024]{1,0:T(8,128)(2,1)} %copy-done.12, bf16[4,304,512]{2,1,0:T(8,128)(2,1)} %get-tuple-element.177.y1_own, bf16[4,304,512]{2,1,0:T(8,128)(2,1)} %get-tuple-element.178.y1_far, ...), custom_call_target="tpu_custom_call" | custom-call | flops 24000000000 | tf_op jit(solution)/shard_map/pallas_call | solution.py:755
  409.7 14.3 %shard_map.277 = (bf16[4,304,384]{2,1,0:T(8,128)(2,1)}, f32[4,8,384]{2,1,0:T(8,128)}, bf16[304,1024]{1,0:T(8,128)(2,1)}) custom-call(s32[8]{0:T(128)} %stack.35.place, bf16[304,1024]{1,0:T(8,128)(2,1)} %copy-done.15, bf16[4,304,384]{2,1,0:T(8,128)(2,1)} %get-tuple-element.182.qkv_ref, bf16[2,3,1024,256]{3,2,1,0:T(8,128)(2,1)} %bitcast.53, ...), custom_call_target="tpu_custom_call" | custom-call | flops 48000000000 | tf_op jit(solution)/shard_map/pallas_call | solution.py:557
  424.5 8.0 %shard_map.279 = bf16[2,4,256,512]{3,2,1,0:T(8,128)(2,1)} custom-call(s32[8]{0:T(128)} %stack.35.place, bf16[304,1024]{1,0:T(8,128)(2,1)} %get-tuple-element.123.a_ref.x1_own, bf16[304,1024]{1,0:T(8,128)(2,1)} %copy-done.11, bf16[4,304,384]{2,1,0:T(8,128)(2,1)} %get-tuple-element.185.y1_own, bf16[4,304,384]{2,1,0:T(8,128)(2,1)} %get-tuple-element.186.y1_far, ...), custom_call_target="tpu_custom_call" | custom-call | flops 32000000000 | tf_op jit(solution)/shard_map/pallas_call | solution.py:755
  432.6 4.2 collective-permute-done.30.far_ref
  437.7 4.9 shard_map.278
  442.6 3.8 collective-permute-start.35
  449.6 6.5 %shard_map.280 = bf16[4,256,512]{2,1,0:T(8,128)(2,1)} custom-call(s32[8]{0:T(128)} %stack.35.place, bf16[304,1024]{1,0:T(8,128)(2,1)} %get-tuple-element.123.a_ref.x1_own, bf16[304,1024]{1,0:T(8,128)(2,1)} %copy-done.11, bf16[4,304,384]{2,1,0:T(8,128)(2,1)} %get-tuple-element.185.y1_own, bf16[4,304,384]{2,1,0:T(8,128)(2,1)} %get-tuple-element.186.y1_far, ...), custom_call_target="tpu_custom_call" | custom-call | flops 20000000000 | tf_op jit(solution)/shard_map/pallas_call | solution.py:755
  457.7 14.2 %collective-permute-done.31.refs_1_ = bf16[304,1024]{1,0:T(8,128)(2,1)S(1)} collective-permute-done((bf16[304,1024]{1,0:T(8,128)(2,1)}, bf16[304,1024]{1,0:T(8,128)(2,1)S(1)}, u32[]{:S(2)}, u32[]{:S(2)}) %collective-permute-start.31) | collective-permute-done | bytes 622624 | tf_op jit(solution)/shard_map/ppermute | solution.py:911
  471.9 8.0 %shard_map.281 = bf16[4,256,1024]{2,1,0:T(8,128)(2,1)} custom-call(s32[8]{0:T(128)} %stack.35.place, bf16[304,1024]{1,0:T(8,128)(2,1)} %get-tuple-element.130.a_ref.x1_own, bf16[304,1024]{1,0:T(8,128)(2,1)} %copy-done.12, bf16[4,304,512]{2,1,0:T(8,128)(2,1)} %get-tuple-element.177.y1_own, bf16[4,304,512]{2,1,0:T(8,128)(2,1)} %get-tuple-element.178.y1_far, ...), custom_call_target="tpu_custom_call" | custom-call | flops 24000000000 | tf_op jit(solution)/shard_map/pallas_call | solution.py:755
  480.0 8.9 %shard_map.263 = bf16[1200,1024]{1,0:T(8,128)(2,1)} custom-call(s32[8]{0:T(128)} %stack.35.place, bf16[4,304,1024]{2,1,0:T(8,128)(2,1)} %bitcast.54), custom_call_target="tpu_custom_call" | custom-call | flops 35999997952 | tf_op jit(solution)/shard_map/pallas_call | solution.py:180
  489.0 20.4 %collective-permute-done.36.refs_3_ = bf16[304,1024]{1,0:T(8,128)(2,1)S(1)} collective-permute-done((bf16[304,1024]{1,0:T(8,128)(2,1)}, bf16[304,1024]{1,0:T(8,128)(2,1)S(1)}, u32[]{:S(2)}, u32[]{:S(2)}) %collective-permute-start.36) | collective-permute-done | bytes 622624 | tf_op jit(solution)/shard_map/ppermute | solution.py:911
  510.4 6.5 %shard_map.282 = bf16[4,256,512]{2,1,0:T(8,128)(2,1)} custom-call(s32[8]{0:T(128)} %stack.35.place, bf16[304,1024]{1,0:T(8,128)(2,1)} %get-tuple-element.123.a_ref.x1_own, bf16[304,1024]{1,0:T(8,128)(2,1)} %copy-done.11, bf16[4,304,384]{2,1,0:T(8,128)(2,1)} %get-tuple-element.185.y1_own, bf16[4,304,384]{2,1,0:T(8,128)(2,1)} %get-tuple-element.186.y1_far, ...), custom_call_target="tpu_custom_call" | custom-call | flops 20000000000 | tf_op jit(solution)/shard_map/pallas_call | solution.py:755
  524.8 1.9 shard_map.289
  528.2 3.4 collective-permute-start.40
  531.6 16.8 %reduce-scatter.9.cloned.1.call-done.refs_0_ = bf16[256,1024]{1,0:T(8,128)(2,1)} async-done(((bf16[1024,1024]{1,0:T(8,128)(2,1)}), bf16[256,1024]{1,0:T(8,128)(2,1)}) %reduce-scatter.9.cloned.1.call-update) | async-done | bytes 524304 | tf_op jit(solution)/shard_map/reduce_scatter | solution.py:985
  553.7 9.5 %shard_map.283 = f32[1200,1024]{1,0:T(8,128)} custom-call(s32[8]{0:T(128)} %stack.35.place, bf16[304,1024]{1,0:T(8,128)(2,1)} %get-tuple-element.184.refs_0_, bf16[304,1024]{1,0:T(8,128)(2,1)} %copy-done.16, bf16[304,1024]{1,0:T(8,128)(2,1)} %copy-done.17, bf16[304,1024]{1,0:T(8,128)(2,1)} %copy-done.18), custom_call_target="tpu_custom_call" | custom-call | flops 35999997952 | tf_op jit(solution)/shard_map/pallas_call | solution.py:180
  563.9 13.9 %reduce-scatter.7.cloned.1.call-done.refs_0_ = bf16[256,512]{1,0:T(8,128)(2,1)} async-done(((bf16[1024,512]{1,0:T(8,128)(2,1)}), bf16[256,512]{1,0:T(8,128)(2,1)}) %reduce-scatter.7.cloned.1.call-update) | async-done | bytes 262160 | tf_op jit(solution)/shard_map/reduce_scatter | solution.py:985
  582.5 2.2 collective-permute-done.42.refs_1_
  585.4 3.3 shard_map.290
  (194 shorter events, 71.7 us)
Async XLA Ops:
  7.2 126.9 %all-gather.7.cloned.1.call-start = ((), (), s32[]{:S(2)}) async-start(), calls=%async_computation.8 | async-start | bytes 13926400 | tf_op jit(solution)/shard_map/all_gather | solution.py:934
  7.9 10.7 %copy-start.1 = (f32[2,1024]{1,0:T(2,128)S(1)}, f32[2,1024]{1,0:T(2,128)}, u32[]{:S(2)}) copy-start(f32[2,1024]{1,0:T(2,128)} %param.16) | copy-start | bytes 24580
  7.9 11.3 %copy-start.2 = (f32[2,1024]{1,0:T(2,128)S(1)}, f32[2,1024]{1,0:T(2,128)}, u32[]{:S(2)}) copy-start(f32[2,1024]{1,0:T(2,128)} %param.17) | copy-start | bytes 24580
  11.5 200.5 %all-gather.9.cloned.1.call-start = ((), (), s32[]{:S(2)}) async-start(), calls=%async_computation.9 | async-start | bytes 9191424 | tf_op jit(solution)/shard_map/all_gather | solution.py:934
  11.5 12.9 %collective-permute-start = (bf16[272,512]{1,0:T(8,128)(2,1)}, bf16[272,512]{1,0:T(8,128)(2,1)S(1)}, u32[]{:S(2)}, u32[]{:S(2)}) collective-permute-start(bf16[272,512]{1,0:T(8,128)(2,1)} %get-tuple-element.124), channel_id=1, source_target_pairs={{0,1},{1,2},{2,3},{3,0},{4,5},{5,6},{6,7},{7,4},{8,9},{9,10},{10,1... | collective-permute-start | bytes 835592 | tf_op jit(solution)/shard_map/ppermute | solution.py:911
  14.6 33.6 %collective-permute-start.4 = (bf16[272,512]{1,0:T(8,128)(2,1)}, bf16[272,512]{1,0:T(8,128)(2,1)S(1)}, u32[]{:S(2)}, u32[]{:S(2)}) collective-permute-start(bf16[272,512]{1,0:T(8,128)(2,1)} %get-tuple-element.124), channel_id=1, source_target_pairs={{0,2},{1,3},{2,0},{3,1},{4,6},{5,7},{6,4},{7,5},{8,10},{9,11},{10,... | collective-permute-start | bytes 835592 | tf_op jit(solution)/shard_map/ppermute | solution.py:911
  17.2 32.5 %collective-permute-start.8 = (bf16[272,512]{1,0:T(8,128)(2,1)}, bf16[272,512]{1,0:T(8,128)(2,1)S(1)}, u32[]{:S(2)}, u32[]{:S(2)}) collective-permute-start(bf16[272,512]{1,0:T(8,128)(2,1)} %get-tuple-element.124), channel_id=1, source_target_pairs={{0,3},{1,0},{2,1},{3,2},{4,7},{5,4},{6,5},{7,6},{8,11},{9,8},{10,9... | collective-permute-start | bytes 835592 | tf_op jit(solution)/shard_map/ppermute | solution.py:911
  24.5 25.2 %collective-permute-start.1 = (bf16[272,512]{1,0:T(8,128)(2,1)S(1)}, bf16[272,512]{1,0:T(8,128)(2,1)S(1)}, u32[]{:S(2)}, u32[]{:S(2)}) collective-permute-start(bf16[272,512]{1,0:T(8,128)(2,1)S(1)} %collective-permute-done.refs_0_), channel_id=1, source_target_pairs={{0,16},{16,0},{1,17},{17,1},{2,18},{18,2},{3,19},{19,3},{4,20},{20... | collective-permute-start | bytes 835592 | tf_op jit(solution)/shard_map/ppermute | solution.py:908
  30.2 35.2 %collective-permute-start.12 = (bf16[304,1024]{1,0:T(8,128)(2,1)}, bf16[304,1024]{1,0:T(8,128)(2,1)S(1)}, u32[]{:S(2)}, u32[]{:S(2)}) collective-permute-start(bf16[304,1024]{1,0:T(8,128)(2,1)} %get-tuple-element.123.a_ref.x1_own), channel_id=1, source_target_pairs={{0,8},{8,0},{1,9},{9,1},{2,10},{10,2},{3,11},{11,3},{4,12},{12,4},... | collective-permute-start | bytes 1867784 | tf_op jit(solution)/shard_map/ppermute | solution.py:908
  31.7 346.9 %reduce-scatter.5.cloned.1.call-start = ((), (), s32[]{:S(2)}) async-start(), calls=%async_computation.4 | async-start | bytes 8912896 | tf_op jit(solution)/shard_map/reduce_scatter | solution.py:995
  31.7 22.6 %collective-permute-start.2 = (bf16[272,512]{1,0:T(8,128)(2,1)S(1)}, bf16[272,512]{1,0:T(8,128)(2,1)S(1)}, u32[]{:S(2)}, u32[]{:S(2)}) collective-permute-start(bf16[272,512]{1,0:T(8,128)(2,1)S(1)} %collective-permute-done.refs_0_), channel_id=1, source_target_pairs={{0,4},{4,0},{1,5},{5,1},{2,6},{6,2},{3,7},{7,3},{8,12},{12,8},{9,1... | collective-permute-start | bytes 835592 | tf_op jit(solution)/shard_map/ppermute | solution.py:908
  48.2 9.5 %collective-permute-start.5 = (bf16[272,512]{1,0:T(8,128)(2,1)S(1)}, bf16[272,512]{1,0:T(8,128)(2,1)S(1)}, u32[]{:S(2)}, u32[]{:S(2)}) collective-permute-start(bf16[272,512]{1,0:T(8,128)(2,1)S(1)} %collective-permute-done.4.refs_4_), channel_id=1, source_target_pairs={{0,16},{16,0},{1,17},{17,1},{2,18},{18,2},{3,19},{19,3},{4,20},{20... | collective-permute-start | bytes 835592 | tf_op jit(solution)/shard_map/ppermute | solution.py:908
  49.7 8.0 %collective-permute-start.6 = (bf16[272,512]{1,0:T(8,128)(2,1)S(1)}, bf16[272,512]{1,0:T(8,128)(2,1)S(1)}, u32[]{:S(2)}, u32[]{:S(2)}) collective-permute-start(bf16[272,512]{1,0:T(8,128)(2,1)S(1)} %collective-permute-done.4.refs_4_), channel_id=1, source_target_pairs={{0,4},{4,0},{1,5},{5,1},{2,6},{6,2},{3,7},{7,3},{8,12},{12,8},{9,1... | collective-permute-start | bytes 835592 | tf_op jit(solution)/shard_map/ppermute | solution.py:908
  49.7 12.8 %collective-permute-start.9 = (bf16[272,512]{1,0:T(8,128)(2,1)S(1)}, bf16[272,512]{1,0:T(8,128)(2,1)S(1)}, u32[]{:S(2)}, u32[]{:S(2)}) collective-permute-start(bf16[272,512]{1,0:T(8,128)(2,1)S(1)} %collective-permute-done.8.refs_8_), channel_id=1, source_target_pairs={{0,16},{16,0},{1,17},{17,1},{2,18},{18,2},{3,19},{19,3},{4,20},{20... | collective-permute-start | bytes 835592 | tf_op jit(solution)/shard_map/ppermute | solution.py:908
  50.3 12.2 %copy-start.3 = (f32[2,1024]{1,0:T(2,128)S(1)}, f32[2,1024]{1,0:T(2,128)}, u32[]{:S(2)}) copy-start(f32[2,1024]{1,0:T(2,128)} %param.22) | copy-start | bytes 24580
  50.3 12.9 %copy-start.5 = (f32[2,1024]{1,0:T(2,128)S(1)}, f32[2,1024]{1,0:T(2,128)}, u32[]{:S(2)}) copy-start(f32[2,1024]{1,0:T(2,128)} %param.23) | copy-start | bytes 24580
  50.3 12.9 %copy-start.6 = (f32[2,1024]{1,0:T(2,128)S(1)}, f32[2,1024]{1,0:T(2,128)}, u32[]{:S(2)}) copy-start(f32[2,1024]{1,0:T(2,128)} %param.21) | copy-start | bytes 24580
  54.3 11.1 %copy-start.33 = (bf16[272,512]{1,0:T(8,128)(2,1)}, bf16[272,512]{1,0:T(8,128)(2,1)S(1)}, u32[]{:S(2)}) copy-start(bf16[272,512]{1,0:T(8,128)(2,1)S(1)} %collective-permute-done.2.refs_2_) | copy-start | bytes 835588
  54.4 9.5 %collective-permute-start.10 = (bf16[272,512]{1,0:T(8,128)(2,1)S(1)}, bf16[272,512]{1,0:T(8,128)(2,1)S(1)}, u32[]{:S(2)}, u32[]{:S(2)}) collective-permute-start(bf16[272,512]{1,0:T(8,128)(2,1)S(1)} %collective-permute-done.8.refs_8_), channel_id=1, source_target_pairs={{0,4},{4,0},{1,5},{5,1},{2,6},{6,2},{3,7},{7,3},{8,12},{12,8},{9,1... | collective-permute-start | bytes 835592 | tf_op jit(solution)/shard_map/ppermute | solution.py:908
  57.7 7.7 %collective-permute-start.3 = (bf16[272,512]{1,0:T(8,128)(2,1)S(1)}, bf16[272,512]{1,0:T(8,128)(2,1)S(1)}, u32[]{:S(2)}, u32[]{:S(2)}) collective-permute-start(bf16[272,512]{1,0:T(8,128)(2,1)S(1)} %collective-permute-done.1.refs_1_), channel_id=1, source_target_pairs={{0,4},{4,0},{1,5},{5,1},{2,6},{6,2},{3,7},{7,3},{8,12},{12,8},{9,1... | collective-permute-start | bytes 835592 | tf_op jit(solution)/shard_map/ppermute | solution.py:908
  57.8 7.6 %collective-permute-start.7 = (bf16[272,512]{1,0:T(8,128)(2,1)S(1)}, bf16[272,512]{1,0:T(8,128)(2,1)S(1)}, u32[]{:S(2)}, u32[]{:S(2)}) collective-permute-start(bf16[272,512]{1,0:T(8,128)(2,1)S(1)} %collective-permute-done.5.refs_5_), channel_id=1, source_target_pairs={{0,4},{4,0},{1,5},{5,1},{2,6},{6,2},{3,7},{7,3},{8,12},{12,8},{9,1... | collective-permute-start | bytes 835592 | tf_op jit(solution)/shard_map/ppermute | solution.py:908
  62.5 2.9 collective-permute-start.11
  63.8 37.2 %collective-permute-start.14 = (bf16[304,1024]{1,0:T(8,128)(2,1)}, bf16[304,1024]{1,0:T(8,128)(2,1)S(1)}, u32[]{:S(2)}, u32[]{:S(2)}) collective-permute-start(bf16[304,1024]{1,0:T(8,128)(2,1)} %get-tuple-element.129.g_ref.x2_own), channel_id=1, source_target_pairs={{0,8},{8,0},{1,9},{9,1},{2,10},{10,2},{3,11},{11,3},{4,12},{12,4},... | collective-permute-start | bytes 1867784 | tf_op jit(solution)/shard_map/ppermute | solution.py:908
  76.4 17.4 %collective-permute-start.13 = (bf16[304,1024]{1,0:T(8,128)(2,1)}, bf16[304,1024]{1,0:T(8,128)(2,1)S(1)}, u32[]{:S(2)}, u32[]{:S(2)}) collective-permute-start(bf16[304,1024]{1,0:T(8,128)(2,1)} %get-tuple-element.126), channel_id=1, source_target_pairs={{0,8},{8,0},{1,9},{9,1},{2,10},{10,2},{3,11},{11,3},{4,12},{12,4},... | collective-permute-start | bytes 1867784 | tf_op jit(solution)/shard_map/ppermute | solution.py:908
  98.8 16.0 %collective-permute-start.15 = (bf16[304,1024]{1,0:T(8,128)(2,1)}, bf16[304,1024]{1,0:T(8,128)(2,1)S(1)}, u32[]{:S(2)}, u32[]{:S(2)}) collective-permute-start(bf16[304,1024]{1,0:T(8,128)(2,1)} %get-tuple-element.130.a_ref.x1_own), channel_id=1, source_target_pairs={{0,8},{8,0},{1,9},{9,1},{2,10},{10,2},{3,11},{11,3},{4,12},{12,4},... | collective-permute-start | bytes 1867784 | tf_op jit(solution)/shard_map/ppermute | solution.py:908
  101.0 42.6 %copy-start.19 = (bf16[304,1024]{1,0:T(8,128)(2,1)}, bf16[304,1024]{1,0:T(8,128)(2,1)S(1)}, u32[]{:S(2)}) copy-start(bf16[304,1024]{1,0:T(8,128)(2,1)S(1)} %collective-permute-done.14.g_ref.x2_far) | copy-start | bytes 1867780
  114.8 19.3 %copy-start.12 = (bf16[304,1024]{1,0:T(8,128)(2,1)}, bf16[304,1024]{1,0:T(8,128)(2,1)S(1)}, u32[]{:S(2)}) copy-start(bf16[304,1024]{1,0:T(8,128)(2,1)S(1)} %collective-permute-done.15.a_ref.x1_far) | copy-start | bytes 1867780
  143.6 16.5 %collective-permute-start.16 = (bf16[304,1024]{1,0:T(8,128)(2,1)}, bf16[304,1024]{1,0:T(8,128)(2,1)S(1)}, u32[]{:S(2)}, u32[]{:S(2)}) collective-permute-start(bf16[304,1024]{1,0:T(8,128)(2,1)} %get-tuple-element.133), channel_id=1, source_target_pairs={{0,8},{8,0},{1,9},{9,1},{2,10},{10,2},{3,11},{11,3},{4,12},{12,4},... | collective-permute-start | bytes 1867784 | tf_op jit(solution)/shard_map/ppermute | solution.py:908
  165.0 15.8 %collective-permute-start.17 = (bf16[304,1024]{1,0:T(8,128)(2,1)}, bf16[304,1024]{1,0:T(8,128)(2,1)S(1)}, u32[]{:S(2)}, u32[]{:S(2)}) collective-permute-start(bf16[304,1024]{1,0:T(8,128)(2,1)} %get-tuple-element.135.a_ref.x1_own), channel_id=1, source_target_pairs={{0,8},{8,0},{1,9},{9,1},{2,10},{10,2},{3,11},{11,3},{4,12},{12,4},... | collective-permute-start | bytes 1867784 | tf_op jit(solution)/shard_map/ppermute | solution.py:908
  190.5 15.0 %collective-permute-start.18 = (bf16[304,1024]{1,0:T(8,128)(2,1)}, bf16[304,1024]{1,0:T(8,128)(2,1)S(1)}, u32[]{:S(2)}, u32[]{:S(2)}) collective-permute-start(bf16[304,1024]{1,0:T(8,128)(2,1)} %get-tuple-element.137), channel_id=1, source_target_pairs={{0,8},{8,0},{1,9},{9,1},{2,10},{10,2},{3,11},{11,3},{4,12},{12,4},... | collective-permute-start | bytes 1867784 | tf_op jit(solution)/shard_map/ppermute | solution.py:908
  210.5 19.5 %collective-permute-start.19 = (bf16[304,1024]{1,0:T(8,128)(2,1)}, bf16[304,1024]{1,0:T(8,128)(2,1)S(1)}, u32[]{:S(2)}, u32[]{:S(2)}) collective-permute-start(bf16[304,1024]{1,0:T(8,128)(2,1)} %get-tuple-element.140.a_ref.x1_own), channel_id=1, source_target_pairs={{0,8},{8,0},{1,9},{9,1},{2,10},{10,2},{3,11},{11,3},{4,12},{12,4},... | collective-permute-start | bytes 1867784 | tf_op jit(solution)/shard_map/ppermute | solution.py:908
  240.4 50.2 %collective-permute-start.20 = (bf16[304,1024]{1,0:T(8,128)(2,1)}, bf16[304,1024]{1,0:T(8,128)(2,1)}, u32[]{:S(2)}, u32[]{:S(2)}) collective-permute-start(bf16[304,1024]{1,0:T(8,128)(2,1)} %get-tuple-element.144), channel_id=1, source_target_pairs={{0,8},{8,0},{1,9},{9,1},{2,10},{10,2},{3,11},{11,3},{4,12},{12,4},... | collective-permute-start | bytes 1867784 | tf_op jit(solution)/shard_map/ppermute | solution.py:908
  249.6 19.8 %collective-permute-start.21 = (bf16[304,1024]{1,0:T(8,128)(2,1)}, bf16[304,1024]{1,0:T(8,128)(2,1)S(1)}, u32[]{:S(2)}, u32[]{:S(2)}) collective-permute-start(bf16[304,1024]{1,0:T(8,128)(2,1)} %get-tuple-element.154), channel_id=1, source_target_pairs={{0,8},{8,0},{1,9},{9,1},{2,10},{10,2},{3,11},{11,3},{4,12},{12,4},... | collective-permute-start | bytes 1867784 | tf_op jit(solution)/shard_map/ppermute | solution.py:908
  266.2 213.9 %all-gather.11.cloned.1.call-start = ((), (), s32[]{:S(2)}) async-start(), calls=%async_computation.10 | async-start | bytes 3112960 | tf_op jit(solution)/shard_map/all_gather | solution.py:1030
  275.6 18.7 %collective-permute-start.22 = (bf16[304,1024]{1,0:T(8,128)(2,1)}, bf16[304,1024]{1,0:T(8,128)(2,1)S(1)}, u32[]{:S(2)}, u32[]{:S(2)}) collective-permute-start(bf16[304,1024]{1,0:T(8,128)(2,1)} %get-tuple-element.156.g_ref.x2_own), channel_id=1, source_target_pairs={{0,8},{8,0},{1,9},{9,1},{2,10},{10,2},{3,11},{11,3},{4,12},{12,4},... | collective-permute-start | bytes 1867784 | tf_op jit(solution)/shard_map/ppermute | solution.py:908
  308.6 15.3 %collective-permute-start.23 = (bf16[304,1024]{1,0:T(8,128)(2,1)}, bf16[304,1024]{1,0:T(8,128)(2,1)S(1)}, u32[]{:S(2)}, u32[]{:S(2)}) collective-permute-start(bf16[304,1024]{1,0:T(8,128)(2,1)} %get-tuple-element.160), channel_id=1, source_target_pairs={{0,8},{8,0},{1,9},{9,1},{2,10},{10,2},{3,11},{11,3},{4,12},{12,4},... | collective-permute-start | bytes 1867784 | tf_op jit(solution)/shard_map/ppermute | solution.py:908
  317.4 21.2 %collective-permute-start.25 = (bf16[2,4,256,512]{3,2,1,0:T(8,128)(2,1)}, bf16[2,4,256,512]{3,2,1,0:T(8,128)(2,1)S(1)}, u32[]{:S(2)}, u32[]{:S(2)}) collective-permute-start(bf16[2,4,256,512]{3,2,1,0:T(8,128)(2,1)} %shard_map.269), channel_id=1, source_target_pairs={{0,4},{4,0},{1,5},{5,1},{2,6},{6,2},{3,7},{7,3},{8,12},{12,8},{9,1... | collective-permute-start | bytes 6291464 | tf_op jit(solution)/shard_map/ppermute | solution.py:908
  329.7 17.3 %collective-permute-start.24 = (bf16[304,1024]{1,0:T(8,128)(2,1)}, bf16[304,1024]{1,0:T(8,128)(2,1)S(1)}, u32[]{:S(2)}, u32[]{:S(2)}) collective-permute-start(bf16[304,1024]{1,0:T(8,128)(2,1)} %get-tuple-element.162.g_ref.x2_own), channel_id=1, source_target_pairs={{0,8},{8,0},{1,9},{9,1},{2,10},{10,2},{3,11},{11,3},{4,12},{12,4},... | collective-permute-start | bytes 1867784 | tf_op jit(solution)/shard_map/ppermute | solution.py:908
  346.2 46.9 %collective-permute-start.27 = (bf16[4,256,512]{2,1,0:T(8,128)(2,1)}, bf16[4,256,512]{2,1,0:T(8,128)(2,1)S(1)}, u32[]{:S(2)}, u32[]{:S(2)}) collective-permute-start(bf16[4,256,512]{2,1,0:T(8,128)(2,1)} %shard_map.270), channel_id=1, source_target_pairs={{0,16},{16,0},{1,17},{17,1},{2,18},{18,2},{3,19},{19,3},{4,20},{20... | collective-permute-start | bytes 3145736 | tf_op jit(solution)/shard_map/ppermute | solution.py:908
  356.5 14.6 %collective-permute-start.26 = (bf16[304,1024]{1,0:T(8,128)(2,1)}, bf16[304,1024]{1,0:T(8,128)(2,1)S(1)}, u32[]{:S(2)}, u32[]{:S(2)}) collective-permute-start(bf16[304,1024]{1,0:T(8,128)(2,1)} %get-tuple-element.171), channel_id=1, source_target_pairs={{0,8},{8,0},{1,9},{9,1},{2,10},{10,2},{3,11},{11,3},{4,12},{12,4},... | collective-permute-start | bytes 1867784 | tf_op jit(solution)/shard_map/ppermute | solution.py:908
  368.3 32.2 %collective-permute-start.29 = (bf16[2,4,256,1024]{3,2,1,0:T(8,128)(2,1)}, bf16[2,4,256,1024]{3,2,1,0:T(8,128)(2,1)}, u32[]{:S(2)}, u32[]{:S(2)}) collective-permute-start(bf16[2,4,256,1024]{3,2,1,0:T(8,128)(2,1)} %shard_map.275), channel_id=1, source_target_pairs={{0,4},{4,0},{1,5},{5,1},{2,6},{6,2},{3,7},{7,3},{8,12},{12,8},{9,1... | collective-permute-start | bytes 12582920 | tf_op jit(solution)/shard_map/ppermute | solution.py:908
  376.8 32.0 %collective-permute-start.28 = (bf16[304,1024]{1,0:T(8,128)(2,1)}, bf16[304,1024]{1,0:T(8,128)(2,1)S(1)}, u32[]{:S(2)}, u32[]{:S(2)}) collective-permute-start(bf16[304,1024]{1,0:T(8,128)(2,1)} %get-tuple-element.174.g_ref.x2_own), channel_id=1, source_target_pairs={{0,8},{8,0},{1,9},{9,1},{2,10},{10,2},{3,11},{11,3},{4,12},{12,4},... | collective-permute-start | bytes 1867784 | tf_op jit(solution)/shard_map/ppermute | solution.py:908
  378.6 141.3 %reduce-scatter.11.cloned.1.call-start = ((), (), s32[]{:S(2)}) async-start(), calls=%async_computation.7 | async-start | bytes 1310720 | tf_op jit(solution)/shard_map/reduce_scatter | solution.py:985
  400.4 148.0 %reduce-scatter.9.cloned.1.call-start = ((), (), s32[]{:S(2)}) async-start(), calls=%async_computation.6 | async-start | bytes 2621440 | tf_op jit(solution)/shard_map/reduce_scatter | solution.py:985
  408.0 63.9 %collective-permute-start.34 = (bf16[4,256,1024]{2,1,0:T(8,128)(2,1)}, bf16[4,256,1024]{2,1,0:T(8,128)(2,1)}, u32[]{:S(2)}, u32[]{:S(2)}) collective-permute-start(bf16[4,256,1024]{2,1,0:T(8,128)(2,1)} %shard_map.276), channel_id=1, source_target_pairs={{0,16},{16,0},{1,17},{17,1},{2,18},{18,2},{3,19},{19,3},{4,20},{20... | collective-permute-start | bytes 6291464 | tf_op jit(solution)/shard_map/ppermute | solution.py:908
  424.1 12.8 %collective-permute-start.30 = (bf16[304,1024]{1,0:T(8,128)(2,1)}, bf16[304,1024]{1,0:T(8,128)(2,1)S(1)}, u32[]{:S(2)}, u32[]{:S(2)}) collective-permute-start(bf16[304,1024]{1,0:T(8,128)(2,1)} %get-tuple-element.183), channel_id=1, source_target_pairs={{0,8},{8,0},{1,9},{9,1},{2,10},{10,2},{3,11},{11,3},{4,12},{12,4},... | collective-permute-start | bytes 1867784 | tf_op jit(solution)/shard_map/ppermute | solution.py:908
  432.5 15.8 %collective-permute-start.32 = (bf16[2,4,256,512]{3,2,1,0:T(8,128)(2,1)}, bf16[2,4,256,512]{3,2,1,0:T(8,128)(2,1)S(1)}, u32[]{:S(2)}, u32[]{:S(2)}) collective-permute-start(bf16[2,4,256,512]{3,2,1,0:T(8,128)(2,1)} %shard_map.279), channel_id=1, source_target_pairs={{0,4},{4,0},{1,5},{5,1},{2,6},{6,2},{3,7},{7,3},{8,12},{12,8},{9,1... | collective-permute-start | bytes 6291464 | tf_op jit(solution)/shard_map/ppermute | solution.py:908
  442.6 29.3 %collective-permute-start.31 = (bf16[304,1024]{1,0:T(8,128)(2,1)}, bf16[304,1024]{1,0:T(8,128)(2,1)S(1)}, u32[]{:S(2)}, u32[]{:S(2)}) collective-permute-start(bf16[304,1024]{1,0:T(8,128)(2,1)} %get-tuple-element.184.refs_0_), channel_id=1, source_target_pairs={{0,1},{1,2},{2,3},{3,0},{4,5},{5,6},{6,7},{7,4},{8,9},{9,10},{10,1... | collective-permute-start | bytes 1867784 | tf_op jit(solution)/shard_map/ppermute | solution.py:911
  442.6 46.3 %collective-permute-start.35 = (bf16[304,1024]{1,0:T(8,128)(2,1)}, bf16[304,1024]{1,0:T(8,128)(2,1)S(1)}, u32[]{:S(2)}, u32[]{:S(2)}) collective-permute-start(bf16[304,1024]{1,0:T(8,128)(2,1)} %get-tuple-element.184.refs_0_), channel_id=1, source_target_pairs={{0,3},{1,0},{2,1},{3,2},{4,7},{5,4},{6,5},{7,6},{8,11},{9,8},{10,9... | collective-permute-start | bytes 1867784 | tf_op jit(solution)/shard_map/ppermute | solution.py:911
  446.5 63.0 %collective-permute-start.36 = (bf16[304,1024]{1,0:T(8,128)(2,1)}, bf16[304,1024]{1,0:T(8,128)(2,1)S(1)}, u32[]{:S(2)}, u32[]{:S(2)}) collective-permute-start(bf16[304,1024]{1,0:T(8,128)(2,1)} %get-tuple-element.184.refs_0_), channel_id=1, source_target_pairs={{0,2},{1,3},{2,0},{3,1},{4,6},{5,7},{6,4},{7,5},{8,10},{9,11},{10,... | collective-permute-start | bytes 1867784 | tf_op jit(solution)/shard_map/ppermute | solution.py:911
  456.1 53.4 %collective-permute-start.33 = (bf16[4,256,512]{2,1,0:T(8,128)(2,1)}, bf16[4,256,512]{2,1,0:T(8,128)(2,1)S(1)}, u32[]{:S(2)}, u32[]{:S(2)}) collective-permute-start(bf16[4,256,512]{2,1,0:T(8,128)(2,1)} %shard_map.280), channel_id=1, source_target_pairs={{0,16},{16,0},{1,17},{17,1},{2,18},{18,2},{3,19},{19,3},{4,20},{20... | collective-permute-start | bytes 3145736 | tf_op jit(solution)/shard_map/ppermute | solution.py:908
  471.9 8.0 %copy-start.16 = (bf16[304,1024]{1,0:T(8,128)(2,1)}, bf16[304,1024]{1,0:T(8,128)(2,1)S(1)}, u32[]{:S(2)}) copy-start(bf16[304,1024]{1,0:T(8,128)(2,1)S(1)} %collective-permute-done.31.refs_1_) | copy-start | bytes 1867780
  480.0 97.8 %reduce-scatter.7.cloned.1.call-start = ((), (), s32[]{:S(2)}) async-start(), calls=%async_computation.5 | async-start | bytes 1310720 | tf_op jit(solution)/shard_map/reduce_scatter | solution.py:985
  489.0 28.0 %copy-start = (f32[24,1024]{1,0:T(8,128)S(1)}, f32[24,1024]{1,0:T(8,128)}, u32[]{:S(2)}) copy-start(f32[24,1024]{1,0:T(8,128)} %shard_map.284) | copy-start | bytes 294916
  489.0 28.0 %copy-start.17 = (bf16[304,1024]{1,0:T(8,128)(2,1)}, bf16[304,1024]{1,0:T(8,128)(2,1)S(1)}, u32[]{:S(2)}) copy-start(bf16[304,1024]{1,0:T(8,128)(2,1)S(1)} %collective-permute-done.35.refs_2_) | copy-start | bytes 1867780
  517.0 1.4 collective-permute-start.37
  518.3 4.9 collective-permute-start.38
  521.6 60.9 %collective-permute-start.44 = (bf16[128,512]{1,0:T(8,128)(2,1)}, bf16[128,512]{1,0:T(8,128)(2,1)S(1)}, u32[]{:S(2)}, u32[]{:S(2)}) collective-permute-start(bf16[128,512]{1,0:T(8,128)(2,1)} %get-tuple-element.217), channel_id=1, source_target_pairs={{0,8},{8,0},{1,9},{9,1},{2,10},{10,2},{3,11},{11,3},{4,12},{12,4},... | collective-permute-start | bytes 393224 | tf_op jit(solution)/shard_map/ppermute | solution.py:908
  523.3 4.9 collective-permute-start.39
  526.7 55.7 %collective-permute-start.45 = (bf16[128,1024]{1,0:T(8,128)(2,1)}, bf16[128,1024]{1,0:T(8,128)(2,1)S(1)}, u32[]{:S(2)}, u32[]{:S(2)}) collective-permute-start(bf16[128,1024]{1,0:T(8,128)(2,1)} %get-tuple-element.219), channel_id=1, source_target_pairs={{0,8},{8,0},{1,9},{9,1},{2,10},{10,2},{3,11},{11,3},{4,12},{12,4},... | collective-permute-start | bytes 786440 | tf_op jit(solution)/shard_map/ppermute | solution.py:908
  528.2 23.6 %collective-permute-start.40 = (f32[24,1024]{1,0:T(8,128)S(1)}, f32[24,1024]{1,0:T(8,128)S(1)}, u32[]{:S(2)}, u32[]{:S(2)}) collective-permute-start(f32[24,1024]{1,0:T(8,128)S(1)} %add.41), channel_id=1, source_target_pairs={{0,1},{1,0},{2,3},{3,2},{4,5},{5,4},{6,7},{7,6},{8,9},{9,8},{10,11... | collective-permute-start | bytes 294920 | tf_op jit(solution)/shard_map/ppermute | solution.py:1048
  550.3 32.2 %collective-permute-start.43 = (bf16[128,1024]{1,0:T(8,128)(2,1)}, bf16[128,1024]{1,0:T(8,128)(2,1)S(1)}, u32[]{:S(2)}, u32[]{:S(2)}) collective-permute-start(bf16[128,1024]{1,0:T(8,128)(2,1)} %get-tuple-element.215), channel_id=1, source_target_pairs={{0,8},{8,0},{1,9},{9,1},{2,10},{10,2},{3,11},{11,3},{4,12},{12,4},... | collective-permute-start | bytes 786440 | tf_op jit(solution)/shard_map/ppermute | solution.py:908
  551.9 11.4 %collective-permute-start.41 = (f32[24,1024]{1,0:T(8,128)S(1)}, f32[24,1024]{1,0:T(8,128)S(1)}, u32[]{:S(2)}, u32[]{:S(2)}) collective-permute-start(f32[24,1024]{1,0:T(8,128)S(1)} %add.42), channel_id=1, source_target_pairs={{0,2},{1,3},{2,0},{3,1},{4,6},{5,7},{6,4},{7,5},{8,10},{9,11},{10,... | collective-permute-start | bytes 294920 | tf_op jit(solution)/shard_map/ppermute | solution.py:1048
  579.5 5.3 collective-permute-start.42
  (33 other events, 84.0 us)
Sparse Core Ops, SparseCore 0:
  11.6 122.4 all-gather.6
  136.4 74.7 all-gather.8
  266.3 106.6 reduce-scatter.4
  378.7 50.5 all-gather.10
  431.4 43.3 reduce-scatter.10
  480.1 68.2 reduce-scatter.8
  551.9 25.7 reduce-scatter.6

commit v4 on v3

--- a/solution.py
+++ b/solution.py
@@ -445,7 +445,7 @@
 
 def attention_forward_kernel(layer, count, place, a_ref, wqkv, wproj, bqv, *refs):
     pieces = refs[:count] if count > 1 else (refs[0], ATTN_SPAN)
-    qkv_ref, o_ref, r_ref, wq, wp, bs, rows, total, masks, sems = refs[count:]
+    qkv_ref, probs_ref, o_ref, r_ref, wq, wp, bs, rows, total, masks, sems = refs[count:]
     own_quarter = place[DEPTH] if count > 1 else None
     copy = start_rows(a_ref, rows, sems)
     start_attention_copies(layer, place, wqkv, wproj, bqv, pieces, wq, wp, sems, bs)
@@ -466,13 +466,14 @@
             probs = window_probs(
                 query, qkv_ref[chunk, span, 128:256], masks[window], window_rows_ok(window)
             )
+            probs_ref[chunk, window] = probs.astype(BF16)
             mixed = dot_nn(probs.astype(BF16), qkv_ref[chunk, span, 256:384])
             outs.append(jnp.where(first, mixed[:WIN], mixed[WIN:]))
         o_ref[chunk] = join_windows(outs).astype(BF16)
         add_part(chunk, total, dot_nn(o_ref[chunk], wp[chunk]))
         return carry
 
-    lax.fori_loop(0, 4, chunk_step, 0)
+    lax.fori_loop(0, 4, chunk_step, 0, unroll=True)
     r_ref[...] = total[...].astype(BF16)
 
 
@@ -492,11 +493,12 @@
         functools.partial(attention_forward_kernel, layer, len(pieces)),
         out_shape=(
             jax.ShapeDtypeStruct((4, ROWS, 384), BF16),
+            jax.ShapeDtypeStruct((4, 3, 2 * WIN, WIN), BF16),
             jax.ShapeDtypeStruct((4, ROWS, 128), BF16),
             jax.ShapeDtypeStruct((ROWS, width), BF16),
         ),
         in_specs=[SM, HB, HB, HB, VM] + [HB] * len(pieces),
-        out_specs=(VM,) * 3,
+        out_specs=(VM,) * 4,
         scratch_shapes=[
             pltpu.VMEM((4, width, 384), BF16),
             pltpu.VMEM((4, 128, width), BF16),
@@ -510,13 +512,13 @@
     )(place, rows, *weights, *pieces)
 
 
-def attention_backward_kernel(layer, count, place, g_ref, qkv_ref, wqkv, wproj, *refs):
+def attention_backward_kernel(
+    layer, count, place, g_ref, qkv_ref, probs_ref, wqkv, wproj, *refs
+):
     pieces = refs[:count] if count > 1 else (refs[0], ATTN_SPAN)
-    dqkv_ref, sums_ref, d_ref, wq, wp, rows, total, masks, gmix, sems = refs[count:]
+    dqkv_ref, sums_ref, d_ref, wq, wp, rows, total, gmix, sems = refs[count:]
     copy = start_rows(g_ref, rows, sems)
     start_attention_copies(layer, place, wqkv, wproj, None, pieces, wq, wp, sems)
-    for window in range(3):
-        masks[window] = window_masks(window)
     copy.wait()
 
     def chunk_step(chunk, carry):
@@ -530,9 +532,10 @@
             query = stack_heads(qkv_ref[chunk, span, 0:128], first)
             key = qkv_ref[chunk, span, 128:256]
             grad = stack_heads(gmix[span, :], first)
-            probs = window_probs(query, key, masks[window], window_rows_ok(window))
+            probs = probs_ref[chunk, window]
             gprobs = dot_nt(grad, qkv_ref[chunk, span, 256:384])
-            gvalue = dot_tn(probs.astype(BF16), grad)
+            gvalue = dot_tn(probs, grad)
+            probs = probs.astype(F32)
             inner = jnp.sum(gprobs * probs, axis=-1, keepdims=True)
             gscores = (probs * (gprobs - inner)).astype(BF16)
             gquery = dot_nn(gscores, key) * scale
@@ -548,11 +551,11 @@
         add_part(chunk, total, dot_nt(dqkv_ref[chunk], wq[chunk]))
         return carry
 
-    lax.fori_loop(0, 4, chunk_step, 0)
+    lax.fori_loop(0, 4, chunk_step, 0, unroll=True)
     d_ref[...] = total[...].astype(BF16)
 
 
-def run_attention_backward(layer, place, grad, qkv, weights, pieces):
+def run_attention_backward(layer, place, grad, qkv, probs, weights, pieces):
     width = grad.shape[1]
     return pl.pallas_call(
         functools.partial(attention_backward_kernel, layer, len(pieces)),
@@ -561,19 +564,18 @@
             jax.ShapeDtypeStruct((4, 8, 384), F32),
             jax.ShapeDtypeStruct((ROWS, width), BF16),
         ),
-        in_specs=[SM, HB, VM, HB, HB] + [HB] * len(pieces),
+        in_specs=[SM, HB, VM, VM, HB, HB] + [HB] * len(pieces),
         out_specs=(VM,) * 3,
         scratch_shapes=[
             pltpu.VMEM((4, width, 384), BF16),
             pltpu.VMEM((4, 128, width), BF16),
             pltpu.VMEM((ROWS, width), BF16),
             pltpu.VMEM((ROWS, width), F32),
-            pltpu.VMEM((3, 2 * WIN, WIN), F32),
             pltpu.VMEM((ROWS, 128), BF16),
             pltpu.SemaphoreType.DMA((4, 4)),
         ],
         **params(12),
-    )(place, grad, qkv, *weights[:2], *pieces)
+    )(place, grad, qkv, probs, *weights[:2], *pieces)
 
 
 def gelu_pair(u):
@@ -606,7 +608,7 @@
         add_part(chunk, total, dot_nn(h_ref[chunk], w2[chunk]))
         return carry
 
-    lax.fori_loop(0, 4, chunk_step, 0)
+    lax.fori_loop(0, 4, chunk_step, 0, unroll=True)
     m_ref[...] = total[...].astype(BF16)
 
 
@@ -651,7 +653,7 @@
         add_part(chunk, total, dot_nt(du_ref[chunk], w1[chunk]))
         return carry
 
-    lax.fori_loop(0, 4, chunk_step, 0)
+    lax.fori_loop(0, 4, chunk_step, 0, unroll=True)
     d_ref[...] = total[...].astype(BF16)
 
 
@@ -743,7 +745,7 @@
             out[chunk, :, span1:] = second.astype(BF16)
         return carry
 
-    lax.fori_loop(0, 4, chunk_step, 0)
+    lax.fori_loop(0, 4, chunk_step, 0, unroll=True)
 
 
 def run_weight_grad(stage, place, x1, y1, x2, y2, *got):
@@ -944,7 +946,7 @@
     saved = []
     for layer in range(layers):
         normed_far = swap(normed, "x")
-        qkv, mixed, part = both(
+        qkv, probs, mixed, part = both(
             lambda rows: run_attention_forward(layer, here, rows, attn_weights, attn_pieces[layer]),
             normed, normed_far,
         )
@@ -958,7 +960,7 @@
             after(normed2, grad_b_far), normed2_far,
         )
         saved.append(
-            (stream, (normed, normed_far), qkv, mixed, middle, (normed2, normed2_far), active, slope)
+            (stream, (normed, normed_far), list(zip(qkv, probs)), mixed, middle, (normed2, normed2_far), active, slope)
         )
         if layer + 1 < layers:
             stream, normed = run_residual_norm(
@@ -1012,7 +1014,7 @@
         grad_b_far = swap(grad_b, "x")
         dqkv, qv_sum, part = both(
             lambda rows: run_attention_backward(
-                layer, here, rows, qkvs.pop(0), attn_weights, attn_pieces[layer]
+                layer, here, rows, *qkvs.pop(0), attn_weights, attn_pieces[layer]
             ),
             grad_b, grad_b_far, *([] if layer else [mlp.away()]),
         )
@@ -1031,7 +1033,7 @@
     parts = [shift(grad_b, step) for step in (1, 3, 2)]
     attn.core = after(attn.core, grad_b)
     attn.away()
-    kept = mlp.near(parts[0])
+    kept = mlp.near()
     kept = attn.near(kept, block_out, *parts)
     parts = [after(part, kept) for part in parts]
     input_grad = run_leave(here, [grad_b, *parts], seq, mine, F32)

time: 601 us -> 597 us (level); the launches traced: 596 us -> 586 us
  Pallas kernels: 328 us -> 307 us
  waiting for transfers between devices: 179 us -> 192 us
    pallas_call x4, Pallas kernels: 55.7 us -> 46.6 us  [run_attention_backward(): pl.pallas_call(functools.partial(attention_backward_kernel, layer, len(pi...]
    ppermute x38, waiting for transfers between devices: 73.4 us -> 79.7 us  [swap(): return lax.ppermute(value, axis, [(0, 1), (1, 0)])]
  transfers between devices with their start and end apart: 53 -> 53, of which waited for: 21 -> 24; matrix products, arithmetic and copies ran while one was open for 1% -> 1% of each run, Pallas kernels for 52% -> 50%
where the time goes in v4:
time: 597 us; the launch traced here: 586 us
  Pallas kernels  307 us (51%)
  waiting for transfers between devices  192 us (32%)
  starting transfers between devices  50.4 us (8%)
  local copies, waits for them, and re-layouts  20 us (3%)
  between operations  15.1 us (3%)
    pallas_call x10, Pallas kernels, run_weight_grad(): pl.pallas_call(functools.partial(weight_grad_kernel, stage), out_shape=ja...  82.2 us
    ppermute x38, waiting for transfers between devices, swap(): return lax.ppermute(value, axis, [(0, 1), (1, 0)])  79.7 us
    ppermute x6, waiting for transfers between devices, shift(): lax.ppermute(value, 'mp', [(index, (index + step) % n_mp) for index in ra...  59.9 us
    pallas_call x4, Pallas kernels, run_attention_backward(): pl.pallas_call(functools.partial(attention_backward_kernel, layer, len(pi...  46.6 us
    ppermute x38, starting transfers between devices, swap(): return lax.ppermute(value, axis, [(0, 1), (1, 0)])  36.4 us
    pallas_call x4, Pallas kernels, run_attention_forward(): pl.pallas_call(functools.partial(attention_forward_kernel, layer, len(pie...  34.3 us
    pallas_call x4, Pallas kernels, run_mlp_forward(): pl.pallas_call(mlp_forward_kernel, out_shape=(jax.ShapeDtypeStruct((4, RO...  33.9 us
    reduce_scatter x3, waiting for transfers between devices, near(): self.total = lax.psum_scatter(flat, 'mp', tiled=True)  32 us
  transfers between devices with their start and end apart: 53, of which 24 were waited for; matrix products, arithmetic and copies ran while one was open for 1% of the time, Pallas kernels for 50%

profile of v4, /device:TPU:0, one launch (start us, length us, event | category | flops | bytes accessed | tf_op | source)
XLA Modules:
  0.0 585.6 jit_solution(13675469608598544860)
XLA Ops:
  7.9 3.6 shard_map.246
  11.5 3.1 collective-permute-start
  14.6 2.6 collective-permute-start.4
  19.8 4.7 collective-permute-done.refs_0_
  26.2 4.0 shard_map.245
  31.9 16.3 %collective-permute-done.4.refs_4_ = bf16[272,512]{1,0:T(8,128)(2,1)S(1)} collective-permute-done((bf16[272,512]{1,0:T(8,128)(2,1)}, bf16[272,512]{1,0:T(8,128)(2,1)S(1)}, u32[]{:S(2)}, u32[]{:S(2)}) %collective-permute-start.4) | collective-permute-done | bytes 278560 | tf_op jit(solution)/shard_map/ppermute | solution.py:913
  50.3 4.0 shard_map.250
  54.5 3.2 collective-permute-done.5.refs_5_
  58.3 4.3 collective-permute-done.9.refs_9_
  66.4 9.0 %shard_map.248 = (bf16[4,304,384]{2,1,0:T(8,128)(2,1)}, bf16[4,3,224,112]{3,2,1,0:T(8,128)(2,1)}, bf16[4,304,128]{2,1,0:T(8,128)(2,1)}, bf16[304,1024]{1,0:T(8,128)(2,1)}) custom-call(s32[8]{0:T(128)} %stack.35.place, bf16[304,1024]{1,0:T(8,128)(2,1)} %copy-done.11, bf16[2,3,1024,256]{3,2,1,0:T(8,128)(2,1)} %bitcast.46, bf16[2,256,1024]{2,1,0:T(8,128)(2,1)} %wproj.17, ...), custom_call_target="tpu_custom_call" | custom-call | flops 28000000000 | tf_op jit(solution)/shard_map/pallas_call | solution.py:492
  76.1 9.0 %shard_map.247 = (bf16[4,304,384]{2,1,0:T(8,128)(2,1)}, bf16[4,3,224,112]{3,2,1,0:T(8,128)(2,1)}, bf16[4,304,128]{2,1,0:T(8,128)(2,1)}, bf16[304,1024]{1,0:T(8,128)(2,1)}) custom-call(s32[8]{0:T(128)} %stack.35.place, bf16[304,1024]{1,0:T(8,128)(2,1)} %get-tuple-element.126.a_ref.x1_own, bf16[2,3,1024,256]{3,2,1,0:T(8,128)(2,1)} %bitcast.47, ...), custom_call_target="tpu_custom_call" | custom-call | flops 28000000000 | tf_op jit(solution)/shard_map/pallas_call | solution.py:492
  85.1 8.7 %collective-permute-done.13.far_ref = bf16[304,1024]{1,0:T(8,128)(2,1)S(1)} collective-permute-done((bf16[304,1024]{1,0:T(8,128)(2,1)}, bf16[304,1024]{1,0:T(8,128)(2,1)S(1)}, u32[]{:S(2)}, u32[]{:S(2)}) %collective-permute-start.13) | collective-permute-done | bytes 622624 | tf_op jit(solution)/shard_map/ppermute | solution.py:910
  94.7 4.1 shard_map.249
  100.9 13.8 %collective-permute-done.15.a_ref.x1_far = bf16[304,1024]{1,0:T(8,128)(2,1)S(1)} collective-permute-done((bf16[304,1024]{1,0:T(8,128)(2,1)}, bf16[304,1024]{1,0:T(8,128)(2,1)S(1)}, u32[]{:S(2)}, u32[]{:S(2)}) %collective-permute-start.15) | collective-permute-done | bytes 622624 | tf_op jit(solution)/shard_map/ppermute | solution.py:910
  114.7 19.4 %all-gather.7.cloned.1.call-done = bf16[12800,512]{1,0:T(8,128)(2,1)} async-done(((bf16[800,512]{1,0:T(8,128)(2,1)}), bf16[12800,512]{1,0:T(8,128)(2,1)}) %all-gather.7.cloned.1.call-update) | async-done | bytes 13107216 | tf_op jit(solution)/shard_map/all_gather | solution.py:936
  134.1 8.7 %shard_map.252 = (bf16[4,304,512]{2,1,0:T(8,128)(2,1)}, bf16[4,304,512]{2,1,0:T(8,128)(2,1)}, bf16[304,1024]{1,0:T(8,128)(2,1)}) custom-call(bf16[304,1024]{1,0:T(8,128)(2,1)} %copy-done.12, bf16[2,2,4,800,512]{4,3,2,1,0:T(8,128)(2,1)} %bitcast.33), custom_call_target="tpu_custom_call" | custom-call | flops 32000000000 | tf_op jit(solution)/shard_map/pallas_call | solution.py:617
  144.4 8.4 %shard_map.251 = (bf16[4,304,512]{2,1,0:T(8,128)(2,1)}, bf16[4,304,512]{2,1,0:T(8,128)(2,1)}, bf16[304,1024]{1,0:T(8,128)(2,1)}) custom-call(bf16[304,1024]{1,0:T(8,128)(2,1)} %get-tuple-element.133.a_ref.x1_own, bf16[2,2,4,800,512]{4,3,2,1,0:T(8,128)(2,1)} %bitcast.34), custom_call_target="tpu_custom_call" | custom-call | flops 32000000000 | tf_op jit(solution)/shard_map/pallas_call | solution.py:617
  152.8 6.5 %collective-permute-done.16.far_ref = bf16[304,1024]{1,0:T(8,128)(2,1)S(1)} collective-permute-done((bf16[304,1024]{1,0:T(8,128)(2,1)}, bf16[304,1024]{1,0:T(8,128)(2,1)S(1)}, u32[]{:S(2)}, u32[]{:S(2)}) %collective-permute-start.16) | collective-permute-done | bytes 622624 | tf_op jit(solution)/shard_map/ppermute | solution.py:910
  160.1 4.1 shard_map.253
  165.8 14.2 %collective-permute-done.17.a_ref.x1_far = bf16[304,1024]{1,0:T(8,128)(2,1)S(1)} collective-permute-done((bf16[304,1024]{1,0:T(8,128)(2,1)}, bf16[304,1024]{1,0:T(8,128)(2,1)S(1)}, u32[]{:S(2)}, u32[]{:S(2)}) %collective-permute-start.17) | collective-permute-done | bytes 622624 | tf_op jit(solution)/shard_map/ppermute | solution.py:910
  180.8 8.0 %shard_map.255 = (bf16[4,304,384]{2,1,0:T(8,128)(2,1)}, bf16[4,3,224,112]{3,2,1,0:T(8,128)(2,1)}, bf16[4,304,128]{2,1,0:T(8,128)(2,1)}, bf16[304,1024]{1,0:T(8,128)(2,1)}) custom-call(s32[8]{0:T(128)} %stack.35.place, bf16[304,1024]{1,0:T(8,128)(2,1)} %copy-done.13, bf16[2,3,1024,256]{3,2,1,0:T(8,128)(2,1)} %bitcast.48, bf16[2,256,1024]{2,1,0:T(8,128)(2,1)} %wproj.17, ...), custom_call_target="tpu_custom_call" | custom-call | flops 28000000000 | tf_op jit(solution)/shard_map/pallas_call | solution.py:492
  190.4 8.2 %shard_map.254 = (bf16[4,304,384]{2,1,0:T(8,128)(2,1)}, bf16[4,3,224,112]{3,2,1,0:T(8,128)(2,1)}, bf16[4,304,128]{2,1,0:T(8,128)(2,1)}, bf16[304,1024]{1,0:T(8,128)(2,1)}) custom-call(s32[8]{0:T(128)} %stack.35.place, bf16[304,1024]{1,0:T(8,128)(2,1)} %get-tuple-element.138.a_ref.x1_own, bf16[2,3,1024,256]{3,2,1,0:T(8,128)(2,1)} %bitcast.49, ...), custom_call_target="tpu_custom_call" | custom-call | flops 28000000000 | tf_op jit(solution)/shard_map/pallas_call | solution.py:492
  198.6 5.2 collective-permute-done.18.far_ref
  204.6 4.2 shard_map.256
  211.0 8.4 %shard_map.257 = (bf16[4,304,512]{2,1,0:T(8,128)(2,1)}, bf16[4,304,512]{2,1,0:T(8,128)(2,1)}, bf16[304,1024]{1,0:T(8,128)(2,1)}) custom-call(bf16[304,1024]{1,0:T(8,128)(2,1)} %get-tuple-element.143.a_ref.x1_own, bf16[2,2,4,528,512]{4,3,2,1,0:T(8,128)(2,1)} %bitcast.41), custom_call_target="tpu_custom_call" | custom-call | flops 32000000000 | tf_op jit(solution)/shard_map/pallas_call | solution.py:617
  219.5 7.5 %shard_map.260 = (bf16[4,304,512]{2,1,0:T(8,128)(2,1)}, f32[4,8,512]{2,1,0:T(8,128)}, bf16[304,1024]{1,0:T(8,128)(2,1)}) custom-call(bf16[304,1024]{1,0:T(8,128)(2,1)} %get-tuple-element.132.g_ref.x2_own, bf16[4,304,512]{2,1,0:T(8,128)(2,1)} %get-tuple-element.148.slope_ref, bf16[2,2,4,528,512]{4,3,2,1,0:T(8,128)(2,1)} %bitcast.42), custom_call_target="tpu_custom_call" | custom-call | flops 28000000000 | tf_op jit(solution)/shard_map/pallas_call | solution.py:662
  227.8 8.4 %shard_map.258 = (bf16[4,304,512]{2,1,0:T(8,128)(2,1)}, bf16[4,304,512]{2,1,0:T(8,128)(2,1)}, bf16[304,1024]{1,0:T(8,128)(2,1)}) custom-call(bf16[304,1024]{1,0:T(8,128)(2,1)} %copy-done.21, bf16[2,2,4,528,512]{4,3,2,1,0:T(8,128)(2,1)} %bitcast.43), custom_call_target="tpu_custom_call" | custom-call | flops 32000000000 | tf_op jit(solution)/shard_map/pallas_call | solution.py:617
  237.8 7.5 %shard_map.261 = (bf16[4,304,512]{2,1,0:T(8,128)(2,1)}, f32[4,8,512]{2,1,0:T(8,128)}, bf16[304,1024]{1,0:T(8,128)(2,1)}) custom-call(bf16[304,1024]{1,0:T(8,128)(2,1)} %copy-done.19, bf16[4,304,512]{2,1,0:T(8,128)(2,1)} %get-tuple-element.150.slope_ref, bf16[2,2,4,528,512]{4,3,2,1,0:T(8,128)(2,1)} %bitcast.44), custom_call_target="tpu_custom_call" | custom-call | flops 28000000000 | tf_op jit(solution)/shard_map/pallas_call | solution.py:662
  245.9 15.1 %shard_map.262 = bf16[4,4,256,1024]{3,2,1,0:T(8,128)(2,1)} custom-call(s32[8]{0:T(128)} %stack.35.place, bf16[304,1024]{1,0:T(8,128)(2,1)} %get-tuple-element.143.a_ref.x1_own, bf16[304,1024]{1,0:T(8,128)(2,1)} %copy-done.21, bf16[4,304,512]{2,1,0:T(8,128)(2,1)} %get-tuple-element.149.y1_own, bf16[4,304,512]{2,1,0:T(8,128)(2,1)} %get-tuple-element.151.y1_far, ...), custom_call_target="tpu_custom_call" | custom-call | flops 71999995904 | tf_op jit(solution)/shard_map/pallas_call | solution.py:757
  261.5 4.6 collective-permute-done.21.far_ref
  266.9 5.4 shard_map.264
  273.7 11.4 %shard_map.265 = (bf16[4,304,384]{2,1,0:T(8,128)(2,1)}, f32[4,8,384]{2,1,0:T(8,128)}, bf16[304,1024]{1,0:T(8,128)(2,1)}) custom-call(s32[8]{0:T(128)} %stack.35.place, bf16[304,1024]{1,0:T(8,128)(2,1)} %get-tuple-element.159.g_ref.x2_own, bf16[4,304,384]{2,1,0:T(8,128)(2,1)} %get-tuple-element.160.qkv_ref, ...), custom_call_target="tpu_custom_call" | custom-call | flops 48000000000 | tf_op jit(solution)/shard_map/pallas_call | solution.py:560
  285.1 3.6 shard_map.259
  289.6 11.1 %shard_map.266 = (bf16[4,304,384]{2,1,0:T(8,128)(2,1)}, f32[4,8,384]{2,1,0:T(8,128)}, bf16[304,1024]{1,0:T(8,128)(2,1)}) custom-call(s32[8]{0:T(128)} %stack.35.place, bf16[304,1024]{1,0:T(8,128)(2,1)} %copy-done.20, bf16[4,304,384]{2,1,0:T(8,128)(2,1)} %get-tuple-element.163.qkv_ref, bf16[4,3,224,112]{3,2,1,0:T(8,128)(2,1)} %get-tuple-element.164.probs_ref, ...), custom_call_target="tpu_custom_call" | custom-call | flops 48000000000 | tf_op jit(solution)/shard_map/pallas_call | solution.py:560
  301.6 8.2 %shard_map.269 = bf16[2,4,256,512]{3,2,1,0:T(8,128)(2,1)} custom-call(s32[8]{0:T(128)} %stack.35.place, bf16[304,1024]{1,0:T(8,128)(2,1)} %get-tuple-element.138.a_ref.x1_own, bf16[304,1024]{1,0:T(8,128)(2,1)} %copy-done.13, bf16[4,304,384]{2,1,0:T(8,128)(2,1)} %get-tuple-element.170.y1_own, bf16[4,304,384]{2,1,0:T(8,128)(2,1)} %get-tuple-element.171.y1_far, ...), custom_call_target="tpu_custom_call" | custom-call | flops 32000000000 | tf_op jit(solution)/shard_map/pallas_call | solution.py:757
  309.9 6.6 %collective-permute-done.23.far_ref = bf16[304,1024]{1,0:T(8,128)(2,1)S(1)} collective-permute-done((bf16[304,1024]{1,0:T(8,128)(2,1)}, bf16[304,1024]{1,0:T(8,128)(2,1)S(1)}, u32[]{:S(2)}, u32[]{:S(2)}) %collective-permute-start.23) | collective-permute-done | bytes 622624 | tf_op jit(solution)/shard_map/ppermute | solution.py:910
  317.3 5.0 shard_map.267
  322.6 7.5 %shard_map.268 = (bf16[4,304,512]{2,1,0:T(8,128)(2,1)}, f32[4,8,512]{2,1,0:T(8,128)}, bf16[304,1024]{1,0:T(8,128)(2,1)}) custom-call(bf16[304,1024]{1,0:T(8,128)(2,1)} %get-tuple-element.167.g_ref.x2_own, bf16[4,304,512]{2,1,0:T(8,128)(2,1)} %get-tuple-element.168.slope_ref, bf16[2,2,4,800,512]{4,3,2,1,0:T(8,128)(2,1)} %bitcast.39), custom_call_target="tpu_custom_call" | custom-call | flops 28000000000 | tf_op jit(solution)/shard_map/pallas_call | solution.py:662
  331.5 6.3 %shard_map.270 = bf16[4,256,512]{2,1,0:T(8,128)(2,1)} custom-call(s32[8]{0:T(128)} %stack.35.place, bf16[304,1024]{1,0:T(8,128)(2,1)} %get-tuple-element.138.a_ref.x1_own, bf16[304,1024]{1,0:T(8,128)(2,1)} %copy-done.13, bf16[4,304,384]{2,1,0:T(8,128)(2,1)} %get-tuple-element.170.y1_own, bf16[4,304,384]{2,1,0:T(8,128)(2,1)} %get-tuple-element.171.y1_far, ...), custom_call_target="tpu_custom_call" | custom-call | flops 20000000000 | tf_op jit(solution)/shard_map/pallas_call | solution.py:757
  339.0 7.5 %shard_map.271 = (bf16[4,304,512]{2,1,0:T(8,128)(2,1)}, f32[4,8,512]{2,1,0:T(8,128)}, bf16[304,1024]{1,0:T(8,128)(2,1)}) custom-call(bf16[304,1024]{1,0:T(8,128)(2,1)} %copy-done.14, bf16[4,304,512]{2,1,0:T(8,128)(2,1)} %get-tuple-element.175.slope_ref, bf16[2,2,4,800,512]{4,3,2,1,0:T(8,128)(2,1)} %bitcast.40), custom_call_target="tpu_custom_call" | custom-call | flops 28000000000 | tf_op jit(solution)/shard_map/pallas_call | solution.py:662
  348.1 10.0 %shard_map.275 = bf16[2,4,256,1024]{3,2,1,0:T(8,128)(2,1)} custom-call(s32[8]{0:T(128)} %stack.35.place, bf16[304,1024]{1,0:T(8,128)(2,1)} %get-tuple-element.133.a_ref.x1_own, bf16[304,1024]{1,0:T(8,128)(2,1)} %copy-done.12, bf16[4,304,512]{2,1,0:T(8,128)(2,1)} %get-tuple-element.183.y1_own, bf16[4,304,512]{2,1,0:T(8,128)(2,1)} %get-tuple-element.184.y1_far, ...), custom_call_target="tpu_custom_call" | custom-call | flops 40000000000 | tf_op jit(solution)/shard_map/pallas_call | solution.py:757
  358.2 2.7 collective-permute-done.26.far_ref
  361.8 5.0 shard_map.272
  369.0 12.0 %shard_map.274 = (bf16[4,304,384]{2,1,0:T(8,128)(2,1)}, f32[4,8,384]{2,1,0:T(8,128)}, bf16[304,1024]{1,0:T(8,128)(2,1)}) custom-call(s32[8]{0:T(128)} %stack.35.place, bf16[304,1024]{1,0:T(8,128)(2,1)} %get-tuple-element.179.g_ref.x2_own, bf16[4,304,384]{2,1,0:T(8,128)(2,1)} %get-tuple-element.180.qkv_ref, ...), custom_call_target="tpu_custom_call" | custom-call | flops 48000000000 | tf_op jit(solution)/shard_map/pallas_call | solution.py:560
  382.0 6.4 %shard_map.273 = bf16[4,256,512]{2,1,0:T(8,128)(2,1)} custom-call(s32[8]{0:T(128)} %stack.35.place, bf16[304,1024]{1,0:T(8,128)(2,1)} %get-tuple-element.138.a_ref.x1_own, bf16[304,1024]{1,0:T(8,128)(2,1)} %copy-done.13, bf16[4,304,384]{2,1,0:T(8,128)(2,1)} %get-tuple-element.170.y1_own, bf16[4,304,384]{2,1,0:T(8,128)(2,1)} %get-tuple-element.171.y1_far, ...), custom_call_target="tpu_custom_call" | custom-call | flops 20000000000 | tf_op jit(solution)/shard_map/pallas_call | solution.py:757
  389.0 7.5 %shard_map.276 = bf16[4,256,1024]{2,1,0:T(8,128)(2,1)} custom-call(s32[8]{0:T(128)} %stack.35.place, bf16[304,1024]{1,0:T(8,128)(2,1)} %get-tuple-element.133.a_ref.x1_own, bf16[304,1024]{1,0:T(8,128)(2,1)} %copy-done.12, bf16[4,304,512]{2,1,0:T(8,128)(2,1)} %get-tuple-element.183.y1_own, bf16[4,304,512]{2,1,0:T(8,128)(2,1)} %get-tuple-element.184.y1_far, ...), custom_call_target="tpu_custom_call" | custom-call | flops 24000000000 | tf_op jit(solution)/shard_map/pallas_call | solution.py:757
  398.8 12.0 %shard_map.277 = (bf16[4,304,384]{2,1,0:T(8,128)(2,1)}, f32[4,8,384]{2,1,0:T(8,128)}, bf16[304,1024]{1,0:T(8,128)(2,1)}) custom-call(s32[8]{0:T(128)} %stack.35.place, bf16[304,1024]{1,0:T(8,128)(2,1)} %copy-done.15, bf16[4,304,384]{2,1,0:T(8,128)(2,1)} %get-tuple-element.188.qkv_ref, bf16[4,3,224,112]{3,2,1,0:T(8,128)(2,1)} %get-tuple-element.189.probs_ref, ...), custom_call_target="tpu_custom_call" | custom-call | flops 48000000000 | tf_op jit(solution)/shard_map/pallas_call | solution.py:560
  411.6 8.1 %shard_map.279 = bf16[2,4,256,512]{3,2,1,0:T(8,128)(2,1)} custom-call(s32[8]{0:T(128)} %stack.35.place, bf16[304,1024]{1,0:T(8,128)(2,1)} %get-tuple-element.126.a_ref.x1_own, bf16[304,1024]{1,0:T(8,128)(2,1)} %copy-done.11, bf16[4,304,384]{2,1,0:T(8,128)(2,1)} %get-tuple-element.192.y1_own, bf16[4,304,384]{2,1,0:T(8,128)(2,1)} %get-tuple-element.193.y1_far, ...), custom_call_target="tpu_custom_call" | custom-call | flops 32000000000 | tf_op jit(solution)/shard_map/pallas_call | solution.py:757
  419.7 5.2 collective-permute-done.30.far_ref
  425.8 5.0 shard_map.278
  430.8 3.8 collective-permute-start.35
  437.8 6.3 %shard_map.280 = bf16[4,256,512]{2,1,0:T(8,128)(2,1)} custom-call(s32[8]{0:T(128)} %stack.35.place, bf16[304,1024]{1,0:T(8,128)(2,1)} %get-tuple-element.126.a_ref.x1_own, bf16[304,1024]{1,0:T(8,128)(2,1)} %copy-done.11, bf16[4,304,384]{2,1,0:T(8,128)(2,1)} %get-tuple-element.192.y1_own, bf16[4,304,384]{2,1,0:T(8,128)(2,1)} %get-tuple-element.193.y1_far, ...), custom_call_target="tpu_custom_call" | custom-call | flops 20000000000 | tf_op jit(solution)/shard_map/pallas_call | solution.py:757
  445.6 7.9 %shard_map.281 = bf16[4,256,1024]{2,1,0:T(8,128)(2,1)} custom-call(s32[8]{0:T(128)} %stack.35.place, bf16[304,1024]{1,0:T(8,128)(2,1)} %get-tuple-element.133.a_ref.x1_own, bf16[304,1024]{1,0:T(8,128)(2,1)} %copy-done.12, bf16[4,304,512]{2,1,0:T(8,128)(2,1)} %get-tuple-element.183.y1_own, bf16[4,304,512]{2,1,0:T(8,128)(2,1)} %get-tuple-element.184.y1_far, ...), custom_call_target="tpu_custom_call" | custom-call | flops 24000000000 | tf_op jit(solution)/shard_map/pallas_call | solution.py:757
  453.8 8.9 %shard_map.263 = bf16[1200,1024]{1,0:T(8,128)(2,1)} custom-call(s32[8]{0:T(128)} %stack.35.place, bf16[4,304,1024]{2,1,0:T(8,128)(2,1)} %bitcast.54), custom_call_target="tpu_custom_call" | custom-call | flops 35999997952 | tf_op jit(solution)/shard_map/pallas_call | solution.py:180
  463.0 10.9 %collective-permute-done.35.refs_2_ = bf16[304,1024]{1,0:T(8,128)(2,1)S(1)} collective-permute-done((bf16[304,1024]{1,0:T(8,128)(2,1)}, bf16[304,1024]{1,0:T(8,128)(2,1)S(1)}, u32[]{:S(2)}, u32[]{:S(2)}) %collective-permute-start.35) | collective-permute-done | bytes 622624 | tf_op jit(solution)/shard_map/ppermute | solution.py:913
  473.9 27.7 %collective-permute-done.36.refs_3_ = bf16[304,1024]{1,0:T(8,128)(2,1)S(1)} collective-permute-done((bf16[304,1024]{1,0:T(8,128)(2,1)}, bf16[304,1024]{1,0:T(8,128)(2,1)S(1)}, u32[]{:S(2)}, u32[]{:S(2)}) %collective-permute-start.36) | collective-permute-done | bytes 622624 | tf_op jit(solution)/shard_map/ppermute | solution.py:913
  502.6 6.4 %shard_map.282 = bf16[4,256,512]{2,1,0:T(8,128)(2,1)} custom-call(s32[8]{0:T(128)} %stack.35.place, bf16[304,1024]{1,0:T(8,128)(2,1)} %get-tuple-element.126.a_ref.x1_own, bf16[304,1024]{1,0:T(8,128)(2,1)} %copy-done.11, bf16[4,304,384]{2,1,0:T(8,128)(2,1)} %get-tuple-element.192.y1_own, bf16[4,304,384]{2,1,0:T(8,128)(2,1)} %get-tuple-element.193.y1_far, ...), custom_call_target="tpu_custom_call" | custom-call | flops 20000000000 | tf_op jit(solution)/shard_map/pallas_call | solution.py:757
  516.9 1.9 shard_map.289
  520.4 18.0 %reduce-scatter.9.cloned.1.call-done.refs_0_ = bf16[256,1024]{1,0:T(8,128)(2,1)} async-done(((bf16[1024,1024]{1,0:T(8,128)(2,1)}), bf16[256,1024]{1,0:T(8,128)(2,1)}) %reduce-scatter.9.cloned.1.call-update) | async-done | bytes 524304 | tf_op jit(solution)/shard_map/reduce_scatter | solution.py:987
  538.4 1.9 shard_map.287
  543.6 9.5 %shard_map.283 = f32[1200,1024]{1,0:T(8,128)} custom-call(s32[8]{0:T(128)} %stack.35.place, bf16[304,1024]{1,0:T(8,128)(2,1)} %get-tuple-element.191.refs_0_, bf16[304,1024]{1,0:T(8,128)(2,1)} %copy-done.16, bf16[304,1024]{1,0:T(8,128)(2,1)} %copy-done.17, bf16[304,1024]{1,0:T(8,128)(2,1)} %copy-done.18), custom_call_target="tpu_custom_call" | custom-call | flops 35999997952 | tf_op jit(solution)/shard_map/pallas_call | solution.py:180
  553.8 13.9 %reduce-scatter.7.cloned.1.call-done.refs_0_ = bf16[256,512]{1,0:T(8,128)(2,1)} async-done(((bf16[1024,512]{1,0:T(8,128)(2,1)}), bf16[256,512]{1,0:T(8,128)(2,1)}) %reduce-scatter.7.cloned.1.call-update) | async-done | bytes 262160 | tf_op jit(solution)/shard_map/reduce_scatter | solution.py:987
  572.5 2.2 collective-permute-done.42.refs_1_
  575.3 3.3 shard_map.290
  (194 shorter events, 72.3 us)
Async XLA Ops:
  7.2 126.9 %all-gather.7.cloned.1.call-start = ((), (), s32[]{:S(2)}) async-start(), calls=%async_computation.8 | async-start | bytes 13926400 | tf_op jit(solution)/shard_map/all_gather | solution.py:936
  7.9 10.7 %copy-start.1 = (f32[2,1024]{1,0:T(2,128)S(1)}, f32[2,1024]{1,0:T(2,128)}, u32[]{:S(2)}) copy-start(f32[2,1024]{1,0:T(2,128)} %param.16) | copy-start | bytes 24580
  7.9 11.3 %copy-start.2 = (f32[2,1024]{1,0:T(2,128)S(1)}, f32[2,1024]{1,0:T(2,128)}, u32[]{:S(2)}) copy-start(f32[2,1024]{1,0:T(2,128)} %param.17) | copy-start | bytes 24580
  11.5 199.6 %all-gather.9.cloned.1.call-start = ((), (), s32[]{:S(2)}) async-start(), calls=%async_computation.9 | async-start | bytes 9191424 | tf_op jit(solution)/shard_map/all_gather | solution.py:936
  11.5 12.9 %collective-permute-start = (bf16[272,512]{1,0:T(8,128)(2,1)}, bf16[272,512]{1,0:T(8,128)(2,1)S(1)}, u32[]{:S(2)}, u32[]{:S(2)}) collective-permute-start(bf16[272,512]{1,0:T(8,128)(2,1)} %get-tuple-element.127), channel_id=1, source_target_pairs={{0,1},{1,2},{2,3},{3,0},{4,5},{5,6},{6,7},{7,4},{8,9},{9,10},{10,1... | collective-permute-start | bytes 835592 | tf_op jit(solution)/shard_map/ppermute | solution.py:913
  14.6 33.6 %collective-permute-start.4 = (bf16[272,512]{1,0:T(8,128)(2,1)}, bf16[272,512]{1,0:T(8,128)(2,1)S(1)}, u32[]{:S(2)}, u32[]{:S(2)}) collective-permute-start(bf16[272,512]{1,0:T(8,128)(2,1)} %get-tuple-element.127), channel_id=1, source_target_pairs={{0,2},{1,3},{2,0},{3,1},{4,6},{5,7},{6,4},{7,5},{8,10},{9,11},{10,... | collective-permute-start | bytes 835592 | tf_op jit(solution)/shard_map/ppermute | solution.py:913
  17.2 32.5 %collective-permute-start.8 = (bf16[272,512]{1,0:T(8,128)(2,1)}, bf16[272,512]{1,0:T(8,128)(2,1)S(1)}, u32[]{:S(2)}, u32[]{:S(2)}) collective-permute-start(bf16[272,512]{1,0:T(8,128)(2,1)} %get-tuple-element.127), channel_id=1, source_target_pairs={{0,3},{1,0},{2,1},{3,2},{4,7},{5,4},{6,5},{7,6},{8,11},{9,8},{10,9... | collective-permute-start | bytes 835592 | tf_op jit(solution)/shard_map/ppermute | solution.py:913
  24.5 25.2 %collective-permute-start.1 = (bf16[272,512]{1,0:T(8,128)(2,1)S(1)}, bf16[272,512]{1,0:T(8,128)(2,1)S(1)}, u32[]{:S(2)}, u32[]{:S(2)}) collective-permute-start(bf16[272,512]{1,0:T(8,128)(2,1)S(1)} %collective-permute-done.refs_0_), channel_id=1, source_target_pairs={{0,16},{16,0},{1,17},{17,1},{2,18},{18,2},{3,19},{19,3},{4,20},{20... | collective-permute-start | bytes 835592 | tf_op jit(solution)/shard_map/ppermute | solution.py:910
  30.2 35.2 %collective-permute-start.12 = (bf16[304,1024]{1,0:T(8,128)(2,1)}, bf16[304,1024]{1,0:T(8,128)(2,1)S(1)}, u32[]{:S(2)}, u32[]{:S(2)}) collective-permute-start(bf16[304,1024]{1,0:T(8,128)(2,1)} %get-tuple-element.126.a_ref.x1_own), channel_id=1, source_target_pairs={{0,8},{8,0},{1,9},{9,1},{2,10},{10,2},{3,11},{11,3},{4,12},{12,4},... | collective-permute-start | bytes 1867784 | tf_op jit(solution)/shard_map/ppermute | solution.py:910
  31.7 337.2 %reduce-scatter.5.cloned.1.call-start = ((), (), s32[]{:S(2)}) async-start(), calls=%async_computation.4 | async-start | bytes 8912896 | tf_op jit(solution)/shard_map/reduce_scatter | solution.py:997
  31.8 22.5 %collective-permute-start.2 = (bf16[272,512]{1,0:T(8,128)(2,1)S(1)}, bf16[272,512]{1,0:T(8,128)(2,1)S(1)}, u32[]{:S(2)}, u32[]{:S(2)}) collective-permute-start(bf16[272,512]{1,0:T(8,128)(2,1)S(1)} %collective-permute-done.refs_0_), channel_id=1, source_target_pairs={{0,4},{4,0},{1,5},{5,1},{2,6},{6,2},{3,7},{7,3},{8,12},{12,8},{9,1... | collective-permute-start | bytes 835592 | tf_op jit(solution)/shard_map/ppermute | solution.py:910
  48.2 9.5 %collective-permute-start.5 = (bf16[272,512]{1,0:T(8,128)(2,1)S(1)}, bf16[272,512]{1,0:T(8,128)(2,1)S(1)}, u32[]{:S(2)}, u32[]{:S(2)}) collective-permute-start(bf16[272,512]{1,0:T(8,128)(2,1)S(1)} %collective-permute-done.4.refs_4_), channel_id=1, source_target_pairs={{0,16},{16,0},{1,17},{17,1},{2,18},{18,2},{3,19},{19,3},{4,20},{20... | collective-permute-start | bytes 835592 | tf_op jit(solution)/shard_map/ppermute | solution.py:910
  49.7 8.0 %collective-permute-start.6 = (bf16[272,512]{1,0:T(8,128)(2,1)S(1)}, bf16[272,512]{1,0:T(8,128)(2,1)S(1)}, u32[]{:S(2)}, u32[]{:S(2)}) collective-permute-start(bf16[272,512]{1,0:T(8,128)(2,1)S(1)} %collective-permute-done.4.refs_4_), channel_id=1, source_target_pairs={{0,4},{4,0},{1,5},{5,1},{2,6},{6,2},{3,7},{7,3},{8,12},{12,8},{9,1... | collective-permute-start | bytes 835592 | tf_op jit(solution)/shard_map/ppermute | solution.py:910
  49.7 12.8 %collective-permute-start.9 = (bf16[272,512]{1,0:T(8,128)(2,1)S(1)}, bf16[272,512]{1,0:T(8,128)(2,1)S(1)}, u32[]{:S(2)}, u32[]{:S(2)}) collective-permute-start(bf16[272,512]{1,0:T(8,128)(2,1)S(1)} %collective-permute-done.8.refs_8_), channel_id=1, source_target_pairs={{0,16},{16,0},{1,17},{17,1},{2,18},{18,2},{3,19},{19,3},{4,20},{20... | collective-permute-start | bytes 835592 | tf_op jit(solution)/shard_map/ppermute | solution.py:910
  50.3 12.2 %copy-start.3 = (f32[2,1024]{1,0:T(2,128)S(1)}, f32[2,1024]{1,0:T(2,128)}, u32[]{:S(2)}) copy-start(f32[2,1024]{1,0:T(2,128)} %param.22) | copy-start | bytes 24580
  50.3 12.9 %copy-start.5 = (f32[2,1024]{1,0:T(2,128)S(1)}, f32[2,1024]{1,0:T(2,128)}, u32[]{:S(2)}) copy-start(f32[2,1024]{1,0:T(2,128)} %param.23) | copy-start | bytes 24580
  50.3 12.9 %copy-start.6 = (f32[2,1024]{1,0:T(2,128)S(1)}, f32[2,1024]{1,0:T(2,128)}, u32[]{:S(2)}) copy-start(f32[2,1024]{1,0:T(2,128)} %param.21) | copy-start | bytes 24580
  54.3 11.1 %copy-start.33 = (bf16[272,512]{1,0:T(8,128)(2,1)}, bf16[272,512]{1,0:T(8,128)(2,1)S(1)}, u32[]{:S(2)}) copy-start(bf16[272,512]{1,0:T(8,128)(2,1)S(1)} %collective-permute-done.2.refs_2_) | copy-start | bytes 835588
  54.3 9.5 %collective-permute-start.10 = (bf16[272,512]{1,0:T(8,128)(2,1)S(1)}, bf16[272,512]{1,0:T(8,128)(2,1)S(1)}, u32[]{:S(2)}, u32[]{:S(2)}) collective-permute-start(bf16[272,512]{1,0:T(8,128)(2,1)S(1)} %collective-permute-done.8.refs_8_), channel_id=1, source_target_pairs={{0,4},{4,0},{1,5},{5,1},{2,6},{6,2},{3,7},{7,3},{8,12},{12,8},{9,1... | collective-permute-start | bytes 835592 | tf_op jit(solution)/shard_map/ppermute | solution.py:910
  57.7 7.7 %collective-permute-start.3 = (bf16[272,512]{1,0:T(8,128)(2,1)S(1)}, bf16[272,512]{1,0:T(8,128)(2,1)S(1)}, u32[]{:S(2)}, u32[]{:S(2)}) collective-permute-start(bf16[272,512]{1,0:T(8,128)(2,1)S(1)} %collective-permute-done.1.refs_1_), channel_id=1, source_target_pairs={{0,4},{4,0},{1,5},{5,1},{2,6},{6,2},{3,7},{7,3},{8,12},{12,8},{9,1... | collective-permute-start | bytes 835592 | tf_op jit(solution)/shard_map/ppermute | solution.py:910
  57.8 7.6 %collective-permute-start.7 = (bf16[272,512]{1,0:T(8,128)(2,1)S(1)}, bf16[272,512]{1,0:T(8,128)(2,1)S(1)}, u32[]{:S(2)}, u32[]{:S(2)}) collective-permute-start(bf16[272,512]{1,0:T(8,128)(2,1)S(1)} %collective-permute-done.5.refs_5_), channel_id=1, source_target_pairs={{0,4},{4,0},{1,5},{5,1},{2,6},{6,2},{3,7},{7,3},{8,12},{12,8},{9,1... | collective-permute-start | bytes 835592 | tf_op jit(solution)/shard_map/ppermute | solution.py:910
  62.5 2.9 collective-permute-start.11
  63.8 37.1 %collective-permute-start.14 = (bf16[304,1024]{1,0:T(8,128)(2,1)}, bf16[304,1024]{1,0:T(8,128)(2,1)S(1)}, u32[]{:S(2)}, u32[]{:S(2)}) collective-permute-start(bf16[304,1024]{1,0:T(8,128)(2,1)} %get-tuple-element.132.g_ref.x2_own), channel_id=1, source_target_pairs={{0,8},{8,0},{1,9},{9,1},{2,10},{10,2},{3,11},{11,3},{4,12},{12,4},... | collective-permute-start | bytes 1867784 | tf_op jit(solution)/shard_map/ppermute | solution.py:910
  75.5 18.4 %collective-permute-start.13 = (bf16[304,1024]{1,0:T(8,128)(2,1)}, bf16[304,1024]{1,0:T(8,128)(2,1)S(1)}, u32[]{:S(2)}, u32[]{:S(2)}) collective-permute-start(bf16[304,1024]{1,0:T(8,128)(2,1)} %get-tuple-element.129), channel_id=1, source_target_pairs={{0,8},{8,0},{1,9},{9,1},{2,10},{10,2},{3,11},{11,3},{4,12},{12,4},... | collective-permute-start | bytes 1867784 | tf_op jit(solution)/shard_map/ppermute | solution.py:910
  98.7 16.0 %collective-permute-start.15 = (bf16[304,1024]{1,0:T(8,128)(2,1)}, bf16[304,1024]{1,0:T(8,128)(2,1)S(1)}, u32[]{:S(2)}, u32[]{:S(2)}) collective-permute-start(bf16[304,1024]{1,0:T(8,128)(2,1)} %get-tuple-element.133.a_ref.x1_own), channel_id=1, source_target_pairs={{0,8},{8,0},{1,9},{9,1},{2,10},{10,2},{3,11},{11,3},{4,12},{12,4},... | collective-permute-start | bytes 1867784 | tf_op jit(solution)/shard_map/ppermute | solution.py:910
  100.9 41.9 %copy-start.19 = (bf16[304,1024]{1,0:T(8,128)(2,1)}, bf16[304,1024]{1,0:T(8,128)(2,1)S(1)}, u32[]{:S(2)}) copy-start(bf16[304,1024]{1,0:T(8,128)(2,1)S(1)} %collective-permute-done.14.g_ref.x2_far) | copy-start | bytes 1867780
  114.7 19.4 %copy-start.12 = (bf16[304,1024]{1,0:T(8,128)(2,1)}, bf16[304,1024]{1,0:T(8,128)(2,1)S(1)}, u32[]{:S(2)}) copy-start(bf16[304,1024]{1,0:T(8,128)(2,1)S(1)} %collective-permute-done.15.a_ref.x1_far) | copy-start | bytes 1867780
  142.8 16.5 %collective-permute-start.16 = (bf16[304,1024]{1,0:T(8,128)(2,1)}, bf16[304,1024]{1,0:T(8,128)(2,1)S(1)}, u32[]{:S(2)}, u32[]{:S(2)}) collective-permute-start(bf16[304,1024]{1,0:T(8,128)(2,1)} %get-tuple-element.136), channel_id=1, source_target_pairs={{0,8},{8,0},{1,9},{9,1},{2,10},{10,2},{3,11},{11,3},{4,12},{12,4},... | collective-permute-start | bytes 1867784 | tf_op jit(solution)/shard_map/ppermute | solution.py:910
  164.2 15.8 %collective-permute-start.17 = (bf16[304,1024]{1,0:T(8,128)(2,1)}, bf16[304,1024]{1,0:T(8,128)(2,1)S(1)}, u32[]{:S(2)}, u32[]{:S(2)}) collective-permute-start(bf16[304,1024]{1,0:T(8,128)(2,1)} %get-tuple-element.138.a_ref.x1_own), channel_id=1, source_target_pairs={{0,8},{8,0},{1,9},{9,1},{2,10},{10,2},{3,11},{11,3},{4,12},{12,4},... | collective-permute-start | bytes 1867784 | tf_op jit(solution)/shard_map/ppermute | solution.py:910
  188.9 15.0 %collective-permute-start.18 = (bf16[304,1024]{1,0:T(8,128)(2,1)}, bf16[304,1024]{1,0:T(8,128)(2,1)S(1)}, u32[]{:S(2)}, u32[]{:S(2)}) collective-permute-start(bf16[304,1024]{1,0:T(8,128)(2,1)} %get-tuple-element.140), channel_id=1, source_target_pairs={{0,8},{8,0},{1,9},{9,1},{2,10},{10,2},{3,11},{11,3},{4,12},{12,4},... | collective-permute-start | bytes 1867784 | tf_op jit(solution)/shard_map/ppermute | solution.py:910
  208.9 18.1 %collective-permute-start.19 = (bf16[304,1024]{1,0:T(8,128)(2,1)}, bf16[304,1024]{1,0:T(8,128)(2,1)S(1)}, u32[]{:S(2)}, u32[]{:S(2)}) collective-permute-start(bf16[304,1024]{1,0:T(8,128)(2,1)} %get-tuple-element.143.a_ref.x1_own), channel_id=1, source_target_pairs={{0,8},{8,0},{1,9},{9,1},{2,10},{10,2},{3,11},{11,3},{4,12},{12,4},... | collective-permute-start | bytes 1867784 | tf_op jit(solution)/shard_map/ppermute | solution.py:910
  236.2 48.9 %collective-permute-start.20 = (bf16[304,1024]{1,0:T(8,128)(2,1)}, bf16[304,1024]{1,0:T(8,128)(2,1)}, u32[]{:S(2)}, u32[]{:S(2)}) collective-permute-start(bf16[304,1024]{1,0:T(8,128)(2,1)} %get-tuple-element.147), channel_id=1, source_target_pairs={{0,8},{8,0},{1,9},{9,1},{2,10},{10,2},{3,11},{11,3},{4,12},{12,4},... | collective-permute-start | bytes 1867784 | tf_op jit(solution)/shard_map/ppermute | solution.py:910
  245.3 20.7 %collective-permute-start.21 = (bf16[304,1024]{1,0:T(8,128)(2,1)}, bf16[304,1024]{1,0:T(8,128)(2,1)S(1)}, u32[]{:S(2)}, u32[]{:S(2)}) collective-permute-start(bf16[304,1024]{1,0:T(8,128)(2,1)} %get-tuple-element.157), channel_id=1, source_target_pairs={{0,8},{8,0},{1,9},{9,1},{2,10},{10,2},{3,11},{11,3},{4,12},{12,4},... | collective-permute-start | bytes 1867784 | tf_op jit(solution)/shard_map/ppermute | solution.py:910
  261.0 192.8 %all-gather.11.cloned.1.call-start = ((), (), s32[]{:S(2)}) async-start(), calls=%async_computation.10 | async-start | bytes 3112960 | tf_op jit(solution)/shard_map/all_gather | solution.py:1032
  272.3 16.5 %collective-permute-start.22 = (bf16[304,1024]{1,0:T(8,128)(2,1)}, bf16[304,1024]{1,0:T(8,128)(2,1)S(1)}, u32[]{:S(2)}, u32[]{:S(2)}) collective-permute-start(bf16[304,1024]{1,0:T(8,128)(2,1)} %get-tuple-element.159.g_ref.x2_own), channel_id=1, source_target_pairs={{0,8},{8,0},{1,9},{9,1},{2,10},{10,2},{3,11},{11,3},{4,12},{12,4},... | collective-permute-start | bytes 1867784 | tf_op jit(solution)/shard_map/ppermute | solution.py:910
  300.8 15.7 %collective-permute-start.23 = (bf16[304,1024]{1,0:T(8,128)(2,1)}, bf16[304,1024]{1,0:T(8,128)(2,1)S(1)}, u32[]{:S(2)}, u32[]{:S(2)}) collective-permute-start(bf16[304,1024]{1,0:T(8,128)(2,1)} %get-tuple-element.165), channel_id=1, source_target_pairs={{0,8},{8,0},{1,9},{9,1},{2,10},{10,2},{3,11},{11,3},{4,12},{12,4},... | collective-permute-start | bytes 1867784 | tf_op jit(solution)/shard_map/ppermute | solution.py:910
  309.8 20.4 %collective-permute-start.25 = (bf16[2,4,256,512]{3,2,1,0:T(8,128)(2,1)}, bf16[2,4,256,512]{3,2,1,0:T(8,128)(2,1)S(1)}, u32[]{:S(2)}, u32[]{:S(2)}) collective-permute-start(bf16[2,4,256,512]{3,2,1,0:T(8,128)(2,1)} %shard_map.269), channel_id=1, source_target_pairs={{0,4},{4,0},{1,5},{5,1},{2,6},{6,2},{3,7},{7,3},{8,12},{12,8},{9,1... | collective-permute-start | bytes 6291464 | tf_op jit(solution)/shard_map/ppermute | solution.py:910
  322.3 15.9 %collective-permute-start.24 = (bf16[304,1024]{1,0:T(8,128)(2,1)}, bf16[304,1024]{1,0:T(8,128)(2,1)S(1)}, u32[]{:S(2)}, u32[]{:S(2)}) collective-permute-start(bf16[304,1024]{1,0:T(8,128)(2,1)} %get-tuple-element.167.g_ref.x2_own), channel_id=1, source_target_pairs={{0,8},{8,0},{1,9},{9,1},{2,10},{10,2},{3,11},{11,3},{4,12},{12,4},... | collective-permute-start | bytes 1867784 | tf_op jit(solution)/shard_map/ppermute | solution.py:910
  337.8 43.2 %collective-permute-start.27 = (bf16[4,256,512]{2,1,0:T(8,128)(2,1)}, bf16[4,256,512]{2,1,0:T(8,128)(2,1)S(1)}, u32[]{:S(2)}, u32[]{:S(2)}) collective-permute-start(bf16[4,256,512]{2,1,0:T(8,128)(2,1)} %shard_map.270), channel_id=1, source_target_pairs={{0,16},{16,0},{1,17},{17,1},{2,18},{18,2},{3,19},{19,3},{4,20},{20... | collective-permute-start | bytes 3145736 | tf_op jit(solution)/shard_map/ppermute | solution.py:910
  346.6 14.4 %collective-permute-start.26 = (bf16[304,1024]{1,0:T(8,128)(2,1)}, bf16[304,1024]{1,0:T(8,128)(2,1)S(1)}, u32[]{:S(2)}, u32[]{:S(2)}) collective-permute-start(bf16[304,1024]{1,0:T(8,128)(2,1)} %get-tuple-element.176), channel_id=1, source_target_pairs={{0,8},{8,0},{1,9},{9,1},{2,10},{10,2},{3,11},{11,3},{4,12},{12,4},... | collective-permute-start | bytes 1867784 | tf_op jit(solution)/shard_map/ppermute | solution.py:910
  358.2 30.8 %collective-permute-start.29 = (bf16[2,4,256,1024]{3,2,1,0:T(8,128)(2,1)}, bf16[2,4,256,1024]{3,2,1,0:T(8,128)(2,1)}, u32[]{:S(2)}, u32[]{:S(2)}) collective-permute-start(bf16[2,4,256,1024]{3,2,1,0:T(8,128)(2,1)} %shard_map.275), channel_id=1, source_target_pairs={{0,4},{4,0},{1,5},{5,1},{2,6},{6,2},{3,7},{7,3},{8,12},{12,8},{9,1... | collective-permute-start | bytes 12582920 | tf_op jit(solution)/shard_map/ppermute | solution.py:910
  366.8 31.2 %collective-permute-start.28 = (bf16[304,1024]{1,0:T(8,128)(2,1)}, bf16[304,1024]{1,0:T(8,128)(2,1)S(1)}, u32[]{:S(2)}, u32[]{:S(2)}) collective-permute-start(bf16[304,1024]{1,0:T(8,128)(2,1)} %get-tuple-element.179.g_ref.x2_own), channel_id=1, source_target_pairs={{0,8},{8,0},{1,9},{9,1},{2,10},{10,2},{3,11},{11,3},{4,12},{12,4},... | collective-permute-start | bytes 1867784 | tf_op jit(solution)/shard_map/ppermute | solution.py:910
  368.9 143.0 %reduce-scatter.11.cloned.1.call-start = ((), (), s32[]{:S(2)}) async-start(), calls=%async_computation.7 | async-start | bytes 1310720 | tf_op jit(solution)/shard_map/reduce_scatter | solution.py:987
  388.4 150.0 %reduce-scatter.9.cloned.1.call-start = ((), (), s32[]{:S(2)}) async-start(), calls=%async_computation.6 | async-start | bytes 2621440 | tf_op jit(solution)/shard_map/reduce_scatter | solution.py:987
  396.5 49.1 %collective-permute-start.34 = (bf16[4,256,1024]{2,1,0:T(8,128)(2,1)}, bf16[4,256,1024]{2,1,0:T(8,128)(2,1)}, u32[]{:S(2)}, u32[]{:S(2)}) collective-permute-start(bf16[4,256,1024]{2,1,0:T(8,128)(2,1)} %shard_map.276), channel_id=1, source_target_pairs={{0,16},{16,0},{1,17},{17,1},{2,18},{18,2},{3,19},{19,3},{4,20},{20... | collective-permute-start | bytes 6291464 | tf_op jit(solution)/shard_map/ppermute | solution.py:910
  410.8 14.1 %collective-permute-start.30 = (bf16[304,1024]{1,0:T(8,128)(2,1)}, bf16[304,1024]{1,0:T(8,128)(2,1)S(1)}, u32[]{:S(2)}, u32[]{:S(2)}) collective-permute-start(bf16[304,1024]{1,0:T(8,128)(2,1)} %get-tuple-element.190), channel_id=1, source_target_pairs={{0,8},{8,0},{1,9},{9,1},{2,10},{10,2},{3,11},{11,3},{4,12},{12,4},... | collective-permute-start | bytes 1867784 | tf_op jit(solution)/shard_map/ppermute | solution.py:910
  419.6 16.8 %collective-permute-start.32 = (bf16[2,4,256,512]{3,2,1,0:T(8,128)(2,1)}, bf16[2,4,256,512]{3,2,1,0:T(8,128)(2,1)S(1)}, u32[]{:S(2)}, u32[]{:S(2)}) collective-permute-start(bf16[2,4,256,512]{3,2,1,0:T(8,128)(2,1)} %shard_map.279), channel_id=1, source_target_pairs={{0,4},{4,0},{1,5},{5,1},{2,6},{6,2},{3,7},{7,3},{8,12},{12,8},{9,1... | collective-permute-start | bytes 6291464 | tf_op jit(solution)/shard_map/ppermute | solution.py:910
  430.8 32.3 %collective-permute-start.31 = (bf16[304,1024]{1,0:T(8,128)(2,1)}, bf16[304,1024]{1,0:T(8,128)(2,1)S(1)}, u32[]{:S(2)}, u32[]{:S(2)}) collective-permute-start(bf16[304,1024]{1,0:T(8,128)(2,1)} %get-tuple-element.191.refs_0_), channel_id=1, source_target_pairs={{0,1},{1,2},{2,3},{3,0},{4,5},{5,6},{6,7},{7,4},{8,9},{9,10},{10,1... | collective-permute-start | bytes 1867784 | tf_op jit(solution)/shard_map/ppermute | solution.py:913
  430.8 43.1 %collective-permute-start.35 = (bf16[304,1024]{1,0:T(8,128)(2,1)}, bf16[304,1024]{1,0:T(8,128)(2,1)S(1)}, u32[]{:S(2)}, u32[]{:S(2)}) collective-permute-start(bf16[304,1024]{1,0:T(8,128)(2,1)} %get-tuple-element.191.refs_0_), channel_id=1, source_target_pairs={{0,3},{1,0},{2,1},{3,2},{4,7},{5,4},{6,5},{7,6},{8,11},{9,8},{10,9... | collective-permute-start | bytes 1867784 | tf_op jit(solution)/shard_map/ppermute | solution.py:913
  434.6 67.0 %collective-permute-start.36 = (bf16[304,1024]{1,0:T(8,128)(2,1)}, bf16[304,1024]{1,0:T(8,128)(2,1)S(1)}, u32[]{:S(2)}, u32[]{:S(2)}) collective-permute-start(bf16[304,1024]{1,0:T(8,128)(2,1)} %get-tuple-element.191.refs_0_), channel_id=1, source_target_pairs={{0,2},{1,3},{2,0},{3,1},{4,6},{5,7},{6,4},{7,5},{8,10},{9,11},{10,... | collective-permute-start | bytes 1867784 | tf_op jit(solution)/shard_map/ppermute | solution.py:913
  444.1 57.5 %collective-permute-start.33 = (bf16[4,256,512]{2,1,0:T(8,128)(2,1)}, bf16[4,256,512]{2,1,0:T(8,128)(2,1)S(1)}, u32[]{:S(2)}, u32[]{:S(2)}) collective-permute-start(bf16[4,256,512]{2,1,0:T(8,128)(2,1)} %shard_map.280), channel_id=1, source_target_pairs={{0,16},{16,0},{1,17},{17,1},{2,18},{18,2},{3,19},{19,3},{4,20},{20... | collective-permute-start | bytes 3145736 | tf_op jit(solution)/shard_map/ppermute | solution.py:910
  453.5 114.2 %reduce-scatter.7.cloned.1.call-start = ((), (), s32[]{:S(2)}) async-start(), calls=%async_computation.5 | async-start | bytes 1310720 | tf_op jit(solution)/shard_map/reduce_scatter | solution.py:987
  462.7 46.3 %copy-start = (f32[24,1024]{1,0:T(8,128)S(1)}, f32[24,1024]{1,0:T(8,128)}, u32[]{:S(2)}) copy-start(f32[24,1024]{1,0:T(8,128)} %shard_map.284) | copy-start | bytes 294916
  463.0 46.0 %copy-start.16 = (bf16[304,1024]{1,0:T(8,128)(2,1)}, bf16[304,1024]{1,0:T(8,128)(2,1)S(1)}, u32[]{:S(2)}) copy-start(bf16[304,1024]{1,0:T(8,128)(2,1)S(1)} %collective-permute-done.31.refs_1_) | copy-start | bytes 1867780
  473.9 35.1 %copy-start.17 = (bf16[304,1024]{1,0:T(8,128)(2,1)}, bf16[304,1024]{1,0:T(8,128)(2,1)S(1)}, u32[]{:S(2)}) copy-start(bf16[304,1024]{1,0:T(8,128)(2,1)S(1)} %collective-permute-done.35.refs_2_) | copy-start | bytes 1867780
  509.1 1.4 collective-permute-start.37
  510.4 4.9 collective-permute-start.38
  513.7 58.7 %collective-permute-start.44 = (bf16[128,512]{1,0:T(8,128)(2,1)}, bf16[128,512]{1,0:T(8,128)(2,1)S(1)}, u32[]{:S(2)}, u32[]{:S(2)}) collective-permute-start(bf16[128,512]{1,0:T(8,128)(2,1)} %get-tuple-element.223), channel_id=1, source_target_pairs={{0,8},{8,0},{1,9},{9,1},{2,10},{10,2},{3,11},{11,3},{4,12},{12,4},... | collective-permute-start | bytes 393224 | tf_op jit(solution)/shard_map/ppermute | solution.py:910
  515.4 4.9 collective-permute-start.39
  518.8 53.6 %collective-permute-start.45 = (bf16[128,1024]{1,0:T(8,128)(2,1)}, bf16[128,1024]{1,0:T(8,128)(2,1)S(1)}, u32[]{:S(2)}, u32[]{:S(2)}) collective-permute-start(bf16[128,1024]{1,0:T(8,128)(2,1)} %get-tuple-element.225), channel_id=1, source_target_pairs={{0,8},{8,0},{1,9},{9,1},{2,10},{10,2},{3,11},{11,3},{4,12},{12,4},... | collective-permute-start | bytes 786440 | tf_op jit(solution)/shard_map/ppermute | solution.py:910
  520.3 21.5 %collective-permute-start.40 = (f32[24,1024]{1,0:T(8,128)S(1)}, f32[24,1024]{1,0:T(8,128)S(1)}, u32[]{:S(2)}, u32[]{:S(2)}) collective-permute-start(f32[24,1024]{1,0:T(8,128)S(1)} %add.41), channel_id=1, source_target_pairs={{0,1},{1,0},{2,3},{3,2},{4,5},{5,4},{6,7},{7,6},{8,9},{9,8},{10,11... | collective-permute-start | bytes 294920 | tf_op jit(solution)/shard_map/ppermute | solution.py:1050
  540.3 32.1 %collective-permute-start.43 = (bf16[128,1024]{1,0:T(8,128)(2,1)}, bf16[128,1024]{1,0:T(8,128)(2,1)S(1)}, u32[]{:S(2)}, u32[]{:S(2)}) collective-permute-start(bf16[128,1024]{1,0:T(8,128)(2,1)} %get-tuple-element.221), channel_id=1, source_target_pairs={{0,8},{8,0},{1,9},{9,1},{2,10},{10,2},{3,11},{11,3},{4,12},{12,4},... | collective-permute-start | bytes 786440 | tf_op jit(solution)/shard_map/ppermute | solution.py:910
  541.9 11.2 %collective-permute-start.41 = (f32[24,1024]{1,0:T(8,128)S(1)}, f32[24,1024]{1,0:T(8,128)S(1)}, u32[]{:S(2)}, u32[]{:S(2)}) collective-permute-start(f32[24,1024]{1,0:T(8,128)S(1)} %add.42), channel_id=1, source_target_pairs={{0,2},{1,3},{2,0},{3,1},{4,6},{5,7},{6,4},{7,5},{8,10},{9,11},{10,... | collective-permute-start | bytes 294920 | tf_op jit(solution)/shard_map/ppermute | solution.py:1050
  569.4 5.3 collective-permute-start.42
  (33 other events, 83.9 us)
Sparse Core Ops, SparseCore 0:
  11.6 122.4 all-gather.6
  136.4 74.6 all-gather.8
  261.1 107.7 reduce-scatter.4
  370.3 51.0 all-gather.10
  423.6 45.5 reduce-scatter.10
  471.4 66.9 reduce-scatter.8
  542.0 25.7 reduce-scatter.6

commit v5 on v4

--- a/solution.py
+++ b/solution.py
@@ -657,6 +657,64 @@
     d_ref[...] = total[...].astype(BF16)
 
 
+def mlp_both_kernel(
+    a_ref, g_ref, pieces, h_ref, m_ref, du_ref, sums_ref, d_ref,
+    w1, w2, bs, rows, grads, total, back, sems,
+):
+    copy = start_rows(a_ref, rows, sems)
+    other = pltpu.make_async_copy(g_ref, grads, sems.at[3, 1])
+    other.start()
+    start_mlp_copies((pieces, MLP_SPAN), w1, w2, sems, bs)
+    copy.wait()
+    other.wait()
+
+    def chunk_step(chunk, carry):
+        wait_chunk(chunk, (w1, w2), sems)
+        wait_bias(chunk, bs, sems)
+        bias = jnp.sum(bs[chunk].astype(F32), axis=0, keepdims=True)
+        value, slope = gelu_pair(dot_nn(rows[...], w1[chunk]) + bias)
+        h_ref[chunk] = value.astype(BF16)
+        grad = (dot_nt(grads[...], w2[chunk]) * slope).astype(BF16)
+        du_ref[chunk] = grad
+        sums_ref[chunk] = jnp.broadcast_to(
+            jnp.sum(grad.astype(F32), axis=0, keepdims=True), (8, 512)
+        )
+        add_part(chunk, total, dot_nn(h_ref[chunk], w2[chunk]))
+        add_part(chunk, back, dot_nt(du_ref[chunk], w1[chunk]))
+        return carry
+
+    lax.fori_loop(0, 4, chunk_step, 0, unroll=True)
+    m_ref[...] = total[...].astype(BF16)
+    d_ref[...] = back[...].astype(BF16)
+
+
+def run_mlp_both(rows, grad, pieces):
+    width = rows.shape[1]
+    return pl.pallas_call(
+        mlp_both_kernel,
+        out_shape=(
+            jax.ShapeDtypeStruct((4, ROWS, 512), BF16),
+            jax.ShapeDtypeStruct((ROWS, width), BF16),
+            jax.ShapeDtypeStruct((4, ROWS, 512), BF16),
+            jax.ShapeDtypeStruct((4, 8, 512), F32),
+            jax.ShapeDtypeStruct((ROWS, width), BF16),
+        ),
+        in_specs=[HB, HB, HB],
+        out_specs=(VM,) * 5,
+        scratch_shapes=[
+            pltpu.VMEM((4, width, 512), BF16),
+            pltpu.VMEM((4, 512, width), BF16),
+            pltpu.VMEM((4, 16, 512), BF16),
+            pltpu.VMEM((ROWS, width), BF16),
+            pltpu.VMEM((ROWS, width), BF16),
+            pltpu.VMEM((ROWS, width), F32),
+            pltpu.VMEM((ROWS, width), F32),
+            pltpu.SemaphoreType.DMA((4, 4)),
+        ],
+        **params(15),
+    )(rows, grad, pieces)
+
+
 def run_mlp_backward(grad, slope, pieces):
     width = grad.shape[1]
     return pl.pallas_call(
@@ -690,6 +748,9 @@
     (xs, y1, y2, turned, added, sems), refs = refs[-6:], refs[:-6]
     out_ref = refs[-1]
     got = [refs[0].at[0 if stage == NEAR else 1], *refs[1:-1]] if stage in (AWAY, NEAR) else []
+    whole = out_ref
+    if stage == ALL:
+        out_ref = added
     outs = [out_ref.at[slot] for slot in range(len(slots))] if len(slots) > 1 else [out_ref]
     copies = []
     for slot, (side, core) in enumerate(slots):
@@ -743,9 +804,19 @@
                 second += added[index, chunk, :, span1:].astype(F32)
             out[chunk, :, 0:span1] = first.astype(BF16)
             out[chunk, :, span1:] = second.astype(BF16)
+            if stage == ALL:
+                pltpu.make_async_copy(
+                    out.at[chunk], whole.at[slot, chunk], sems.at[chunk, 8 + slot]
+                ).start()
         return carry
 
     lax.fori_loop(0, 4, chunk_step, 0, unroll=True)
+    if stage == ALL:
+        for chunk in range(4):
+            for slot, out in enumerate(outs):
+                pltpu.make_async_copy(
+                    out.at[chunk], whole.at[slot, chunk], sems.at[chunk, 8 + slot]
+                ).wait()
 
 
 def run_weight_grad(stage, place, x1, y1, x2, y2, *got):
@@ -758,13 +829,13 @@
         functools.partial(weight_grad_kernel, stage),
         out_shape=jax.ShapeDtypeStruct((slots, *shape) if slots > 1 else shape, BF16),
         in_specs=[SM] + [HB] * (8 + len(got)),
-        out_specs=VM,
+        out_specs=HB if stage == ALL else VM,
         scratch_shapes=[
             pltpu.VMEM((2, slots, rows, part), BF16),
             pltpu.VMEM((4, rows, span1), BF16),
             pltpu.VMEM((4, rows, span2), BF16),
             pltpu.VMEM((2, slots, part, rows), BF16),
-            pltpu.VMEM((max(len(got), 1), *shape), BF16),
+            pltpu.VMEM((4 if stage == ALL else max(len(got), 1), *shape), BF16),
             pltpu.SemaphoreType.DMA((5, 32)),
         ],
         **params((4 if span1 > 384 else 3) * slots + 2),
@@ -955,10 +1026,17 @@
             norm2_bias[layer],
         )
         normed2_far = swap(normed2, "x")
-        active, slope, part = both(
-            lambda rows: run_mlp_forward(rows, mlp_pieces[layer]),
-            after(normed2, grad_b_far), normed2_far,
-        )
+        if layer + 1 < layers:
+            active, slope, part = both(
+                lambda rows: run_mlp_forward(rows, mlp_pieces[layer]),
+                after(normed2, grad_b_far), normed2_far,
+            )
+        else:
+            cotangents, slope = [grad_b, grad_b_far], None
+            active, part, *last_back = both(
+                lambda rows: run_mlp_both(rows, cotangents.pop(0), mlp_pieces[layer]),
+                normed2, normed2_far,
+            )
         saved.append(
             (stream, (normed, normed_far), list(zip(qkv, probs)), mixed, middle, (normed2, normed2_far), active, slope)
         )
@@ -968,7 +1046,7 @@
                 norm1_bias[layer + 1],
             )
         else:
-            last = run_residual(middle, part[0], swap(part[1], "x"), fc2_bias[layer])
+            last = (middle, *part, fc2_bias[layer])
 
     class Sum:
         def __init__(self, *arrays):
@@ -1000,14 +1078,16 @@
     small = [None] * layers
     for layer in reversed(range(layers)):
         stream, normed, qkv, mixed, middle, normed2, active, slope = saved[layer]
-        slopes, qkvs = list(slope), list(qkv)
-        du, fc1_sum, part = both(
-            lambda rows: run_mlp_backward(rows, slopes.pop(0), mlp_pieces[layer]),
-            grad_b, grad_b_far, *([attn.away()] if attn else []),
-        )
+        qkvs = list(qkv)
+        if attn is None:
+            du, fc1_sum, part = last_back
+        else:
+            slopes = list(slope)
+            du, fc1_sum, part = both(
+                lambda rows: run_mlp_backward(rows, slopes.pop(0), mlp_pieces[layer]),
+                grad_b, grad_b_far, attn.away(),
+            )
         mlp = (SumAtOnce if layer else Sum)(normed2, du, (grad_b, grad_b_far), active)
-        if layer:
-            last = after(last, mlp.total)
         grad, grad_b, sums2 = run_norm_back(
             grad, part[0], swap(part[1], "x"), middle, norm2_gain[layer]
         )
@@ -1018,6 +1098,10 @@
             ),
             grad_b, grad_b_far, *([] if layer else [mlp.away()]),
         )
+        if layer:
+            stream_in, near, away, bias = last
+            last = run_residual(stream_in, near, swap(after(away, dqkv[0]), "x"), bias)
+            last = after(last, mlp.total)
         above, attn = attn, Sum(normed, dqkv, (grad_b, grad_b_far), mixed)
         if above:
             grad = after(grad, above.near())

time: 597 us -> 586 us (0.982)
  Pallas kernels: 307 us -> 295 us
  starting transfers between devices: 50.4 us -> 61.5 us
  waiting for transfers between devices: 192 us -> 182 us
    pallas_call x0 -> x2, Pallas kernels: none -> 21.7 us  [run_mlp_both(): pl.pallas_call(mlp_both_kernel, out_shape=(jax.ShapeDtypeStruct((4, ROWS,...]
    pallas_call x4 -> x2, Pallas kernels: 33.9 us -> 17.2 us  [run_mlp_forward(): pl.pallas_call(mlp_forward_kernel, out_shape=(jax.ShapeDtypeStruct((4, RO...]
    pallas_call x4 -> x2, Pallas kernels: 30.1 us -> 15.1 us  [run_mlp_backward(): pl.pallas_call(mlp_backward_kernel, out_shape=(jax.ShapeDtypeStruct((4, R...]
    ppermute x2, starting transfers between devices: 1.78 us -> 14.5 us  [on_device(): total = total + lax.ppermute(total, 'mp', pairs)]
    all_gather x2, waiting for transfers between devices: 20 us -> 11.5 us  [on_device(): lax.all_gather(after(packed[index], *gathered) if gathered else packed[in...]
    unnamed x88 -> x92, local copies, waits for them, and re-layouts: 16.3 us -> 16.9 us
  transfers between devices with their start and end apart: 53 -> 53, of which waited for: 24 -> 24; matrix products, arithmetic and copies ran while one was open for 1% -> 1% of each run, Pallas kernels for 50% -> 48%
where the time goes in v5:
time: 586 us; the launch traced here: 575 us
  Pallas kernels  295 us (50%)
  waiting for transfers between devices  182 us (31%)
  starting transfers between devices  61.5 us (10%)
  local copies, waits for them, and re-layouts  20.7 us (4%)
  between operations  15.1 us (3%)
    pallas_call x10, Pallas kernels, run_weight_grad(): pl.pallas_call(functools.partial(weight_grad_kernel, stage), out_shape=ja...  79.9 us
    ppermute x38, waiting for transfers between devices, swap(): return lax.ppermute(value, axis, [(0, 1), (1, 0)])  75.8 us
    ppermute x6, waiting for transfers between devices, shift(): lax.ppermute(value, 'mp', [(index, (index + step) % n_mp) for index in ra...  59.4 us
    pallas_call x4, Pallas kernels, run_attention_backward(): pl.pallas_call(functools.partial(attention_backward_kernel, layer, len(pi...  46.5 us
    ppermute x38, starting transfers between devices, swap(): return lax.ppermute(value, axis, [(0, 1), (1, 0)])  36.8 us
    pallas_call x4, Pallas kernels, run_attention_forward(): pl.pallas_call(functools.partial(attention_forward_kernel, layer, len(pie...  34.3 us
    reduce_scatter x3, waiting for transfers between devices, near(): self.total = lax.psum_scatter(flat, 'mp', tiled=True)  32.2 us
    pallas_call x2, Pallas kernels, run_mlp_both(): pl.pallas_call(mlp_both_kernel, out_shape=(jax.ShapeDtypeStruct((4, ROWS,...  21.7 us
  transfers between devices with their start and end apart: 53, of which 24 were waited for; matrix products, arithmetic and copies ran while one was open for 1% of the time, Pallas kernels for 48%

profile of v5, /device:TPU:0, one launch (start us, length us, event | category | flops | bytes accessed | tf_op | source)
XLA Modules:
  0.0 574.9 jit_solution(16607247939418226173)
XLA Ops:
  7.9 3.6 shard_map.246
  11.6 5.1 collective-permute-start.8
  18.9 5.5 collective-permute-done.8.refs_8_
  24.4 4.1 shard_map.245
  31.4 26.3 %collective-permute-done.4.refs_4_ = bf16[272,512]{1,0:T(8,128)(2,1)S(1)} collective-permute-done((bf16[272,512]{1,0:T(8,128)(2,1)}, bf16[272,512]{1,0:T(8,128)(2,1)S(1)}, u32[]{:S(2)}, u32[]{:S(2)}) %collective-permute-start.4) | collective-permute-done | bytes 278560 | tf_op jit(solution)/shard_map/ppermute | solution.py:984
  59.8 4.0 shard_map.250
  64.4 2.8 collective-permute-done.5.refs_5_
  67.3 5.5 collective-permute-done.1.refs_1_
  77.4 9.1 %shard_map.248 = (bf16[4,304,384]{2,1,0:T(8,128)(2,1)}, bf16[4,3,224,112]{3,2,1,0:T(8,128)(2,1)}, bf16[4,304,128]{2,1,0:T(8,128)(2,1)}, bf16[304,1024]{1,0:T(8,128)(2,1)}) custom-call(s32[8]{0:T(128)} %stack.35.place, bf16[304,1024]{1,0:T(8,128)(2,1)} %copy-done.11, bf16[2,3,1024,256]{3,2,1,0:T(8,128)(2,1)} %bitcast.44, bf16[2,256,1024]{2,1,0:T(8,128)(2,1)} %wproj.17, ...), custom_call_target="tpu_custom_call" | custom-call | flops 28000000000 | tf_op jit(solution)/shard_map/pallas_call | solution.py:492
  87.0 9.0 %shard_map.247 = (bf16[4,304,384]{2,1,0:T(8,128)(2,1)}, bf16[4,3,224,112]{3,2,1,0:T(8,128)(2,1)}, bf16[4,304,128]{2,1,0:T(8,128)(2,1)}, bf16[304,1024]{1,0:T(8,128)(2,1)}) custom-call(s32[8]{0:T(128)} %stack.35.place, bf16[304,1024]{1,0:T(8,128)(2,1)} %get-tuple-element.124.a_ref.x1_own, bf16[2,3,1024,256]{3,2,1,0:T(8,128)(2,1)} %bitcast.45, ...), custom_call_target="tpu_custom_call" | custom-call | flops 28000000000 | tf_op jit(solution)/shard_map/pallas_call | solution.py:492
  96.1 8.0 %collective-permute-done.13.far_ref = bf16[304,1024]{1,0:T(8,128)(2,1)S(1)} collective-permute-done((bf16[304,1024]{1,0:T(8,128)(2,1)}, bf16[304,1024]{1,0:T(8,128)(2,1)S(1)}, u32[]{:S(2)}, u32[]{:S(2)}) %collective-permute-start.13) | collective-permute-done | bytes 622624 | tf_op jit(solution)/shard_map/ppermute | solution.py:981
  104.9 4.1 shard_map.249
  111.2 13.8 %collective-permute-done.15.a_ref.x1_far = bf16[304,1024]{1,0:T(8,128)(2,1)S(1)} collective-permute-done((bf16[304,1024]{1,0:T(8,128)(2,1)}, bf16[304,1024]{1,0:T(8,128)(2,1)S(1)}, u32[]{:S(2)}, u32[]{:S(2)}) %collective-permute-start.15) | collective-permute-done | bytes 622624 | tf_op jit(solution)/shard_map/ppermute | solution.py:981
  125.0 9.6 %all-gather.7.cloned.1.call-done = bf16[12800,512]{1,0:T(8,128)(2,1)} async-done(((bf16[800,512]{1,0:T(8,128)(2,1)}), bf16[12800,512]{1,0:T(8,128)(2,1)}) %all-gather.7.cloned.1.call-update) | async-done | bytes 13107216 | tf_op jit(solution)/shard_map/all_gather | solution.py:1007
  134.6 8.8 %shard_map.252 = (bf16[4,304,512]{2,1,0:T(8,128)(2,1)}, bf16[4,304,512]{2,1,0:T(8,128)(2,1)}, bf16[304,1024]{1,0:T(8,128)(2,1)}) custom-call(bf16[304,1024]{1,0:T(8,128)(2,1)} %copy-done.12, bf16[2,2,4,800,512]{4,3,2,1,0:T(8,128)(2,1)} %bitcast.33), custom_call_target="tpu_custom_call" | custom-call | flops 32000000000 | tf_op jit(solution)/shard_map/pallas_call | solution.py:617
  144.9 8.4 %shard_map.251 = (bf16[4,304,512]{2,1,0:T(8,128)(2,1)}, bf16[4,304,512]{2,1,0:T(8,128)(2,1)}, bf16[304,1024]{1,0:T(8,128)(2,1)}) custom-call(bf16[304,1024]{1,0:T(8,128)(2,1)} %get-tuple-element.131.a_ref.x1_own, bf16[2,2,4,800,512]{4,3,2,1,0:T(8,128)(2,1)} %bitcast.34), custom_call_target="tpu_custom_call" | custom-call | flops 32000000000 | tf_op jit(solution)/shard_map/pallas_call | solution.py:617
  153.4 6.5 %collective-permute-done.16.far_ref = bf16[304,1024]{1,0:T(8,128)(2,1)S(1)} collective-permute-done((bf16[304,1024]{1,0:T(8,128)(2,1)}, bf16[304,1024]{1,0:T(8,128)(2,1)S(1)}, u32[]{:S(2)}, u32[]{:S(2)}) %collective-permute-start.16) | collective-permute-done | bytes 622624 | tf_op jit(solution)/shard_map/ppermute | solution.py:981
  160.7 4.1 shard_map.253
  166.3 14.2 %collective-permute-done.17.a_ref.x1_far = bf16[304,1024]{1,0:T(8,128)(2,1)S(1)} collective-permute-done((bf16[304,1024]{1,0:T(8,128)(2,1)}, bf16[304,1024]{1,0:T(8,128)(2,1)S(1)}, u32[]{:S(2)}, u32[]{:S(2)}) %collective-permute-start.17) | collective-permute-done | bytes 622624 | tf_op jit(solution)/shard_map/ppermute | solution.py:981
  181.3 8.0 %shard_map.255 = (bf16[4,304,384]{2,1,0:T(8,128)(2,1)}, bf16[4,3,224,112]{3,2,1,0:T(8,128)(2,1)}, bf16[4,304,128]{2,1,0:T(8,128)(2,1)}, bf16[304,1024]{1,0:T(8,128)(2,1)}) custom-call(s32[8]{0:T(128)} %stack.35.place, bf16[304,1024]{1,0:T(8,128)(2,1)} %copy-done.13, bf16[2,3,1024,256]{3,2,1,0:T(8,128)(2,1)} %bitcast.46, bf16[2,256,1024]{2,1,0:T(8,128)(2,1)} %wproj.17, ...), custom_call_target="tpu_custom_call" | custom-call | flops 28000000000 | tf_op jit(solution)/shard_map/pallas_call | solution.py:492
  190.9 8.2 %shard_map.254 = (bf16[4,304,384]{2,1,0:T(8,128)(2,1)}, bf16[4,3,224,112]{3,2,1,0:T(8,128)(2,1)}, bf16[4,304,128]{2,1,0:T(8,128)(2,1)}, bf16[304,1024]{1,0:T(8,128)(2,1)}) custom-call(s32[8]{0:T(128)} %stack.35.place, bf16[304,1024]{1,0:T(8,128)(2,1)} %get-tuple-element.136.a_ref.x1_own, bf16[2,3,1024,256]{3,2,1,0:T(8,128)(2,1)} %bitcast.47, ...), custom_call_target="tpu_custom_call" | custom-call | flops 28000000000 | tf_op jit(solution)/shard_map/pallas_call | solution.py:492
  199.1 5.3 collective-permute-done.18.far_ref
  205.2 4.1 shard_map.256
  210.8 1.9 all-gather.9.cloned.1.call-done
  212.7 10.7 %shard_map.257 = (bf16[4,304,512]{2,1,0:T(8,128)(2,1)}, bf16[304,1024]{1,0:T(8,128)(2,1)}, bf16[4,304,512]{2,1,0:T(8,128)(2,1)}, f32[4,8,512]{2,1,0:T(8,128)}, bf16[304,1024]{1,0:T(8,128)(2,1)}) custom-call(bf16[304,1024]{1,0:T(8,128)(2,1)} %get-tuple-element.140.a_ref.x1_own, bf16[304,1024]{1,0:T(8,128)(2,1)} %get-tuple-element.130.g_ref.x2_own, ...), custom_call_target="tpu_custom_call" | custom-call | flops 60000002048 | tf_op jit(solution)/shard_map/pallas_call | solution.py:693
  224.3 10.9 %shard_map.258 = (bf16[4,304,512]{2,1,0:T(8,128)(2,1)}, bf16[304,1024]{1,0:T(8,128)(2,1)}, bf16[4,304,512]{2,1,0:T(8,128)(2,1)}, f32[4,8,512]{2,1,0:T(8,128)}, bf16[304,1024]{1,0:T(8,128)(2,1)}) custom-call(bf16[304,1024]{1,0:T(8,128)(2,1)} %copy-done.24, bf16[304,1024]{1,0:T(8,128)(2,1)} %copy-done.19, bf16[2,2,4,528,512]{4,3,2,1,0:T(8,128)(2,1)} %bitcast.42), custom_call_target="tpu_custom_call" | custom-call | flops 60000002048 | tf_op jit(solution)/shard_map/pallas_call | solution.py:693
  236.8 12.6 %shard_map.262 = bf16[4,4,256,1024]{3,2,1,0:T(8,128)(2,1)} custom-call(s32[8]{0:T(128)} %stack.35.place, bf16[304,1024]{1,0:T(8,128)(2,1)} %get-tuple-element.140.a_ref.x1_own, bf16[304,1024]{1,0:T(8,128)(2,1)} %copy-done.24, bf16[4,304,512]{2,1,0:T(8,128)(2,1)} %get-tuple-element.153.y1_own, bf16[4,304,512]{2,1,0:T(8,128)(2,1)} %get-tuple-element.154.y1_far, ...), custom_call_target="tpu_custom_call" | custom-call | flops 71999995904 | tf_op jit(solution)/shard_map/pallas_call | solution.py:828
  252.6 5.4 shard_map.259
  259.6 11.4 %shard_map.260 = (bf16[4,304,384]{2,1,0:T(8,128)(2,1)}, f32[4,8,384]{2,1,0:T(8,128)}, bf16[304,1024]{1,0:T(8,128)(2,1)}) custom-call(s32[8]{0:T(128)} %stack.35.place, bf16[304,1024]{1,0:T(8,128)(2,1)} %get-tuple-element.148.g_ref.x2_own, bf16[4,304,384]{2,1,0:T(8,128)(2,1)} %get-tuple-element.149.qkv_ref, ...), custom_call_target="tpu_custom_call" | custom-call | flops 48000000000 | tf_op jit(solution)/shard_map/pallas_call | solution.py:560
  271.6 2.6 collective-permute-done.22.g_ref.x2_far
  275.1 11.0 %shard_map.264 = (bf16[4,304,384]{2,1,0:T(8,128)(2,1)}, f32[4,8,384]{2,1,0:T(8,128)}, bf16[304,1024]{1,0:T(8,128)(2,1)}) custom-call(s32[8]{0:T(128)} %stack.35.place, bf16[304,1024]{1,0:T(8,128)(2,1)} %copy-done.20, bf16[4,304,384]{2,1,0:T(8,128)(2,1)} %get-tuple-element.160.qkv_ref, bf16[4,3,224,112]{3,2,1,0:T(8,128)(2,1)} %get-tuple-element.161.probs_ref, ...), custom_call_target="tpu_custom_call" | custom-call | flops 48000000000 | tf_op jit(solution)/shard_map/pallas_call | solution.py:560
  286.1 2.2 collective-permute-start.23
  288.2 8.3 %shard_map.267 = bf16[2,4,256,512]{3,2,1,0:T(8,128)(2,1)} custom-call(s32[8]{0:T(128)} %stack.35.place, bf16[304,1024]{1,0:T(8,128)(2,1)} %get-tuple-element.136.a_ref.x1_own, bf16[304,1024]{1,0:T(8,128)(2,1)} %copy-done.13, bf16[4,304,384]{2,1,0:T(8,128)(2,1)} %get-tuple-element.151.y1_own, bf16[4,304,384]{2,1,0:T(8,128)(2,1)} %get-tuple-element.167.y1_far, ...), custom_call_target="tpu_custom_call" | custom-call | flops 32000000000 | tf_op jit(solution)/shard_map/pallas_call | solution.py:828
  296.6 3.7 shard_map.261
  301.1 5.0 shard_map.265
  307.3 7.5 %shard_map.266 = (bf16[4,304,512]{2,1,0:T(8,128)(2,1)}, f32[4,8,512]{2,1,0:T(8,128)}, bf16[304,1024]{1,0:T(8,128)(2,1)}) custom-call(bf16[304,1024]{1,0:T(8,128)(2,1)} %get-tuple-element.164.g_ref.x2_own, bf16[4,304,512]{2,1,0:T(8,128)(2,1)} %get-tuple-element.165.slope_ref, bf16[2,2,4,800,512]{4,3,2,1,0:T(8,128)(2,1)} %bitcast.39), custom_call_target="tpu_custom_call" | custom-call | flops 28000000000 | tf_op jit(solution)/shard_map/pallas_call | solution.py:720
  316.1 6.3 %shard_map.268 = bf16[4,256,512]{2,1,0:T(8,128)(2,1)} custom-call(s32[8]{0:T(128)} %stack.35.place, bf16[304,1024]{1,0:T(8,128)(2,1)} %get-tuple-element.136.a_ref.x1_own, bf16[304,1024]{1,0:T(8,128)(2,1)} %copy-done.13, bf16[4,304,384]{2,1,0:T(8,128)(2,1)} %get-tuple-element.151.y1_own, bf16[4,304,384]{2,1,0:T(8,128)(2,1)} %get-tuple-element.167.y1_far, ...), custom_call_target="tpu_custom_call" | custom-call | flops 20000000000 | tf_op jit(solution)/shard_map/pallas_call | solution.py:828
  323.7 7.5 %shard_map.269 = (bf16[4,304,512]{2,1,0:T(8,128)(2,1)}, f32[4,8,512]{2,1,0:T(8,128)}, bf16[304,1024]{1,0:T(8,128)(2,1)}) custom-call(bf16[304,1024]{1,0:T(8,128)(2,1)} %copy-done.14, bf16[4,304,512]{2,1,0:T(8,128)(2,1)} %get-tuple-element.171.slope_ref, bf16[2,2,4,800,512]{4,3,2,1,0:T(8,128)(2,1)} %bitcast.40), custom_call_target="tpu_custom_call" | custom-call | flops 28000000000 | tf_op jit(solution)/shard_map/pallas_call | solution.py:720
  331.9 10.0 %shard_map.273 = bf16[2,4,256,1024]{3,2,1,0:T(8,128)(2,1)} custom-call(s32[8]{0:T(128)} %stack.35.place, bf16[304,1024]{1,0:T(8,128)(2,1)} %get-tuple-element.131.a_ref.x1_own, bf16[304,1024]{1,0:T(8,128)(2,1)} %copy-done.12, bf16[4,304,512]{2,1,0:T(8,128)(2,1)} %get-tuple-element.179.y1_own, bf16[4,304,512]{2,1,0:T(8,128)(2,1)} %get-tuple-element.180.y1_far, ...), custom_call_target="tpu_custom_call" | custom-call | flops 40000000000 | tf_op jit(solution)/shard_map/pallas_call | solution.py:828
  342.1 5.1 collective-permute-done.26.far_ref
  348.1 5.1 shard_map.270
  354.3 3.0 reduce-scatter.5.cloned.1.call-done.refs_0_
  357.5 12.1 %shard_map.272 = (bf16[4,304,384]{2,1,0:T(8,128)(2,1)}, f32[4,8,384]{2,1,0:T(8,128)}, bf16[304,1024]{1,0:T(8,128)(2,1)}) custom-call(s32[8]{0:T(128)} %stack.35.place, bf16[304,1024]{1,0:T(8,128)(2,1)} %get-tuple-element.175.g_ref.x2_own, bf16[4,304,384]{2,1,0:T(8,128)(2,1)} %get-tuple-element.176.qkv_ref, ...), custom_call_target="tpu_custom_call" | custom-call | flops 48000000000 | tf_op jit(solution)/shard_map/pallas_call | solution.py:560
  370.5 6.4 %shard_map.271 = bf16[4,256,512]{2,1,0:T(8,128)(2,1)} custom-call(s32[8]{0:T(128)} %stack.35.place, bf16[304,1024]{1,0:T(8,128)(2,1)} %get-tuple-element.136.a_ref.x1_own, bf16[304,1024]{1,0:T(8,128)(2,1)} %copy-done.13, bf16[4,304,384]{2,1,0:T(8,128)(2,1)} %get-tuple-element.151.y1_own, bf16[4,304,384]{2,1,0:T(8,128)(2,1)} %get-tuple-element.167.y1_far, ...), custom_call_target="tpu_custom_call" | custom-call | flops 20000000000 | tf_op jit(solution)/shard_map/pallas_call | solution.py:828
  377.5 7.5 %shard_map.274 = bf16[4,256,1024]{2,1,0:T(8,128)(2,1)} custom-call(s32[8]{0:T(128)} %stack.35.place, bf16[304,1024]{1,0:T(8,128)(2,1)} %get-tuple-element.131.a_ref.x1_own, bf16[304,1024]{1,0:T(8,128)(2,1)} %copy-done.12, bf16[4,304,512]{2,1,0:T(8,128)(2,1)} %get-tuple-element.179.y1_own, bf16[4,304,512]{2,1,0:T(8,128)(2,1)} %get-tuple-element.180.y1_far, ...), custom_call_target="tpu_custom_call" | custom-call | flops 24000000000 | tf_op jit(solution)/shard_map/pallas_call | solution.py:828
  386.4 12.0 %shard_map.275 = (bf16[4,304,384]{2,1,0:T(8,128)(2,1)}, f32[4,8,384]{2,1,0:T(8,128)}, bf16[304,1024]{1,0:T(8,128)(2,1)}) custom-call(s32[8]{0:T(128)} %stack.35.place, bf16[304,1024]{1,0:T(8,128)(2,1)} %copy-done.15, bf16[4,304,384]{2,1,0:T(8,128)(2,1)} %get-tuple-element.184.qkv_ref, bf16[4,3,224,112]{3,2,1,0:T(8,128)(2,1)} %get-tuple-element.185.probs_ref, ...), custom_call_target="tpu_custom_call" | custom-call | flops 48000000000 | tf_op jit(solution)/shard_map/pallas_call | solution.py:560
  400.0 8.1 %shard_map.277 = bf16[2,4,256,512]{3,2,1,0:T(8,128)(2,1)} custom-call(s32[8]{0:T(128)} %stack.35.place, bf16[304,1024]{1,0:T(8,128)(2,1)} %get-tuple-element.124.a_ref.x1_own, bf16[304,1024]{1,0:T(8,128)(2,1)} %copy-done.11, bf16[4,304,384]{2,1,0:T(8,128)(2,1)} %get-tuple-element.188.y1_own, bf16[4,304,384]{2,1,0:T(8,128)(2,1)} %get-tuple-element.189.y1_far, ...), custom_call_target="tpu_custom_call" | custom-call | flops 32000000000 | tf_op jit(solution)/shard_map/pallas_call | solution.py:828
  408.2 5.2 collective-permute-done.30.far_ref
  414.2 5.0 shard_map.276
  425.1 6.3 %shard_map.278 = bf16[4,256,512]{2,1,0:T(8,128)(2,1)} custom-call(s32[8]{0:T(128)} %stack.35.place, bf16[304,1024]{1,0:T(8,128)(2,1)} %get-tuple-element.124.a_ref.x1_own, bf16[304,1024]{1,0:T(8,128)(2,1)} %copy-done.11, bf16[4,304,384]{2,1,0:T(8,128)(2,1)} %get-tuple-element.188.y1_own, bf16[4,304,384]{2,1,0:T(8,128)(2,1)} %get-tuple-element.189.y1_far, ...), custom_call_target="tpu_custom_call" | custom-call | flops 20000000000 | tf_op jit(solution)/shard_map/pallas_call | solution.py:828
  432.9 8.0 %shard_map.279 = bf16[4,256,1024]{2,1,0:T(8,128)(2,1)} custom-call(s32[8]{0:T(128)} %stack.35.place, bf16[304,1024]{1,0:T(8,128)(2,1)} %get-tuple-element.131.a_ref.x1_own, bf16[304,1024]{1,0:T(8,128)(2,1)} %copy-done.12, bf16[4,304,512]{2,1,0:T(8,128)(2,1)} %get-tuple-element.179.y1_own, bf16[4,304,512]{2,1,0:T(8,128)(2,1)} %get-tuple-element.180.y1_far, ...), custom_call_target="tpu_custom_call" | custom-call | flops 24000000000 | tf_op jit(solution)/shard_map/pallas_call | solution.py:828
  441.2 8.9 %shard_map.263 = bf16[1200,1024]{1,0:T(8,128)(2,1)} custom-call(s32[8]{0:T(128)} %stack.35.place, bf16[4,304,1024]{2,1,0:T(8,128)(2,1)} %bitcast.52), custom_call_target="tpu_custom_call" | custom-call | flops 35999997952 | tf_op jit(solution)/shard_map/pallas_call | solution.py:180
  450.1 12.4 %collective-permute-done.36.refs_3_ = bf16[304,1024]{1,0:T(8,128)(2,1)S(1)} collective-permute-done((bf16[304,1024]{1,0:T(8,128)(2,1)}, bf16[304,1024]{1,0:T(8,128)(2,1)S(1)}, u32[]{:S(2)}, u32[]{:S(2)}) %collective-permute-start.36) | collective-permute-done | bytes 622624 | tf_op jit(solution)/shard_map/ppermute | solution.py:984
  462.5 15.2 %collective-permute-done.31.refs_1_ = bf16[304,1024]{1,0:T(8,128)(2,1)S(1)} collective-permute-done((bf16[304,1024]{1,0:T(8,128)(2,1)}, bf16[304,1024]{1,0:T(8,128)(2,1)S(1)}, u32[]{:S(2)}, u32[]{:S(2)}) %collective-permute-start.31) | collective-permute-done | bytes 622624 | tf_op jit(solution)/shard_map/ppermute | solution.py:984
  478.7 6.4 %shard_map.280 = bf16[4,256,512]{2,1,0:T(8,128)(2,1)} custom-call(s32[8]{0:T(128)} %stack.35.place, bf16[304,1024]{1,0:T(8,128)(2,1)} %get-tuple-element.124.a_ref.x1_own, bf16[304,1024]{1,0:T(8,128)(2,1)} %copy-done.11, bf16[4,304,384]{2,1,0:T(8,128)(2,1)} %get-tuple-element.188.y1_own, bf16[4,304,384]{2,1,0:T(8,128)(2,1)} %get-tuple-element.189.y1_far, ...), custom_call_target="tpu_custom_call" | custom-call | flops 20000000000 | tf_op jit(solution)/shard_map/pallas_call | solution.py:828
  492.8 1.9 shard_map.287
  494.7 1.9 collective-permute-start.45
  496.6 12.7 %collective-permute-start.40 = (f32[24,1024]{1,0:T(8,128)S(1)}, f32[24,1024]{1,0:T(8,128)S(1)}, u32[]{:S(2)}, u32[]{:S(2)}) collective-permute-start(f32[24,1024]{1,0:T(8,128)S(1)} %add.41), channel_id=1, source_target_pairs={{0,1},{1,0},{2,3},{3,2},{4,5},{5,4},{6,7},{7,6},{8,9},{9,8},{10,11... | collective-permute-start | bytes 294920 | tf_op jit(solution)/shard_map/ppermute | solution.py:1134
  509.3 18.2 %reduce-scatter.9.cloned.1.call-done.refs_0_ = bf16[256,1024]{1,0:T(8,128)(2,1)} async-done(((bf16[1024,1024]{1,0:T(8,128)(2,1)}), bf16[256,1024]{1,0:T(8,128)(2,1)}) %reduce-scatter.9.cloned.1.call-update) | async-done | bytes 524304 | tf_op jit(solution)/shard_map/reduce_scatter | solution.py:1065
  527.6 1.9 shard_map.285
  532.8 9.5 %shard_map.281 = f32[1200,1024]{1,0:T(8,128)} custom-call(s32[8]{0:T(128)} %stack.35.place, bf16[304,1024]{1,0:T(8,128)(2,1)} %get-tuple-element.187.refs_0_, bf16[304,1024]{1,0:T(8,128)(2,1)} %copy-done.18, bf16[304,1024]{1,0:T(8,128)(2,1)} %copy-done.17, bf16[304,1024]{1,0:T(8,128)(2,1)} %copy-done.16), custom_call_target="tpu_custom_call" | custom-call | flops 35999997952 | tf_op jit(solution)/shard_map/pallas_call | solution.py:180
  543.0 13.9 %reduce-scatter.7.cloned.1.call-done.refs_0_ = bf16[256,512]{1,0:T(8,128)(2,1)} async-done(((bf16[1024,512]{1,0:T(8,128)(2,1)}), bf16[256,512]{1,0:T(8,128)(2,1)}) %reduce-scatter.7.cloned.1.call-update) | async-done | bytes 262160 | tf_op jit(solution)/shard_map/reduce_scatter | solution.py:1065
  561.7 2.2 collective-permute-done.42.refs_1_
  564.5 3.3 shard_map.288
  (196 shorter events, 72.4 us)
Async XLA Ops:
  7.2 127.4 %all-gather.7.cloned.1.call-start = ((), (), s32[]{:S(2)}) async-start(), calls=%async_computation.8 | async-start | bytes 13926400 | tf_op jit(solution)/shard_map/all_gather | solution.py:1007
  7.9 10.4 %copy-start.2 = (f32[2,1024]{1,0:T(2,128)S(1)}, f32[2,1024]{1,0:T(2,128)}, u32[]{:S(2)}) copy-start(f32[2,1024]{1,0:T(2,128)} %param.17) | copy-start | bytes 24580
  11.5 201.2 %all-gather.9.cloned.1.call-start = ((), (), s32[]{:S(2)}) async-start(), calls=%async_computation.9 | async-start | bytes 9191424 | tf_op jit(solution)/shard_map/all_gather | solution.py:1007
  11.6 12.8 %collective-permute-start.8 = (bf16[272,512]{1,0:T(8,128)(2,1)}, bf16[272,512]{1,0:T(8,128)(2,1)S(1)}, u32[]{:S(2)}, u32[]{:S(2)}) collective-permute-start(bf16[272,512]{1,0:T(8,128)(2,1)} %get-tuple-element.125), channel_id=1, source_target_pairs={{0,3},{1,0},{2,1},{3,2},{4,7},{5,4},{6,5},{7,6},{8,11},{9,8},{10,9... | collective-permute-start | bytes 835592 | tf_op jit(solution)/shard_map/ppermute | solution.py:984
  16.7 41.0 %collective-permute-start.4 = (bf16[272,512]{1,0:T(8,128)(2,1)}, bf16[272,512]{1,0:T(8,128)(2,1)S(1)}, u32[]{:S(2)}, u32[]{:S(2)}) collective-permute-start(bf16[272,512]{1,0:T(8,128)(2,1)} %get-tuple-element.125), channel_id=1, source_target_pairs={{0,2},{1,3},{2,0},{3,1},{4,6},{5,7},{6,4},{7,5},{8,10},{9,11},{10,... | collective-permute-start | bytes 835592 | tf_op jit(solution)/shard_map/ppermute | solution.py:984
  16.7 41.0 %collective-permute-start = (bf16[272,512]{1,0:T(8,128)(2,1)}, bf16[272,512]{1,0:T(8,128)(2,1)S(1)}, u32[]{:S(2)}, u32[]{:S(2)}) collective-permute-start(bf16[272,512]{1,0:T(8,128)(2,1)} %get-tuple-element.125), channel_id=1, source_target_pairs={{0,1},{1,2},{2,3},{3,0},{4,5},{5,6},{6,7},{7,4},{8,9},{9,10},{10,1... | collective-permute-start | bytes 835592 | tf_op jit(solution)/shard_map/ppermute | solution.py:984
  24.4 34.9 %collective-permute-start.10 = (bf16[272,512]{1,0:T(8,128)(2,1)S(1)}, bf16[272,512]{1,0:T(8,128)(2,1)S(1)}, u32[]{:S(2)}, u32[]{:S(2)}) collective-permute-start(bf16[272,512]{1,0:T(8,128)(2,1)S(1)} %collective-permute-done.8.refs_8_), channel_id=1, source_target_pairs={{0,4},{4,0},{1,5},{5,1},{2,6},{6,2},{3,7},{7,3},{8,12},{12,8},{9,1... | collective-permute-start | bytes 835592 | tf_op jit(solution)/shard_map/ppermute | solution.py:981
  28.5 47.1 %collective-permute-start.12 = (bf16[304,1024]{1,0:T(8,128)(2,1)}, bf16[304,1024]{1,0:T(8,128)(2,1)S(1)}, u32[]{:S(2)}, u32[]{:S(2)}) collective-permute-start(bf16[304,1024]{1,0:T(8,128)(2,1)} %get-tuple-element.124.a_ref.x1_own), channel_id=1, source_target_pairs={{0,8},{8,0},{1,9},{9,1},{2,10},{10,2},{3,11},{11,3},{4,12},{12,4},... | collective-permute-start | bytes 1867784 | tf_op jit(solution)/shard_map/ppermute | solution.py:981
  29.8 327.6 %reduce-scatter.5.cloned.1.call-start = ((), (), s32[]{:S(2)}) async-start(), calls=%async_computation.4 | async-start | bytes 8912896 | tf_op jit(solution)/shard_map/reduce_scatter | solution.py:1075
  29.8 34.0 %collective-permute-start.9 = (bf16[272,512]{1,0:T(8,128)(2,1)S(1)}, bf16[272,512]{1,0:T(8,128)(2,1)S(1)}, u32[]{:S(2)}, u32[]{:S(2)}) collective-permute-start(bf16[272,512]{1,0:T(8,128)(2,1)S(1)} %collective-permute-done.8.refs_8_), channel_id=1, source_target_pairs={{0,16},{16,0},{1,17},{17,1},{2,18},{18,2},{3,19},{19,3},{4,20},{20... | collective-permute-start | bytes 835592 | tf_op jit(solution)/shard_map/ppermute | solution.py:981
  57.7 6.2 %collective-permute-start.6 = (bf16[272,512]{1,0:T(8,128)(2,1)S(1)}, bf16[272,512]{1,0:T(8,128)(2,1)S(1)}, u32[]{:S(2)}, u32[]{:S(2)}) collective-permute-start(bf16[272,512]{1,0:T(8,128)(2,1)S(1)} %collective-permute-done.4.refs_4_), channel_id=1, source_target_pairs={{0,4},{4,0},{1,5},{5,1},{2,6},{6,2},{3,7},{7,3},{8,12},{12,8},{9,1... | collective-permute-start | bytes 835592 | tf_op jit(solution)/shard_map/ppermute | solution.py:981
  57.7 9.5 %collective-permute-start.5 = (bf16[272,512]{1,0:T(8,128)(2,1)S(1)}, bf16[272,512]{1,0:T(8,128)(2,1)S(1)}, u32[]{:S(2)}, u32[]{:S(2)}) collective-permute-start(bf16[272,512]{1,0:T(8,128)(2,1)S(1)} %collective-permute-done.4.refs_4_), channel_id=1, source_target_pairs={{0,16},{16,0},{1,17},{17,1},{2,18},{18,2},{3,19},{19,3},{4,20},{20... | collective-permute-start | bytes 835592 | tf_op jit(solution)/shard_map/ppermute | solution.py:981
  59.3 13.5 %collective-permute-start.1 = (bf16[272,512]{1,0:T(8,128)(2,1)S(1)}, bf16[272,512]{1,0:T(8,128)(2,1)S(1)}, u32[]{:S(2)}, u32[]{:S(2)}) collective-permute-start(bf16[272,512]{1,0:T(8,128)(2,1)S(1)} %collective-permute-done.refs_0_), channel_id=1, source_target_pairs={{0,16},{16,0},{1,17},{17,1},{2,18},{18,2},{3,19},{19,3},{4,20},{20... | collective-permute-start | bytes 835592 | tf_op jit(solution)/shard_map/ppermute | solution.py:981
  59.8 13.0 %copy-start.3 = (f32[2,1024]{1,0:T(2,128)S(1)}, f32[2,1024]{1,0:T(2,128)}, u32[]{:S(2)}) copy-start(f32[2,1024]{1,0:T(2,128)} %param.22) | copy-start | bytes 24580
  59.8 13.6 %copy-start.5 = (f32[2,1024]{1,0:T(2,128)S(1)}, f32[2,1024]{1,0:T(2,128)}, u32[]{:S(2)}) copy-start(f32[2,1024]{1,0:T(2,128)} %param.23) | copy-start | bytes 24580
  59.8 13.6 %copy-start.6 = (f32[2,1024]{1,0:T(2,128)S(1)}, f32[2,1024]{1,0:T(2,128)}, u32[]{:S(2)}) copy-start(f32[2,1024]{1,0:T(2,128)} %param.21) | copy-start | bytes 24580
  63.9 11.8 %copy-start.34 = (bf16[272,512]{1,0:T(8,128)(2,1)}, bf16[272,512]{1,0:T(8,128)(2,1)S(1)}, u32[]{:S(2)}) copy-start(bf16[272,512]{1,0:T(8,128)(2,1)S(1)} %collective-permute-done.9.refs_9_) | copy-start | bytes 835588
  63.9 10.2 %collective-permute-start.2 = (bf16[272,512]{1,0:T(8,128)(2,1)S(1)}, bf16[272,512]{1,0:T(8,128)(2,1)S(1)}, u32[]{:S(2)}, u32[]{:S(2)}) collective-permute-start(bf16[272,512]{1,0:T(8,128)(2,1)S(1)} %collective-permute-done.refs_0_), channel_id=1, source_target_pairs={{0,4},{4,0},{1,5},{5,1},{2,6},{6,2},{3,7},{7,3},{8,12},{12,8},{9,1... | collective-permute-start | bytes 835592 | tf_op jit(solution)/shard_map/ppermute | solution.py:981
  64.0 11.7 %copy-start.35 = (bf16[272,512]{1,0:T(8,128)(2,1)}, bf16[272,512]{1,0:T(8,128)(2,1)S(1)}, u32[]{:S(2)}) copy-start(bf16[272,512]{1,0:T(8,128)(2,1)S(1)} %collective-permute-done.6.refs_6_) | copy-start | bytes 835588
  64.0 11.7 %collective-permute-start.11 = (bf16[272,512]{1,0:T(8,128)(2,1)S(1)}, bf16[272,512]{1,0:T(8,128)(2,1)S(1)}, u32[]{:S(2)}, u32[]{:S(2)}) collective-permute-start(bf16[272,512]{1,0:T(8,128)(2,1)S(1)} %collective-permute-done.9.refs_9_), channel_id=1, source_target_pairs={{0,4},{4,0},{1,5},{5,1},{2,6},{6,2},{3,7},{7,3},{8,12},{12,8},{9,1... | collective-permute-start | bytes 835592 | tf_op jit(solution)/shard_map/ppermute | solution.py:981
  67.3 8.4 %collective-permute-start.7 = (bf16[272,512]{1,0:T(8,128)(2,1)S(1)}, bf16[272,512]{1,0:T(8,128)(2,1)S(1)}, u32[]{:S(2)}, u32[]{:S(2)}) collective-permute-start(bf16[272,512]{1,0:T(8,128)(2,1)S(1)} %collective-permute-done.5.refs_5_), channel_id=1, source_target_pairs={{0,4},{4,0},{1,5},{5,1},{2,6},{6,2},{3,7},{7,3},{8,12},{12,8},{9,1... | collective-permute-start | bytes 835592 | tf_op jit(solution)/shard_map/ppermute | solution.py:981
  72.8 2.9 collective-permute-start.3
  74.1 37.1 %collective-permute-start.14 = (bf16[304,1024]{1,0:T(8,128)(2,1)}, bf16[304,1024]{1,0:T(8,128)(2,1)S(1)}, u32[]{:S(2)}, u32[]{:S(2)}) collective-permute-start(bf16[304,1024]{1,0:T(8,128)(2,1)} %get-tuple-element.130.g_ref.x2_own), channel_id=1, source_target_pairs={{0,8},{8,0},{1,9},{9,1},{2,10},{10,2},{3,11},{11,3},{4,12},{12,4},... | collective-permute-start | bytes 1867784 | tf_op jit(solution)/shard_map/ppermute | solution.py:981
  86.4 17.6 %collective-permute-start.13 = (bf16[304,1024]{1,0:T(8,128)(2,1)}, bf16[304,1024]{1,0:T(8,128)(2,1)S(1)}, u32[]{:S(2)}, u32[]{:S(2)}) collective-permute-start(bf16[304,1024]{1,0:T(8,128)(2,1)} %get-tuple-element.127), channel_id=1, source_target_pairs={{0,8},{8,0},{1,9},{9,1},{2,10},{10,2},{3,11},{11,3},{4,12},{12,4},... | collective-permute-start | bytes 1867784 | tf_op jit(solution)/shard_map/ppermute | solution.py:981
  109.0 16.0 %collective-permute-start.15 = (bf16[304,1024]{1,0:T(8,128)(2,1)}, bf16[304,1024]{1,0:T(8,128)(2,1)S(1)}, u32[]{:S(2)}, u32[]{:S(2)}) collective-permute-start(bf16[304,1024]{1,0:T(8,128)(2,1)} %get-tuple-element.131.a_ref.x1_own), channel_id=1, source_target_pairs={{0,8},{8,0},{1,9},{9,1},{2,10},{10,2},{3,11},{11,3},{4,12},{12,4},... | collective-permute-start | bytes 1867784 | tf_op jit(solution)/shard_map/ppermute | solution.py:981
  111.2 32.2 %copy-start.19 = (bf16[304,1024]{1,0:T(8,128)(2,1)}, bf16[304,1024]{1,0:T(8,128)(2,1)S(1)}, u32[]{:S(2)}) copy-start(bf16[304,1024]{1,0:T(8,128)(2,1)S(1)} %collective-permute-done.14.g_ref.x2_far) | copy-start | bytes 1867780
  143.4 16.5 %collective-permute-start.16 = (bf16[304,1024]{1,0:T(8,128)(2,1)}, bf16[304,1024]{1,0:T(8,128)(2,1)S(1)}, u32[]{:S(2)}, u32[]{:S(2)}) collective-permute-start(bf16[304,1024]{1,0:T(8,128)(2,1)} %get-tuple-element.134), channel_id=1, source_target_pairs={{0,8},{8,0},{1,9},{9,1},{2,10},{10,2},{3,11},{11,3},{4,12},{12,4},... | collective-permute-start | bytes 1867784 | tf_op jit(solution)/shard_map/ppermute | solution.py:981
  164.8 15.8 %collective-permute-start.17 = (bf16[304,1024]{1,0:T(8,128)(2,1)}, bf16[304,1024]{1,0:T(8,128)(2,1)S(1)}, u32[]{:S(2)}, u32[]{:S(2)}) collective-permute-start(bf16[304,1024]{1,0:T(8,128)(2,1)} %get-tuple-element.136.a_ref.x1_own), channel_id=1, source_target_pairs={{0,8},{8,0},{1,9},{9,1},{2,10},{10,2},{3,11},{11,3},{4,12},{12,4},... | collective-permute-start | bytes 1867784 | tf_op jit(solution)/shard_map/ppermute | solution.py:981
  189.4 15.0 %collective-permute-start.18 = (bf16[304,1024]{1,0:T(8,128)(2,1)}, bf16[304,1024]{1,0:T(8,128)(2,1)S(1)}, u32[]{:S(2)}, u32[]{:S(2)}) collective-permute-start(bf16[304,1024]{1,0:T(8,128)(2,1)} %get-tuple-element.138), channel_id=1, source_target_pairs={{0,8},{8,0},{1,9},{9,1},{2,10},{10,2},{3,11},{11,3},{4,12},{12,4},... | collective-permute-start | bytes 1867784 | tf_op jit(solution)/shard_map/ppermute | solution.py:981
  209.3 14.2 %collective-permute-start.19 = (bf16[304,1024]{1,0:T(8,128)(2,1)}, bf16[304,1024]{1,0:T(8,128)(2,1)S(1)}, u32[]{:S(2)}, u32[]{:S(2)}) collective-permute-start(bf16[304,1024]{1,0:T(8,128)(2,1)} %get-tuple-element.140.a_ref.x1_own), channel_id=1, source_target_pairs={{0,8},{8,0},{1,9},{9,1},{2,10},{10,2},{3,11},{11,3},{4,12},{12,4},... | collective-permute-start | bytes 1867784 | tf_op jit(solution)/shard_map/ppermute | solution.py:981
  235.3 16.5 %collective-permute-start.20 = (bf16[304,1024]{1,0:T(8,128)(2,1)}, bf16[304,1024]{1,0:T(8,128)(2,1)S(1)}, u32[]{:S(2)}, u32[]{:S(2)}) collective-permute-start(bf16[304,1024]{1,0:T(8,128)(2,1)} %get-tuple-element.147), channel_id=1, source_target_pairs={{0,8},{8,0},{1,9},{9,1},{2,10},{10,2},{3,11},{11,3},{4,12},{12,4},... | collective-permute-start | bytes 1867784 | tf_op jit(solution)/shard_map/ppermute | solution.py:981
  249.5 191.7 %all-gather.11.cloned.1.call-start = ((), (), s32[]{:S(2)}) async-start(), calls=%async_computation.10 | async-start | bytes 3112960 | tf_op jit(solution)/shard_map/all_gather | solution.py:1116
  257.9 16.3 %collective-permute-start.22 = (bf16[304,1024]{1,0:T(8,128)(2,1)}, bf16[304,1024]{1,0:T(8,128)(2,1)S(1)}, u32[]{:S(2)}, u32[]{:S(2)}) collective-permute-start(bf16[304,1024]{1,0:T(8,128)(2,1)} %get-tuple-element.148.g_ref.x2_own), channel_id=1, source_target_pairs={{0,8},{8,0},{1,9},{9,1},{2,10},{10,2},{3,11},{11,3},{4,12},{12,4},... | collective-permute-start | bytes 1867784 | tf_op jit(solution)/shard_map/ppermute | solution.py:981
  259.6 11.4 %copy-start.21 = (bf16[304,1024]{1,0:T(8,128)(2,1)S(1)}, bf16[304,1024]{1,0:T(8,128)(2,1)}, u32[]{:S(2)}) copy-start(bf16[304,1024]{1,0:T(8,128)(2,1)} %get-tuple-element.152) | copy-start | bytes 1867780
  271.0 25.6 %collective-permute-start.21 = (bf16[304,1024]{1,0:T(8,128)(2,1)S(1)}, bf16[304,1024]{1,0:T(8,128)(2,1)}, u32[]{:S(2)}, u32[]{:S(2)}) collective-permute-start(bf16[304,1024]{1,0:T(8,128)(2,1)S(1)} %copy-done.21), channel_id=1, source_target_pairs={{0,8},{8,0},{1,9},{9,1},{2,10},{10,2},{3,11},{11,3},{4,12},{12,4},... | collective-permute-start | bytes 1867784 | tf_op jit(solution)/shard_map/ppermute | solution.py:981
  286.1 14.2 %collective-permute-start.23 = (bf16[304,1024]{1,0:T(8,128)(2,1)}, bf16[304,1024]{1,0:T(8,128)(2,1)S(1)}, u32[]{:S(2)}, u32[]{:S(2)}) collective-permute-start(bf16[304,1024]{1,0:T(8,128)(2,1)} %get-tuple-element.162), channel_id=1, source_target_pairs={{0,8},{8,0},{1,9},{9,1},{2,10},{10,2},{3,11},{11,3},{4,12},{12,4},... | collective-permute-start | bytes 1867784 | tf_op jit(solution)/shard_map/ppermute | solution.py:981
  296.5 18.3 %collective-permute-start.25 = (bf16[2,4,256,512]{3,2,1,0:T(8,128)(2,1)}, bf16[2,4,256,512]{3,2,1,0:T(8,128)(2,1)S(1)}, u32[]{:S(2)}, u32[]{:S(2)}) collective-permute-start(bf16[2,4,256,512]{3,2,1,0:T(8,128)(2,1)} %shard_map.267), channel_id=1, source_target_pairs={{0,4},{4,0},{1,5},{5,1},{2,6},{6,2},{3,7},{7,3},{8,12},{12,8},{9,1... | collective-permute-start | bytes 6291464 | tf_op jit(solution)/shard_map/ppermute | solution.py:981
  306.1 16.7 %collective-permute-start.24 = (bf16[304,1024]{1,0:T(8,128)(2,1)}, bf16[304,1024]{1,0:T(8,128)(2,1)S(1)}, u32[]{:S(2)}, u32[]{:S(2)}) collective-permute-start(bf16[304,1024]{1,0:T(8,128)(2,1)} %get-tuple-element.164.g_ref.x2_own), channel_id=1, source_target_pairs={{0,8},{8,0},{1,9},{9,1},{2,10},{10,2},{3,11},{11,3},{4,12},{12,4},... | collective-permute-start | bytes 1867784 | tf_op jit(solution)/shard_map/ppermute | solution.py:981
  322.5 47.1 %collective-permute-start.27 = (bf16[4,256,512]{2,1,0:T(8,128)(2,1)}, bf16[4,256,512]{2,1,0:T(8,128)(2,1)S(1)}, u32[]{:S(2)}, u32[]{:S(2)}) collective-permute-start(bf16[4,256,512]{2,1,0:T(8,128)(2,1)} %shard_map.268), channel_id=1, source_target_pairs={{0,16},{16,0},{1,17},{17,1},{2,18},{18,2},{3,19},{19,3},{4,20},{20... | collective-permute-start | bytes 3145736 | tf_op jit(solution)/shard_map/ppermute | solution.py:981
  331.2 16.0 %collective-permute-start.26 = (bf16[304,1024]{1,0:T(8,128)(2,1)}, bf16[304,1024]{1,0:T(8,128)(2,1)S(1)}, u32[]{:S(2)}, u32[]{:S(2)}) collective-permute-start(bf16[304,1024]{1,0:T(8,128)(2,1)} %get-tuple-element.172), channel_id=1, source_target_pairs={{0,8},{8,0},{1,9},{9,1},{2,10},{10,2},{3,11},{11,3},{4,12},{12,4},... | collective-permute-start | bytes 1867784 | tf_op jit(solution)/shard_map/ppermute | solution.py:981
  341.9 35.5 %collective-permute-start.29 = (bf16[2,4,256,1024]{3,2,1,0:T(8,128)(2,1)}, bf16[2,4,256,1024]{3,2,1,0:T(8,128)(2,1)}, u32[]{:S(2)}, u32[]{:S(2)}) collective-permute-start(bf16[2,4,256,1024]{3,2,1,0:T(8,128)(2,1)} %shard_map.273), channel_id=1, source_target_pairs={{0,4},{4,0},{1,5},{5,1},{2,6},{6,2},{3,7},{7,3},{8,12},{12,8},{9,1... | collective-permute-start | bytes 12582920 | tf_op jit(solution)/shard_map/ppermute | solution.py:981
  353.1 32.5 %collective-permute-start.28 = (bf16[304,1024]{1,0:T(8,128)(2,1)}, bf16[304,1024]{1,0:T(8,128)(2,1)S(1)}, u32[]{:S(2)}, u32[]{:S(2)}) collective-permute-start(bf16[304,1024]{1,0:T(8,128)(2,1)} %get-tuple-element.175.g_ref.x2_own), channel_id=1, source_target_pairs={{0,8},{8,0},{1,9},{9,1},{2,10},{10,2},{3,11},{11,3},{4,12},{12,4},... | collective-permute-start | bytes 1867784 | tf_op jit(solution)/shard_map/ppermute | solution.py:981
  357.4 130.7 %reduce-scatter.11.cloned.1.call-start = ((), (), s32[]{:S(2)}) async-start(), calls=%async_computation.7 | async-start | bytes 1310720 | tf_op jit(solution)/shard_map/reduce_scatter | solution.py:1065
  376.9 150.6 %reduce-scatter.9.cloned.1.call-start = ((), (), s32[]{:S(2)}) async-start(), calls=%async_computation.6 | async-start | bytes 2621440 | tf_op jit(solution)/shard_map/reduce_scatter | solution.py:1065
  385.0 47.9 %collective-permute-start.34 = (bf16[4,256,1024]{2,1,0:T(8,128)(2,1)}, bf16[4,256,1024]{2,1,0:T(8,128)(2,1)}, u32[]{:S(2)}, u32[]{:S(2)}) collective-permute-start(bf16[4,256,1024]{2,1,0:T(8,128)(2,1)} %shard_map.274), channel_id=1, source_target_pairs={{0,16},{16,0},{1,17},{17,1},{2,18},{18,2},{3,19},{19,3},{4,20},{20... | collective-permute-start | bytes 6291464 | tf_op jit(solution)/shard_map/ppermute | solution.py:981
  398.5 14.9 %collective-permute-start.30 = (bf16[304,1024]{1,0:T(8,128)(2,1)}, bf16[304,1024]{1,0:T(8,128)(2,1)S(1)}, u32[]{:S(2)}, u32[]{:S(2)}) collective-permute-start(bf16[304,1024]{1,0:T(8,128)(2,1)} %get-tuple-element.186), channel_id=1, source_target_pairs={{0,8},{8,0},{1,9},{9,1},{2,10},{10,2},{3,11},{11,3},{4,12},{12,4},... | collective-permute-start | bytes 1867784 | tf_op jit(solution)/shard_map/ppermute | solution.py:981
  408.1 15.7 %collective-permute-start.32 = (bf16[2,4,256,512]{3,2,1,0:T(8,128)(2,1)}, bf16[2,4,256,512]{3,2,1,0:T(8,128)(2,1)S(1)}, u32[]{:S(2)}, u32[]{:S(2)}) collective-permute-start(bf16[2,4,256,512]{3,2,1,0:T(8,128)(2,1)} %shard_map.277), channel_id=1, source_target_pairs={{0,4},{4,0},{1,5},{5,1},{2,6},{6,2},{3,7},{7,3},{8,12},{12,8},{9,1... | collective-permute-start | bytes 6291464 | tf_op jit(solution)/shard_map/ppermute | solution.py:981
  419.2 43.3 %collective-permute-start.36 = (bf16[304,1024]{1,0:T(8,128)(2,1)}, bf16[304,1024]{1,0:T(8,128)(2,1)S(1)}, u32[]{:S(2)}, u32[]{:S(2)}) collective-permute-start(bf16[304,1024]{1,0:T(8,128)(2,1)} %get-tuple-element.187.refs_0_), channel_id=1, source_target_pairs={{0,2},{1,3},{2,0},{3,1},{4,6},{5,7},{6,4},{7,5},{8,10},{9,11},{10,... | collective-permute-start | bytes 1867784 | tf_op jit(solution)/shard_map/ppermute | solution.py:984
  419.9 42.6 %collective-permute-start.35 = (bf16[304,1024]{1,0:T(8,128)(2,1)}, bf16[304,1024]{1,0:T(8,128)(2,1)S(1)}, u32[]{:S(2)}, u32[]{:S(2)}) collective-permute-start(bf16[304,1024]{1,0:T(8,128)(2,1)} %get-tuple-element.187.refs_0_), channel_id=1, source_target_pairs={{0,3},{1,0},{2,1},{3,2},{4,7},{5,4},{6,5},{7,6},{8,11},{9,8},{10,9... | collective-permute-start | bytes 1867784 | tf_op jit(solution)/shard_map/ppermute | solution.py:984
  421.2 56.6 %collective-permute-start.31 = (bf16[304,1024]{1,0:T(8,128)(2,1)}, bf16[304,1024]{1,0:T(8,128)(2,1)S(1)}, u32[]{:S(2)}, u32[]{:S(2)}) collective-permute-start(bf16[304,1024]{1,0:T(8,128)(2,1)} %get-tuple-element.187.refs_0_), channel_id=1, source_target_pairs={{0,1},{1,2},{2,3},{3,0},{4,5},{5,6},{6,7},{7,4},{8,9},{9,10},{10,1... | collective-permute-start | bytes 1867784 | tf_op jit(solution)/shard_map/ppermute | solution.py:984
  431.4 46.4 %collective-permute-start.33 = (bf16[4,256,512]{2,1,0:T(8,128)(2,1)}, bf16[4,256,512]{2,1,0:T(8,128)(2,1)S(1)}, u32[]{:S(2)}, u32[]{:S(2)}) collective-permute-start(bf16[4,256,512]{2,1,0:T(8,128)(2,1)} %shard_map.278), channel_id=1, source_target_pairs={{0,16},{16,0},{1,17},{17,1},{2,18},{18,2},{3,19},{19,3},{4,20},{20... | collective-permute-start | bytes 3145736 | tf_op jit(solution)/shard_map/ppermute | solution.py:981
  440.9 116.0 %reduce-scatter.7.cloned.1.call-start = ((), (), s32[]{:S(2)}) async-start(), calls=%async_computation.5 | async-start | bytes 1310720 | tf_op jit(solution)/shard_map/reduce_scatter | solution.py:1065
  450.1 35.1 %copy-start = (f32[24,1024]{1,0:T(8,128)S(1)}, f32[24,1024]{1,0:T(8,128)}, u32[]{:S(2)}) copy-start(f32[24,1024]{1,0:T(8,128)} %shard_map.282) | copy-start | bytes 294916
  462.5 22.6 %copy-start.16 = (bf16[304,1024]{1,0:T(8,128)(2,1)}, bf16[304,1024]{1,0:T(8,128)(2,1)S(1)}, u32[]{:S(2)}) copy-start(bf16[304,1024]{1,0:T(8,128)(2,1)S(1)} %collective-permute-done.36.refs_3_) | copy-start | bytes 1867780
  462.5 22.6 %copy-start.17 = (bf16[304,1024]{1,0:T(8,128)(2,1)}, bf16[304,1024]{1,0:T(8,128)(2,1)S(1)}, u32[]{:S(2)}) copy-start(bf16[304,1024]{1,0:T(8,128)(2,1)S(1)} %collective-permute-done.35.refs_2_) | copy-start | bytes 1867780
  485.2 1.4 collective-permute-start.37
  486.6 4.9 collective-permute-start.38
  489.9 71.8 %collective-permute-start.44 = (bf16[128,512]{1,0:T(8,128)(2,1)}, bf16[128,512]{1,0:T(8,128)(2,1)S(1)}, u32[]{:S(2)}, u32[]{:S(2)}) collective-permute-start(bf16[128,512]{1,0:T(8,128)(2,1)} %get-tuple-element.219), channel_id=1, source_target_pairs={{0,8},{8,0},{1,9},{9,1},{2,10},{10,2},{3,11},{11,3},{4,12},{12,4},... | collective-permute-start | bytes 393224 | tf_op jit(solution)/shard_map/ppermute | solution.py:981
  491.5 5.1 collective-permute-start.39
  494.7 66.9 %collective-permute-start.45 = (bf16[128,1024]{1,0:T(8,128)(2,1)}, bf16[128,1024]{1,0:T(8,128)(2,1)S(1)}, u32[]{:S(2)}, u32[]{:S(2)}) collective-permute-start(bf16[128,1024]{1,0:T(8,128)(2,1)} %get-tuple-element.221), channel_id=1, source_target_pairs={{0,8},{8,0},{1,9},{9,1},{2,10},{10,2},{3,11},{11,3},{4,12},{12,4},... | collective-permute-start | bytes 786440 | tf_op jit(solution)/shard_map/ppermute | solution.py:981
  496.6 34.4 %collective-permute-start.40 = (f32[24,1024]{1,0:T(8,128)S(1)}, f32[24,1024]{1,0:T(8,128)S(1)}, u32[]{:S(2)}, u32[]{:S(2)}) collective-permute-start(f32[24,1024]{1,0:T(8,128)S(1)} %add.41), channel_id=1, source_target_pairs={{0,1},{1,0},{2,3},{3,2},{4,5},{5,4},{6,7},{7,6},{8,9},{9,8},{10,11... | collective-permute-start | bytes 294920 | tf_op jit(solution)/shard_map/ppermute | solution.py:1134
  529.5 32.2 %collective-permute-start.43 = (bf16[128,1024]{1,0:T(8,128)(2,1)}, bf16[128,1024]{1,0:T(8,128)(2,1)S(1)}, u32[]{:S(2)}, u32[]{:S(2)}) collective-permute-start(bf16[128,1024]{1,0:T(8,128)(2,1)} %get-tuple-element.217), channel_id=1, source_target_pairs={{0,8},{8,0},{1,9},{9,1},{2,10},{10,2},{3,11},{11,3},{4,12},{12,4},... | collective-permute-start | bytes 786440 | tf_op jit(solution)/shard_map/ppermute | solution.py:981
  531.0 11.3 %collective-permute-start.41 = (f32[24,1024]{1,0:T(8,128)S(1)}, f32[24,1024]{1,0:T(8,128)S(1)}, u32[]{:S(2)}, u32[]{:S(2)}) collective-permute-start(f32[24,1024]{1,0:T(8,128)S(1)} %add.42), channel_id=1, source_target_pairs={{0,2},{1,3},{2,0},{3,1},{4,6},{5,7},{6,4},{7,5},{8,10},{9,11},{10,... | collective-permute-start | bytes 294920 | tf_op jit(solution)/shard_map/ppermute | solution.py:1134
  558.6 5.3 collective-permute-start.42
  (35 other events, 93.1 us)
Sparse Core Ops, SparseCore 0:
  11.7 122.9 all-gather.6
  136.9 75.7 all-gather.8
  249.6 107.7 reduce-scatter.4
  358.8 51.0 all-gather.10
  412.0 66.8 reduce-scatter.10
  481.2 46.3 reduce-scatter.8
  531.1 25.7 reduce-scatter.6

commit v6 on v5

--- a/solution.py
+++ b/solution.py
@@ -784,12 +784,9 @@
             ).start()
     for copy in copies:
         copy.wait()
-    for slot in range(len(slots)):
-        for index in range(2):
-            turned[index, slot] = xs[index, slot].T
     span1 = y1.shape[2]
 
-    def chunk_step(chunk, carry):
+    def chunk_step(chunk):
         for index, target in enumerate((y1, y1, y2, y2)):
             half = target.at[chunk, pl.ds(ROWS * (index % 2), ROWS)]
             pltpu.make_async_copy(half, half, sems.at[chunk, index]).wait()
@@ -797,6 +794,9 @@
             array = added.at[index, chunk]
             pltpu.make_async_copy(array, array, sems.at[chunk, 4 + index]).wait()
         for slot, out in enumerate(outs):
+            if chunk == 0:
+                for index in range(2):
+                    turned[index, slot] = xs[index, slot].T
             first = dot_nn(turned[0, slot], y1[chunk])
             second = dot_nn(turned[1, slot], y2[chunk])
             for index in range(len(got)):
@@ -808,9 +808,9 @@
                 pltpu.make_async_copy(
                     out.at[chunk], whole.at[slot, chunk], sems.at[chunk, 8 + slot]
                 ).start()
-        return carry
-
-    lax.fori_loop(0, 4, chunk_step, 0, unroll=True)
+
+    for chunk in range(4):
+        chunk_step(chunk)
     if stage == ALL:
         for chunk in range(4):
             for slot, out in enumerate(outs):
@@ -937,9 +937,9 @@
                 qkv[layer, item, :, pl.ds(narrow, 128)] = attn[
                     :, item * 128 : item * 128 + 128
                 ].astype(F32)
-            proj[layer, pl.ds(narrow, 128), :] = attn[:, 384:512].astype(F32).T
+            proj[layer, pl.ds(narrow, 128), :] = attn[:, 384:512].T.astype(F32)
             fc1[layer, :, pl.ds(wide, 512)] = mlp[:, 0:512].astype(F32)
-            fc2[layer, pl.ds(wide, 512), :] = mlp[:, 512:1024].astype(F32).T
+            fc2[layer, pl.ds(wide, 512), :] = mlp[:, 512:1024].T.astype(F32)
 
 
 def run_finish(place, parts):

time: 586 us -> 586 us (level)
  transfers between devices with their start and end apart: 53 -> 53, of which waited for: 24 -> 25; matrix products, arithmetic and copies ran while one was open for 1% -> 1% of each run, Pallas kernels for 48% -> 48%
where the time goes in v6:
time: 586 us; the launch traced here: 574 us
  Pallas kernels  295 us (50%)
  waiting for transfers between devices  182 us (31%)
  starting transfers between devices  60.9 us (10%)
  local copies, waits for them, and re-layouts  20.7 us (4%)
  between operations  15 us (3%)
    pallas_call x10, Pallas kernels, run_weight_grad(): pl.pallas_call(functools.partial(weight_grad_kernel, stage), out_shape=ja...  79.6 us
    ppermute x38, waiting for transfers between devices, swap(): return lax.ppermute(value, axis, [(0, 1), (1, 0)])  76.6 us
    ppermute x6, waiting for transfers between devices, shift(): lax.ppermute(value, 'mp', [(index, (index + step) % n_mp) for index in ra...  59.5 us
    pallas_call x4, Pallas kernels, run_attention_backward(): pl.pallas_call(functools.partial(attention_backward_kernel, layer, len(pi...  46.6 us
    ppermute x38, starting transfers between devices, swap(): return lax.ppermute(value, axis, [(0, 1), (1, 0)])  36.8 us
    pallas_call x4, Pallas kernels, run_attention_forward(): pl.pallas_call(functools.partial(attention_forward_kernel, layer, len(pie...  34.5 us
    reduce_scatter x3, waiting for transfers between devices, near(): self.total = lax.psum_scatter(flat, 'mp', tiled=True)  32.1 us
    pallas_call x2, Pallas kernels, run_mlp_both(): pl.pallas_call(mlp_both_kernel, out_shape=(jax.ShapeDtypeStruct((4, ROWS,...  21.6 us
  transfers between devices with their start and end apart: 53, of which 25 were waited for; matrix products, arithmetic and copies ran while one was open for 1% of the time, Pallas kernels for 48%

profile of v6, /device:TPU:0, one launch (start us, length us, event | category | flops | bytes accessed | tf_op | source)
XLA Modules:
  0.0 574.4 jit_solution(17861123380857226247)
XLA Ops:
  7.9 3.6 shard_map.246
  11.6 5.1 collective-permute-start.8
  18.9 5.5 collective-permute-done.8.refs_8_
  24.4 4.1 shard_map.245
  31.4 26.3 %collective-permute-done.4.refs_4_ = bf16[272,512]{1,0:T(8,128)(2,1)S(1)} collective-permute-done((bf16[272,512]{1,0:T(8,128)(2,1)}, bf16[272,512]{1,0:T(8,128)(2,1)S(1)}, u32[]{:S(2)}, u32[]{:S(2)}) %collective-permute-start.4) | collective-permute-done | bytes 278560 | tf_op jit(solution)/shard_map/ppermute | solution.py:984
  59.8 4.0 shard_map.250
  64.4 2.8 collective-permute-done.5.refs_5_
  67.3 5.5 collective-permute-done.1.refs_1_
  77.4 9.1 %shard_map.248 = (bf16[4,304,384]{2,1,0:T(8,128)(2,1)}, bf16[4,3,224,112]{3,2,1,0:T(8,128)(2,1)}, bf16[4,304,128]{2,1,0:T(8,128)(2,1)}, bf16[304,1024]{1,0:T(8,128)(2,1)}) custom-call(s32[8]{0:T(128)} %stack.35.place, bf16[304,1024]{1,0:T(8,128)(2,1)} %copy-done.11, bf16[2,3,1024,256]{3,2,1,0:T(8,128)(2,1)} %bitcast.44, bf16[2,256,1024]{2,1,0:T(8,128)(2,1)} %wproj.17, ...), custom_call_target="tpu_custom_call" | custom-call | flops 28000000000 | tf_op jit(solution)/shard_map/pallas_call | solution.py:492
  87.0 9.0 %shard_map.247 = (bf16[4,304,384]{2,1,0:T(8,128)(2,1)}, bf16[4,3,224,112]{3,2,1,0:T(8,128)(2,1)}, bf16[4,304,128]{2,1,0:T(8,128)(2,1)}, bf16[304,1024]{1,0:T(8,128)(2,1)}) custom-call(s32[8]{0:T(128)} %stack.35.place, bf16[304,1024]{1,0:T(8,128)(2,1)} %get-tuple-element.124.a_ref.x1_own, bf16[2,3,1024,256]{3,2,1,0:T(8,128)(2,1)} %bitcast.45, ...), custom_call_target="tpu_custom_call" | custom-call | flops 28000000000 | tf_op jit(solution)/shard_map/pallas_call | solution.py:492
  96.1 8.0 %collective-permute-done.13.far_ref = bf16[304,1024]{1,0:T(8,128)(2,1)S(1)} collective-permute-done((bf16[304,1024]{1,0:T(8,128)(2,1)}, bf16[304,1024]{1,0:T(8,128)(2,1)S(1)}, u32[]{:S(2)}, u32[]{:S(2)}) %collective-permute-start.13) | collective-permute-done | bytes 622624 | tf_op jit(solution)/shard_map/ppermute | solution.py:981
  104.9 4.1 shard_map.249
  111.2 13.8 %collective-permute-done.15.a_ref.x1_far = bf16[304,1024]{1,0:T(8,128)(2,1)S(1)} collective-permute-done((bf16[304,1024]{1,0:T(8,128)(2,1)}, bf16[304,1024]{1,0:T(8,128)(2,1)S(1)}, u32[]{:S(2)}, u32[]{:S(2)}) %collective-permute-start.15) | collective-permute-done | bytes 622624 | tf_op jit(solution)/shard_map/ppermute | solution.py:981
  125.0 9.6 %all-gather.7.cloned.1.call-done = bf16[12800,512]{1,0:T(8,128)(2,1)} async-done(((bf16[800,512]{1,0:T(8,128)(2,1)}), bf16[12800,512]{1,0:T(8,128)(2,1)}) %all-gather.7.cloned.1.call-update) | async-done | bytes 13107216 | tf_op jit(solution)/shard_map/all_gather | solution.py:1007
  134.6 8.6 %shard_map.252 = (bf16[4,304,512]{2,1,0:T(8,128)(2,1)}, bf16[4,304,512]{2,1,0:T(8,128)(2,1)}, bf16[304,1024]{1,0:T(8,128)(2,1)}) custom-call(bf16[304,1024]{1,0:T(8,128)(2,1)} %copy-done.12, bf16[2,2,4,800,512]{4,3,2,1,0:T(8,128)(2,1)} %bitcast.33), custom_call_target="tpu_custom_call" | custom-call | flops 32000000000 | tf_op jit(solution)/shard_map/pallas_call | solution.py:617
  144.8 8.5 %shard_map.251 = (bf16[4,304,512]{2,1,0:T(8,128)(2,1)}, bf16[4,304,512]{2,1,0:T(8,128)(2,1)}, bf16[304,1024]{1,0:T(8,128)(2,1)}) custom-call(bf16[304,1024]{1,0:T(8,128)(2,1)} %get-tuple-element.131.a_ref.x1_own, bf16[2,2,4,800,512]{4,3,2,1,0:T(8,128)(2,1)} %bitcast.34), custom_call_target="tpu_custom_call" | custom-call | flops 32000000000 | tf_op jit(solution)/shard_map/pallas_call | solution.py:617
  153.3 6.4 %collective-permute-done.16.far_ref = bf16[304,1024]{1,0:T(8,128)(2,1)S(1)} collective-permute-done((bf16[304,1024]{1,0:T(8,128)(2,1)}, bf16[304,1024]{1,0:T(8,128)(2,1)S(1)}, u32[]{:S(2)}, u32[]{:S(2)}) %collective-permute-start.16) | collective-permute-done | bytes 622624 | tf_op jit(solution)/shard_map/ppermute | solution.py:981
  160.5 4.1 shard_map.253
  166.1 14.2 %collective-permute-done.17.a_ref.x1_far = bf16[304,1024]{1,0:T(8,128)(2,1)S(1)} collective-permute-done((bf16[304,1024]{1,0:T(8,128)(2,1)}, bf16[304,1024]{1,0:T(8,128)(2,1)S(1)}, u32[]{:S(2)}, u32[]{:S(2)}) %collective-permute-start.17) | collective-permute-done | bytes 622624 | tf_op jit(solution)/shard_map/ppermute | solution.py:981
  181.2 8.0 %shard_map.255 = (bf16[4,304,384]{2,1,0:T(8,128)(2,1)}, bf16[4,3,224,112]{3,2,1,0:T(8,128)(2,1)}, bf16[4,304,128]{2,1,0:T(8,128)(2,1)}, bf16[304,1024]{1,0:T(8,128)(2,1)}) custom-call(s32[8]{0:T(128)} %stack.35.place, bf16[304,1024]{1,0:T(8,128)(2,1)} %copy-done.13, bf16[2,3,1024,256]{3,2,1,0:T(8,128)(2,1)} %bitcast.46, bf16[2,256,1024]{2,1,0:T(8,128)(2,1)} %wproj.17, ...), custom_call_target="tpu_custom_call" | custom-call | flops 28000000000 | tf_op jit(solution)/shard_map/pallas_call | solution.py:492
  190.7 8.4 %shard_map.254 = (bf16[4,304,384]{2,1,0:T(8,128)(2,1)}, bf16[4,3,224,112]{3,2,1,0:T(8,128)(2,1)}, bf16[4,304,128]{2,1,0:T(8,128)(2,1)}, bf16[304,1024]{1,0:T(8,128)(2,1)}) custom-call(s32[8]{0:T(128)} %stack.35.place, bf16[304,1024]{1,0:T(8,128)(2,1)} %get-tuple-element.136.a_ref.x1_own, bf16[2,3,1024,256]{3,2,1,0:T(8,128)(2,1)} %bitcast.47, ...), custom_call_target="tpu_custom_call" | custom-call | flops 28000000000 | tf_op jit(solution)/shard_map/pallas_call | solution.py:492
  199.1 5.0 collective-permute-done.18.far_ref
  205.0 4.2 shard_map.256
  210.7 2.0 all-gather.9.cloned.1.call-done
  212.7 10.8 %shard_map.257 = (bf16[4,304,512]{2,1,0:T(8,128)(2,1)}, bf16[304,1024]{1,0:T(8,128)(2,1)}, bf16[4,304,512]{2,1,0:T(8,128)(2,1)}, f32[4,8,512]{2,1,0:T(8,128)}, bf16[304,1024]{1,0:T(8,128)(2,1)}) custom-call(bf16[304,1024]{1,0:T(8,128)(2,1)} %get-tuple-element.140.a_ref.x1_own, bf16[304,1024]{1,0:T(8,128)(2,1)} %get-tuple-element.130.g_ref.x2_own, ...), custom_call_target="tpu_custom_call" | custom-call | flops 60000002048 | tf_op jit(solution)/shard_map/pallas_call | solution.py:693
  224.4 10.9 %shard_map.258 = (bf16[4,304,512]{2,1,0:T(8,128)(2,1)}, bf16[304,1024]{1,0:T(8,128)(2,1)}, bf16[4,304,512]{2,1,0:T(8,128)(2,1)}, f32[4,8,512]{2,1,0:T(8,128)}, bf16[304,1024]{1,0:T(8,128)(2,1)}) custom-call(bf16[304,1024]{1,0:T(8,128)(2,1)} %copy-done.24, bf16[304,1024]{1,0:T(8,128)(2,1)} %copy-done.19, bf16[2,2,4,528,512]{4,3,2,1,0:T(8,128)(2,1)} %bitcast.42), custom_call_target="tpu_custom_call" | custom-call | flops 60000002048 | tf_op jit(solution)/shard_map/pallas_call | solution.py:693
  236.8 12.3 %shard_map.262 = bf16[4,4,256,1024]{3,2,1,0:T(8,128)(2,1)} custom-call(s32[8]{0:T(128)} %stack.35.place, bf16[304,1024]{1,0:T(8,128)(2,1)} %get-tuple-element.140.a_ref.x1_own, bf16[304,1024]{1,0:T(8,128)(2,1)} %copy-done.24, bf16[4,304,512]{2,1,0:T(8,128)(2,1)} %get-tuple-element.153.y1_own, bf16[4,304,512]{2,1,0:T(8,128)(2,1)} %get-tuple-element.154.y1_far, ...), custom_call_target="tpu_custom_call" | custom-call | flops 71999995904 | tf_op jit(solution)/shard_map/pallas_call | solution.py:828
  249.2 2.6 collective-permute-done.20.far_ref
  252.5 5.1 shard_map.259
  259.2 11.5 %shard_map.260 = (bf16[4,304,384]{2,1,0:T(8,128)(2,1)}, f32[4,8,384]{2,1,0:T(8,128)}, bf16[304,1024]{1,0:T(8,128)(2,1)}) custom-call(s32[8]{0:T(128)} %stack.35.place, bf16[304,1024]{1,0:T(8,128)(2,1)} %get-tuple-element.148.g_ref.x2_own, bf16[4,304,384]{2,1,0:T(8,128)(2,1)} %get-tuple-element.149.qkv_ref, ...), custom_call_target="tpu_custom_call" | custom-call | flops 48000000000 | tf_op jit(solution)/shard_map/pallas_call | solution.py:560
  271.3 3.3 collective-permute-done.22.g_ref.x2_far
  275.4 11.0 %shard_map.264 = (bf16[4,304,384]{2,1,0:T(8,128)(2,1)}, f32[4,8,384]{2,1,0:T(8,128)}, bf16[304,1024]{1,0:T(8,128)(2,1)}) custom-call(s32[8]{0:T(128)} %stack.35.place, bf16[304,1024]{1,0:T(8,128)(2,1)} %copy-done.20, bf16[4,304,384]{2,1,0:T(8,128)(2,1)} %get-tuple-element.160.qkv_ref, bf16[4,3,224,112]{3,2,1,0:T(8,128)(2,1)} %get-tuple-element.161.probs_ref, ...), custom_call_target="tpu_custom_call" | custom-call | flops 48000000000 | tf_op jit(solution)/shard_map/pallas_call | solution.py:560
  286.4 1.9 collective-permute-start.23
  288.3 8.4 %shard_map.267 = bf16[2,4,256,512]{3,2,1,0:T(8,128)(2,1)} custom-call(s32[8]{0:T(128)} %stack.35.place, bf16[304,1024]{1,0:T(8,128)(2,1)} %get-tuple-element.136.a_ref.x1_own, bf16[304,1024]{1,0:T(8,128)(2,1)} %copy-done.13, bf16[4,304,384]{2,1,0:T(8,128)(2,1)} %get-tuple-element.151.y1_own, bf16[4,304,384]{2,1,0:T(8,128)(2,1)} %get-tuple-element.167.y1_far, ...), custom_call_target="tpu_custom_call" | custom-call | flops 32000000000 | tf_op jit(solution)/shard_map/pallas_call | solution.py:828
  296.8 3.7 shard_map.261
  301.4 5.0 shard_map.265
  307.6 7.5 %shard_map.266 = (bf16[4,304,512]{2,1,0:T(8,128)(2,1)}, f32[4,8,512]{2,1,0:T(8,128)}, bf16[304,1024]{1,0:T(8,128)(2,1)}) custom-call(bf16[304,1024]{1,0:T(8,128)(2,1)} %get-tuple-element.164.g_ref.x2_own, bf16[4,304,512]{2,1,0:T(8,128)(2,1)} %get-tuple-element.165.slope_ref, bf16[2,2,4,800,512]{4,3,2,1,0:T(8,128)(2,1)} %bitcast.39), custom_call_target="tpu_custom_call" | custom-call | flops 28000000000 | tf_op jit(solution)/shard_map/pallas_call | solution.py:720
  316.5 6.4 %shard_map.268 = bf16[4,256,512]{2,1,0:T(8,128)(2,1)} custom-call(s32[8]{0:T(128)} %stack.35.place, bf16[304,1024]{1,0:T(8,128)(2,1)} %get-tuple-element.136.a_ref.x1_own, bf16[304,1024]{1,0:T(8,128)(2,1)} %copy-done.13, bf16[4,304,384]{2,1,0:T(8,128)(2,1)} %get-tuple-element.151.y1_own, bf16[4,304,384]{2,1,0:T(8,128)(2,1)} %get-tuple-element.167.y1_far, ...), custom_call_target="tpu_custom_call" | custom-call | flops 20000000000 | tf_op jit(solution)/shard_map/pallas_call | solution.py:828
  323.9 7.5 %shard_map.269 = (bf16[4,304,512]{2,1,0:T(8,128)(2,1)}, f32[4,8,512]{2,1,0:T(8,128)}, bf16[304,1024]{1,0:T(8,128)(2,1)}) custom-call(bf16[304,1024]{1,0:T(8,128)(2,1)} %copy-done.14, bf16[4,304,512]{2,1,0:T(8,128)(2,1)} %get-tuple-element.171.slope_ref, bf16[2,2,4,800,512]{4,3,2,1,0:T(8,128)(2,1)} %bitcast.40), custom_call_target="tpu_custom_call" | custom-call | flops 28000000000 | tf_op jit(solution)/shard_map/pallas_call | solution.py:720
  332.4 10.0 %shard_map.273 = bf16[2,4,256,1024]{3,2,1,0:T(8,128)(2,1)} custom-call(s32[8]{0:T(128)} %stack.35.place, bf16[304,1024]{1,0:T(8,128)(2,1)} %get-tuple-element.131.a_ref.x1_own, bf16[304,1024]{1,0:T(8,128)(2,1)} %copy-done.12, bf16[4,304,512]{2,1,0:T(8,128)(2,1)} %get-tuple-element.179.y1_own, bf16[4,304,512]{2,1,0:T(8,128)(2,1)} %get-tuple-element.180.y1_far, ...), custom_call_target="tpu_custom_call" | custom-call | flops 40000000000 | tf_op jit(solution)/shard_map/pallas_call | solution.py:828
  342.5 4.8 collective-permute-done.26.far_ref
  348.1 5.1 shard_map.270
  354.6 2.3 reduce-scatter.5.cloned.1.call-done.refs_0_
  357.0 12.1 %shard_map.272 = (bf16[4,304,384]{2,1,0:T(8,128)(2,1)}, f32[4,8,384]{2,1,0:T(8,128)}, bf16[304,1024]{1,0:T(8,128)(2,1)}) custom-call(s32[8]{0:T(128)} %stack.35.place, bf16[304,1024]{1,0:T(8,128)(2,1)} %get-tuple-element.175.g_ref.x2_own, bf16[4,304,384]{2,1,0:T(8,128)(2,1)} %get-tuple-element.176.qkv_ref, ...), custom_call_target="tpu_custom_call" | custom-call | flops 48000000000 | tf_op jit(solution)/shard_map/pallas_call | solution.py:560
  370.0 6.4 %shard_map.271 = bf16[4,256,512]{2,1,0:T(8,128)(2,1)} custom-call(s32[8]{0:T(128)} %stack.35.place, bf16[304,1024]{1,0:T(8,128)(2,1)} %get-tuple-element.136.a_ref.x1_own, bf16[304,1024]{1,0:T(8,128)(2,1)} %copy-done.13, bf16[4,304,384]{2,1,0:T(8,128)(2,1)} %get-tuple-element.151.y1_own, bf16[4,304,384]{2,1,0:T(8,128)(2,1)} %get-tuple-element.167.y1_far, ...), custom_call_target="tpu_custom_call" | custom-call | flops 20000000000 | tf_op jit(solution)/shard_map/pallas_call | solution.py:828
  376.9 7.5 %shard_map.274 = bf16[4,256,1024]{2,1,0:T(8,128)(2,1)} custom-call(s32[8]{0:T(128)} %stack.35.place, bf16[304,1024]{1,0:T(8,128)(2,1)} %get-tuple-element.131.a_ref.x1_own, bf16[304,1024]{1,0:T(8,128)(2,1)} %copy-done.12, bf16[4,304,512]{2,1,0:T(8,128)(2,1)} %get-tuple-element.179.y1_own, bf16[4,304,512]{2,1,0:T(8,128)(2,1)} %get-tuple-element.180.y1_far, ...), custom_call_target="tpu_custom_call" | custom-call | flops 24000000000 | tf_op jit(solution)/shard_map/pallas_call | solution.py:828
  386.0 12.0 %shard_map.275 = (bf16[4,304,384]{2,1,0:T(8,128)(2,1)}, f32[4,8,384]{2,1,0:T(8,128)}, bf16[304,1024]{1,0:T(8,128)(2,1)}) custom-call(s32[8]{0:T(128)} %stack.35.place, bf16[304,1024]{1,0:T(8,128)(2,1)} %copy-done.15, bf16[4,304,384]{2,1,0:T(8,128)(2,1)} %get-tuple-element.184.qkv_ref, bf16[4,3,224,112]{3,2,1,0:T(8,128)(2,1)} %get-tuple-element.185.probs_ref, ...), custom_call_target="tpu_custom_call" | custom-call | flops 48000000000 | tf_op jit(solution)/shard_map/pallas_call | solution.py:560
  399.5 7.9 %shard_map.277 = bf16[2,4,256,512]{3,2,1,0:T(8,128)(2,1)} custom-call(s32[8]{0:T(128)} %stack.35.place, bf16[304,1024]{1,0:T(8,128)(2,1)} %get-tuple-element.124.a_ref.x1_own, bf16[304,1024]{1,0:T(8,128)(2,1)} %copy-done.11, bf16[4,304,384]{2,1,0:T(8,128)(2,1)} %get-tuple-element.188.y1_own, bf16[4,304,384]{2,1,0:T(8,128)(2,1)} %get-tuple-element.189.y1_far, ...), custom_call_target="tpu_custom_call" | custom-call | flops 32000000000 | tf_op jit(solution)/shard_map/pallas_call | solution.py:828
  407.5 5.5 collective-permute-done.30.far_ref
  413.8 5.0 shard_map.276
  424.6 6.3 %shard_map.278 = bf16[4,256,512]{2,1,0:T(8,128)(2,1)} custom-call(s32[8]{0:T(128)} %stack.35.place, bf16[304,1024]{1,0:T(8,128)(2,1)} %get-tuple-element.124.a_ref.x1_own, bf16[304,1024]{1,0:T(8,128)(2,1)} %copy-done.11, bf16[4,304,384]{2,1,0:T(8,128)(2,1)} %get-tuple-element.188.y1_own, bf16[4,304,384]{2,1,0:T(8,128)(2,1)} %get-tuple-element.189.y1_far, ...), custom_call_target="tpu_custom_call" | custom-call | flops 20000000000 | tf_op jit(solution)/shard_map/pallas_call | solution.py:828
  432.4 8.0 %shard_map.279 = bf16[4,256,1024]{2,1,0:T(8,128)(2,1)} custom-call(s32[8]{0:T(128)} %stack.35.place, bf16[304,1024]{1,0:T(8,128)(2,1)} %get-tuple-element.131.a_ref.x1_own, bf16[304,1024]{1,0:T(8,128)(2,1)} %copy-done.12, bf16[4,304,512]{2,1,0:T(8,128)(2,1)} %get-tuple-element.179.y1_own, bf16[4,304,512]{2,1,0:T(8,128)(2,1)} %get-tuple-element.180.y1_far, ...), custom_call_target="tpu_custom_call" | custom-call | flops 24000000000 | tf_op jit(solution)/shard_map/pallas_call | solution.py:828
  440.7 8.9 %shard_map.263 = bf16[1200,1024]{1,0:T(8,128)(2,1)} custom-call(s32[8]{0:T(128)} %stack.35.place, bf16[4,304,1024]{2,1,0:T(8,128)(2,1)} %bitcast.52), custom_call_target="tpu_custom_call" | custom-call | flops 35999997952 | tf_op jit(solution)/shard_map/pallas_call | solution.py:180
  449.6 12.5 %collective-permute-done.36.refs_3_ = bf16[304,1024]{1,0:T(8,128)(2,1)S(1)} collective-permute-done((bf16[304,1024]{1,0:T(8,128)(2,1)}, bf16[304,1024]{1,0:T(8,128)(2,1)S(1)}, u32[]{:S(2)}, u32[]{:S(2)}) %collective-permute-start.36) | collective-permute-done | bytes 622624 | tf_op jit(solution)/shard_map/ppermute | solution.py:984
  462.1 15.2 %collective-permute-done.31.refs_1_ = bf16[304,1024]{1,0:T(8,128)(2,1)S(1)} collective-permute-done((bf16[304,1024]{1,0:T(8,128)(2,1)}, bf16[304,1024]{1,0:T(8,128)(2,1)S(1)}, u32[]{:S(2)}, u32[]{:S(2)}) %collective-permute-start.31) | collective-permute-done | bytes 622624 | tf_op jit(solution)/shard_map/ppermute | solution.py:984
  478.3 6.4 %shard_map.280 = bf16[4,256,512]{2,1,0:T(8,128)(2,1)} custom-call(s32[8]{0:T(128)} %stack.35.place, bf16[304,1024]{1,0:T(8,128)(2,1)} %get-tuple-element.124.a_ref.x1_own, bf16[304,1024]{1,0:T(8,128)(2,1)} %copy-done.11, bf16[4,304,384]{2,1,0:T(8,128)(2,1)} %get-tuple-element.188.y1_own, bf16[4,304,384]{2,1,0:T(8,128)(2,1)} %get-tuple-element.189.y1_far, ...), custom_call_target="tpu_custom_call" | custom-call | flops 20000000000 | tf_op jit(solution)/shard_map/pallas_call | solution.py:828
  492.4 1.9 shard_map.287
  496.2 12.7 %collective-permute-start.40 = (f32[24,1024]{1,0:T(8,128)S(1)}, f32[24,1024]{1,0:T(8,128)S(1)}, u32[]{:S(2)}, u32[]{:S(2)}) collective-permute-start(f32[24,1024]{1,0:T(8,128)S(1)} %add.41), channel_id=1, source_target_pairs={{0,1},{1,0},{2,3},{3,2},{4,5},{5,4},{6,7},{7,6},{8,9},{9,8},{10,11... | collective-permute-start | bytes 294920 | tf_op jit(solution)/shard_map/ppermute | solution.py:1134
  508.9 18.2 %reduce-scatter.9.cloned.1.call-done.refs_0_ = bf16[256,1024]{1,0:T(8,128)(2,1)} async-done(((bf16[1024,1024]{1,0:T(8,128)(2,1)}), bf16[256,1024]{1,0:T(8,128)(2,1)}) %reduce-scatter.9.cloned.1.call-update) | async-done | bytes 524304 | tf_op jit(solution)/shard_map/reduce_scatter | solution.py:1065
  527.1 1.9 shard_map.285
  532.3 9.5 %shard_map.281 = f32[1200,1024]{1,0:T(8,128)} custom-call(s32[8]{0:T(128)} %stack.35.place, bf16[304,1024]{1,0:T(8,128)(2,1)} %get-tuple-element.187.refs_0_, bf16[304,1024]{1,0:T(8,128)(2,1)} %copy-done.18, bf16[304,1024]{1,0:T(8,128)(2,1)} %copy-done.17, bf16[304,1024]{1,0:T(8,128)(2,1)} %copy-done.16), custom_call_target="tpu_custom_call" | custom-call | flops 35999997952 | tf_op jit(solution)/shard_map/pallas_call | solution.py:180
  542.5 14.0 %reduce-scatter.7.cloned.1.call-done.refs_0_ = bf16[256,512]{1,0:T(8,128)(2,1)} async-done(((bf16[1024,512]{1,0:T(8,128)(2,1)}), bf16[256,512]{1,0:T(8,128)(2,1)}) %reduce-scatter.7.cloned.1.call-update) | async-done | bytes 262160 | tf_op jit(solution)/shard_map/reduce_scatter | solution.py:1065
  561.3 2.2 collective-permute-done.42.refs_1_
  564.1 3.3 shard_map.288
  (196 shorter events, 72.1 us)
Async XLA Ops:
  7.2 127.4 %all-gather.7.cloned.1.call-start = ((), (), s32[]{:S(2)}) async-start(), calls=%async_computation.8 | async-start | bytes 13926400 | tf_op jit(solution)/shard_map/all_gather | solution.py:1007
  7.9 10.4 %copy-start.2 = (f32[2,1024]{1,0:T(2,128)S(1)}, f32[2,1024]{1,0:T(2,128)}, u32[]{:S(2)}) copy-start(f32[2,1024]{1,0:T(2,128)} %param.17) | copy-start | bytes 24580
  11.5 201.2 %all-gather.9.cloned.1.call-start = ((), (), s32[]{:S(2)}) async-start(), calls=%async_computation.9 | async-start | bytes 9191424 | tf_op jit(solution)/shard_map/all_gather | solution.py:1007
  11.6 12.8 %collective-permute-start.8 = (bf16[272,512]{1,0:T(8,128)(2,1)}, bf16[272,512]{1,0:T(8,128)(2,1)S(1)}, u32[]{:S(2)}, u32[]{:S(2)}) collective-permute-start(bf16[272,512]{1,0:T(8,128)(2,1)} %get-tuple-element.125), channel_id=1, source_target_pairs={{0,3},{1,0},{2,1},{3,2},{4,7},{5,4},{6,5},{7,6},{8,11},{9,8},{10,9... | collective-permute-start | bytes 835592 | tf_op jit(solution)/shard_map/ppermute | solution.py:984
  16.7 41.0 %collective-permute-start.4 = (bf16[272,512]{1,0:T(8,128)(2,1)}, bf16[272,512]{1,0:T(8,128)(2,1)S(1)}, u32[]{:S(2)}, u32[]{:S(2)}) collective-permute-start(bf16[272,512]{1,0:T(8,128)(2,1)} %get-tuple-element.125), channel_id=1, source_target_pairs={{0,2},{1,3},{2,0},{3,1},{4,6},{5,7},{6,4},{7,5},{8,10},{9,11},{10,... | collective-permute-start | bytes 835592 | tf_op jit(solution)/shard_map/ppermute | solution.py:984
  16.7 41.0 %collective-permute-start = (bf16[272,512]{1,0:T(8,128)(2,1)}, bf16[272,512]{1,0:T(8,128)(2,1)S(1)}, u32[]{:S(2)}, u32[]{:S(2)}) collective-permute-start(bf16[272,512]{1,0:T(8,128)(2,1)} %get-tuple-element.125), channel_id=1, source_target_pairs={{0,1},{1,2},{2,3},{3,0},{4,5},{5,6},{6,7},{7,4},{8,9},{9,10},{10,1... | collective-permute-start | bytes 835592 | tf_op jit(solution)/shard_map/ppermute | solution.py:984
  24.4 34.9 %collective-permute-start.10 = (bf16[272,512]{1,0:T(8,128)(2,1)S(1)}, bf16[272,512]{1,0:T(8,128)(2,1)S(1)}, u32[]{:S(2)}, u32[]{:S(2)}) collective-permute-start(bf16[272,512]{1,0:T(8,128)(2,1)S(1)} %collective-permute-done.8.refs_8_), channel_id=1, source_target_pairs={{0,4},{4,0},{1,5},{5,1},{2,6},{6,2},{3,7},{7,3},{8,12},{12,8},{9,1... | collective-permute-start | bytes 835592 | tf_op jit(solution)/shard_map/ppermute | solution.py:981
  28.5 47.1 %collective-permute-start.12 = (bf16[304,1024]{1,0:T(8,128)(2,1)}, bf16[304,1024]{1,0:T(8,128)(2,1)S(1)}, u32[]{:S(2)}, u32[]{:S(2)}) collective-permute-start(bf16[304,1024]{1,0:T(8,128)(2,1)} %get-tuple-element.124.a_ref.x1_own), channel_id=1, source_target_pairs={{0,8},{8,0},{1,9},{9,1},{2,10},{10,2},{3,11},{11,3},{4,12},{12,4},... | collective-permute-start | bytes 1867784 | tf_op jit(solution)/shard_map/ppermute | solution.py:981
  29.7 327.2 %reduce-scatter.5.cloned.1.call-start = ((), (), s32[]{:S(2)}) async-start(), calls=%async_computation.4 | async-start | bytes 8912896 | tf_op jit(solution)/shard_map/reduce_scatter | solution.py:1075
  29.8 34.0 %collective-permute-start.9 = (bf16[272,512]{1,0:T(8,128)(2,1)S(1)}, bf16[272,512]{1,0:T(8,128)(2,1)S(1)}, u32[]{:S(2)}, u32[]{:S(2)}) collective-permute-start(bf16[272,512]{1,0:T(8,128)(2,1)S(1)} %collective-permute-done.8.refs_8_), channel_id=1, source_target_pairs={{0,16},{16,0},{1,17},{17,1},{2,18},{18,2},{3,19},{19,3},{4,20},{20... | collective-permute-start | bytes 835592 | tf_op jit(solution)/shard_map/ppermute | solution.py:981
  57.7 6.2 %collective-permute-start.6 = (bf16[272,512]{1,0:T(8,128)(2,1)S(1)}, bf16[272,512]{1,0:T(8,128)(2,1)S(1)}, u32[]{:S(2)}, u32[]{:S(2)}) collective-permute-start(bf16[272,512]{1,0:T(8,128)(2,1)S(1)} %collective-permute-done.4.refs_4_), channel_id=1, source_target_pairs={{0,4},{4,0},{1,5},{5,1},{2,6},{6,2},{3,7},{7,3},{8,12},{12,8},{9,1... | collective-permute-start | bytes 835592 | tf_op jit(solution)/shard_map/ppermute | solution.py:981
  57.7 9.5 %collective-permute-start.5 = (bf16[272,512]{1,0:T(8,128)(2,1)S(1)}, bf16[272,512]{1,0:T(8,128)(2,1)S(1)}, u32[]{:S(2)}, u32[]{:S(2)}) collective-permute-start(bf16[272,512]{1,0:T(8,128)(2,1)S(1)} %collective-permute-done.4.refs_4_), channel_id=1, source_target_pairs={{0,16},{16,0},{1,17},{17,1},{2,18},{18,2},{3,19},{19,3},{4,20},{20... | collective-permute-start | bytes 835592 | tf_op jit(solution)/shard_map/ppermute | solution.py:981
  59.3 13.5 %collective-permute-start.1 = (bf16[272,512]{1,0:T(8,128)(2,1)S(1)}, bf16[272,512]{1,0:T(8,128)(2,1)S(1)}, u32[]{:S(2)}, u32[]{:S(2)}) collective-permute-start(bf16[272,512]{1,0:T(8,128)(2,1)S(1)} %collective-permute-done.refs_0_), channel_id=1, source_target_pairs={{0,16},{16,0},{1,17},{17,1},{2,18},{18,2},{3,19},{19,3},{4,20},{20... | collective-permute-start | bytes 835592 | tf_op jit(solution)/shard_map/ppermute | solution.py:981
  59.8 13.0 %copy-start.3 = (f32[2,1024]{1,0:T(2,128)S(1)}, f32[2,1024]{1,0:T(2,128)}, u32[]{:S(2)}) copy-start(f32[2,1024]{1,0:T(2,128)} %param.22) | copy-start | bytes 24580
  59.8 13.6 %copy-start.5 = (f32[2,1024]{1,0:T(2,128)S(1)}, f32[2,1024]{1,0:T(2,128)}, u32[]{:S(2)}) copy-start(f32[2,1024]{1,0:T(2,128)} %param.23) | copy-start | bytes 24580
  59.8 13.6 %copy-start.6 = (f32[2,1024]{1,0:T(2,128)S(1)}, f32[2,1024]{1,0:T(2,128)}, u32[]{:S(2)}) copy-start(f32[2,1024]{1,0:T(2,128)} %param.21) | copy-start | bytes 24580
  63.9 11.8 %copy-start.34 = (bf16[272,512]{1,0:T(8,128)(2,1)}, bf16[272,512]{1,0:T(8,128)(2,1)S(1)}, u32[]{:S(2)}) copy-start(bf16[272,512]{1,0:T(8,128)(2,1)S(1)} %collective-permute-done.9.refs_9_) | copy-start | bytes 835588
  63.9 10.2 %collective-permute-start.2 = (bf16[272,512]{1,0:T(8,128)(2,1)S(1)}, bf16[272,512]{1,0:T(8,128)(2,1)S(1)}, u32[]{:S(2)}, u32[]{:S(2)}) collective-permute-start(bf16[272,512]{1,0:T(8,128)(2,1)S(1)} %collective-permute-done.refs_0_), channel_id=1, source_target_pairs={{0,4},{4,0},{1,5},{5,1},{2,6},{6,2},{3,7},{7,3},{8,12},{12,8},{9,1... | collective-permute-start | bytes 835592 | tf_op jit(solution)/shard_map/ppermute | solution.py:981
  64.0 11.7 %copy-start.35 = (bf16[272,512]{1,0:T(8,128)(2,1)}, bf16[272,512]{1,0:T(8,128)(2,1)S(1)}, u32[]{:S(2)}) copy-start(bf16[272,512]{1,0:T(8,128)(2,1)S(1)} %collective-permute-done.6.refs_6_) | copy-start | bytes 835588
  64.0 11.7 %collective-permute-start.11 = (bf16[272,512]{1,0:T(8,128)(2,1)S(1)}, bf16[272,512]{1,0:T(8,128)(2,1)S(1)}, u32[]{:S(2)}, u32[]{:S(2)}) collective-permute-start(bf16[272,512]{1,0:T(8,128)(2,1)S(1)} %collective-permute-done.9.refs_9_), channel_id=1, source_target_pairs={{0,4},{4,0},{1,5},{5,1},{2,6},{6,2},{3,7},{7,3},{8,12},{12,8},{9,1... | collective-permute-start | bytes 835592 | tf_op jit(solution)/shard_map/ppermute | solution.py:981
  67.3 8.4 %collective-permute-start.7 = (bf16[272,512]{1,0:T(8,128)(2,1)S(1)}, bf16[272,512]{1,0:T(8,128)(2,1)S(1)}, u32[]{:S(2)}, u32[]{:S(2)}) collective-permute-start(bf16[272,512]{1,0:T(8,128)(2,1)S(1)} %collective-permute-done.5.refs_5_), channel_id=1, source_target_pairs={{0,4},{4,0},{1,5},{5,1},{2,6},{6,2},{3,7},{7,3},{8,12},{12,8},{9,1... | collective-permute-start | bytes 835592 | tf_op jit(solution)/shard_map/ppermute | solution.py:981
  72.8 2.9 collective-permute-start.3
  74.1 37.1 %collective-permute-start.14 = (bf16[304,1024]{1,0:T(8,128)(2,1)}, bf16[304,1024]{1,0:T(8,128)(2,1)S(1)}, u32[]{:S(2)}, u32[]{:S(2)}) collective-permute-start(bf16[304,1024]{1,0:T(8,128)(2,1)} %get-tuple-element.130.g_ref.x2_own), channel_id=1, source_target_pairs={{0,8},{8,0},{1,9},{9,1},{2,10},{10,2},{3,11},{11,3},{4,12},{12,4},... | collective-permute-start | bytes 1867784 | tf_op jit(solution)/shard_map/ppermute | solution.py:981
  86.4 17.6 %collective-permute-start.13 = (bf16[304,1024]{1,0:T(8,128)(2,1)}, bf16[304,1024]{1,0:T(8,128)(2,1)S(1)}, u32[]{:S(2)}, u32[]{:S(2)}) collective-permute-start(bf16[304,1024]{1,0:T(8,128)(2,1)} %get-tuple-element.127), channel_id=1, source_target_pairs={{0,8},{8,0},{1,9},{9,1},{2,10},{10,2},{3,11},{11,3},{4,12},{12,4},... | collective-permute-start | bytes 1867784 | tf_op jit(solution)/shard_map/ppermute | solution.py:981
  109.0 16.0 %collective-permute-start.15 = (bf16[304,1024]{1,0:T(8,128)(2,1)}, bf16[304,1024]{1,0:T(8,128)(2,1)S(1)}, u32[]{:S(2)}, u32[]{:S(2)}) collective-permute-start(bf16[304,1024]{1,0:T(8,128)(2,1)} %get-tuple-element.131.a_ref.x1_own), channel_id=1, source_target_pairs={{0,8},{8,0},{1,9},{9,1},{2,10},{10,2},{3,11},{11,3},{4,12},{12,4},... | collective-permute-start | bytes 1867784 | tf_op jit(solution)/shard_map/ppermute | solution.py:981
  111.2 32.0 %copy-start.19 = (bf16[304,1024]{1,0:T(8,128)(2,1)}, bf16[304,1024]{1,0:T(8,128)(2,1)S(1)}, u32[]{:S(2)}) copy-start(bf16[304,1024]{1,0:T(8,128)(2,1)S(1)} %collective-permute-done.14.g_ref.x2_far) | copy-start | bytes 1867780
  143.2 16.5 %collective-permute-start.16 = (bf16[304,1024]{1,0:T(8,128)(2,1)}, bf16[304,1024]{1,0:T(8,128)(2,1)S(1)}, u32[]{:S(2)}, u32[]{:S(2)}) collective-permute-start(bf16[304,1024]{1,0:T(8,128)(2,1)} %get-tuple-element.134), channel_id=1, source_target_pairs={{0,8},{8,0},{1,9},{9,1},{2,10},{10,2},{3,11},{11,3},{4,12},{12,4},... | collective-permute-start | bytes 1867784 | tf_op jit(solution)/shard_map/ppermute | solution.py:981
  164.6 15.8 %collective-permute-start.17 = (bf16[304,1024]{1,0:T(8,128)(2,1)}, bf16[304,1024]{1,0:T(8,128)(2,1)S(1)}, u32[]{:S(2)}, u32[]{:S(2)}) collective-permute-start(bf16[304,1024]{1,0:T(8,128)(2,1)} %get-tuple-element.136.a_ref.x1_own), channel_id=1, source_target_pairs={{0,8},{8,0},{1,9},{9,1},{2,10},{10,2},{3,11},{11,3},{4,12},{12,4},... | collective-permute-start | bytes 1867784 | tf_op jit(solution)/shard_map/ppermute | solution.py:981
  189.2 14.9 %collective-permute-start.18 = (bf16[304,1024]{1,0:T(8,128)(2,1)}, bf16[304,1024]{1,0:T(8,128)(2,1)S(1)}, u32[]{:S(2)}, u32[]{:S(2)}) collective-permute-start(bf16[304,1024]{1,0:T(8,128)(2,1)} %get-tuple-element.138), channel_id=1, source_target_pairs={{0,8},{8,0},{1,9},{9,1},{2,10},{10,2},{3,11},{11,3},{4,12},{12,4},... | collective-permute-start | bytes 1867784 | tf_op jit(solution)/shard_map/ppermute | solution.py:981
  209.2 14.3 %collective-permute-start.19 = (bf16[304,1024]{1,0:T(8,128)(2,1)}, bf16[304,1024]{1,0:T(8,128)(2,1)S(1)}, u32[]{:S(2)}, u32[]{:S(2)}) collective-permute-start(bf16[304,1024]{1,0:T(8,128)(2,1)} %get-tuple-element.140.a_ref.x1_own), channel_id=1, source_target_pairs={{0,8},{8,0},{1,9},{9,1},{2,10},{10,2},{3,11},{11,3},{4,12},{12,4},... | collective-permute-start | bytes 1867784 | tf_op jit(solution)/shard_map/ppermute | solution.py:981
  235.3 16.5 %collective-permute-start.20 = (bf16[304,1024]{1,0:T(8,128)(2,1)}, bf16[304,1024]{1,0:T(8,128)(2,1)S(1)}, u32[]{:S(2)}, u32[]{:S(2)}) collective-permute-start(bf16[304,1024]{1,0:T(8,128)(2,1)} %get-tuple-element.147), channel_id=1, source_target_pairs={{0,8},{8,0},{1,9},{9,1},{2,10},{10,2},{3,11},{11,3},{4,12},{12,4},... | collective-permute-start | bytes 1867784 | tf_op jit(solution)/shard_map/ppermute | solution.py:981
  249.1 191.6 %all-gather.11.cloned.1.call-start = ((), (), s32[]{:S(2)}) async-start(), calls=%async_computation.10 | async-start | bytes 3112960 | tf_op jit(solution)/shard_map/all_gather | solution.py:1116
  257.7 16.9 %collective-permute-start.22 = (bf16[304,1024]{1,0:T(8,128)(2,1)}, bf16[304,1024]{1,0:T(8,128)(2,1)S(1)}, u32[]{:S(2)}, u32[]{:S(2)}) collective-permute-start(bf16[304,1024]{1,0:T(8,128)(2,1)} %get-tuple-element.148.g_ref.x2_own), channel_id=1, source_target_pairs={{0,8},{8,0},{1,9},{9,1},{2,10},{10,2},{3,11},{11,3},{4,12},{12,4},... | collective-permute-start | bytes 1867784 | tf_op jit(solution)/shard_map/ppermute | solution.py:981
  259.2 11.5 %copy-start.21 = (bf16[304,1024]{1,0:T(8,128)(2,1)S(1)}, bf16[304,1024]{1,0:T(8,128)(2,1)}, u32[]{:S(2)}) copy-start(bf16[304,1024]{1,0:T(8,128)(2,1)} %get-tuple-element.152) | copy-start | bytes 1867780
  270.7 26.0 %collective-permute-start.21 = (bf16[304,1024]{1,0:T(8,128)(2,1)S(1)}, bf16[304,1024]{1,0:T(8,128)(2,1)}, u32[]{:S(2)}, u32[]{:S(2)}) collective-permute-start(bf16[304,1024]{1,0:T(8,128)(2,1)S(1)} %copy-done.21), channel_id=1, source_target_pairs={{0,8},{8,0},{1,9},{9,1},{2,10},{10,2},{3,11},{11,3},{4,12},{12,4},... | collective-permute-start | bytes 1867784 | tf_op jit(solution)/shard_map/ppermute | solution.py:981
  286.4 14.2 %collective-permute-start.23 = (bf16[304,1024]{1,0:T(8,128)(2,1)}, bf16[304,1024]{1,0:T(8,128)(2,1)S(1)}, u32[]{:S(2)}, u32[]{:S(2)}) collective-permute-start(bf16[304,1024]{1,0:T(8,128)(2,1)} %get-tuple-element.162), channel_id=1, source_target_pairs={{0,8},{8,0},{1,9},{9,1},{2,10},{10,2},{3,11},{11,3},{4,12},{12,4},... | collective-permute-start | bytes 1867784 | tf_op jit(solution)/shard_map/ppermute | solution.py:981
  296.7 18.5 %collective-permute-start.25 = (bf16[2,4,256,512]{3,2,1,0:T(8,128)(2,1)}, bf16[2,4,256,512]{3,2,1,0:T(8,128)(2,1)S(1)}, u32[]{:S(2)}, u32[]{:S(2)}) collective-permute-start(bf16[2,4,256,512]{3,2,1,0:T(8,128)(2,1)} %shard_map.267), channel_id=1, source_target_pairs={{0,4},{4,0},{1,5},{5,1},{2,6},{6,2},{3,7},{7,3},{8,12},{12,8},{9,1... | collective-permute-start | bytes 6291464 | tf_op jit(solution)/shard_map/ppermute | solution.py:981
  306.4 16.7 %collective-permute-start.24 = (bf16[304,1024]{1,0:T(8,128)(2,1)}, bf16[304,1024]{1,0:T(8,128)(2,1)S(1)}, u32[]{:S(2)}, u32[]{:S(2)}) collective-permute-start(bf16[304,1024]{1,0:T(8,128)(2,1)} %get-tuple-element.164.g_ref.x2_own), channel_id=1, source_target_pairs={{0,8},{8,0},{1,9},{9,1},{2,10},{10,2},{3,11},{11,3},{4,12},{12,4},... | collective-permute-start | bytes 1867784 | tf_op jit(solution)/shard_map/ppermute | solution.py:981
  322.9 46.2 %collective-permute-start.27 = (bf16[4,256,512]{2,1,0:T(8,128)(2,1)}, bf16[4,256,512]{2,1,0:T(8,128)(2,1)S(1)}, u32[]{:S(2)}, u32[]{:S(2)}) collective-permute-start(bf16[4,256,512]{2,1,0:T(8,128)(2,1)} %shard_map.268), channel_id=1, source_target_pairs={{0,16},{16,0},{1,17},{17,1},{2,18},{18,2},{3,19},{19,3},{4,20},{20... | collective-permute-start | bytes 3145736 | tf_op jit(solution)/shard_map/ppermute | solution.py:981
  331.4 15.9 %collective-permute-start.26 = (bf16[304,1024]{1,0:T(8,128)(2,1)}, bf16[304,1024]{1,0:T(8,128)(2,1)S(1)}, u32[]{:S(2)}, u32[]{:S(2)}) collective-permute-start(bf16[304,1024]{1,0:T(8,128)(2,1)} %get-tuple-element.172), channel_id=1, source_target_pairs={{0,8},{8,0},{1,9},{9,1},{2,10},{10,2},{3,11},{11,3},{4,12},{12,4},... | collective-permute-start | bytes 1867784 | tf_op jit(solution)/shard_map/ppermute | solution.py:981
  342.4 34.5 %collective-permute-start.29 = (bf16[2,4,256,1024]{3,2,1,0:T(8,128)(2,1)}, bf16[2,4,256,1024]{3,2,1,0:T(8,128)(2,1)}, u32[]{:S(2)}, u32[]{:S(2)}) collective-permute-start(bf16[2,4,256,1024]{3,2,1,0:T(8,128)(2,1)} %shard_map.273), channel_id=1, source_target_pairs={{0,4},{4,0},{1,5},{5,1},{2,6},{6,2},{3,7},{7,3},{8,12},{12,8},{9,1... | collective-permute-start | bytes 12582920 | tf_op jit(solution)/shard_map/ppermute | solution.py:981
  353.2 31.9 %collective-permute-start.28 = (bf16[304,1024]{1,0:T(8,128)(2,1)}, bf16[304,1024]{1,0:T(8,128)(2,1)S(1)}, u32[]{:S(2)}, u32[]{:S(2)}) collective-permute-start(bf16[304,1024]{1,0:T(8,128)(2,1)} %get-tuple-element.175.g_ref.x2_own), channel_id=1, source_target_pairs={{0,8},{8,0},{1,9},{9,1},{2,10},{10,2},{3,11},{11,3},{4,12},{12,4},... | collective-permute-start | bytes 1867784 | tf_op jit(solution)/shard_map/ppermute | solution.py:981
  356.9 130.4 %reduce-scatter.11.cloned.1.call-start = ((), (), s32[]{:S(2)}) async-start(), calls=%async_computation.7 | async-start | bytes 1310720 | tf_op jit(solution)/shard_map/reduce_scatter | solution.py:1065
  376.5 150.6 %reduce-scatter.9.cloned.1.call-start = ((), (), s32[]{:S(2)}) async-start(), calls=%async_computation.6 | async-start | bytes 2621440 | tf_op jit(solution)/shard_map/reduce_scatter | solution.py:1065
  384.5 48.0 %collective-permute-start.34 = (bf16[4,256,1024]{2,1,0:T(8,128)(2,1)}, bf16[4,256,1024]{2,1,0:T(8,128)(2,1)}, u32[]{:S(2)}, u32[]{:S(2)}) collective-permute-start(bf16[4,256,1024]{2,1,0:T(8,128)(2,1)} %shard_map.274), channel_id=1, source_target_pairs={{0,16},{16,0},{1,17},{17,1},{2,18},{18,2},{3,19},{19,3},{4,20},{20... | collective-permute-start | bytes 6291464 | tf_op jit(solution)/shard_map/ppermute | solution.py:981
  398.0 15.0 %collective-permute-start.30 = (bf16[304,1024]{1,0:T(8,128)(2,1)}, bf16[304,1024]{1,0:T(8,128)(2,1)S(1)}, u32[]{:S(2)}, u32[]{:S(2)}) collective-permute-start(bf16[304,1024]{1,0:T(8,128)(2,1)} %get-tuple-element.186), channel_id=1, source_target_pairs={{0,8},{8,0},{1,9},{9,1},{2,10},{10,2},{3,11},{11,3},{4,12},{12,4},... | collective-permute-start | bytes 1867784 | tf_op jit(solution)/shard_map/ppermute | solution.py:981
  407.4 15.8 %collective-permute-start.32 = (bf16[2,4,256,512]{3,2,1,0:T(8,128)(2,1)}, bf16[2,4,256,512]{3,2,1,0:T(8,128)(2,1)S(1)}, u32[]{:S(2)}, u32[]{:S(2)}) collective-permute-start(bf16[2,4,256,512]{3,2,1,0:T(8,128)(2,1)} %shard_map.277), channel_id=1, source_target_pairs={{0,4},{4,0},{1,5},{5,1},{2,6},{6,2},{3,7},{7,3},{8,12},{12,8},{9,1... | collective-permute-start | bytes 6291464 | tf_op jit(solution)/shard_map/ppermute | solution.py:981
  418.9 43.2 %collective-permute-start.36 = (bf16[304,1024]{1,0:T(8,128)(2,1)}, bf16[304,1024]{1,0:T(8,128)(2,1)S(1)}, u32[]{:S(2)}, u32[]{:S(2)}) collective-permute-start(bf16[304,1024]{1,0:T(8,128)(2,1)} %get-tuple-element.187.refs_0_), channel_id=1, source_target_pairs={{0,2},{1,3},{2,0},{3,1},{4,6},{5,7},{6,4},{7,5},{8,10},{9,11},{10,... | collective-permute-start | bytes 1867784 | tf_op jit(solution)/shard_map/ppermute | solution.py:984
  419.4 42.7 %collective-permute-start.35 = (bf16[304,1024]{1,0:T(8,128)(2,1)}, bf16[304,1024]{1,0:T(8,128)(2,1)S(1)}, u32[]{:S(2)}, u32[]{:S(2)}) collective-permute-start(bf16[304,1024]{1,0:T(8,128)(2,1)} %get-tuple-element.187.refs_0_), channel_id=1, source_target_pairs={{0,3},{1,0},{2,1},{3,2},{4,7},{5,4},{6,5},{7,6},{8,11},{9,8},{10,9... | collective-permute-start | bytes 1867784 | tf_op jit(solution)/shard_map/ppermute | solution.py:984
  420.7 56.6 %collective-permute-start.31 = (bf16[304,1024]{1,0:T(8,128)(2,1)}, bf16[304,1024]{1,0:T(8,128)(2,1)S(1)}, u32[]{:S(2)}, u32[]{:S(2)}) collective-permute-start(bf16[304,1024]{1,0:T(8,128)(2,1)} %get-tuple-element.187.refs_0_), channel_id=1, source_target_pairs={{0,1},{1,2},{2,3},{3,0},{4,5},{5,6},{6,7},{7,4},{8,9},{9,10},{10,1... | collective-permute-start | bytes 1867784 | tf_op jit(solution)/shard_map/ppermute | solution.py:984
  430.9 46.4 %collective-permute-start.33 = (bf16[4,256,512]{2,1,0:T(8,128)(2,1)}, bf16[4,256,512]{2,1,0:T(8,128)(2,1)S(1)}, u32[]{:S(2)}, u32[]{:S(2)}) collective-permute-start(bf16[4,256,512]{2,1,0:T(8,128)(2,1)} %shard_map.278), channel_id=1, source_target_pairs={{0,16},{16,0},{1,17},{17,1},{2,18},{18,2},{3,19},{19,3},{4,20},{20... | collective-permute-start | bytes 3145736 | tf_op jit(solution)/shard_map/ppermute | solution.py:981
  440.4 116.1 %reduce-scatter.7.cloned.1.call-start = ((), (), s32[]{:S(2)}) async-start(), calls=%async_computation.5 | async-start | bytes 1310720 | tf_op jit(solution)/shard_map/reduce_scatter | solution.py:1065
  449.6 35.2 %copy-start = (f32[24,1024]{1,0:T(8,128)S(1)}, f32[24,1024]{1,0:T(8,128)}, u32[]{:S(2)}) copy-start(f32[24,1024]{1,0:T(8,128)} %shard_map.282) | copy-start | bytes 294916
  462.1 22.7 %copy-start.16 = (bf16[304,1024]{1,0:T(8,128)(2,1)}, bf16[304,1024]{1,0:T(8,128)(2,1)S(1)}, u32[]{:S(2)}) copy-start(bf16[304,1024]{1,0:T(8,128)(2,1)S(1)} %collective-permute-done.36.refs_3_) | copy-start | bytes 1867780
  462.1 22.7 %copy-start.17 = (bf16[304,1024]{1,0:T(8,128)(2,1)}, bf16[304,1024]{1,0:T(8,128)(2,1)S(1)}, u32[]{:S(2)}) copy-start(bf16[304,1024]{1,0:T(8,128)(2,1)S(1)} %collective-permute-done.35.refs_2_) | copy-start | bytes 1867780
  484.8 1.4 collective-permute-start.37
  486.2 4.9 collective-permute-start.38
  489.1 72.2 %collective-permute-start.44 = (bf16[128,512]{1,0:T(8,128)(2,1)}, bf16[128,512]{1,0:T(8,128)(2,1)S(1)}, u32[]{:S(2)}, u32[]{:S(2)}) collective-permute-start(bf16[128,512]{1,0:T(8,128)(2,1)} %get-tuple-element.219), channel_id=1, source_target_pairs={{0,8},{8,0},{1,9},{9,1},{2,10},{10,2},{3,11},{11,3},{4,12},{12,4},... | collective-permute-start | bytes 393224 | tf_op jit(solution)/shard_map/ppermute | solution.py:981
  491.1 5.1 collective-permute-start.39
  494.3 66.9 %collective-permute-start.45 = (bf16[128,1024]{1,0:T(8,128)(2,1)}, bf16[128,1024]{1,0:T(8,128)(2,1)S(1)}, u32[]{:S(2)}, u32[]{:S(2)}) collective-permute-start(bf16[128,1024]{1,0:T(8,128)(2,1)} %get-tuple-element.221), channel_id=1, source_target_pairs={{0,8},{8,0},{1,9},{9,1},{2,10},{10,2},{3,11},{11,3},{4,12},{12,4},... | collective-permute-start | bytes 786440 | tf_op jit(solution)/shard_map/ppermute | solution.py:981
  496.2 34.3 %collective-permute-start.40 = (f32[24,1024]{1,0:T(8,128)S(1)}, f32[24,1024]{1,0:T(8,128)S(1)}, u32[]{:S(2)}, u32[]{:S(2)}) collective-permute-start(f32[24,1024]{1,0:T(8,128)S(1)} %add.41), channel_id=1, source_target_pairs={{0,1},{1,0},{2,3},{3,2},{4,5},{5,4},{6,7},{7,6},{8,9},{9,8},{10,11... | collective-permute-start | bytes 294920 | tf_op jit(solution)/shard_map/ppermute | solution.py:1134
  529.0 32.2 %collective-permute-start.43 = (bf16[128,1024]{1,0:T(8,128)(2,1)}, bf16[128,1024]{1,0:T(8,128)(2,1)S(1)}, u32[]{:S(2)}, u32[]{:S(2)}) collective-permute-start(bf16[128,1024]{1,0:T(8,128)(2,1)} %get-tuple-element.217), channel_id=1, source_target_pairs={{0,8},{8,0},{1,9},{9,1},{2,10},{10,2},{3,11},{11,3},{4,12},{12,4},... | collective-permute-start | bytes 786440 | tf_op jit(solution)/shard_map/ppermute | solution.py:981
  530.5 11.3 %collective-permute-start.41 = (f32[24,1024]{1,0:T(8,128)S(1)}, f32[24,1024]{1,0:T(8,128)S(1)}, u32[]{:S(2)}, u32[]{:S(2)}) collective-permute-start(f32[24,1024]{1,0:T(8,128)S(1)} %add.42), channel_id=1, source_target_pairs={{0,2},{1,3},{2,0},{3,1},{4,6},{5,7},{6,4},{7,5},{8,10},{9,11},{10,... | collective-permute-start | bytes 294920 | tf_op jit(solution)/shard_map/ppermute | solution.py:1134
  558.2 5.3 collective-permute-start.42
  (35 other events, 93.1 us)
Sparse Core Ops, SparseCore 0:
  11.7 122.9 all-gather.6
  136.9 75.7 all-gather.8
  249.2 107.6 reduce-scatter.4
  358.3 51.0 all-gather.10
  411.5 66.9 reduce-scatter.10
  480.8 46.2 reduce-scatter.8
  530.6 25.8 reduce-scatter.6
